TPU v7x, 32 devices: a whole 2x2x4 slice. The times are simulated.
32 devices in a mesh: groups: 2 (over y), seq: 8 (over z, x), head: 2 (over core).
Axes of the slice: x: 2, y: 2, z: 4, core: 2. Of those that a mesh axis runs over, the one named last changes fastest.
Arguments:
- queries: bfloat16 [2048, 64, 128], P(('groups', 'seq'), 'head'), parts along dimension 0, may hold values from -200 to 200
- keys: bfloat16 [2048, 8, 128], P(('groups', 'seq'), 'head'), parts along dimension 0, may hold values from -6 to 6
- values: bfloat16 [2048, 8, 128], P(('groups', 'seq'), 'head'), parts along dimension 0, may hold values from -6 to 6
- chosen: int32 [16, 4], P('groups'), parts along dimension 0, may hold values from -1 to 7, as said below
Outputs:
- attended: bfloat16 [2048, 64, 128], P(('groups', 'seq'), 'head'), parts along dimension 0
There are 2 independent parts, one for each index of `groups`. A program takes and returns all parts, laid end to end along the dimension named above; each array names one. Nothing has to cross between parts.
Inputs may be any that keep to these rules, and one draw needn't show every extreme that they name: `chosen`: row b lists block b itself and min(3, b) distinct earlier blocks, in any order; its other entries are -1.
All inputs are finite; a program needn't handle non-finite values.
Results may differ from a plain program's by a relative error of at most 0.0033.
Values may be sent and summed in bfloat16 or wider, within the bound.
No kernel may reach another device: no remote copies, remote signals or barrier semaphores. Data moves between devices by JAX's collectives and lax.ppermute only.
A program may use at most 64 MiB of HBM per device.

v0:
```python
import jax
import jax.numpy as jnp
from jax import lax
from jax.sharding import PartitionSpec as P


def partial_block(grouped, key_block, value_block, slot_code, score_scale):
    scores = (
        jnp.einsum("qkgd,jkd->kgqj", grouped, key_block, preferred_element_type=jnp.float32)
        * score_scale
    )
    query_rows = jnp.arange(grouped.shape[0])[:, None]
    key_rows = jnp.arange(key_block.shape[0])[None, :]
    allowed = (slot_code == 0) | (slot_code == 1) & (key_rows <= query_rows)
    maxima = jnp.max(jnp.where(allowed, scores, -1e30), axis=-1)
    probs = jnp.where(allowed, jnp.exp(scores - maxima[..., None]), 0.0).astype(jnp.bfloat16)
    totals = jnp.sum(probs.astype(jnp.float32), axis=-1)
    partial_value = jnp.einsum(
        "kgqj,jkd->qkgd", probs, value_block, preferred_element_type=jnp.float32
    )
    return (partial_value, maxima, totals)


def per_device(queries, keys, values, chosen):
    members = lax.axis_size("seq")
    block_rows, heads_dev, head_dim = queries.shape
    kv_dev = keys.shape[1]
    group_size = heads_dev // kv_dev
    piece_rows = block_rows // members
    score_scale = head_dim ** (-0.5)
    grouped = queries.reshape(block_rows, kv_dev, group_size, head_dim)
    stacked = jnp.stack([keys, values]).reshape(2, members, piece_rows, kv_dev, head_dim)
    relayed = lax.all_to_all(stacked, "seq", split_axis=1, concat_axis=1, tiled=True)
    targets = jnp.arange(members, dtype=jnp.int32)
    slot_codes = jnp.where(chosen < 0, 2, jnp.where(chosen == targets[:, None], 1, 0))
    picked = jnp.take(relayed, jnp.maximum(chosen, 0), axis=1)
    slot_flags = slot_codes.astype(jnp.bfloat16)[None, :, :, None]
    blocks = lax.all_to_all(picked, "seq", split_axis=1, concat_axis=3, tiled=True)
    flags_in = lax.all_to_all(slot_flags, "seq", split_axis=1, concat_axis=3, tiled=True)
    codes_in = flags_in[0, 0, :, 0].astype(jnp.int32)

    def one_slot(element):
        return partial_block(grouped, element[0], element[1], element[2], score_scale)

    partial_value, maxima, totals = lax.map(one_slot, (blocks[0, 0], blocks[1, 0], codes_in))
    top = jnp.max(maxima, axis=0)
    weights = jnp.exp(maxima - top)
    denominator = jnp.sum(weights * totals, axis=0)
    numerator = jnp.sum(jnp.transpose(weights, (0, 3, 1, 2))[..., None] * partial_value, axis=0)
    merged = numerator / jnp.transpose(denominator, (2, 0, 1))[..., None]
    return merged.reshape(block_rows, heads_dev, head_dim).astype(jnp.bfloat16)


def solution(mesh):
    in_specs = (
        P(("groups", "seq"), "head", None),
        P(("groups", "seq"), "head", None),
        P(("groups", "seq"), "head", None),
        P("groups", None),
    )
    out_specs = P(("groups", "seq"), "head", None)
    return jax.shard_map(
        per_device, mesh=mesh, in_specs=in_specs, out_specs=out_specs, check_vma=False
    )
```

profile of v0, /device:TPU:0, one launch (start us, length us, event | category | flops | bytes accessed | tf_op | source)
XLA Modules:
  0.0 85.9 jit_solution(6183416869920625072)
XLA Ops:
  0.0 0.0 copy-start.1
  0.0 0.9 %copy.38 = bf16[128,4,128]{2,0,1:T(8,128)(2,1)S(1)} copy(bf16[128,4,128]{2,1,0:T(4,128)(2,1)} %param.7) | data formatting | bytes 262144 | tf_op args[1]
  0.9 0.9 %copy.39 = bf16[128,4,128]{2,0,1:T(8,128)(2,1)S(1)} copy(bf16[128,4,128]{2,1,0:T(4,128)(2,1)} %param.8) | data formatting | bytes 262144 | tf_op args[2]
  1.9 0.7 copy.40
  2.6 7.3 %all-to-all-start = ((bf16[2,8,16,4,128]{4,2,3,0,1:T(8,128)(2,1)}), bf16[2,8,16,4,128]{4,2,3,0,1:T(8,128)(2,1)S(1)}, u32[]{:S(2)}, u32[]{:S(2)}) async-start(bf16[2,8,16,4,128]{4,2,3,0,1:T(8,128)(2,1)} %copy.40), calls=%async_computation | async-start | bytes 524288 | tf_op jit(solution)/shard_map/all_to_all | solution.py:33
  9.9 0.0 copy-done.1
  9.9 0.1 copy.41
  10.0 0.1 reshape.35
  10.1 0.1 copy.37
  10.2 0.7 copy.44
  10.9 7.9 %all-to-all-done = bf16[2,8,16,4,128]{4,2,3,0,1:T(8,128)(2,1)S(1)} async-done(((bf16[2,8,16,4,128]{4,2,3,0,1:T(8,128)(2,1)}), bf16[2,8,16,4,128]{4,2,3,0,1:T(8,128)(2,1)S(1)}, u32[]{:S(2)}, u32[]{:S(2)}) %all-to-all-start) | async-done | bytes 262176 | tf_op jit(solution)/shard_map/all_to_all | solution.py:33
  18.8 3.6 %all-to-all-start.2 = ((bf16[1,8,4,1]{2,3,0,1:T(2,128)(2,1)}), bf16[1,8,4,1]{2,3,0,1:T(2,128)(2,1)S(1)}, u32[]{:S(2)}, u32[]{:S(2)}) async-start(bf16[1,8,4,1]{2,3,0,1:T(2,128)(2,1)} %copy.44), calls=%async_computation.2 | async-start | bytes 8192 | tf_op jit(solution)/shard_map/all_to_all | solution.py:39
  22.4 0.7 gather_fusion
  23.2 0.0 copy-start
  23.2 1.1 %select_bitcast_fusion = bf16[2,8,4,16,4,128]{5,3,4,0,2,1:T(8,128)(2,1)} fusion(bf16[8,4,2,16,4,128]{5,3,4,2,1,0:T(8,128)(2,1)S(1)} %bitcast.87, pred[8,4]{1,0:T(8,128)(4,1)S(1)} %copy.37), kind=kLoop, calls=%fused_computation.25 | loop fusion | flops 524288 | bytes 2097184 | tf_op jit(solution)/shard_map/jit(_take)/select_n | solution.py:36
  24.3 4.5 %all-to-all-done.2 = bf16[1,8,4,1]{2,3,0,1:T(2,128)(2,1)S(1)} async-done(((bf16[1,8,4,1]{2,3,0,1:T(2,128)(2,1)}), bf16[1,8,4,1]{2,3,0,1:T(2,128)(2,1)S(1)}, u32[]{:S(2)}, u32[]{:S(2)}) %all-to-all-start.2) | async-done | bytes 96 | tf_op jit(solution)/shard_map/all_to_all | solution.py:39
  28.9 3.6 %all-to-all-start.1 = ((bf16[2,8,4,16,4,128]{5,3,4,0,2,1:T(8,128)(2,1)}), bf16[2,8,4,16,4,128]{5,3,4,0,2,1:T(8,128)(2,1)S(1)}, u32[]{:S(2)}, u32[]{:S(2)}) async-start(bf16[2,8,4,16,4,128]{5,3,4,0,2,1:T(8,128)(2,1)} %select_bitcast_fusion), calls=%async_computation.1 | async-start | bytes 2097152 | tf_op jit(solution)/shard_map/all_to_all | solution.py:38
  32.5 0.0 copy-done
  32.5 0.4 copy.47
  32.9 0.1 copy.45
  33.0 0.1 convert_reduce_fusion.1
  33.1 23.7 %all-to-all-done.1 = bf16[2,8,4,16,4,128]{5,3,4,0,2,1:T(8,128)(2,1)S(1)} async-done(((bf16[2,8,4,16,4,128]{5,3,4,0,2,1:T(8,128)(2,1)}), bf16[2,8,4,16,4,128]{5,3,4,0,2,1:T(8,128)(2,1)S(1)}, u32[]{:S(2)}, u32[]{:S(2)}) %all-to-all-start.1) | async-done | bytes 1048608 | tf_op jit(solution)/shard_map/all_to_all | solution.py:38
  56.8 0.2 fusion.18
  57.2 18.9 %while.14 = (s32[]{:T(128)}, f32[4,128,4,8,128]{1,4,3,2,0:T(8,128)}, f32[4,4,8,128]{3,2,1,0:T(8,128)S(1)}, f32[4,4,8,128]{3,2,1,0:T(8,128)S(1)}, bf16[4,128,4,12...) while((s32[]{:T(128)}, ...), condition=%wide.region_3.4_spmd, body=%wide.region_0.3_spmd.sunk | while | flops 275292160 | bytes 9897109 | solution.py:45
  57.2 0.6 dynamic_slice.26
  59.1 0.5 fusion.29
  59.5 1.9 %bitcast_dynamic-update-slice_fusion.5 = f32[4,128,4,8,128]{1,4,3,2,0:T(8,128)} fusion(f32[4,128,4,8,128]{1,4,3,2,0:T(8,128)} %get-tuple-element.179, s32[]{:T(128)} %get-tuple-element.178, bf16[4,128,4,128]{3,1,2,0:T(8,128)(2,1)S(1)} %get-tuple-element.193, f32[4,128,128,8]{2,1,3,0:T(8,128)S(1)} %get-tuple-element.163, ...), kind=kOutput, calls=%fused_computation.1.clone.1 | convolution fusion | flops 136314880 | bytes 4359168 | tf_op jit(solution)/shard_map/while/body/eval_jaxpr/kgqj,jkd->qkgd/dot_general | solution.py:18
  61.4 0.5 convert_reduce_fusion.3
  61.9 0.6 dynamic_slice.26
  63.8 0.5 fusion.29
  64.3 1.8 %bitcast_dynamic-update-slice_fusion.5 = f32[4,128,4,8,128]{1,4,3,2,0:T(8,128)} fusion(f32[4,128,4,8,128]{1,4,3,2,0:T(8,128)} %get-tuple-element.179, s32[]{:T(128)} %get-tuple-element.178, bf16[4,128,4,128]{3,1,2,0:T(8,128)(2,1)S(1)} %get-tuple-element.193, f32[4,128,128,8]{2,1,3,0:T(8,128)S(1)} %get-tuple-element.163, ...), kind=kOutput, calls=%fused_computation.1.clone.1 | convolution fusion | flops 136314880 | bytes 4359168 | tf_op jit(solution)/shard_map/while/body/eval_jaxpr/kgqj,jkd->qkgd/dot_general | solution.py:18
  66.1 0.5 convert_reduce_fusion.3
  66.6 0.6 dynamic_slice.26
  68.5 0.5 fusion.29
  69.0 1.9 %bitcast_dynamic-update-slice_fusion.5 = f32[4,128,4,8,128]{1,4,3,2,0:T(8,128)} fusion(f32[4,128,4,8,128]{1,4,3,2,0:T(8,128)} %get-tuple-element.179, s32[]{:T(128)} %get-tuple-element.178, bf16[4,128,4,128]{3,1,2,0:T(8,128)(2,1)S(1)} %get-tuple-element.193, f32[4,128,128,8]{2,1,3,0:T(8,128)S(1)} %get-tuple-element.163, ...), kind=kOutput, calls=%fused_computation.1.clone.1 | convolution fusion | flops 136314880 | bytes 4359168 | tf_op jit(solution)/shard_map/while/body/eval_jaxpr/kgqj,jkd->qkgd/dot_general | solution.py:18
  70.9 0.5 convert_reduce_fusion.3
  71.4 0.6 dynamic_slice.26
  73.3 0.5 fusion.29
  73.7 1.9 %bitcast_dynamic-update-slice_fusion.5 = f32[4,128,4,8,128]{1,4,3,2,0:T(8,128)} fusion(f32[4,128,4,8,128]{1,4,3,2,0:T(8,128)} %get-tuple-element.179, s32[]{:T(128)} %get-tuple-element.178, bf16[4,128,4,128]{3,1,2,0:T(8,128)(2,1)S(1)} %get-tuple-element.193, f32[4,128,128,8]{2,1,3,0:T(8,128)S(1)} %get-tuple-element.163, ...), kind=kOutput, calls=%fused_computation.1.clone.1 | convolution fusion | flops 136314880 | bytes 4359168 | tf_op jit(solution)/shard_map/while/body/eval_jaxpr/kgqj,jkd->qkgd/dot_general | solution.py:18
  75.6 0.5 convert_reduce_fusion.3
  76.1 4.9 %multiply_reduce_fusion = f32[128,4,8,128]{0,3,2,1:T(8,128)S(1)} fusion(f32[4,128,4,8,128]{1,4,3,2,0:T(8,128)} %get-tuple-element.50, f32[4,128,4,8]{1,3,2,0:T(8,128)S(1)} %get-tuple-element.107), kind=kLoop, calls=%fused_computation.23 | loop fusion | flops 3670016 | bytes 10551296 | tf_op jit(solution)/shard_map/reduce_sum | solution.py:49
  81.0 2.1 %copy.50 = f32[128,32,128]{2,1,0:T(8,128)} copy(f32[128,32,128]{0,2,1:T(8,128)S(1)} %bitcast.85) | data formatting | bytes 4194304 | tf_op jit(solution)/shard_map/reduce_sum | solution.py:49
  83.1 0.1 copy.49
  83.2 2.7 %divide_convert_fusion = bf16[128,32,128]{2,1,0:T(8,128)(2,1)} fusion(f32[128,32,128]{2,1,0:T(8,128)} %copy.50, f32[128,32]{1,0:T(8,128)S(1)} %copy.49), kind=kLoop, calls=%fused_computation.24 | loop fusion | flops 1048576 | bytes 3162112 | tf_op jit(solution)/shard_map/convert_element_type | solution.py:51
  (20 shorter events, 0.3 us)
Async XLA Ops:
  0.0 9.9 %copy-start.1 = (s32[8,4]{0,1:T(4,128)S(1)}, s32[8,4]{0,1:T(4,128)}, u32[]{:S(2)}) copy-start(s32[8,4]{0,1:T(4,128)} %param.9) | copy-start | bytes 388
  2.6 16.2 %all-to-all-start = ((bf16[2,8,16,4,128]{4,2,3,0,1:T(8,128)(2,1)}), bf16[2,8,16,4,128]{4,2,3,0,1:T(8,128)(2,1)S(1)}, u32[]{:S(2)}, u32[]{:S(2)}) async-start(bf16[2,8,16,4,128]{4,2,3,0,1:T(8,128)(2,1)} %copy.40), calls=%async_computation | async-start | bytes 524288 | tf_op jit(solution)/shard_map/all_to_all | solution.py:33
  18.8 10.1 %all-to-all-start.2 = ((bf16[1,8,4,1]{2,3,0,1:T(2,128)(2,1)}), bf16[1,8,4,1]{2,3,0,1:T(2,128)(2,1)S(1)}, u32[]{:S(2)}, u32[]{:S(2)}) async-start(bf16[1,8,4,1]{2,3,0,1:T(2,128)(2,1)} %copy.44), calls=%async_computation.2 | async-start | bytes 8192 | tf_op jit(solution)/shard_map/all_to_all | solution.py:39
  23.2 9.3 %copy-start = (bf16[128,32,128]{2,1,0:T(8,128)(2,1)S(1)}, bf16[128,32,128]{2,1,0:T(8,128)(2,1)}, u32[]{:S(2)}) copy-start(bf16[128,32,128]{2,1,0:T(8,128)(2,1)} %param.6) | copy-start | bytes 3145732
  28.9 27.9 %all-to-all-start.1 = ((bf16[2,8,4,16,4,128]{5,3,4,0,2,1:T(8,128)(2,1)}), bf16[2,8,4,16,4,128]{5,3,4,0,2,1:T(8,128)(2,1)S(1)}, u32[]{:S(2)}, u32[]{:S(2)}) async-start(bf16[2,8,4,16,4,128]{5,3,4,0,2,1:T(8,128)(2,1)} %select_bitcast_fusion), calls=%async_computation.1 | async-start | bytes 2097152 | tf_op jit(solution)/shard_map/all_to_all | solution.py:38
where the time goes:
time: 86.4 us; the launch traced here: 85.9 us
  waiting for transfers between devices  36.2 us (42%)
  starting transfers between devices  14.4 us (17%)
  other arithmetic  10.9 us (13%)
  local copies, waits for them, and re-layouts  9.69 us (11%)
  matrix products  9.24 us (11%)
  loops' own time  5.35 us (6%)
    all_to_all x1, waiting for transfers between devices, per_device(): lax.all_to_all(picked, 'seq', split_axis=1, concat_axis=3, tiled=True)  23.7 us
    all_to_all x1, waiting for transfers between devices, per_device(): lax.all_to_all(stacked, 'seq', split_axis=1, concat_axis=1, tiled=True)  7.93 us
    dot_general x4, matrix products, partial_block(): jnp.einsum('kgqj,jkd->qkgd', probs, value_block, preferred_element_type=j...  7.41 us
    all_to_all x1, starting transfers between devices, per_device(): lax.all_to_all(stacked, 'seq', split_axis=1, concat_axis=1, tiled=True)  7.25 us
    another operation x1, loops' own time, per_device(): lax.map(one_slot, (blocks[0, 0], blocks[1, 0], codes_in))  5.35 us
    reduce_sum x1, other arithmetic, per_device(): jnp.sum(jnp.transpose(weights, (0, 3, 1, 2))[..., None] * partial_value,...  4.87 us
    all_to_all x1, waiting for transfers between devices, per_device(): lax.all_to_all(slot_flags, 'seq', split_axis=1, concat_axis=3, tiled=True)  4.54 us
    all_to_all x1, starting transfers between devices, per_device(): lax.all_to_all(slot_flags, 'seq', split_axis=1, concat_axis=3, tiled=True)  3.59 us
  transfers between devices with their start and end apart: 3, of which 3 were waited for; matrix products, arithmetic and copies ran while one was open for 4% of the time, Pallas kernels for 0%

commit v1 on v0

v1 whole, which is shorter than its diff:
```python
import functools
import math

import jax
import jax.numpy as jnp
from jax import lax
from jax.experimental import pallas as pl
from jax.experimental.pallas import tpu as pltpu
from jax.sharding import PartitionSpec as P

NO_KEY = -1e30
ROW_CHUNK = 256


def attend_kernel(
    listed_ref, q_ref, k_own_ref, v_own_ref, k_all_ref, v_all_ref, out_ref,
    k_buf, v_buf, k_wide, v_wide, sems, *, kv_dev, slots,
):
    tokens, heads, dim = q_ref.shape
    group = heads // kv_dev
    block = tokens * kv_dev
    target = listed_ref[slots]
    own_at = jnp.int32(0)
    for j in range(slots):
        own_at = jnp.where(listed_ref[j] == target, j, own_at)
    copies = []
    bias = []
    for j in range(slots - 1):
        source = listed_ref[jnp.where(j >= own_at, j + 1, j)]
        bias.append(jnp.where(source < 0, NO_KEY, 0.0).astype(jnp.float32))
        begin = pl.multiple_of(jnp.maximum(source, 0) * block, block)
        for n, (whole, buf) in enumerate(((k_all_ref, k_buf), (v_all_ref, v_buf))):
            copy = pltpu.make_async_copy(
                whole.at[pl.ds(begin, block), :],
                buf.at[pl.ds(j * block, block), :],
                sems.at[n, j],
            )
            copy.start()
            copies.append(copy)
    k_wide[pl.ds(0, block), :] = k_own_ref[...].astype(jnp.float32)
    v_wide[pl.ds(0, block), :] = v_own_ref[...].astype(jnp.float32)
    for copy in copies:
        copy.wait()
    rest = (slots - 1) * block
    k_wide[pl.ds(block, rest), :] = k_buf[...].astype(jnp.float32)
    v_wide[pl.ds(block, rest), :] = v_buf[...].astype(jnp.float32)

    factor = dim ** (-0.5) * math.log2(math.e)
    keys = slots * tokens
    ones = jnp.ones((keys, dim), jnp.bfloat16)
    chunk_tokens = ROW_CHUNK // group
    for h in range(kv_dev):
        k_h = k_wide[pl.ds(h, keys, stride=kv_dev), :].astype(jnp.bfloat16)
        v_h = v_wide[pl.ds(h, keys, stride=kv_dev), :].astype(jnp.bfloat16)
        v_ones = jnp.concatenate([v_h, ones], axis=1)
        for first in range(0, tokens, chunk_tokens):
            q = q_ref[pl.ds(first, chunk_tokens), pl.ds(h * group, group), :]
            q = q.astype(jnp.float32).reshape(ROW_CHUNK, dim).astype(jnp.bfloat16)
            s = lax.dot_general(
                q, k_h, (((1,), (1,)), ((), ())), preferred_element_type=jnp.float32
            )
            row = lax.broadcasted_iota(jnp.int32, (ROW_CHUNK, tokens), 0) // group + first
            key = lax.broadcasted_iota(jnp.int32, (ROW_CHUNK, tokens), 1)
            parts = [jnp.where(key <= row, s[:, :tokens], NO_KEY)]
            for j in range(1, slots):
                parts.append(s[:, j * tokens : (j + 1) * tokens] + bias[j - 1])
            top = parts[0]
            for part in parts[1:]:
                top = jnp.maximum(top, part)
            top = jnp.max(top, axis=1, keepdims=True)
            probs = jnp.concatenate(
                [jnp.exp2((part - top) * factor).astype(jnp.bfloat16) for part in parts], axis=1
            )
            both = jnp.dot(probs, v_ones, preferred_element_type=jnp.float32)
            merged = both[:, :dim] / both[:, dim:]
            out_ref[pl.ds(first, chunk_tokens), pl.ds(h * group, group), :] = (
                merged.reshape(chunk_tokens, group, dim).astype(jnp.bfloat16)
            )


def attend(listed, queries, k_own, v_own, k_all, v_all, kv_dev, slots):
    block, dim = k_own.shape
    rest = (slots - 1) * block
    vmem = pl.BlockSpec(memory_space=pltpu.VMEM)
    hbm = pl.BlockSpec(memory_space=pl.ANY)
    return pl.pallas_call(
        functools.partial(attend_kernel, kv_dev=kv_dev, slots=slots),
        out_shape=jax.ShapeDtypeStruct(queries.shape, jnp.bfloat16),
        in_specs=[pl.BlockSpec(memory_space=pltpu.SMEM), vmem, vmem, vmem, hbm, hbm],
        out_specs=vmem,
        scratch_shapes=[
            pltpu.VMEM((rest, dim), jnp.bfloat16),
            pltpu.VMEM((rest, dim), jnp.bfloat16),
            pltpu.VMEM((slots * block, dim), jnp.float32),
            pltpu.VMEM((slots * block, dim), jnp.float32),
            pltpu.SemaphoreType.DMA((2, slots - 1)),
        ],
        compiler_params=pltpu.CompilerParams(vmem_limit_bytes=32 * 2**20),
        name="attend",
    )(listed, queries, k_own, v_own, k_all, v_all)


def per_device(queries, keys, values, chosen):
    tokens, kv_dev, dim = keys.shape
    slots = chosen.shape[1]
    target = lax.axis_index("seq").astype(jnp.int32)
    listed = jnp.concatenate([lax.dynamic_index_in_dim(chosen, target, 0, False), target[None]])
    k_own = keys.reshape(tokens * kv_dev, dim)
    v_own = values.reshape(tokens * kv_dev, dim)
    k_all = lax.all_gather(k_own, "seq", axis=0, tiled=True)
    v_all = lax.all_gather(v_own, "seq", axis=0, tiled=True)
    return attend(listed, queries, k_own, v_own, k_all, v_all, kv_dev, slots)


def solution(mesh):
    rows = P(("groups", "seq"), "head", None)
    return jax.shard_map(
        per_device,
        mesh=mesh,
        in_specs=(rows, rows, rows, P("groups", None)),
        out_specs=rows,
        check_vma=False,
    )
```

time: 86.4 us -> 110 us (1.27)
  waiting for transfers between devices: 36.2 us -> 86.5 us
  starting transfers between devices: 14.4 us -> 0.04 us
  between operations: 0.15 us -> 13.4 us
  other arithmetic: 10.9 us -> 0.08 us
  matrix products: 9.24 us -> 0 us
  local copies, waits for them, and re-layouts: 9.69 us -> 3.87 us
  Pallas kernels: 0 us -> 5.53 us
  loops' own time: 5.35 us -> 0 us
    all_gather x0 -> x2, waiting for transfers between devices: none -> 85.1 us  [the longest x1 44.1 us: per_device(): k_all = lax.all_gather(k_own, 'seq', axis=0, tiled=True)]
    all_to_all x3 -> x0, waiting for transfers between devices: 36.2 us -> none  [the longest x1 23.7 us: per_device(): lax.all_to_all(picked, 'seq', split_axis=1, concat_axis=3, tiled=True)]
    all_to_all x3 -> x0, starting transfers between devices: 14.4 us -> none  [the longest x1 7.25 us: per_device(): lax.all_to_all(stacked, 'seq', split_axis=1, concat_axis=1, tiled=True)]
    dot_general x8 -> x0, matrix products: 9.24 us -> none  [the longest x4 7.41 us: partial_block(): jnp.einsum('kgqj,jkd->qkgd', probs, value_block, preferred_element_type=j...]
    reduce_sum x6 -> x0, other arithmetic: 6.76 us -> none  [the longest x1 4.87 us: per_device(): jnp.sum(jnp.transpose(weights, (0, 3, 1, 2))[..., None] * partial_value,...]
    pallas_call x0 -> x1, Pallas kernels: none -> 5.53 us  [attend(): pl.pallas_call(functools.partial(attend_kernel, kv_dev=kv_dev, slots=slot...]
    another operation x1 -> x0, loops' own time: 5.35 us -> none  [per_device(): lax.map(one_slot, (blocks[0, 0], blocks[1, 0], codes_in))]
    convert_element_type x2 -> x0, other arithmetic: 2.84 us -> none  [the longest x1 2.73 us: per_device(): return merged.reshape(block_rows, heads_dev, head_dim).astype(jnp.bfloat16)]
  transfers between devices with their start and end apart: 3 -> 2, of which waited for: 3 -> 2; matrix products, arithmetic and copies ran while one was open for 4% -> 0% of each run, Pallas kernels for 0% -> 0%
where the time goes in v1:
time: 110 us
  waiting for transfers between devices  86.5 us (79%)
  between operations  13.4 us (12%)
  Pallas kernels  5.53 us (5%)
  local copies, waits for them, and re-layouts  3.87 us (4%)
    all_gather x1, waiting for transfers between devices, per_device(): k_all = lax.all_gather(k_own, 'seq', axis=0, tiled=True)  44.1 us
    all_gather x1, waiting for transfers between devices, per_device(): v_all = lax.all_gather(v_own, 'seq', axis=0, tiled=True)  41.1 us
    pallas_call x1, Pallas kernels, attend(): pl.pallas_call(functools.partial(attend_kernel, kv_dev=kv_dev, slots=slot...  5.53 us
    unnamed x12, local copies, waits for them, and re-layouts  3.69 us
  transfers between devices with their start and end apart: 2, of which 2 were waited for; matrix products, arithmetic and copies ran while one was open for 0% of the time, Pallas kernels for 0%

profile of v1, /device:TPU:0, one launch (start us, length us, event | category | flops | bytes accessed | tf_op | source)
XLA Modules:
  0.0 109.5 jit_solution(8546923162399411991)
XLA Ops:
  6.5 0.0 copy-start
  6.5 0.0 all-gather.3.cloned.1.call-start
  6.5 0.0 copy-start.4
  6.5 0.0 copy-start.5
  6.5 0.7 all-gather.3.cloned.1.call-update
  7.3 0.0 all-gather.5.cloned.1.call-start
  7.3 0.7 all-gather.5.cloned.1.call-update
  8.0 0.0 copy-done
  8.0 0.2 dynamic-slice_reduce_fusion
  8.2 0.1 pad_add_fusion.listed_ref
  8.3 44.1 %all-gather.3.cloned.1.call-done.k_all_ref = bf16[4096,128]{1,0:T(8,128)(2,1)} async-done(((bf16[512,128]{1,0:T(8,128)(2,1)}), bf16[4096,128]{1,0:T(8,128)(2,1)}) %all-gather.3.cloned.1.call-update) | async-done | bytes 1048592 | tf_op jit(solution)/shard_map/all_gather | solution.py:110
  52.4 41.1 %all-gather.5.cloned.1.call-done.v_all_ref = bf16[4096,128]{1,0:T(8,128)(2,1)} async-done(((bf16[512,128]{1,0:T(8,128)(2,1)}), bf16[4096,128]{1,0:T(8,128)(2,1)}) %all-gather.5.cloned.1.call-update) | async-done | bytes 1048592 | tf_op jit(solution)/shard_map/all_gather | solution.py:111
  93.4 0.0 copy-done.4
  93.4 0.0 copy-done.5
  93.4 0.0 copy-start.1
  93.4 1.2 %copy-done.1 = bf16[128,32,128]{2,1,0:T(8,128)(2,1)S(1)} copy-done((bf16[128,32,128]{2,1,0:T(8,128)(2,1)S(1)}, bf16[128,32,128]{2,1,0:T(8,128)(2,1)}, u32[]{:S(2)}) %copy-start.1) | copy-done | bytes 1048600
  94.7 0.0 copy-start.2
  94.7 1.2 %copy-done.2 = bf16[4096,128]{1,0:T(8,128)(2,1)S(1)} copy-done((bf16[4096,128]{1,0:T(8,128)(2,1)S(1)}, bf16[4096,128]{1,0:T(8,128)(2,1)}, u32[]{:S(2)}) %copy-start.2) | copy-done | bytes 1048600
  95.9 0.0 copy-start.3
  95.9 1.2 %copy-done.3 = bf16[4096,128]{1,0:T(8,128)(2,1)S(1)} copy-done((bf16[4096,128]{1,0:T(8,128)(2,1)S(1)}, bf16[4096,128]{1,0:T(8,128)(2,1)}, u32[]{:S(2)}) %copy-start.3) | copy-done | bytes 1048600
  97.1 5.5 %attend.1 = bf16[128,32,128]{2,1,0:T(8,128)(2,1)} custom-call(s32[5]{0:T(128)S(1)} %pad_add_fusion.listed_ref, bf16[128,32,128]{2,1,0:T(8,128)(2,1)S(1)} %copy-done.1, bf16[512,128]{1,0:T(8,128)(2,1)S(1)} %bitcast.4, bf16[512,128]{1,0:T(8,128)(2,1)S(1)} %bitcast.6, bf16[4096,128]{1,0:T(8,128)(2,1)S(1)} %copy-done.2, bf16[4096,128]{1,0:T(8,128)(2,1)S(1)} %copy-done.3), custom_call_target="tpu_custom_call" | custom-call | tf_op jit(solution)/shard_map/attend/pallas_call | solution.py:86
Async XLA Ops:
  6.5 1.5 %copy-start = (s32[8,4]{0,1:T(4,128)S(1)}, s32[8,4]{0,1:T(4,128)}, u32[]{:S(2)}) copy-start(s32[8,4]{0,1:T(4,128)} %param.7) | copy-start | bytes 388
  6.5 45.8 %all-gather.3.cloned.1.call-start = ((), (), s32[]{:S(2)}) async-start(), calls=%async_computation | async-start | bytes 1179648 | tf_op jit(solution)/shard_map/all_gather | solution.py:110
  6.5 86.9 %copy-start.4 = (bf16[128,4,128]{2,1,0:T(4,128)(2,1)S(1)}, bf16[128,4,128]{2,1,0:T(4,128)(2,1)}, u32[]{:S(2)}) copy-start(bf16[128,4,128]{2,1,0:T(4,128)(2,1)} %param.5) | copy-start | bytes 393220
  6.5 86.9 %copy-start.5 = (bf16[128,4,128]{2,1,0:T(4,128)(2,1)S(1)}, bf16[128,4,128]{2,1,0:T(4,128)(2,1)}, u32[]{:S(2)}) copy-start(bf16[128,4,128]{2,1,0:T(4,128)(2,1)} %param.6) | copy-start | bytes 393220
  7.3 86.2 %all-gather.5.cloned.1.call-start = ((), (), s32[]{:S(2)}) async-start(), calls=%async_computation.1 | async-start | bytes 1179648 | tf_op jit(solution)/shard_map/all_gather | solution.py:111
  93.4 1.2 %copy-start.1 = (bf16[128,32,128]{2,1,0:T(8,128)(2,1)S(1)}, bf16[128,32,128]{2,1,0:T(8,128)(2,1)}, u32[]{:S(2)}) copy-start(bf16[128,32,128]{2,1,0:T(8,128)(2,1)} %q_ref.1) | copy-start | bytes 3145732
  94.7 1.2 %copy-start.2 = (bf16[4096,128]{1,0:T(8,128)(2,1)S(1)}, bf16[4096,128]{1,0:T(8,128)(2,1)}, u32[]{:S(2)}) copy-start(bf16[4096,128]{1,0:T(8,128)(2,1)} %all-gather.3.cloned.1.call-done.k_all_ref) | copy-start | bytes 3145732
  95.9 1.2 %copy-start.3 = (bf16[4096,128]{1,0:T(8,128)(2,1)S(1)}, bf16[4096,128]{1,0:T(8,128)(2,1)}, u32[]{:S(2)}) copy-start(bf16[4096,128]{1,0:T(8,128)(2,1)} %all-gather.5.cloned.1.call-done.v_all_ref) | copy-start | bytes 3145732
Sparse Core Ops, SparseCore 0:
  9.5 42.8 all-gather.2
  54.5 38.8 all-gather.4

commit v2 on v1

--- a/solution.py
+++ b/solution.py
@@ -10,37 +10,38 @@
 
 NO_KEY = -1e30
 ROW_CHUNK = 256
+PAIR = 2
+MOST_CLIMBED = 16
 
 
 def attend_kernel(
-    listed_ref, q_ref, k_own_ref, v_own_ref, k_all_ref, v_all_ref, out_ref,
-    k_buf, v_buf, k_wide, v_wide, sems, *, kv_dev, slots,
+    listed_ref, q_ref, k_own_ref, v_own_ref, *refs, kv_dev, slots, choices,
 ):
+    k_refs, v_refs = refs[:choices], refs[choices : 2 * choices]
+    out_ref, k_buf, v_buf, k_wide, v_wide, sems = refs[2 * choices :]
     tokens, heads, dim = q_ref.shape
     group = heads // kv_dev
     block = tokens * kv_dev
-    target = listed_ref[slots]
-    own_at = jnp.int32(0)
-    for j in range(slots):
-        own_at = jnp.where(listed_ref[j] == target, j, own_at)
-    copies = []
     bias = []
     for j in range(slots - 1):
-        source = listed_ref[jnp.where(j >= own_at, j + 1, j)]
+        source = listed_ref[j]
         bias.append(jnp.where(source < 0, NO_KEY, 0.0).astype(jnp.float32))
-        begin = pl.multiple_of(jnp.maximum(source, 0) * block, block)
-        for n, (whole, buf) in enumerate(((k_all_ref, k_buf), (v_all_ref, v_buf))):
-            copy = pltpu.make_async_copy(
-                whole.at[pl.ds(begin, block), :],
-                buf.at[pl.ds(j * block, block), :],
-                sems.at[n, j],
-            )
-            copy.start()
-            copies.append(copy)
+        for i in range(choices):
+
+            @pl.when(jnp.maximum(source, 0) == i)
+            def _start(i=i, j=j):
+                for n, (parts, buf) in enumerate(((k_refs, k_buf), (v_refs, v_buf))):
+                    pltpu.make_async_copy(
+                        parts[i], buf.at[pl.ds(j * block, block), :], sems.at[n, j]
+                    ).start()
+
     k_wide[pl.ds(0, block), :] = k_own_ref[...].astype(jnp.float32)
     v_wide[pl.ds(0, block), :] = v_own_ref[...].astype(jnp.float32)
-    for copy in copies:
-        copy.wait()
+    for j in range(slots - 1):
+        for n, (parts, buf) in enumerate(((k_refs, k_buf), (v_refs, v_buf))):
+            pltpu.make_async_copy(
+                parts[0], buf.at[pl.ds(j * block, block), :], sems.at[n, j]
+            ).wait()
     rest = (slots - 1) * block
     k_wide[pl.ds(block, rest), :] = k_buf[...].astype(jnp.float32)
     v_wide[pl.ds(block, rest), :] = v_buf[...].astype(jnp.float32)
@@ -78,15 +79,16 @@
             )
 
 
-def attend(listed, queries, k_own, v_own, k_all, v_all, kv_dev, slots):
+def attend(listed, queries, k_own, v_own, k_parts, v_parts, kv_dev, slots):
     block, dim = k_own.shape
     rest = (slots - 1) * block
+    choices = len(k_parts)
     vmem = pl.BlockSpec(memory_space=pltpu.VMEM)
-    hbm = pl.BlockSpec(memory_space=pl.ANY)
+    hbm = pl.BlockSpec(memory_space=pltpu.HBM)
     return pl.pallas_call(
-        functools.partial(attend_kernel, kv_dev=kv_dev, slots=slots),
+        functools.partial(attend_kernel, kv_dev=kv_dev, slots=slots, choices=choices),
         out_shape=jax.ShapeDtypeStruct(queries.shape, jnp.bfloat16),
-        in_specs=[pl.BlockSpec(memory_space=pltpu.SMEM), vmem, vmem, vmem, hbm, hbm],
+        in_specs=[pl.BlockSpec(memory_space=pltpu.SMEM), vmem, vmem, vmem] + [hbm] * (2 * choices),
         out_specs=vmem,
         scratch_shapes=[
             pltpu.VMEM((rest, dim), jnp.bfloat16),
@@ -97,19 +99,57 @@
         ],
         compiler_params=pltpu.CompilerParams(vmem_limit_bytes=32 * 2**20),
         name="attend",
-    )(listed, queries, k_own, v_own, k_all, v_all)
+    )(listed, queries, k_own, v_own, *k_parts, *v_parts)
+
+
+def others(row, target):
+    slots = row.shape[-1]
+    own_at = jnp.argmax(row == target[..., None], axis=-1)
+    j = jnp.arange(slots - 1)
+    return jnp.where(j >= own_at[..., None], row[..., 1:], row[..., :-1])
+
+
+def climb(own, members):
+    same = [own]
+    for step in range(1, members // PAIR):
+        up = [(s, s + PAIR) for s in range((step - 1) * PAIR, members - PAIR)]
+        same.append(lax.ppermute(same[-1], "seq", up))
+    crossed = [
+        lax.ppermute(part, "seq", [(s, s ^ 1) for s in range(step * PAIR, members)])
+        for step, part in enumerate(same)
+    ]
+    return same[1:] + crossed
+
+
+def relay(own, chosen, members):
+    block, dim = own[0].shape
+    stacked = jnp.stack(own).reshape(len(own), members, block // members, dim)
+    shares = lax.all_to_all(stacked, "seq", split_axis=1, concat_axis=1, tiled=True)
+    wanted = jnp.maximum(others(chosen, jnp.arange(members, dtype=jnp.int32)), 0)
+    picked = jnp.take(shares, wanted, axis=1)
+    arrived = lax.all_to_all(picked, "seq", split_axis=1, concat_axis=3, tiled=True)
+    return arrived.reshape(len(own), wanted.shape[1], block, dim)
 
 
 def per_device(queries, keys, values, chosen):
+    members = lax.axis_size("seq")
     tokens, kv_dev, dim = keys.shape
     slots = chosen.shape[1]
     target = lax.axis_index("seq").astype(jnp.int32)
-    listed = jnp.concatenate([lax.dynamic_index_in_dim(chosen, target, 0, False), target[None]])
+    listed = others(lax.dynamic_index_in_dim(chosen, target, 0, False), target)
     k_own = keys.reshape(tokens * kv_dev, dim)
     v_own = values.reshape(tokens * kv_dev, dim)
-    k_all = lax.all_gather(k_own, "seq", axis=0, tiled=True)
-    v_all = lax.all_gather(v_own, "seq", axis=0, tiled=True)
-    return attend(listed, queries, k_own, v_own, k_all, v_all, kv_dev, slots)
+    if members <= MOST_CLIMBED:
+        k_parts, v_parts = climb(k_own, members), climb(v_own, members)
+        steps = target // PAIR - listed // PAIR
+        crossed = (target ^ listed) & 1
+        at = steps - 1 + crossed * (members // PAIR)
+    else:
+        arrived = relay((k_own, v_own), chosen, members)
+        k_parts, v_parts = ([arrived[n, j] for j in range(slots - 1)] for n in range(2))
+        at = jnp.arange(slots - 1, dtype=jnp.int32)
+    at = jnp.where(listed < 0, -1, at)
+    return attend(at, queries, k_own, v_own, k_parts, v_parts, kv_dev, slots)
 
 
 def solution(mesh):

time: 110 us -> 49 us (0.45)
  the two profiles are of different devices: /device:TPU:0 before, /device:TPU:24 now
where the time goes in v2:
time: 49 us; the launch traced here: 48.5 us
  starting transfers between devices  27.3 us (56%)
  waiting for transfers between devices  10.1 us (21%)
  Pallas kernels  5.62 us (11%)
  local copies, waits for them, and re-layouts  3.86 us (8%)
  other arithmetic  1.4 us (3%)
    ppermute x8, starting transfers between devices, climb(): lax.ppermute(part, 'seq', [(s, s ^ 1) for s in range(step * PAIR, members)])  19.6 us
    ppermute x6, starting transfers between devices, climb(): same.append(lax.ppermute(same[-1], 'seq', up))  7.72 us
    ppermute x6, waiting for transfers between devices, climb(): same.append(lax.ppermute(same[-1], 'seq', up))  6.27 us
    pallas_call x1, Pallas kernels, attend(): pl.pallas_call(functools.partial(attend_kernel, kv_dev=kv_dev, slots=slot...  5.62 us
    ppermute x8, waiting for transfers between devices, climb(): lax.ppermute(part, 'seq', [(s, s ^ 1) for s in range(step * PAIR, members)])  3.82 us
    unnamed x8, local copies, waits for them, and re-layouts  3.71 us
  transfers between devices with their start and end apart: 14, of which 4 were waited for; matrix products, arithmetic and copies ran while one was open for 3% of the time, Pallas kernels for 0%

profile of v2, /device:TPU:24, one launch (start us, length us, event | category | flops | bytes accessed | tf_op | source)
XLA Modules:
  0.0 48.5 jit_solution(3854261042055068125)
XLA Ops:
  0.0 1.3 %collective-permute-start = (bf16[512,128]{1,0:T(8,128)(2,1)}, bf16[512,128]{1,0:T(8,128)(2,1)S(1)}, u32[]{:S(2)}, u32[]{:S(2)}) collective-permute-start(bf16[512,128]{1,0:T(8,128)(2,1)} %bitcast.2), channel_id=1, source_target_pairs={{0,4},{2,6},{4,8},{6,10},{8,12},{10,14},{1,5},{3,7},{5,9},{7,11},{... | collective-permute-start | bytes 393224 | tf_op jit(solution)/shard_map/ppermute | solution.py:116
  1.3 1.3 %collective-permute-start.7 = (bf16[512,128]{1,0:T(8,128)(2,1)}, bf16[512,128]{1,0:T(8,128)(2,1)S(1)}, u32[]{:S(2)}, u32[]{:S(2)}) collective-permute-start(bf16[512,128]{1,0:T(8,128)(2,1)} %bitcast.5), channel_id=1, source_target_pairs={{0,4},{2,6},{4,8},{6,10},{8,12},{10,14},{1,5},{3,7},{5,9},{7,11},{... | collective-permute-start | bytes 393224 | tf_op jit(solution)/shard_map/ppermute | solution.py:116
  2.6 5.7 %collective-permute-done.refs_0_ = bf16[512,128]{1,0:T(8,128)(2,1)S(1)} collective-permute-done((bf16[512,128]{1,0:T(8,128)(2,1)}, bf16[512,128]{1,0:T(8,128)(2,1)S(1)}, u32[]{:S(2)}, u32[]{:S(2)}) %collective-permute-start) | collective-permute-done | bytes 131104 | tf_op jit(solution)/shard_map/ppermute | solution.py:116
  8.2 1.3 %collective-permute-start.1 = (bf16[512,128]{1,0:T(8,128)(2,1)S(1)}, bf16[512,128]{1,0:T(8,128)(2,1)S(1)}, u32[]{:S(2)}, u32[]{:S(2)}) collective-permute-start(bf16[512,128]{1,0:T(8,128)(2,1)S(1)} %collective-permute-done.refs_0_), channel_id=1, source_target_pairs={{4,8},{6,10},{8,12},{10,14},{5,9},{7,11},{9,13},{11,15},{20,24},{2... | collective-permute-start | bytes 393224 | tf_op jit(solution)/shard_map/ppermute | solution.py:116
  9.5 0.6 %collective-permute-done.7.refs_7_ = bf16[512,128]{1,0:T(8,128)(2,1)S(1)} collective-permute-done((bf16[512,128]{1,0:T(8,128)(2,1)}, bf16[512,128]{1,0:T(8,128)(2,1)S(1)}, u32[]{:S(2)}, u32[]{:S(2)}) %collective-permute-start.7) | collective-permute-done | bytes 131104 | tf_op jit(solution)/shard_map/ppermute | solution.py:116
  10.1 1.3 %collective-permute-start.8 = (bf16[512,128]{1,0:T(8,128)(2,1)S(1)}, bf16[512,128]{1,0:T(8,128)(2,1)S(1)}, u32[]{:S(2)}, u32[]{:S(2)}) collective-permute-start(bf16[512,128]{1,0:T(8,128)(2,1)S(1)} %collective-permute-done.7.refs_7_), channel_id=1, source_target_pairs={{4,8},{6,10},{8,12},{10,14},{5,9},{7,11},{9,13},{11,15},{20,24},{2... | collective-permute-start | bytes 393224 | tf_op jit(solution)/shard_map/ppermute | solution.py:116
  11.4 1.6 %collective-permute-start.3 = (bf16[512,128]{1,0:T(8,128)(2,1)}, bf16[512,128]{1,0:T(8,128)(2,1)S(1)}, u32[]{:S(2)}, u32[]{:S(2)}) collective-permute-start(bf16[512,128]{1,0:T(8,128)(2,1)} %bitcast.3), channel_id=1, source_target_pairs={{0,2},{2,0},{4,6},{6,4},{8,10},{10,8},{12,14},{14,12},{1,3},{3,1},... | collective-permute-start | bytes 393224 | tf_op jit(solution)/shard_map/ppermute | solution.py:118
  13.0 0.5 %collective-permute-start.10 = (bf16[512,128]{1,0:T(8,128)(2,1)}, bf16[512,128]{1,0:T(8,128)(2,1)S(1)}, u32[]{:S(2)}, u32[]{:S(2)}) collective-permute-start(bf16[512,128]{1,0:T(8,128)(2,1)} %bitcast.6), channel_id=1, source_target_pairs={{0,2},{2,0},{4,6},{6,4},{8,10},{10,8},{12,14},{14,12},{1,3},{3,1},... | collective-permute-start | bytes 393224 | tf_op jit(solution)/shard_map/ppermute | solution.py:118
  13.5 0.0 copy-start.3
  13.5 0.7 %copy-done.3 = s32[8,4]{0,1:T(4,128)S(1)} copy-done((s32[8,4]{0,1:T(4,128)S(1)}, s32[8,4]{0,1:T(4,128)}, u32[]{:S(2)}) %copy-start.3) | copy-done | bytes 152
  14.2 0.2 compare_reduce_fusion
  14.4 3.4 %collective-permute-start.4 = (bf16[512,128]{1,0:T(8,128)(2,1)S(1)}, bf16[512,128]{1,0:T(8,128)(2,1)S(1)}, u32[]{:S(2)}, u32[]{:S(2)}) collective-permute-start(bf16[512,128]{1,0:T(8,128)(2,1)S(1)} %collective-permute-done.refs_0_), channel_id=1, source_target_pairs={{4,6},{6,4},{8,10},{10,8},{12,14},{14,12},{5,7},{7,5},{9,11},{11,9... | collective-permute-start | bytes 393224 | tf_op jit(solution)/shard_map/ppermute | solution.py:118
  17.8 0.0 collective-permute-done.1.refs_1_
  17.8 1.3 %collective-permute-start.2 = (bf16[512,128]{1,0:T(8,128)(2,1)S(1)}, bf16[512,128]{1,0:T(8,128)(2,1)S(1)}, u32[]{:S(2)}, u32[]{:S(2)}) collective-permute-start(bf16[512,128]{1,0:T(8,128)(2,1)S(1)} %collective-permute-done.1.refs_1_), channel_id=1, source_target_pairs={{8,12},{10,14},{9,13},{11,15},{24,28},{26,30},{25,29},{27,31}} | collective-permute-start | bytes 393224 | tf_op jit(solution)/shard_map/ppermute | solution.py:116
  19.1 0.0 collective-permute-done.8.refs_8_
  19.1 1.3 %collective-permute-start.9 = (bf16[512,128]{1,0:T(8,128)(2,1)S(1)}, bf16[512,128]{1,0:T(8,128)(2,1)S(1)}, u32[]{:S(2)}, u32[]{:S(2)}) collective-permute-start(bf16[512,128]{1,0:T(8,128)(2,1)S(1)} %collective-permute-done.8.refs_8_), channel_id=1, source_target_pairs={{8,12},{10,14},{9,13},{11,15},{24,28},{26,30},{25,29},{27,31}} | collective-permute-start | bytes 393224 | tf_op jit(solution)/shard_map/ppermute | solution.py:116
  20.4 0.6 %iota_reduce_fusion = (pred[]{:T(512)}, s32[]{:T(128)}) fusion(pred[4]{0:T(512)(128)(4,1)S(1)} %get-tuple-element.9), kind=kLoop, calls=%fused_computation.9 | loop fusion | flops 21 | bytes 9 | tf_op jit(solution)/shard_map/others/reduce | solution.py:107
  21.1 0.1 slice_reduce_fusion
  21.2 0.0 collective-permute-done.3.refs_3_
  21.2 2.4 %collective-permute-start.11 = (bf16[512,128]{1,0:T(8,128)(2,1)S(1)}, bf16[512,128]{1,0:T(8,128)(2,1)S(1)}, u32[]{:S(2)}, u32[]{:S(2)}) collective-permute-start(bf16[512,128]{1,0:T(8,128)(2,1)S(1)} %collective-permute-done.7.refs_7_), channel_id=1, source_target_pairs={{4,6},{6,4},{8,10},{10,8},{12,14},{14,12},{5,7},{7,5},{9,11},{11,9... | collective-permute-start | bytes 393224 | tf_op jit(solution)/shard_map/ppermute | solution.py:118
  23.7 0.0 collective-permute-done.10.refs_10_
  23.7 3.4 %collective-permute-start.5 = (bf16[512,128]{1,0:T(8,128)(2,1)S(1)}, bf16[512,128]{1,0:T(8,128)(2,1)S(1)}, u32[]{:S(2)}, u32[]{:S(2)}) collective-permute-start(bf16[512,128]{1,0:T(8,128)(2,1)S(1)} %collective-permute-done.1.refs_1_), channel_id=1, source_target_pairs={{8,10},{10,8},{12,14},{14,12},{9,11},{11,9},{13,15},{15,13},{24,26... | collective-permute-start | bytes 393224 | tf_op jit(solution)/shard_map/ppermute | solution.py:118
  27.1 0.0 collective-permute-done.4.refs_4_
  27.1 2.4 %collective-permute-start.12 = (bf16[512,128]{1,0:T(8,128)(2,1)S(1)}, bf16[512,128]{1,0:T(8,128)(2,1)S(1)}, u32[]{:S(2)}, u32[]{:S(2)}) collective-permute-start(bf16[512,128]{1,0:T(8,128)(2,1)S(1)} %collective-permute-done.8.refs_8_), channel_id=1, source_target_pairs={{8,10},{10,8},{12,14},{14,12},{9,11},{11,9},{13,15},{15,13},{24,26... | collective-permute-start | bytes 393224 | tf_op jit(solution)/shard_map/ppermute | solution.py:118
  29.5 0.0 collective-permute-done.2.refs_2_
  29.6 3.4 %collective-permute-start.6 = (bf16[512,128]{1,0:T(8,128)(2,1)S(1)}, bf16[512,128]{1,0:T(8,128)(2,1)S(1)}, u32[]{:S(2)}, u32[]{:S(2)}) collective-permute-start(bf16[512,128]{1,0:T(8,128)(2,1)S(1)} %collective-permute-done.2.refs_2_), channel_id=1, source_target_pairs={{12,14},{14,12},{13,15},{15,13},{28,30},{30,28},{29,31},{31,29}} | collective-permute-start | bytes 393224 | tf_op jit(solution)/shard_map/ppermute | solution.py:118
  33.0 0.0 collective-permute-done.9.refs_9_
  33.0 2.4 %collective-permute-start.13 = (bf16[512,128]{1,0:T(8,128)(2,1)S(1)}, bf16[512,128]{1,0:T(8,128)(2,1)S(1)}, u32[]{:S(2)}, u32[]{:S(2)}) collective-permute-start(bf16[512,128]{1,0:T(8,128)(2,1)S(1)} %collective-permute-done.9.refs_9_), channel_id=1, source_target_pairs={{12,14},{14,12},{13,15},{15,13},{28,30},{30,28},{29,31},{31,29}} | collective-permute-start | bytes 393224 | tf_op jit(solution)/shard_map/ppermute | solution.py:118
  35.4 0.6 %compare_select_fusion.1.listed_ref = s32[3]{0:T(128)S(1)} fusion(s32[3]{0:T(128)S(1)} %get-tuple-element.8, s32[3]{0:T(128)S(1)} %get-tuple-element.7, s32[]{:T(128)S(6)} %axis_index.15, s32[]{:T(128)S(6)} %select_n.27, s32[]{:T(128)} %get-tuple-element.6), kind=kLoop, calls=%fused_computation.8 | loop fusion | flops 72 | bytes 48 | tf_op jit(solution)/shard_map/jit(_where)/select_n | solution.py:151
  36.0 0.0 collective-permute-done.11.refs_11_
  36.0 0.0 collective-permute-done.5.refs_5_
  36.0 0.0 collective-permute-done.12.refs_12_
  36.0 1.7 %collective-permute-done.6.refs_6_ = bf16[512,128]{1,0:T(8,128)(2,1)S(1)} collective-permute-done((bf16[512,128]{1,0:T(8,128)(2,1)S(1)}, bf16[512,128]{1,0:T(8,128)(2,1)S(1)}, u32[]{:S(2)}, u32[]{:S(2)}) %collective-permute-start.6) | collective-permute-done | bytes 131104 | tf_op jit(solution)/shard_map/ppermute | solution.py:118
  37.7 2.1 %collective-permute-done.13.refs_13_ = bf16[512,128]{1,0:T(8,128)(2,1)S(1)} collective-permute-done((bf16[512,128]{1,0:T(8,128)(2,1)S(1)}, bf16[512,128]{1,0:T(8,128)(2,1)S(1)}, u32[]{:S(2)}, u32[]{:S(2)}) %collective-permute-start.13) | collective-permute-done | bytes 131104 | tf_op jit(solution)/shard_map/ppermute | solution.py:118
  39.8 0.0 copy-start
  39.8 1.2 %copy-done = bf16[128,32,128]{2,1,0:T(8,128)(2,1)S(1)} copy-done((bf16[128,32,128]{2,1,0:T(8,128)(2,1)S(1)}, bf16[128,32,128]{2,1,0:T(8,128)(2,1)}, u32[]{:S(2)}) %copy-start) | copy-done | bytes 1048600
  41.1 0.0 copy-start.1
  41.1 0.9 %copy-done.1 = bf16[128,4,128]{2,1,0:T(4,128)(2,1)S(1)} copy-done((bf16[128,4,128]{2,1,0:T(4,128)(2,1)S(1)}, bf16[128,4,128]{2,1,0:T(4,128)(2,1)}, u32[]{:S(2)}) %copy-start.1) | copy-done | bytes 131096
  42.0 0.0 copy-start.2
  42.0 0.9 %copy-done.2 = bf16[128,4,128]{2,1,0:T(4,128)(2,1)S(1)} copy-done((bf16[128,4,128]{2,1,0:T(4,128)(2,1)S(1)}, bf16[128,4,128]{2,1,0:T(4,128)(2,1)}, u32[]{:S(2)}) %copy-start.2) | copy-done | bytes 131096
  42.9 5.6 %attend.1 = bf16[128,32,128]{2,1,0:T(8,128)(2,1)} custom-call(s32[3]{0:T(128)S(1)} %compare_select_fusion.1.listed_ref, bf16[128,32,128]{2,1,0:T(8,128)(2,1)S(1)} %copy-done, bf16[512,128]{1,0:T(8,128)(2,1)S(1)} %bitcast.4, bf16[512,128]{1,0:T(8,128)(2,1)S(1)} %bitcast.7, bf16[512,128]{1,0:T(8,128)(2,1)S(1)} %collective-permute-done.refs_0_, ...), custom_call_target="tpu_custom_call" | custom-call | tf_op jit(solution)/shard_map/attend/pallas_call | solution.py:88
Async XLA Ops:
  0.0 8.2 %collective-permute-start = (bf16[512,128]{1,0:T(8,128)(2,1)}, bf16[512,128]{1,0:T(8,128)(2,1)S(1)}, u32[]{:S(2)}, u32[]{:S(2)}) collective-permute-start(bf16[512,128]{1,0:T(8,128)(2,1)} %bitcast.2), channel_id=1, source_target_pairs={{0,4},{2,6},{4,8},{6,10},{8,12},{10,14},{1,5},{3,7},{5,9},{7,11},{... | collective-permute-start | bytes 393224 | tf_op jit(solution)/shard_map/ppermute | solution.py:116
  1.3 8.9 %collective-permute-start.7 = (bf16[512,128]{1,0:T(8,128)(2,1)}, bf16[512,128]{1,0:T(8,128)(2,1)S(1)}, u32[]{:S(2)}, u32[]{:S(2)}) collective-permute-start(bf16[512,128]{1,0:T(8,128)(2,1)} %bitcast.5), channel_id=1, source_target_pairs={{0,4},{2,6},{4,8},{6,10},{8,12},{10,14},{1,5},{3,7},{5,9},{7,11},{... | collective-permute-start | bytes 393224 | tf_op jit(solution)/shard_map/ppermute | solution.py:116
  8.2 9.6 %collective-permute-start.1 = (bf16[512,128]{1,0:T(8,128)(2,1)S(1)}, bf16[512,128]{1,0:T(8,128)(2,1)S(1)}, u32[]{:S(2)}, u32[]{:S(2)}) collective-permute-start(bf16[512,128]{1,0:T(8,128)(2,1)S(1)} %collective-permute-done.refs_0_), channel_id=1, source_target_pairs={{4,8},{6,10},{8,12},{10,14},{5,9},{7,11},{9,13},{11,15},{20,24},{2... | collective-permute-start | bytes 393224 | tf_op jit(solution)/shard_map/ppermute | solution.py:116
  10.1 9.0 %collective-permute-start.8 = (bf16[512,128]{1,0:T(8,128)(2,1)S(1)}, bf16[512,128]{1,0:T(8,128)(2,1)S(1)}, u32[]{:S(2)}, u32[]{:S(2)}) collective-permute-start(bf16[512,128]{1,0:T(8,128)(2,1)S(1)} %collective-permute-done.7.refs_7_), channel_id=1, source_target_pairs={{4,8},{6,10},{8,12},{10,14},{5,9},{7,11},{9,13},{11,15},{20,24},{2... | collective-permute-start | bytes 393224 | tf_op jit(solution)/shard_map/ppermute | solution.py:116
  11.4 9.8 %collective-permute-start.3 = (bf16[512,128]{1,0:T(8,128)(2,1)}, bf16[512,128]{1,0:T(8,128)(2,1)S(1)}, u32[]{:S(2)}, u32[]{:S(2)}) collective-permute-start(bf16[512,128]{1,0:T(8,128)(2,1)} %bitcast.3), channel_id=1, source_target_pairs={{0,2},{2,0},{4,6},{6,4},{8,10},{10,8},{12,14},{14,12},{1,3},{3,1},... | collective-permute-start | bytes 393224 | tf_op jit(solution)/shard_map/ppermute | solution.py:118
  13.0 10.7 %collective-permute-start.10 = (bf16[512,128]{1,0:T(8,128)(2,1)}, bf16[512,128]{1,0:T(8,128)(2,1)S(1)}, u32[]{:S(2)}, u32[]{:S(2)}) collective-permute-start(bf16[512,128]{1,0:T(8,128)(2,1)} %bitcast.6), channel_id=1, source_target_pairs={{0,2},{2,0},{4,6},{6,4},{8,10},{10,8},{12,14},{14,12},{1,3},{3,1},... | collective-permute-start | bytes 393224 | tf_op jit(solution)/shard_map/ppermute | solution.py:118
  13.5 0.7 %copy-start.3 = (s32[8,4]{0,1:T(4,128)S(1)}, s32[8,4]{0,1:T(4,128)}, u32[]{:S(2)}) copy-start(s32[8,4]{0,1:T(4,128)} %param.7) | copy-start | bytes 388
  14.4 12.7 %collective-permute-start.4 = (bf16[512,128]{1,0:T(8,128)(2,1)S(1)}, bf16[512,128]{1,0:T(8,128)(2,1)S(1)}, u32[]{:S(2)}, u32[]{:S(2)}) collective-permute-start(bf16[512,128]{1,0:T(8,128)(2,1)S(1)} %collective-permute-done.refs_0_), channel_id=1, source_target_pairs={{4,6},{6,4},{8,10},{10,8},{12,14},{14,12},{5,7},{7,5},{9,11},{11,9... | collective-permute-start | bytes 393224 | tf_op jit(solution)/shard_map/ppermute | solution.py:118
  17.8 11.7 %collective-permute-start.2 = (bf16[512,128]{1,0:T(8,128)(2,1)S(1)}, bf16[512,128]{1,0:T(8,128)(2,1)S(1)}, u32[]{:S(2)}, u32[]{:S(2)}) collective-permute-start(bf16[512,128]{1,0:T(8,128)(2,1)S(1)} %collective-permute-done.1.refs_1_), channel_id=1, source_target_pairs={{8,12},{10,14},{9,13},{11,15},{24,28},{26,30},{25,29},{27,31}} | collective-permute-start | bytes 393224 | tf_op jit(solution)/shard_map/ppermute | solution.py:116
  19.1 13.8 %collective-permute-start.9 = (bf16[512,128]{1,0:T(8,128)(2,1)S(1)}, bf16[512,128]{1,0:T(8,128)(2,1)S(1)}, u32[]{:S(2)}, u32[]{:S(2)}) collective-permute-start(bf16[512,128]{1,0:T(8,128)(2,1)S(1)} %collective-permute-done.8.refs_8_), channel_id=1, source_target_pairs={{8,12},{10,14},{9,13},{11,15},{24,28},{26,30},{25,29},{27,31}} | collective-permute-start | bytes 393224 | tf_op jit(solution)/shard_map/ppermute | solution.py:116
  21.2 14.8 %collective-permute-start.11 = (bf16[512,128]{1,0:T(8,128)(2,1)S(1)}, bf16[512,128]{1,0:T(8,128)(2,1)S(1)}, u32[]{:S(2)}, u32[]{:S(2)}) collective-permute-start(bf16[512,128]{1,0:T(8,128)(2,1)S(1)} %collective-permute-done.7.refs_7_), channel_id=1, source_target_pairs={{4,6},{6,4},{8,10},{10,8},{12,14},{14,12},{5,7},{7,5},{9,11},{11,9... | collective-permute-start | bytes 393224 | tf_op jit(solution)/shard_map/ppermute | solution.py:118
  23.7 12.3 %collective-permute-start.5 = (bf16[512,128]{1,0:T(8,128)(2,1)S(1)}, bf16[512,128]{1,0:T(8,128)(2,1)S(1)}, u32[]{:S(2)}, u32[]{:S(2)}) collective-permute-start(bf16[512,128]{1,0:T(8,128)(2,1)S(1)} %collective-permute-done.1.refs_1_), channel_id=1, source_target_pairs={{8,10},{10,8},{12,14},{14,12},{9,11},{11,9},{13,15},{15,13},{24,26... | collective-permute-start | bytes 393224 | tf_op jit(solution)/shard_map/ppermute | solution.py:118
  27.1 8.9 %collective-permute-start.12 = (bf16[512,128]{1,0:T(8,128)(2,1)S(1)}, bf16[512,128]{1,0:T(8,128)(2,1)S(1)}, u32[]{:S(2)}, u32[]{:S(2)}) collective-permute-start(bf16[512,128]{1,0:T(8,128)(2,1)S(1)} %collective-permute-done.8.refs_8_), channel_id=1, source_target_pairs={{8,10},{10,8},{12,14},{14,12},{9,11},{11,9},{13,15},{15,13},{24,26... | collective-permute-start | bytes 393224 | tf_op jit(solution)/shard_map/ppermute | solution.py:118
  29.6 8.1 %collective-permute-start.6 = (bf16[512,128]{1,0:T(8,128)(2,1)S(1)}, bf16[512,128]{1,0:T(8,128)(2,1)S(1)}, u32[]{:S(2)}, u32[]{:S(2)}) collective-permute-start(bf16[512,128]{1,0:T(8,128)(2,1)S(1)} %collective-permute-done.2.refs_2_), channel_id=1, source_target_pairs={{12,14},{14,12},{13,15},{15,13},{28,30},{30,28},{29,31},{31,29}} | collective-permute-start | bytes 393224 | tf_op jit(solution)/shard_map/ppermute | solution.py:118
  33.0 6.9 %collective-permute-start.13 = (bf16[512,128]{1,0:T(8,128)(2,1)S(1)}, bf16[512,128]{1,0:T(8,128)(2,1)S(1)}, u32[]{:S(2)}, u32[]{:S(2)}) collective-permute-start(bf16[512,128]{1,0:T(8,128)(2,1)S(1)} %collective-permute-done.9.refs_9_), channel_id=1, source_target_pairs={{12,14},{14,12},{13,15},{15,13},{28,30},{30,28},{29,31},{31,29}} | collective-permute-start | bytes 393224 | tf_op jit(solution)/shard_map/ppermute | solution.py:118
  39.8 1.2 %copy-start = (bf16[128,32,128]{2,1,0:T(8,128)(2,1)S(1)}, bf16[128,32,128]{2,1,0:T(8,128)(2,1)}, u32[]{:S(2)}) copy-start(bf16[128,32,128]{2,1,0:T(8,128)(2,1)} %q_ref.1) | copy-start | bytes 3145732
  41.1 0.9 %copy-start.1 = (bf16[128,4,128]{2,1,0:T(4,128)(2,1)S(1)}, bf16[128,4,128]{2,1,0:T(4,128)(2,1)}, u32[]{:S(2)}) copy-start(bf16[128,4,128]{2,1,0:T(4,128)(2,1)} %param.5) | copy-start | bytes 393220
  42.0 0.9 %copy-start.2 = (bf16[128,4,128]{2,1,0:T(4,128)(2,1)S(1)}, bf16[128,4,128]{2,1,0:T(4,128)(2,1)}, u32[]{:S(2)}) copy-start(bf16[128,4,128]{2,1,0:T(4,128)(2,1)} %param.6) | copy-start | bytes 393220

commit v3 on v2

--- a/solution.py
+++ b/solution.py
@@ -14,13 +14,44 @@
 MOST_CLIMBED = 16
 
 
+def prepare_kernel(q_ref, k_ref, v_ref, q_out, k_out, v_out, k_wide, v_wide, *, kv_dev):
+    tokens, heads, dim = q_ref.shape
+    group = heads // kv_dev
+    k_wide[...] = k_ref[...].astype(jnp.float32)
+    v_wide[...] = v_ref[...].astype(jnp.float32)
+    for h in range(kv_dev):
+        q = q_ref[:, pl.ds(h * group, group), :].astype(jnp.float32)
+        q_out[h] = q.reshape(tokens * group, dim).astype(jnp.bfloat16)
+        k_out[h] = k_wide[pl.ds(h, tokens, stride=kv_dev), :].astype(jnp.bfloat16)
+        v_out[h] = v_wide[pl.ds(h, tokens, stride=kv_dev), :].astype(jnp.bfloat16)
+
+
+def prepare(queries, k_own, v_own, kv_dev):
+    tokens, heads, dim = queries.shape
+    vmem = pl.BlockSpec(memory_space=pltpu.VMEM)
+    by_head = jax.ShapeDtypeStruct((kv_dev, tokens, dim), jnp.bfloat16)
+    return pl.pallas_call(
+        functools.partial(prepare_kernel, kv_dev=kv_dev),
+        out_shape=(
+            jax.ShapeDtypeStruct((kv_dev, tokens * heads // kv_dev, dim), jnp.bfloat16),
+            by_head,
+            by_head,
+        ),
+        in_specs=[vmem] * 3,
+        out_specs=(vmem, vmem, vmem),
+        scratch_shapes=[pltpu.VMEM(k_own.shape, jnp.float32)] * 2,
+        compiler_params=pltpu.CompilerParams(vmem_limit_bytes=32 * 2**20),
+        name="prepare",
+    )(queries, k_own, v_own)
+
+
 def attend_kernel(
-    listed_ref, q_ref, k_own_ref, v_own_ref, *refs, kv_dev, slots, choices,
+    listed_ref, q_ref, k_own_ref, v_own_ref, *refs, slots, choices,
 ):
     k_refs, v_refs = refs[:choices], refs[choices : 2 * choices]
     out_ref, k_buf, v_buf, k_wide, v_wide, sems = refs[2 * choices :]
-    tokens, heads, dim = q_ref.shape
-    group = heads // kv_dev
+    kv_dev, tokens, dim = k_own_ref.shape
+    group = q_ref.shape[1] // tokens
     block = tokens * kv_dev
     bias = []
     for j in range(slots - 1):
@@ -35,28 +66,26 @@
                         parts[i], buf.at[pl.ds(j * block, block), :], sems.at[n, j]
                     ).start()
 
-    k_wide[pl.ds(0, block), :] = k_own_ref[...].astype(jnp.float32)
-    v_wide[pl.ds(0, block), :] = v_own_ref[...].astype(jnp.float32)
     for j in range(slots - 1):
         for n, (parts, buf) in enumerate(((k_refs, k_buf), (v_refs, v_buf))):
             pltpu.make_async_copy(
                 parts[0], buf.at[pl.ds(j * block, block), :], sems.at[n, j]
             ).wait()
-    rest = (slots - 1) * block
-    k_wide[pl.ds(block, rest), :] = k_buf[...].astype(jnp.float32)
-    v_wide[pl.ds(block, rest), :] = v_buf[...].astype(jnp.float32)
+    k_wide[...] = k_buf[...].astype(jnp.float32)
+    v_wide[...] = v_buf[...].astype(jnp.float32)
 
     factor = dim ** (-0.5) * math.log2(math.e)
-    keys = slots * tokens
-    ones = jnp.ones((keys, dim), jnp.bfloat16)
+    rest = (slots - 1) * tokens
+    ones = jnp.ones((slots * tokens, dim), jnp.bfloat16)
     chunk_tokens = ROW_CHUNK // group
     for h in range(kv_dev):
-        k_h = k_wide[pl.ds(h, keys, stride=kv_dev), :].astype(jnp.bfloat16)
-        v_h = v_wide[pl.ds(h, keys, stride=kv_dev), :].astype(jnp.bfloat16)
+        k_h = k_wide[pl.ds(h, rest, stride=kv_dev), :].astype(jnp.bfloat16)
+        v_h = v_wide[pl.ds(h, rest, stride=kv_dev), :].astype(jnp.bfloat16)
+        k_h = jnp.concatenate([k_own_ref[h], k_h], axis=0)
+        v_h = jnp.concatenate([v_own_ref[h], v_h], axis=0)
         v_ones = jnp.concatenate([v_h, ones], axis=1)
         for first in range(0, tokens, chunk_tokens):
-            q = q_ref[pl.ds(first, chunk_tokens), pl.ds(h * group, group), :]
-            q = q.astype(jnp.float32).reshape(ROW_CHUNK, dim).astype(jnp.bfloat16)
+            q = q_ref[h, pl.ds(first * group, ROW_CHUNK), :]
             s = lax.dot_general(
                 q, k_h, (((1,), (1,)), ((), ())), preferred_element_type=jnp.float32
             )
@@ -79,22 +108,23 @@
             )
 
 
-def attend(listed, queries, k_own, v_own, k_parts, v_parts, kv_dev, slots):
-    block, dim = k_own.shape
-    rest = (slots - 1) * block
+def attend(listed, queries, k_own, v_own, k_parts, v_parts, slots):
+    kv_dev, tokens, dim = k_own.shape
+    heads = queries.shape[0] * queries.shape[1] // tokens
+    rest = (slots - 1) * tokens * kv_dev
     choices = len(k_parts)
     vmem = pl.BlockSpec(memory_space=pltpu.VMEM)
     hbm = pl.BlockSpec(memory_space=pltpu.HBM)
     return pl.pallas_call(
-        functools.partial(attend_kernel, kv_dev=kv_dev, slots=slots, choices=choices),
-        out_shape=jax.ShapeDtypeStruct(queries.shape, jnp.bfloat16),
+        functools.partial(attend_kernel, slots=slots, choices=choices),
+        out_shape=jax.ShapeDtypeStruct((tokens, heads, dim), jnp.bfloat16),
         in_specs=[pl.BlockSpec(memory_space=pltpu.SMEM), vmem, vmem, vmem] + [hbm] * (2 * choices),
         out_specs=vmem,
         scratch_shapes=[
             pltpu.VMEM((rest, dim), jnp.bfloat16),
             pltpu.VMEM((rest, dim), jnp.bfloat16),
-            pltpu.VMEM((slots * block, dim), jnp.float32),
-            pltpu.VMEM((slots * block, dim), jnp.float32),
+            pltpu.VMEM((rest, dim), jnp.float32),
+            pltpu.VMEM((rest, dim), jnp.float32),
             pltpu.SemaphoreType.DMA((2, slots - 1)),
         ],
         compiler_params=pltpu.CompilerParams(vmem_limit_bytes=32 * 2**20),
@@ -110,15 +140,12 @@
 
 
 def climb(own, members):
+    up = [(s, (s + PAIR) % members) for s in range(members)]
+    across = [(s, s ^ 1) for s in range(members)]
     same = [own]
-    for step in range(1, members // PAIR):
-        up = [(s, s + PAIR) for s in range((step - 1) * PAIR, members - PAIR)]
+    for _ in range(1, members // PAIR):
         same.append(lax.ppermute(same[-1], "seq", up))
-    crossed = [
-        lax.ppermute(part, "seq", [(s, s ^ 1) for s in range(step * PAIR, members)])
-        for step, part in enumerate(same)
-    ]
-    return same[1:] + crossed
+    return same[1:] + [lax.ppermute(part, "seq", across) for part in same]
 
 
 def relay(own, chosen, members):
@@ -149,7 +176,8 @@
         k_parts, v_parts = ([arrived[n, j] for j in range(slots - 1)] for n in range(2))
         at = jnp.arange(slots - 1, dtype=jnp.int32)
     at = jnp.where(listed < 0, -1, at)
-    return attend(at, queries, k_own, v_own, k_parts, v_parts, kv_dev, slots)
+    ready = prepare(queries, k_own, v_own, kv_dev)
+    return attend(at, *ready, k_parts, v_parts, slots)
 
 
 def solution(mesh):

time: 49 us -> 44.7 us (0.912)
  the two profiles are of different devices: /device:TPU:24 before, /device:TPU:0 now
where the time goes in v3:
time: 44.7 us; the launch traced here: 44.5 us
  waiting for transfers between devices  17.4 us (39%)
  starting transfers between devices  15.9 us (36%)
  Pallas kernels  5.74 us (13%)
  local copies, waits for them, and re-layouts  3.86 us (9%)
  other arithmetic  1.51 us (3%)
    ppermute x8, starting transfers between devices, climb(): return same[1:] + [lax.ppermute(part, 'seq', across) for part in same]  9.8 us
    ppermute x6, waiting for transfers between devices, climb(): same.append(lax.ppermute(same[-1], 'seq', up))  9.3 us
    ppermute x8, waiting for transfers between devices, climb(): return same[1:] + [lax.ppermute(part, 'seq', across) for part in same]  8.14 us
    ppermute x6, starting transfers between devices, climb(): same.append(lax.ppermute(same[-1], 'seq', up))  6.09 us
    pallas_call x1, Pallas kernels, attend(): pl.pallas_call(functools.partial(attend_kernel, slots=slots, choices=choi...  5.46 us
    unnamed x8, local copies, waits for them, and re-layouts  3.71 us
  transfers between devices with their start and end apart: 14, of which 8 were waited for; matrix products, arithmetic and copies ran while one was open for 4% of the time, Pallas kernels for 1%

profile of v3, /device:TPU:0, one launch (start us, length us, event | category | flops | bytes accessed | tf_op | source)
XLA Modules:
  0.0 44.5 jit_solution(17049836005911668349)
XLA Ops:
  0.0 3.0 %collective-permute-start = (bf16[512,128]{1,0:T(8,128)(2,1)}, bf16[512,128]{1,0:T(8,128)(2,1)S(1)}, u32[]{:S(2)}, u32[]{:S(2)}) collective-permute-start(bf16[512,128]{1,0:T(8,128)(2,1)} %bitcast.2), channel_id=1, source_target_pairs={{0,4},{2,6},{4,8},{6,10},{8,12},{10,14},{12,0},{14,2},{1,5},{3,7},... | collective-permute-start | bytes 393224 | tf_op jit(solution)/shard_map/ppermute | solution.py:147
  3.0 1.6 %collective-permute-start.7 = (bf16[512,128]{1,0:T(8,128)(2,1)}, bf16[512,128]{1,0:T(8,128)(2,1)S(1)}, u32[]{:S(2)}, u32[]{:S(2)}) collective-permute-start(bf16[512,128]{1,0:T(8,128)(2,1)} %bitcast.5), channel_id=1, source_target_pairs={{0,4},{2,6},{4,8},{6,10},{8,12},{10,14},{12,0},{14,2},{1,5},{3,7},... | collective-permute-start | bytes 393224 | tf_op jit(solution)/shard_map/ppermute | solution.py:147
  4.6 5.0 %collective-permute-done.refs_0_ = bf16[512,128]{1,0:T(8,128)(2,1)S(1)} collective-permute-done((bf16[512,128]{1,0:T(8,128)(2,1)}, bf16[512,128]{1,0:T(8,128)(2,1)S(1)}, u32[]{:S(2)}, u32[]{:S(2)}) %collective-permute-start) | collective-permute-done | bytes 131104 | tf_op jit(solution)/shard_map/ppermute | solution.py:147
  9.6 0.0 collective-permute-start.1
  9.6 1.9 %collective-permute-done.7.refs_7_ = bf16[512,128]{1,0:T(8,128)(2,1)S(1)} collective-permute-done((bf16[512,128]{1,0:T(8,128)(2,1)}, bf16[512,128]{1,0:T(8,128)(2,1)S(1)}, u32[]{:S(2)}, u32[]{:S(2)}) %collective-permute-start.7) | collective-permute-done | bytes 131104 | tf_op jit(solution)/shard_map/ppermute | solution.py:147
  11.6 0.1 collective-permute-start.8
  11.6 1.7 %collective-permute-start.3 = (bf16[512,128]{1,0:T(8,128)(2,1)}, bf16[512,128]{1,0:T(8,128)(2,1)S(1)}, u32[]{:S(2)}, u32[]{:S(2)}) collective-permute-start(bf16[512,128]{1,0:T(8,128)(2,1)} %bitcast.3), channel_id=1, source_target_pairs={{0,2},{2,0},{4,6},{6,4},{8,10},{10,8},{12,14},{14,12},{1,3},{3,1},... | collective-permute-start | bytes 393224 | tf_op jit(solution)/shard_map/ppermute | solution.py:148
  13.3 0.3 collective-permute-start.10
  13.7 0.0 copy-start.3
  13.7 0.7 %copy-done.3 = s32[8,4]{0,1:T(4,128)S(1)} copy-done((s32[8,4]{0,1:T(4,128)S(1)}, s32[8,4]{0,1:T(4,128)}, u32[]{:S(2)}) %copy-start.3) | copy-done | bytes 152
  14.3 0.2 compare_reduce_fusion
  14.5 1.7 %collective-permute-start.4 = (bf16[512,128]{1,0:T(8,128)(2,1)S(1)}, bf16[512,128]{1,0:T(8,128)(2,1)S(1)}, u32[]{:S(2)}, u32[]{:S(2)}) collective-permute-start(bf16[512,128]{1,0:T(8,128)(2,1)S(1)} %collective-permute-done.refs_0_), channel_id=1, source_target_pairs={{0,2},{2,0},{4,6},{6,4},{8,10},{10,8},{12,14},{14,12},{1,3},{3,1},... | collective-permute-start | bytes 393224 | tf_op jit(solution)/shard_map/ppermute | solution.py:148
  16.3 1.2 %collective-permute-done.1.refs_1_ = bf16[512,128]{1,0:T(8,128)(2,1)S(1)} collective-permute-done((bf16[512,128]{1,0:T(8,128)(2,1)S(1)}, bf16[512,128]{1,0:T(8,128)(2,1)S(1)}, u32[]{:S(2)}, u32[]{:S(2)}) %collective-permute-start.1) | collective-permute-done | bytes 131104 | tf_op jit(solution)/shard_map/ppermute | solution.py:147
  17.5 1.0 %collective-permute-start.2 = (bf16[512,128]{1,0:T(8,128)(2,1)S(1)}, bf16[512,128]{1,0:T(8,128)(2,1)S(1)}, u32[]{:S(2)}, u32[]{:S(2)}) collective-permute-start(bf16[512,128]{1,0:T(8,128)(2,1)S(1)} %collective-permute-done.1.refs_1_), channel_id=1, source_target_pairs={{0,4},{2,6},{4,8},{6,10},{8,12},{10,14},{12,0},{14,2},{1,5},{3,7},... | collective-permute-start | bytes 393224 | tf_op jit(solution)/shard_map/ppermute | solution.py:147
  18.5 1.2 %collective-permute-done.8.refs_8_ = bf16[512,128]{1,0:T(8,128)(2,1)S(1)} collective-permute-done((bf16[512,128]{1,0:T(8,128)(2,1)S(1)}, bf16[512,128]{1,0:T(8,128)(2,1)S(1)}, u32[]{:S(2)}, u32[]{:S(2)}) %collective-permute-start.8) | collective-permute-done | bytes 131104 | tf_op jit(solution)/shard_map/ppermute | solution.py:147
  19.6 0.4 collective-permute-start.9
  20.0 0.7 %iota_reduce_fusion = (pred[]{:T(512)}, s32[]{:T(128)}) fusion(pred[4]{0:T(512)(128)(4,1)S(1)} %get-tuple-element.15), kind=kLoop, calls=%fused_computation.9 | loop fusion | flops 21 | bytes 9 | tf_op jit(solution)/shard_map/others/reduce | solution.py:137
  20.7 0.0 copy-start
  20.7 1.2 %copy-done = bf16[128,32,128]{2,1,0:T(8,128)(2,1)S(1)} copy-done((bf16[128,32,128]{2,1,0:T(8,128)(2,1)S(1)}, bf16[128,32,128]{2,1,0:T(8,128)(2,1)}, u32[]{:S(2)}) %copy-start) | copy-done | bytes 1048600
  21.9 0.0 copy-start.1
  21.9 0.9 %copy-done.1 = bf16[128,4,128]{2,1,0:T(4,128)(2,1)S(1)} copy-done((bf16[128,4,128]{2,1,0:T(4,128)(2,1)S(1)}, bf16[128,4,128]{2,1,0:T(4,128)(2,1)}, u32[]{:S(2)}) %copy-start.1) | copy-done | bytes 131096
  22.8 0.0 copy-start.2
  22.8 0.9 %copy-done.2 = bf16[128,4,128]{2,1,0:T(4,128)(2,1)S(1)} copy-done((bf16[128,4,128]{2,1,0:T(4,128)(2,1)S(1)}, bf16[128,4,128]{2,1,0:T(4,128)(2,1)}, u32[]{:S(2)}) %copy-start.2) | copy-done | bytes 131096
  23.7 0.3 prepare.1
  24.0 0.1 slice_reduce_fusion
  24.2 0.0 collective-permute-done.3.refs_3_
  24.2 2.0 %collective-permute-start.11 = (bf16[512,128]{1,0:T(8,128)(2,1)S(1)}, bf16[512,128]{1,0:T(8,128)(2,1)S(1)}, u32[]{:S(2)}, u32[]{:S(2)}) collective-permute-start(bf16[512,128]{1,0:T(8,128)(2,1)S(1)} %collective-permute-done.7.refs_7_), channel_id=1, source_target_pairs={{0,2},{2,0},{4,6},{6,4},{8,10},{10,8},{12,14},{14,12},{1,3},{3,1},... | collective-permute-start | bytes 393224 | tf_op jit(solution)/shard_map/ppermute | solution.py:148
  26.2 0.0 collective-permute-done.10.refs_10_
  26.2 0.1 collective-permute-start.5
  26.3 0.0 collective-permute-done.4.refs_4_
  26.3 1.9 %collective-permute-start.12 = (bf16[512,128]{1,0:T(8,128)(2,1)S(1)}, bf16[512,128]{1,0:T(8,128)(2,1)S(1)}, u32[]{:S(2)}, u32[]{:S(2)}) collective-permute-start(bf16[512,128]{1,0:T(8,128)(2,1)S(1)} %collective-permute-done.8.refs_8_), channel_id=1, source_target_pairs={{0,2},{2,0},{4,6},{6,4},{8,10},{10,8},{12,14},{14,12},{1,3},{3,1},... | collective-permute-start | bytes 393224 | tf_op jit(solution)/shard_map/ppermute | solution.py:148
  28.2 0.0 collective-permute-done.2.refs_2_
  28.2 0.1 collective-permute-start.6
  28.3 0.0 collective-permute-done.9.refs_9_
  28.3 1.9 %collective-permute-start.13 = (bf16[512,128]{1,0:T(8,128)(2,1)S(1)}, bf16[512,128]{1,0:T(8,128)(2,1)S(1)}, u32[]{:S(2)}, u32[]{:S(2)}) collective-permute-start(bf16[512,128]{1,0:T(8,128)(2,1)S(1)} %collective-permute-done.9.refs_9_), channel_id=1, source_target_pairs={{0,2},{2,0},{4,6},{6,4},{8,10},{10,8},{12,14},{14,12},{1,3},{3,1},... | collective-permute-start | bytes 393224 | tf_op jit(solution)/shard_map/ppermute | solution.py:148
  30.2 0.6 %compare_select_fusion.1.listed_ref = s32[3]{0:T(128)S(1)} fusion(s32[3]{0:T(128)S(1)} %get-tuple-element.14, s32[3]{0:T(128)S(1)} %get-tuple-element.13, s32[]{:T(128)S(6)} %axis_index.15, s32[]{:T(128)S(6)} %select_n.27, s32[]{:T(128)} %get-tuple-element.9), kind=kLoop, calls=%fused_computation.8 | loop fusion | flops 72 | bytes 48 | tf_op jit(solution)/shard_map/jit(_where)/select_n | solution.py:178
  30.9 0.0 collective-permute-done.11.refs_11_
  30.9 2.6 %collective-permute-done.5.refs_5_ = bf16[512,128]{1,0:T(8,128)(2,1)S(1)} collective-permute-done((bf16[512,128]{1,0:T(8,128)(2,1)S(1)}, bf16[512,128]{1,0:T(8,128)(2,1)S(1)}, u32[]{:S(2)}, u32[]{:S(2)}) %collective-permute-start.5) | collective-permute-done | bytes 131104 | tf_op jit(solution)/shard_map/ppermute | solution.py:148
  33.5 2.7 %collective-permute-done.12.refs_12_ = bf16[512,128]{1,0:T(8,128)(2,1)S(1)} collective-permute-done((bf16[512,128]{1,0:T(8,128)(2,1)S(1)}, bf16[512,128]{1,0:T(8,128)(2,1)S(1)}, u32[]{:S(2)}, u32[]{:S(2)}) %collective-permute-start.12) | collective-permute-done | bytes 131104 | tf_op jit(solution)/shard_map/ppermute | solution.py:148
  36.2 1.4 %collective-permute-done.6.refs_6_ = bf16[512,128]{1,0:T(8,128)(2,1)S(1)} collective-permute-done((bf16[512,128]{1,0:T(8,128)(2,1)S(1)}, bf16[512,128]{1,0:T(8,128)(2,1)S(1)}, u32[]{:S(2)}, u32[]{:S(2)}) %collective-permute-start.6) | collective-permute-done | bytes 131104 | tf_op jit(solution)/shard_map/ppermute | solution.py:148
  37.6 1.4 %collective-permute-done.13.refs_13_ = bf16[512,128]{1,0:T(8,128)(2,1)S(1)} collective-permute-done((bf16[512,128]{1,0:T(8,128)(2,1)S(1)}, bf16[512,128]{1,0:T(8,128)(2,1)S(1)}, u32[]{:S(2)}, u32[]{:S(2)}) %collective-permute-start.13) | collective-permute-done | bytes 131104 | tf_op jit(solution)/shard_map/ppermute | solution.py:148
  39.0 5.5 %attend.1 = bf16[128,32,128]{2,1,0:T(8,128)(2,1)} custom-call(s32[3]{0:T(128)S(1)} %compare_select_fusion.1.listed_ref, bf16[4,1024,128]{2,1,0:T(8,128)(2,1)S(1)} %get-tuple-element.10.q_ref, bf16[4,128,128]{2,1,0:T(8,128)(2,1)S(1)} %get-tuple-element.11.k_own_ref, bf16[4,128,128]{2,1,0:T(8,128)(2,1)S(1)} %get-tuple-element.12.v_own_ref, ...), custom_call_target="tpu_custom_call" | custom-call | tf_op jit(solution)/shard_map/attend/pallas_call | solution.py:118
Async XLA Ops:
  0.0 9.6 %collective-permute-start = (bf16[512,128]{1,0:T(8,128)(2,1)}, bf16[512,128]{1,0:T(8,128)(2,1)S(1)}, u32[]{:S(2)}, u32[]{:S(2)}) collective-permute-start(bf16[512,128]{1,0:T(8,128)(2,1)} %bitcast.2), channel_id=1, source_target_pairs={{0,4},{2,6},{4,8},{6,10},{8,12},{10,14},{12,0},{14,2},{1,5},{3,7},... | collective-permute-start | bytes 393224 | tf_op jit(solution)/shard_map/ppermute | solution.py:147
  3.0 8.5 %collective-permute-start.7 = (bf16[512,128]{1,0:T(8,128)(2,1)}, bf16[512,128]{1,0:T(8,128)(2,1)S(1)}, u32[]{:S(2)}, u32[]{:S(2)}) collective-permute-start(bf16[512,128]{1,0:T(8,128)(2,1)} %bitcast.5), channel_id=1, source_target_pairs={{0,4},{2,6},{4,8},{6,10},{8,12},{10,14},{12,0},{14,2},{1,5},{3,7},... | collective-permute-start | bytes 393224 | tf_op jit(solution)/shard_map/ppermute | solution.py:147
  9.6 7.9 %collective-permute-start.1 = (bf16[512,128]{1,0:T(8,128)(2,1)S(1)}, bf16[512,128]{1,0:T(8,128)(2,1)S(1)}, u32[]{:S(2)}, u32[]{:S(2)}) collective-permute-start(bf16[512,128]{1,0:T(8,128)(2,1)S(1)} %collective-permute-done.refs_0_), channel_id=1, source_target_pairs={{0,4},{2,6},{4,8},{6,10},{8,12},{10,14},{12,0},{14,2},{1,5},{3,7},... | collective-permute-start | bytes 393224 | tf_op jit(solution)/shard_map/ppermute | solution.py:147
  11.6 8.1 %collective-permute-start.8 = (bf16[512,128]{1,0:T(8,128)(2,1)S(1)}, bf16[512,128]{1,0:T(8,128)(2,1)S(1)}, u32[]{:S(2)}, u32[]{:S(2)}) collective-permute-start(bf16[512,128]{1,0:T(8,128)(2,1)S(1)} %collective-permute-done.7.refs_7_), channel_id=1, source_target_pairs={{0,4},{2,6},{4,8},{6,10},{8,12},{10,14},{12,0},{14,2},{1,5},{3,7},... | collective-permute-start | bytes 393224 | tf_op jit(solution)/shard_map/ppermute | solution.py:147
  11.6 12.6 %collective-permute-start.3 = (bf16[512,128]{1,0:T(8,128)(2,1)}, bf16[512,128]{1,0:T(8,128)(2,1)S(1)}, u32[]{:S(2)}, u32[]{:S(2)}) collective-permute-start(bf16[512,128]{1,0:T(8,128)(2,1)} %bitcast.3), channel_id=1, source_target_pairs={{0,2},{2,0},{4,6},{6,4},{8,10},{10,8},{12,14},{14,12},{1,3},{3,1},... | collective-permute-start | bytes 393224 | tf_op jit(solution)/shard_map/ppermute | solution.py:148
  13.3 12.8 %collective-permute-start.10 = (bf16[512,128]{1,0:T(8,128)(2,1)}, bf16[512,128]{1,0:T(8,128)(2,1)S(1)}, u32[]{:S(2)}, u32[]{:S(2)}) collective-permute-start(bf16[512,128]{1,0:T(8,128)(2,1)} %bitcast.6), channel_id=1, source_target_pairs={{0,2},{2,0},{4,6},{6,4},{8,10},{10,8},{12,14},{14,12},{1,3},{3,1},... | collective-permute-start | bytes 393224 | tf_op jit(solution)/shard_map/ppermute | solution.py:148
  13.7 0.7 %copy-start.3 = (s32[8,4]{0,1:T(4,128)S(1)}, s32[8,4]{0,1:T(4,128)}, u32[]{:S(2)}) copy-start(s32[8,4]{0,1:T(4,128)} %param.7) | copy-start | bytes 388
  14.5 11.8 %collective-permute-start.4 = (bf16[512,128]{1,0:T(8,128)(2,1)S(1)}, bf16[512,128]{1,0:T(8,128)(2,1)S(1)}, u32[]{:S(2)}, u32[]{:S(2)}) collective-permute-start(bf16[512,128]{1,0:T(8,128)(2,1)S(1)} %collective-permute-done.refs_0_), channel_id=1, source_target_pairs={{0,2},{2,0},{4,6},{6,4},{8,10},{10,8},{12,14},{14,12},{1,3},{3,1},... | collective-permute-start | bytes 393224 | tf_op jit(solution)/shard_map/ppermute | solution.py:148
  17.5 10.7 %collective-permute-start.2 = (bf16[512,128]{1,0:T(8,128)(2,1)S(1)}, bf16[512,128]{1,0:T(8,128)(2,1)S(1)}, u32[]{:S(2)}, u32[]{:S(2)}) collective-permute-start(bf16[512,128]{1,0:T(8,128)(2,1)S(1)} %collective-permute-done.1.refs_1_), channel_id=1, source_target_pairs={{0,4},{2,6},{4,8},{6,10},{8,12},{10,14},{12,0},{14,2},{1,5},{3,7},... | collective-permute-start | bytes 393224 | tf_op jit(solution)/shard_map/ppermute | solution.py:147
  19.6 8.7 %collective-permute-start.9 = (bf16[512,128]{1,0:T(8,128)(2,1)S(1)}, bf16[512,128]{1,0:T(8,128)(2,1)S(1)}, u32[]{:S(2)}, u32[]{:S(2)}) collective-permute-start(bf16[512,128]{1,0:T(8,128)(2,1)S(1)} %collective-permute-done.8.refs_8_), channel_id=1, source_target_pairs={{0,4},{2,6},{4,8},{6,10},{8,12},{10,14},{12,0},{14,2},{1,5},{3,7},... | collective-permute-start | bytes 393224 | tf_op jit(solution)/shard_map/ppermute | solution.py:147
  20.7 1.2 %copy-start = (bf16[128,32,128]{2,1,0:T(8,128)(2,1)S(1)}, bf16[128,32,128]{2,1,0:T(8,128)(2,1)}, u32[]{:S(2)}) copy-start(bf16[128,32,128]{2,1,0:T(8,128)(2,1)} %q_ref.1) | copy-start | bytes 3145732
  21.9 0.9 %copy-start.1 = (bf16[128,4,128]{2,1,0:T(4,128)(2,1)S(1)}, bf16[128,4,128]{2,1,0:T(4,128)(2,1)}, u32[]{:S(2)}) copy-start(bf16[128,4,128]{2,1,0:T(4,128)(2,1)} %param.5) | copy-start | bytes 393220
  22.8 0.9 %copy-start.2 = (bf16[128,4,128]{2,1,0:T(4,128)(2,1)S(1)}, bf16[128,4,128]{2,1,0:T(4,128)(2,1)}, u32[]{:S(2)}) copy-start(bf16[128,4,128]{2,1,0:T(4,128)(2,1)} %param.6) | copy-start | bytes 393220
  24.2 6.7 %collective-permute-start.11 = (bf16[512,128]{1,0:T(8,128)(2,1)S(1)}, bf16[512,128]{1,0:T(8,128)(2,1)S(1)}, u32[]{:S(2)}, u32[]{:S(2)}) collective-permute-start(bf16[512,128]{1,0:T(8,128)(2,1)S(1)} %collective-permute-done.7.refs_7_), channel_id=1, source_target_pairs={{0,2},{2,0},{4,6},{6,4},{8,10},{10,8},{12,14},{14,12},{1,3},{3,1},... | collective-permute-start | bytes 393224 | tf_op jit(solution)/shard_map/ppermute | solution.py:148
  26.2 7.4 %collective-permute-start.5 = (bf16[512,128]{1,0:T(8,128)(2,1)S(1)}, bf16[512,128]{1,0:T(8,128)(2,1)S(1)}, u32[]{:S(2)}, u32[]{:S(2)}) collective-permute-start(bf16[512,128]{1,0:T(8,128)(2,1)S(1)} %collective-permute-done.1.refs_1_), channel_id=1, source_target_pairs={{0,2},{2,0},{4,6},{6,4},{8,10},{10,8},{12,14},{14,12},{1,3},{3,1},... | collective-permute-start | bytes 393224 | tf_op jit(solution)/shard_map/ppermute | solution.py:148
  26.3 9.9 %collective-permute-start.12 = (bf16[512,128]{1,0:T(8,128)(2,1)S(1)}, bf16[512,128]{1,0:T(8,128)(2,1)S(1)}, u32[]{:S(2)}, u32[]{:S(2)}) collective-permute-start(bf16[512,128]{1,0:T(8,128)(2,1)S(1)} %collective-permute-done.8.refs_8_), channel_id=1, source_target_pairs={{0,2},{2,0},{4,6},{6,4},{8,10},{10,8},{12,14},{14,12},{1,3},{3,1},... | collective-permute-start | bytes 393224 | tf_op jit(solution)/shard_map/ppermute | solution.py:148
  28.2 9.4 %collective-permute-start.6 = (bf16[512,128]{1,0:T(8,128)(2,1)S(1)}, bf16[512,128]{1,0:T(8,128)(2,1)S(1)}, u32[]{:S(2)}, u32[]{:S(2)}) collective-permute-start(bf16[512,128]{1,0:T(8,128)(2,1)S(1)} %collective-permute-done.2.refs_2_), channel_id=1, source_target_pairs={{0,2},{2,0},{4,6},{6,4},{8,10},{10,8},{12,14},{14,12},{1,3},{3,1},... | collective-permute-start | bytes 393224 | tf_op jit(solution)/shard_map/ppermute | solution.py:148
  28.3 10.7 %collective-permute-start.13 = (bf16[512,128]{1,0:T(8,128)(2,1)S(1)}, bf16[512,128]{1,0:T(8,128)(2,1)S(1)}, u32[]{:S(2)}, u32[]{:S(2)}) collective-permute-start(bf16[512,128]{1,0:T(8,128)(2,1)S(1)} %collective-permute-done.9.refs_9_), channel_id=1, source_target_pairs={{0,2},{2,0},{4,6},{6,4},{8,10},{10,8},{12,14},{14,12},{1,3},{3,1},... | collective-permute-start | bytes 393224 | tf_op jit(solution)/shard_map/ppermute | solution.py:148

commit v4 on v3

--- a/solution.py
+++ b/solution.py
@@ -14,21 +14,34 @@
 MOST_CLIMBED = 16
 
 
-def prepare_kernel(q_ref, k_ref, v_ref, q_out, k_out, v_out, k_wide, v_wide, *, kv_dev):
+def prepare_kernel(
+    q_hbm, k_hbm, v_hbm, q_out, k_out, v_out, q_ref, k_ref, v_ref, k_wide, v_wide, sems, *, kv_dev
+):
+    copies = [
+        pltpu.make_async_copy(source, here, sems.at[n])
+        for n, (source, here) in enumerate(((k_hbm, k_ref), (v_hbm, v_ref), (q_hbm, q_ref)))
+    ]
+    for copy in copies:
+        copy.start()
     tokens, heads, dim = q_ref.shape
     group = heads // kv_dev
+    copies[0].wait()
     k_wide[...] = k_ref[...].astype(jnp.float32)
+    copies[1].wait()
     v_wide[...] = v_ref[...].astype(jnp.float32)
+    for h in range(kv_dev):
+        k_out[h] = k_wide[pl.ds(h, tokens, stride=kv_dev), :].astype(jnp.bfloat16)
+        v_out[h] = v_wide[pl.ds(h, tokens, stride=kv_dev), :].astype(jnp.bfloat16)
+    copies[2].wait()
     for h in range(kv_dev):
         q = q_ref[:, pl.ds(h * group, group), :].astype(jnp.float32)
         q_out[h] = q.reshape(tokens * group, dim).astype(jnp.bfloat16)
-        k_out[h] = k_wide[pl.ds(h, tokens, stride=kv_dev), :].astype(jnp.bfloat16)
-        v_out[h] = v_wide[pl.ds(h, tokens, stride=kv_dev), :].astype(jnp.bfloat16)
 
 
 def prepare(queries, k_own, v_own, kv_dev):
     tokens, heads, dim = queries.shape
     vmem = pl.BlockSpec(memory_space=pltpu.VMEM)
+    hbm = pl.BlockSpec(memory_space=pltpu.HBM)
     by_head = jax.ShapeDtypeStruct((kv_dev, tokens, dim), jnp.bfloat16)
     return pl.pallas_call(
         functools.partial(prepare_kernel, kv_dev=kv_dev),
@@ -37,29 +50,41 @@
             by_head,
             by_head,
         ),
-        in_specs=[vmem] * 3,
+        in_specs=[hbm] * 3,
         out_specs=(vmem, vmem, vmem),
-        scratch_shapes=[pltpu.VMEM(k_own.shape, jnp.float32)] * 2,
+        scratch_shapes=[
+            pltpu.VMEM(queries.shape, jnp.bfloat16),
+            pltpu.VMEM(k_own.shape, jnp.bfloat16),
+            pltpu.VMEM(k_own.shape, jnp.bfloat16),
+            pltpu.VMEM(k_own.shape, jnp.float32),
+            pltpu.VMEM(k_own.shape, jnp.float32),
+            pltpu.SemaphoreType.DMA((3,)),
+        ],
         compiler_params=pltpu.CompilerParams(vmem_limit_bytes=32 * 2**20),
         name="prepare",
     )(queries, k_own, v_own)
 
 
 def attend_kernel(
-    listed_ref, q_ref, k_own_ref, v_own_ref, *refs, slots, choices,
+    chosen_ref, q_ref, k_own_ref, v_own_ref, *refs, slots, choices, place,
 ):
     k_refs, v_refs = refs[:choices], refs[choices : 2 * choices]
     out_ref, k_buf, v_buf, k_wide, v_wide, sems = refs[2 * choices :]
     kv_dev, tokens, dim = k_own_ref.shape
     group = q_ref.shape[1] // tokens
     block = tokens * kv_dev
+    target = lax.axis_index("seq").astype(jnp.int32)
+    own_at = jnp.int32(0)
+    for j in range(1, slots):
+        own_at = jnp.where(chosen_ref[target, j] == target, j, own_at)
     bias = []
     for j in range(slots - 1):
-        source = listed_ref[j]
+        source = chosen_ref[target, jnp.where(j >= own_at, j + 1, j)]
         bias.append(jnp.where(source < 0, NO_KEY, 0.0).astype(jnp.float32))
+        at = jnp.where(source < 0, 0, place(j, source, target))
         for i in range(choices):
 
-            @pl.when(jnp.maximum(source, 0) == i)
+            @pl.when(at == i)
             def _start(i=i, j=j):
                 for n, (parts, buf) in enumerate(((k_refs, k_buf), (v_refs, v_buf))):
                     pltpu.make_async_copy(
@@ -108,7 +133,8 @@
             )
 
 
-def attend(listed, queries, k_own, v_own, k_parts, v_parts, slots):
+def attend(chosen, queries, k_own, v_own, k_parts, v_parts, place):
+    slots = chosen.shape[1]
     kv_dev, tokens, dim = k_own.shape
     heads = queries.shape[0] * queries.shape[1] // tokens
     rest = (slots - 1) * tokens * kv_dev
@@ -116,7 +142,7 @@
     vmem = pl.BlockSpec(memory_space=pltpu.VMEM)
     hbm = pl.BlockSpec(memory_space=pltpu.HBM)
     return pl.pallas_call(
-        functools.partial(attend_kernel, slots=slots, choices=choices),
+        functools.partial(attend_kernel, slots=slots, choices=choices, place=place),
         out_shape=jax.ShapeDtypeStruct((tokens, heads, dim), jnp.bfloat16),
         in_specs=[pl.BlockSpec(memory_space=pltpu.SMEM), vmem, vmem, vmem] + [hbm] * (2 * choices),
         out_specs=vmem,
@@ -129,7 +155,7 @@
         ],
         compiler_params=pltpu.CompilerParams(vmem_limit_bytes=32 * 2**20),
         name="attend",
-    )(listed, queries, k_own, v_own, *k_parts, *v_parts)
+    )(chosen, queries, k_own, v_own, *k_parts, *v_parts)
 
 
 def others(row, target):
@@ -139,13 +165,20 @@
     return jnp.where(j >= own_at[..., None], row[..., 1:], row[..., :-1])
 
 
-def climb(own, members):
+def climb(k_own, v_own, members):
     up = [(s, (s + PAIR) % members) for s in range(members)]
     across = [(s, s ^ 1) for s in range(members)]
-    same = [own]
-    for _ in range(1, members // PAIR):
-        same.append(lax.ppermute(same[-1], "seq", up))
-    return same[1:] + [lax.ppermute(part, "seq", across) for part in same]
+    same, other = [[k_own], [v_own]], [[], []]
+    for step in range(members // PAIR):
+        last = step == members // PAIR - 1
+        for n in range(2):
+            if step:
+                same[n][-1], other[n][-1] = lax.optimization_barrier((same[n][-1], other[n][-1]))
+            here = same[n][-1]
+            if not last:
+                same[n].append(lax.ppermute(here, "seq", up))
+            other[n].append(lax.ppermute(here, "seq", across))
+    return [same[n][1:] + other[n] for n in range(2)]
 
 
 def relay(own, chosen, members):
@@ -162,22 +195,24 @@
     members = lax.axis_size("seq")
     tokens, kv_dev, dim = keys.shape
     slots = chosen.shape[1]
-    target = lax.axis_index("seq").astype(jnp.int32)
-    listed = others(lax.dynamic_index_in_dim(chosen, target, 0, False), target)
     k_own = keys.reshape(tokens * kv_dev, dim)
     v_own = values.reshape(tokens * kv_dev, dim)
     if members <= MOST_CLIMBED:
-        k_parts, v_parts = climb(k_own, members), climb(v_own, members)
-        steps = target // PAIR - listed // PAIR
-        crossed = (target ^ listed) & 1
-        at = steps - 1 + crossed * (members // PAIR)
+        k_parts, v_parts = climb(k_own, v_own, members)
+        queries, _ = lax.optimization_barrier((queries, v_parts[1]))
+
+        def place(slot, source, target):
+            return (target >> 1) - (source >> 1) - 1 + ((target ^ source) & 1) * (members // PAIR)
+
     else:
         arrived = relay((k_own, v_own), chosen, members)
         k_parts, v_parts = ([arrived[n, j] for j in range(slots - 1)] for n in range(2))
-        at = jnp.arange(slots - 1, dtype=jnp.int32)
-    at = jnp.where(listed < 0, -1, at)
+
+        def place(slot, source, target):
+            return jnp.int32(slot)
+
     ready = prepare(queries, k_own, v_own, kv_dev)
-    return attend(at, *ready, k_parts, v_parts, slots)
+    return attend(chosen, *ready, k_parts, v_parts, place)
 
 
 def solution(mesh):

time: 44.7 us -> 40.3 us (0.902)
  starting transfers between devices: 15.9 us -> 12.7 us
  other arithmetic: 1.51 us -> 0 us
  local copies, waits for them, and re-layouts: 3.86 us -> 3.12 us
  waiting for transfers between devices: 17.4 us -> 18 us
  Pallas kernels: 5.74 us -> 6.25 us
    ppermute x14, starting transfers between devices: 15.9 us -> 12.7 us  [the longest x8 8.49 us: climb(): other[n].append(lax.ppermute(here, 'seq', across))]
    another operation x1 -> x0, other arithmetic: 0.68 us -> none  [others(): own_at = jnp.argmax(row == target[..., None], axis=-1)]
    select_n x1 -> x0, other arithmetic: 0.65 us -> none  [per_device(): at = jnp.where(listed < 0, -1, at)]
    unnamed x8 -> x9, local copies, waits for them, and re-layouts: 3.71 us -> 3.12 us
    ppermute x14, waiting for transfers between devices: 17.4 us -> 18 us  [the longest x6 13 us: climb(): same[n].append(lax.ppermute(here, 'seq', up))]
  transfers between devices with their start and end apart: 14 -> 14, of which waited for: 8 -> 9; matrix products, arithmetic and copies ran while one was open for 4% -> 0% of each run, Pallas kernels for 1% -> 2%
where the time goes in v4:
time: 40.3 us; the launch traced here: 40.1 us
  waiting for transfers between devices  18 us (45%)
  starting transfers between devices  12.7 us (32%)
  Pallas kernels  6.25 us (16%)
  local copies, waits for them, and re-layouts  3.12 us (8%)
    ppermute x6, waiting for transfers between devices, climb(): same[n].append(lax.ppermute(here, 'seq', up))  13 us
    ppermute x8, starting transfers between devices, climb(): other[n].append(lax.ppermute(here, 'seq', across))  8.49 us
    pallas_call x1, Pallas kernels, attend(): pl.pallas_call(functools.partial(attend_kernel, slots=slots, choices=choi...  5.61 us
    ppermute x8, waiting for transfers between devices, climb(): other[n].append(lax.ppermute(here, 'seq', across))  5.03 us
    ppermute x6, starting transfers between devices, climb(): same[n].append(lax.ppermute(here, 'seq', up))  4.24 us
    unnamed x9, local copies, waits for them, and re-layouts  3.12 us
  transfers between devices with their start and end apart: 14, of which 9 were waited for; matrix products, arithmetic and copies ran while one was open for 0% of the time, Pallas kernels for 2%

profile of v4, /device:TPU:0, one launch (start us, length us, event | category | flops | bytes accessed | tf_op | source)
XLA Modules:
  0.0 40.1 jit_solution(1052562703349449177)
XLA Ops:
  0.0 0.0 copy-start.3
  0.0 2.9 %collective-permute-start.5 = (bf16[512,128]{1,0:T(8,128)(2,1)}, bf16[512,128]{1,0:T(8,128)(2,1)S(1)}, u32[]{:S(2)}, u32[]{:S(2)}) collective-permute-start(bf16[512,128]{1,0:T(8,128)(2,1)} %bitcast.2), channel_id=1, source_target_pairs={{0,2},{2,0},{4,6},{6,4},{8,10},{10,8},{12,14},{14,12},{1,3},{3,1},... | collective-permute-start | bytes 393224 | tf_op jit(solution)/shard_map/ppermute | solution.py:180
  2.9 1.6 %collective-permute-start.4 = (bf16[512,128]{1,0:T(8,128)(2,1)}, bf16[512,128]{1,0:T(8,128)(2,1)S(1)}, u32[]{:S(2)}, u32[]{:S(2)}) collective-permute-start(bf16[512,128]{1,0:T(8,128)(2,1)} %bitcast.3), channel_id=1, source_target_pairs={{0,4},{2,6},{4,8},{6,10},{8,12},{10,14},{12,0},{14,2},{1,5},{3,7},... | collective-permute-start | bytes 393224 | tf_op jit(solution)/shard_map/ppermute | solution.py:179
  4.5 0.5 %collective-permute-start.1 = (bf16[512,128]{1,0:T(8,128)(2,1)}, bf16[512,128]{1,0:T(8,128)(2,1)S(1)}, u32[]{:S(2)}, u32[]{:S(2)}) collective-permute-start(bf16[512,128]{1,0:T(8,128)(2,1)} %bitcast.5), channel_id=1, source_target_pairs={{0,2},{2,0},{4,6},{6,4},{8,10},{10,8},{12,14},{14,12},{1,3},{3,1},... | collective-permute-start | bytes 393224 | tf_op jit(solution)/shard_map/ppermute | solution.py:180
  5.1 1.6 %collective-permute-start = (bf16[512,128]{1,0:T(8,128)(2,1)}, bf16[512,128]{1,0:T(8,128)(2,1)S(1)}, u32[]{:S(2)}, u32[]{:S(2)}) collective-permute-start(bf16[512,128]{1,0:T(8,128)(2,1)} %bitcast.6), channel_id=1, source_target_pairs={{0,4},{2,6},{4,8},{6,10},{8,12},{10,14},{12,0},{14,2},{1,5},{3,7},... | collective-permute-start | bytes 393224 | tf_op jit(solution)/shard_map/ppermute | solution.py:179
  6.6 0.5 %collective-permute-done.5.refs_3_ = bf16[512,128]{1,0:T(8,128)(2,1)S(1)} collective-permute-done((bf16[512,128]{1,0:T(8,128)(2,1)}, bf16[512,128]{1,0:T(8,128)(2,1)S(1)}, u32[]{:S(2)}, u32[]{:S(2)}) %collective-permute-start.5) | collective-permute-done | bytes 131104 | tf_op jit(solution)/shard_map/ppermute | solution.py:180
  7.2 4.2 %collective-permute-done.4.refs_0_ = bf16[512,128]{1,0:T(8,128)(2,1)S(1)} collective-permute-done((bf16[512,128]{1,0:T(8,128)(2,1)}, bf16[512,128]{1,0:T(8,128)(2,1)S(1)}, u32[]{:S(2)}, u32[]{:S(2)}) %collective-permute-start.4) | collective-permute-done | bytes 131104 | tf_op jit(solution)/shard_map/ppermute | solution.py:179
  11.3 0.0 collective-permute-start.7
  11.4 0.0 collective-permute-start.6
  11.4 0.0 collective-permute-done.1.refs_10_
  11.4 1.4 %collective-permute-done.refs_7_ = bf16[512,128]{1,0:T(8,128)(2,1)S(1)} collective-permute-done((bf16[512,128]{1,0:T(8,128)(2,1)}, bf16[512,128]{1,0:T(8,128)(2,1)S(1)}, u32[]{:S(2)}, u32[]{:S(2)}) %collective-permute-start) | collective-permute-done | bytes 131104 | tf_op jit(solution)/shard_map/ppermute | solution.py:179
  12.8 0.7 %collective-permute-start.3 = (bf16[512,128]{1,0:T(8,128)(2,1)S(1)}, bf16[512,128]{1,0:T(8,128)(2,1)S(1)}, u32[]{:S(2)}, u32[]{:S(2)}) collective-permute-start(bf16[512,128]{1,0:T(8,128)(2,1)S(1)} %collective-permute-done.refs_7_), channel_id=1, source_target_pairs={{0,2},{2,0},{4,6},{6,4},{8,10},{10,8},{12,14},{14,12},{1,3},{3,1},... | collective-permute-start | bytes 393224 | tf_op jit(solution)/shard_map/ppermute | solution.py:180
  13.5 1.1 %collective-permute-start.2 = (bf16[512,128]{1,0:T(8,128)(2,1)S(1)}, bf16[512,128]{1,0:T(8,128)(2,1)S(1)}, u32[]{:S(2)}, u32[]{:S(2)}) collective-permute-start(bf16[512,128]{1,0:T(8,128)(2,1)S(1)} %collective-permute-done.refs_7_), channel_id=1, source_target_pairs={{0,4},{2,6},{4,8},{6,10},{8,12},{10,14},{12,0},{14,2},{1,5},{3,7},... | collective-permute-start | bytes 393224 | tf_op jit(solution)/shard_map/ppermute | solution.py:179
  14.6 2.4 %collective-permute-done.7.refs_4_ = bf16[512,128]{1,0:T(8,128)(2,1)S(1)} collective-permute-done((bf16[512,128]{1,0:T(8,128)(2,1)S(1)}, bf16[512,128]{1,0:T(8,128)(2,1)S(1)}, u32[]{:S(2)}, u32[]{:S(2)}) %collective-permute-start.7) | collective-permute-done | bytes 131104 | tf_op jit(solution)/shard_map/ppermute | solution.py:180
  17.0 1.8 %collective-permute-done.6.refs_1_ = bf16[512,128]{1,0:T(8,128)(2,1)S(1)} collective-permute-done((bf16[512,128]{1,0:T(8,128)(2,1)S(1)}, bf16[512,128]{1,0:T(8,128)(2,1)S(1)}, u32[]{:S(2)}, u32[]{:S(2)}) %collective-permute-start.6) | collective-permute-done | bytes 131104 | tf_op jit(solution)/shard_map/ppermute | solution.py:179
  18.8 1.7 %collective-permute-start.9 = (bf16[512,128]{1,0:T(8,128)(2,1)S(1)}, bf16[512,128]{1,0:T(8,128)(2,1)S(1)}, u32[]{:S(2)}, u32[]{:S(2)}) collective-permute-start(bf16[512,128]{1,0:T(8,128)(2,1)S(1)} %collective-permute-done.6.refs_1_), channel_id=1, source_target_pairs={{0,2},{2,0},{4,6},{6,4},{8,10},{10,8},{12,14},{14,12},{1,3},{3,1},... | collective-permute-start | bytes 393224 | tf_op jit(solution)/shard_map/ppermute | solution.py:180
  20.5 0.0 collective-permute-start.8
  20.5 0.0 collective-permute-done.3.refs_11_
  20.5 0.0 collective-permute-done.2.refs_8_
  20.5 2.3 %collective-permute-start.12 = (bf16[512,128]{1,0:T(8,128)(2,1)S(1)}, bf16[512,128]{1,0:T(8,128)(2,1)S(1)}, u32[]{:S(2)}, u32[]{:S(2)}) collective-permute-start(bf16[512,128]{1,0:T(8,128)(2,1)S(1)} %collective-permute-done.2.refs_8_), channel_id=1, source_target_pairs={{0,2},{2,0},{4,6},{6,4},{8,10},{10,8},{12,14},{14,12},{1,3},{3,1},... | collective-permute-start | bytes 393224 | tf_op jit(solution)/shard_map/ppermute | solution.py:180
  22.8 0.0 collective-permute-start.11
  22.8 0.9 %collective-permute-done.9.refs_5_ = bf16[512,128]{1,0:T(8,128)(2,1)S(1)} collective-permute-done((bf16[512,128]{1,0:T(8,128)(2,1)S(1)}, bf16[512,128]{1,0:T(8,128)(2,1)S(1)}, u32[]{:S(2)}, u32[]{:S(2)}) %collective-permute-start.9) | collective-permute-done | bytes 131104 | tf_op jit(solution)/shard_map/ppermute | solution.py:180
  23.7 3.5 %collective-permute-done.8.refs_2_ = bf16[512,128]{1,0:T(8,128)(2,1)S(1)} collective-permute-done((bf16[512,128]{1,0:T(8,128)(2,1)S(1)}, bf16[512,128]{1,0:T(8,128)(2,1)S(1)}, u32[]{:S(2)}, u32[]{:S(2)}) %collective-permute-start.8) | collective-permute-done | bytes 131104 | tf_op jit(solution)/shard_map/ppermute | solution.py:179
  27.3 0.3 collective-permute-start.10
  27.6 0.0 collective-permute-done.12.refs_12_
  27.6 2.0 %collective-permute-done.11.refs_9_ = bf16[512,128]{1,0:T(8,128)(2,1)S(1)} collective-permute-done((bf16[512,128]{1,0:T(8,128)(2,1)S(1)}, bf16[512,128]{1,0:T(8,128)(2,1)S(1)}, u32[]{:S(2)}, u32[]{:S(2)}) %collective-permute-start.11) | collective-permute-done | bytes 131104 | tf_op jit(solution)/shard_map/ppermute | solution.py:179
  29.6 0.0 collective-permute-start.13
  29.6 0.0 copy-done.3
  29.6 0.1 copy.5.chosen_ref
  29.7 0.0 copy-start
  29.7 1.2 %copy-done = bf16[128,32,128]{2,1,0:T(8,128)(2,1)S(1)} copy-done((bf16[128,32,128]{2,1,0:T(8,128)(2,1)S(1)}, bf16[128,32,128]{2,1,0:T(8,128)(2,1)}, u32[]{:S(2)}) %copy-start) | copy-done | bytes 1048600
  30.9 0.0 copy-start.1
  30.9 0.9 %copy-done.1 = bf16[128,4,128]{2,1,0:T(4,128)(2,1)S(1)} copy-done((bf16[128,4,128]{2,1,0:T(4,128)(2,1)S(1)}, bf16[128,4,128]{2,1,0:T(4,128)(2,1)}, u32[]{:S(2)}) %copy-start.1) | copy-done | bytes 131096
  31.8 0.0 copy-start.2
  31.8 0.9 %copy-done.2 = bf16[128,4,128]{2,1,0:T(4,128)(2,1)S(1)} copy-done((bf16[128,4,128]{2,1,0:T(4,128)(2,1)S(1)}, bf16[128,4,128]{2,1,0:T(4,128)(2,1)}, u32[]{:S(2)}) %copy-start.2) | copy-done | bytes 131096
  32.7 0.6 %prepare.1 = (bf16[4,1024,128]{2,1,0:T(8,128)(2,1)S(1)}, bf16[4,128,128]{2,1,0:T(8,128)(2,1)S(1)}, bf16[4,128,128]{2,1,0:T(8,128)(2,1)S(1)}) custom-call(bf16[128,32,128]{2,1,0:T(8,128)(2,1)S(1)} %copy-done, bf16[512,128]{1,0:T(8,128)(2,1)S(1)} %bitcast.4, bf16[512,128]{1,0:T(8,128)(2,1)S(1)} %bitcast.7), custom_call_target="tpu_custom_call" | custom-call | tf_op jit(solution)/shard_map/prepare/pallas_call | solution.py:46
  33.3 0.0 collective-permute-done.10.refs_6_
  33.4 1.2 %collective-permute-done.13.refs_13_ = bf16[512,128]{1,0:T(8,128)(2,1)S(1)} collective-permute-done((bf16[512,128]{1,0:T(8,128)(2,1)S(1)}, bf16[512,128]{1,0:T(8,128)(2,1)S(1)}, u32[]{:S(2)}, u32[]{:S(2)}) %collective-permute-start.13) | collective-permute-done | bytes 131104 | tf_op jit(solution)/shard_map/ppermute | solution.py:180
  34.5 5.6 %attend.1 = bf16[128,32,128]{2,1,0:T(8,128)(2,1)} custom-call(s32[8,4]{1,0:T(8,128)S(1)} %copy.5.chosen_ref, bf16[4,1024,128]{2,1,0:T(8,128)(2,1)S(1)} %get-tuple-element.24.q_ref, bf16[4,128,128]{2,1,0:T(8,128)(2,1)S(1)} %get-tuple-element.25.k_own_ref, bf16[4,128,128]{2,1,0:T(8,128)(2,1)S(1)} %get-tuple-element.26.v_own_ref, ...), custom_call_target="tpu_custom_call" | custom-call | tf_op jit(solution)/shard_map/attend/pallas_call | solution.py:144
Async XLA Ops:
  0.0 29.6 %copy-start.3 = (s32[8,4]{0,1:T(4,128)S(1)}, s32[8,4]{0,1:T(4,128)}, u32[]{:S(2)}) copy-start(s32[8,4]{0,1:T(4,128)} %param.7) | copy-start | bytes 388
  0.0 7.2 %collective-permute-start.5 = (bf16[512,128]{1,0:T(8,128)(2,1)}, bf16[512,128]{1,0:T(8,128)(2,1)S(1)}, u32[]{:S(2)}, u32[]{:S(2)}) collective-permute-start(bf16[512,128]{1,0:T(8,128)(2,1)} %bitcast.2), channel_id=1, source_target_pairs={{0,2},{2,0},{4,6},{6,4},{8,10},{10,8},{12,14},{14,12},{1,3},{3,1},... | collective-permute-start | bytes 393224 | tf_op jit(solution)/shard_map/ppermute | solution.py:180
  2.9 8.4 %collective-permute-start.4 = (bf16[512,128]{1,0:T(8,128)(2,1)}, bf16[512,128]{1,0:T(8,128)(2,1)S(1)}, u32[]{:S(2)}, u32[]{:S(2)}) collective-permute-start(bf16[512,128]{1,0:T(8,128)(2,1)} %bitcast.3), channel_id=1, source_target_pairs={{0,4},{2,6},{4,8},{6,10},{8,12},{10,14},{12,0},{14,2},{1,5},{3,7},... | collective-permute-start | bytes 393224 | tf_op jit(solution)/shard_map/ppermute | solution.py:179
  4.5 6.8 %collective-permute-start.1 = (bf16[512,128]{1,0:T(8,128)(2,1)}, bf16[512,128]{1,0:T(8,128)(2,1)S(1)}, u32[]{:S(2)}, u32[]{:S(2)}) collective-permute-start(bf16[512,128]{1,0:T(8,128)(2,1)} %bitcast.5), channel_id=1, source_target_pairs={{0,2},{2,0},{4,6},{6,4},{8,10},{10,8},{12,14},{14,12},{1,3},{3,1},... | collective-permute-start | bytes 393224 | tf_op jit(solution)/shard_map/ppermute | solution.py:180
  5.1 7.8 %collective-permute-start = (bf16[512,128]{1,0:T(8,128)(2,1)}, bf16[512,128]{1,0:T(8,128)(2,1)S(1)}, u32[]{:S(2)}, u32[]{:S(2)}) collective-permute-start(bf16[512,128]{1,0:T(8,128)(2,1)} %bitcast.6), channel_id=1, source_target_pairs={{0,4},{2,6},{4,8},{6,10},{8,12},{10,14},{12,0},{14,2},{1,5},{3,7},... | collective-permute-start | bytes 393224 | tf_op jit(solution)/shard_map/ppermute | solution.py:179
  11.3 5.6 %collective-permute-start.7 = (bf16[512,128]{1,0:T(8,128)(2,1)S(1)}, bf16[512,128]{1,0:T(8,128)(2,1)S(1)}, u32[]{:S(2)}, u32[]{:S(2)}) collective-permute-start(bf16[512,128]{1,0:T(8,128)(2,1)S(1)} %collective-permute-done.4.refs_0_), channel_id=1, source_target_pairs={{0,2},{2,0},{4,6},{6,4},{8,10},{10,8},{12,14},{14,12},{1,3},{3,1},... | collective-permute-start | bytes 393224 | tf_op jit(solution)/shard_map/ppermute | solution.py:180
  11.4 7.4 %collective-permute-start.6 = (bf16[512,128]{1,0:T(8,128)(2,1)S(1)}, bf16[512,128]{1,0:T(8,128)(2,1)S(1)}, u32[]{:S(2)}, u32[]{:S(2)}) collective-permute-start(bf16[512,128]{1,0:T(8,128)(2,1)S(1)} %collective-permute-done.4.refs_0_), channel_id=1, source_target_pairs={{0,4},{2,6},{4,8},{6,10},{8,12},{10,14},{12,0},{14,2},{1,5},{3,7},... | collective-permute-start | bytes 393224 | tf_op jit(solution)/shard_map/ppermute | solution.py:179
  12.8 7.7 %collective-permute-start.3 = (bf16[512,128]{1,0:T(8,128)(2,1)S(1)}, bf16[512,128]{1,0:T(8,128)(2,1)S(1)}, u32[]{:S(2)}, u32[]{:S(2)}) collective-permute-start(bf16[512,128]{1,0:T(8,128)(2,1)S(1)} %collective-permute-done.refs_7_), channel_id=1, source_target_pairs={{0,2},{2,0},{4,6},{6,4},{8,10},{10,8},{12,14},{14,12},{1,3},{3,1},... | collective-permute-start | bytes 393224 | tf_op jit(solution)/shard_map/ppermute | solution.py:180
  13.5 7.0 %collective-permute-start.2 = (bf16[512,128]{1,0:T(8,128)(2,1)S(1)}, bf16[512,128]{1,0:T(8,128)(2,1)S(1)}, u32[]{:S(2)}, u32[]{:S(2)}) collective-permute-start(bf16[512,128]{1,0:T(8,128)(2,1)S(1)} %collective-permute-done.refs_7_), channel_id=1, source_target_pairs={{0,4},{2,6},{4,8},{6,10},{8,12},{10,14},{12,0},{14,2},{1,5},{3,7},... | collective-permute-start | bytes 393224 | tf_op jit(solution)/shard_map/ppermute | solution.py:179
  18.8 5.0 %collective-permute-start.9 = (bf16[512,128]{1,0:T(8,128)(2,1)S(1)}, bf16[512,128]{1,0:T(8,128)(2,1)S(1)}, u32[]{:S(2)}, u32[]{:S(2)}) collective-permute-start(bf16[512,128]{1,0:T(8,128)(2,1)S(1)} %collective-permute-done.6.refs_1_), channel_id=1, source_target_pairs={{0,2},{2,0},{4,6},{6,4},{8,10},{10,8},{12,14},{14,12},{1,3},{3,1},... | collective-permute-start | bytes 393224 | tf_op jit(solution)/shard_map/ppermute | solution.py:180
  20.5 6.8 %collective-permute-start.8 = (bf16[512,128]{1,0:T(8,128)(2,1)S(1)}, bf16[512,128]{1,0:T(8,128)(2,1)S(1)}, u32[]{:S(2)}, u32[]{:S(2)}) collective-permute-start(bf16[512,128]{1,0:T(8,128)(2,1)S(1)} %collective-permute-done.6.refs_1_), channel_id=1, source_target_pairs={{0,4},{2,6},{4,8},{6,10},{8,12},{10,14},{12,0},{14,2},{1,5},{3,7},... | collective-permute-start | bytes 393224 | tf_op jit(solution)/shard_map/ppermute | solution.py:179
  20.5 7.0 %collective-permute-start.12 = (bf16[512,128]{1,0:T(8,128)(2,1)S(1)}, bf16[512,128]{1,0:T(8,128)(2,1)S(1)}, u32[]{:S(2)}, u32[]{:S(2)}) collective-permute-start(bf16[512,128]{1,0:T(8,128)(2,1)S(1)} %collective-permute-done.2.refs_8_), channel_id=1, source_target_pairs={{0,2},{2,0},{4,6},{6,4},{8,10},{10,8},{12,14},{14,12},{1,3},{3,1},... | collective-permute-start | bytes 393224 | tf_op jit(solution)/shard_map/ppermute | solution.py:180
  22.8 6.8 %collective-permute-start.11 = (bf16[512,128]{1,0:T(8,128)(2,1)S(1)}, bf16[512,128]{1,0:T(8,128)(2,1)S(1)}, u32[]{:S(2)}, u32[]{:S(2)}) collective-permute-start(bf16[512,128]{1,0:T(8,128)(2,1)S(1)} %collective-permute-done.2.refs_8_), channel_id=1, source_target_pairs={{0,4},{2,6},{4,8},{6,10},{8,12},{10,14},{12,0},{14,2},{1,5},{3,7},... | collective-permute-start | bytes 393224 | tf_op jit(solution)/shard_map/ppermute | solution.py:179
  27.3 6.1 %collective-permute-start.10 = (bf16[512,128]{1,0:T(8,128)(2,1)S(1)}, bf16[512,128]{1,0:T(8,128)(2,1)S(1)}, u32[]{:S(2)}, u32[]{:S(2)}) collective-permute-start(bf16[512,128]{1,0:T(8,128)(2,1)S(1)} %collective-permute-done.8.refs_2_), channel_id=1, source_target_pairs={{0,2},{2,0},{4,6},{6,4},{8,10},{10,8},{12,14},{14,12},{1,3},{3,1},... | collective-permute-start | bytes 393224 | tf_op jit(solution)/shard_map/ppermute | solution.py:180
  29.6 5.0 %collective-permute-start.13 = (bf16[512,128]{1,0:T(8,128)(2,1)S(1)}, bf16[512,128]{1,0:T(8,128)(2,1)S(1)}, u32[]{:S(2)}, u32[]{:S(2)}) collective-permute-start(bf16[512,128]{1,0:T(8,128)(2,1)S(1)} %collective-permute-done.11.refs_9_), channel_id=1, source_target_pairs={{0,2},{2,0},{4,6},{6,4},{8,10},{10,8},{12,14},{14,12},{1,3},{3,1},... | collective-permute-start | bytes 393224 | tf_op jit(solution)/shard_map/ppermute | solution.py:180
  29.7 1.2 %copy-start = (bf16[128,32,128]{2,1,0:T(8,128)(2,1)S(1)}, bf16[128,32,128]{2,1,0:T(8,128)(2,1)}, u32[]{:S(2)}) copy-start(bf16[128,32,128]{2,1,0:T(8,128)(2,1)} %q_hbm) | copy-start | bytes 3145732
  30.9 0.9 %copy-start.1 = (bf16[128,4,128]{2,1,0:T(4,128)(2,1)S(1)}, bf16[128,4,128]{2,1,0:T(4,128)(2,1)}, u32[]{:S(2)}) copy-start(bf16[128,4,128]{2,1,0:T(4,128)(2,1)} %param.5) | copy-start | bytes 393220
  31.8 0.9 %copy-start.2 = (bf16[128,4,128]{2,1,0:T(4,128)(2,1)S(1)}, bf16[128,4,128]{2,1,0:T(4,128)(2,1)}, u32[]{:S(2)}) copy-start(bf16[128,4,128]{2,1,0:T(4,128)(2,1)} %param.6) | copy-start | bytes 393220

commit v5 on v0

v5 whole, which is shorter than its diff:
```python
import functools
import math

import jax
import jax.numpy as jnp
from jax import lax
from jax.experimental import pallas as pl
from jax.experimental.pallas import tpu as pltpu
from jax.sharding import PartitionSpec as P

NO_KEY = -1e30
ROW_CHUNK = 256
MOST_ROUND = 16


def params():
    return pltpu.CompilerParams(vmem_limit_bytes=16 * 2**20)


def vmem():
    return pl.BlockSpec(memory_space=pltpu.VMEM)


def prepare_kernel(
    q_hbm, k_hbm, v_hbm, q_out, k_out, v_out, q_ref, k_ref, v_ref, k_wide, v_wide, sems, *, kv_dev
):
    copies = [
        pltpu.make_async_copy(source, here, sems.at[n])
        for n, (source, here) in enumerate(((k_hbm, k_ref), (v_hbm, v_ref), (q_hbm, q_ref)))
    ]
    for copy in copies:
        copy.start()
    tokens, heads, dim = q_ref.shape
    group = heads // kv_dev
    for copy, ref, wide, out in zip(copies, (k_ref, v_ref), (k_wide, v_wide), (k_out, v_out)):
        copy.wait()
        wide[...] = ref[...].astype(jnp.float32)
        for h in range(kv_dev):
            out[h] = wide[pl.ds(h, tokens, stride=kv_dev), :].astype(jnp.bfloat16)
    copies[2].wait()
    for h in range(kv_dev):
        q = q_ref[:, pl.ds(h * group, group), :].astype(jnp.float32)
        q_out[h] = q.reshape(tokens * group, dim).astype(jnp.bfloat16)


def prepare(queries, k_own, v_own, kv_dev):
    tokens, heads, dim = queries.shape
    operands = [pltpu.with_memory_space_constraint(x, pltpu.HBM) for x in (queries, k_own, v_own)]
    by_head = jax.ShapeDtypeStruct((kv_dev, tokens, dim), jnp.bfloat16)
    return pl.pallas_call(
        functools.partial(prepare_kernel, kv_dev=kv_dev),
        out_shape=(
            jax.ShapeDtypeStruct((kv_dev, tokens * heads // kv_dev, dim), jnp.bfloat16),
            by_head,
            by_head,
        ),
        in_specs=[pl.BlockSpec(memory_space=pltpu.HBM)] * 3,
        out_specs=(vmem(), vmem(), vmem()),
        scratch_shapes=[
            pltpu.VMEM(queries.shape, jnp.bfloat16),
            pltpu.VMEM(k_own.shape, jnp.bfloat16),
            pltpu.VMEM(k_own.shape, jnp.bfloat16),
            pltpu.VMEM(k_own.shape, jnp.float32),
            pltpu.VMEM(k_own.shape, jnp.float32),
            pltpu.SemaphoreType.DMA((3,)),
        ],
        compiler_params=params(),
        name="prepare",
    )(*operands)


def gather_listed(chosen_ref, parts, wide, sources):
    target = lax.axis_index("seq").astype(jnp.int32)
    block = parts[0].shape[0]
    most = wide.shape[0] // block
    count = jnp.int32(0)
    for part, source in zip(parts, sources(target)):
        is_listed = chosen_ref[target, 0] == source
        for j in range(1, chosen_ref.shape[1]):
            is_listed |= chosen_ref[target, j] == source
        is_listed &= count < most

        @pl.when(is_listed)
        def _take(part=part, count=count):
            rows = pl.ds(pl.multiple_of(count * block, block), block)
            wide[rows, :] = part[...].astype(jnp.float32)

        count += is_listed.astype(jnp.int32)
    for j in range(most):

        @pl.when(count <= j)
        def _clear(j=j):
            wide[pl.ds(j * block, block), :] = jnp.zeros((block, wide.shape[1]), jnp.float32)

    return count


def weights_kernel(chosen_ref, q_ref, own_ref, *refs, sources):
    *parts, out_ref, wide = refs
    kv_dev, tokens, dim = own_ref.shape
    rows_all = q_ref.shape[1]
    group = rows_all // tokens
    others = wide.shape[0] // (tokens * kv_dev)
    count = gather_listed(chosen_ref, parts, wide, sources)
    bias = [jnp.where(count <= j, NO_KEY, 0.0).astype(jnp.float32) for j in range(others)]
    factor = dim ** (-0.5) * math.log2(math.e)
    for h in range(kv_dev):
        k_h = wide[pl.ds(h, others * tokens, stride=kv_dev), :].astype(jnp.bfloat16)
        k_h = jnp.concatenate([own_ref[h], k_h], axis=0)
        for first in range(0, rows_all, ROW_CHUNK):
            rows = pl.ds(first, ROW_CHUNK)
            s = lax.dot_general(
                q_ref[h, rows, :], k_h, (((1,), (1,)), ((), ())), preferred_element_type=jnp.float32
            )
            row = (lax.broadcasted_iota(jnp.int32, (ROW_CHUNK, tokens), 0) + first) // group
            key = lax.broadcasted_iota(jnp.int32, (ROW_CHUNK, tokens), 1)
            parts_s = [jnp.where(key <= row, s[:, :tokens], NO_KEY)]
            for j in range(others):
                parts_s.append(s[:, (j + 1) * tokens : (j + 2) * tokens] + bias[j])
            top = parts_s[0]
            for part in parts_s[1:]:
                top = jnp.maximum(top, part)
            top = jnp.max(top, axis=1, keepdims=True)
            for j, part in enumerate(parts_s):
                probs = jnp.exp2((part - top) * factor).astype(jnp.bfloat16)
                out_ref[h, rows, pl.ds(j * tokens, tokens)] = probs


def weights(chosen, queries, k_own, k_parts, sources, slots):
    kv_dev, rows, _ = queries.shape
    block, dim = k_parts[0].shape
    return pl.pallas_call(
        functools.partial(weights_kernel, sources=sources),
        out_shape=jax.ShapeDtypeStruct((kv_dev, rows, slots * block // kv_dev), jnp.bfloat16),
        in_specs=[pl.BlockSpec(memory_space=pltpu.SMEM)] + [vmem()] * (2 + len(k_parts)),
        out_specs=vmem(),
        scratch_shapes=[pltpu.VMEM(((slots - 1) * block, dim), jnp.float32)],
        compiler_params=params(),
        name="weights",
    )(chosen, queries, k_own, *k_parts)


def merge_kernel(chosen_ref, weights_ref, own_ref, *refs, sources):
    *parts, out_ref, wide = refs
    kv_dev, tokens, dim = own_ref.shape
    rows_all = weights_ref.shape[1]
    group = rows_all // tokens
    others = wide.shape[0] // (tokens * kv_dev)
    gather_listed(chosen_ref, parts, wide, sources)
    ones = jnp.ones(((others + 1) * tokens, dim), jnp.bfloat16)
    for h in range(kv_dev):
        v_h = wide[pl.ds(h, others * tokens, stride=kv_dev), :].astype(jnp.bfloat16)
        v_ones = jnp.concatenate([jnp.concatenate([own_ref[h], v_h], axis=0), ones], axis=1)
        for first in range(0, rows_all, ROW_CHUNK):
            both = jnp.dot(
                weights_ref[h, pl.ds(first, ROW_CHUNK), :], v_ones, preferred_element_type=jnp.float32
            )
            merged = (both[:, :dim] / both[:, dim:]).reshape(ROW_CHUNK // group, group, dim)
            rows = pl.ds(first // group, ROW_CHUNK // group)
            out_ref[rows, pl.ds(h * group, group), :] = merged.astype(jnp.bfloat16)


def merge(chosen, probs, v_own, v_parts, sources, slots):
    kv_dev, rows, _ = probs.shape
    block, dim = v_parts[0].shape
    tokens = block // kv_dev
    return pl.pallas_call(
        functools.partial(merge_kernel, sources=sources),
        out_shape=jax.ShapeDtypeStruct((tokens, rows * kv_dev // tokens, dim), jnp.bfloat16),
        in_specs=[pl.BlockSpec(memory_space=pltpu.SMEM)] + [vmem()] * (2 + len(v_parts)),
        out_specs=vmem(),
        scratch_shapes=[pltpu.VMEM(((slots - 1) * block, dim), jnp.float32)],
        compiler_params=params(),
        name="merge",
    )(chosen, probs, v_own, *v_parts)


def ring_at(place, members):
    back = members - 1 - place
    return jnp.where(place < members // 2, 2 * place, 2 * back + 1)


def ring_place(block, members):
    return jnp.where(block % 2 == 0, block // 2, members - 1 - block // 2)


def round_the_ring(k_own, v_own, ready, members):
    ring = list(range(0, members, 2)) + list(range(members - 1, 0, -2))
    ways = [
        [(ring[p], ring[(p + turn) % members]) for p in range(members)] for turn in (1, -1)
    ]

    def send(x, way):
        return lax.ppermute(x, "seq", ways[way])

    half = members // 2
    k_two, v_two, k_all, v_all = (k_own, k_own), (v_own, v_own), [], []
    for distance in range(1, half):
        k_two = tuple(send(x, way) for way, x in enumerate(k_two))
        if distance == half - 1:
            forward, k_first = lax.optimization_barrier((v_two[0], k_two[0]))
            v_two, k_two = (forward, v_two[1]), (k_first, k_two[1])
        v_two = tuple(send(x, way) for way, x in enumerate(v_two))
        if distance == 1:
            k_two, ready = lax.optimization_barrier((k_two, ready))
        elif distance < half - 1:
            k_two = lax.optimization_barrier(k_two)
        if distance < half - 1:
            v_two = lax.optimization_barrier(v_two)
        k_all += k_two
        v_all += v_two
    k_all.append(send(k_two[0], 0))
    v_all.append(send(v_two[1], 1))
    return k_all, v_all, ready


def ring_sources(members):
    def sources(target):
        place = ring_place(target, members)
        turns = [turn for far in range(1, members // 2) for turn in (-far, far)] + [members // 2]
        return [ring_at(lax.rem(place + turn + members, members), members) for turn in turns]

    return sources


def others(row, target):
    slots = row.shape[-1]
    own_at = jnp.argmax(row == target[..., None], axis=-1)
    j = jnp.arange(slots - 1)
    return jnp.where(j >= own_at[..., None], row[..., 1:], row[..., :-1])


def relay(k_own, v_own, chosen, members):
    block, dim = k_own.shape
    stacked = jnp.stack([k_own, v_own]).reshape(2, members, block // members, dim)
    shares = lax.all_to_all(stacked, "seq", split_axis=1, concat_axis=1, tiled=True)
    wanted = others(chosen, jnp.arange(members, dtype=jnp.int32))
    picked = jnp.take(shares, jnp.maximum(wanted, 0), axis=1)
    arrived = lax.all_to_all(picked, "seq", split_axis=1, concat_axis=3, tiled=True)
    count = wanted.shape[1]
    k_parts, v_parts = ([arrived[n, 0, j].reshape(block, dim) for j in range(count)] for n in range(2))
    return k_parts, v_parts, jnp.where(wanted < 0, -1, jnp.arange(count, dtype=jnp.int32))


def per_device(queries, keys, values, chosen):
    members = lax.axis_size("seq")
    tokens, kv_dev, dim = keys.shape
    slots = chosen.shape[1]
    k_own = keys.reshape(tokens * kv_dev, dim)
    v_own = values.reshape(tokens * kv_dev, dim)
    ready = prepare(queries, k_own, v_own, kv_dev)
    if members <= MOST_ROUND:
        k_parts, v_parts, ready = round_the_ring(k_own, v_own, ready, members)
        sources = ring_sources(members)
    else:
        k_parts, v_parts, chosen = relay(k_own, v_own, chosen, members)

        def sources(_):
            return [jnp.int32(j) for j in range(slots - 1)]

    q_ready, k_ready, v_ready = ready
    probs = weights(chosen, q_ready, k_ready, k_parts, sources, slots)
    return merge(chosen, probs, v_ready, v_parts, sources, slots)


def solution(mesh):
    rows = P(("groups", "seq"), "head", None)
    return jax.shard_map(
        per_device,
        mesh=mesh,
        in_specs=(rows, rows, rows, P("groups", None)),
        out_specs=rows,
        check_vma=False,
    )
```

time: 86.4 us -> 33.7 us (0.39)
  waiting for transfers between devices: 36.2 us -> 9.12 us
  other arithmetic: 10.9 us -> 0 us
  matrix products: 9.24 us -> 0 us
  local copies, waits for them, and re-layouts: 9.69 us -> 0.76 us
  Pallas kernels: 0 us -> 7.48 us
  loops' own time: 5.35 us -> 0 us
  starting transfers between devices: 14.4 us -> 16.1 us
    all_to_all x3 -> x0, waiting for transfers between devices: 36.2 us -> none  [the longest x1 23.7 us: per_device(): lax.all_to_all(picked, 'seq', split_axis=1, concat_axis=3, tiled=True)]
    ppermute x0 -> x14, starting transfers between devices: none -> 16.1 us  [send(): return lax.ppermute(x, 'seq', ways[way])]
    all_to_all x3 -> x0, starting transfers between devices: 14.4 us -> none  [the longest x1 7.25 us: per_device(): lax.all_to_all(stacked, 'seq', split_axis=1, concat_axis=1, tiled=True)]
    dot_general x8 -> x0, matrix products: 9.24 us -> none  [the longest x4 7.41 us: partial_block(): jnp.einsum('kgqj,jkd->qkgd', probs, value_block, preferred_element_type=j...]
    ppermute x0 -> x14, waiting for transfers between devices: none -> 9.12 us  [send(): return lax.ppermute(x, 'seq', ways[way])]
    pallas_call x0 -> x3, Pallas kernels: none -> 7.48 us  [the longest x1 3.01 us: merge(): pl.pallas_call(functools.partial(merge_kernel, sources=sources), out_shap...]
    reduce_sum x6 -> x0, other arithmetic: 6.76 us -> none  [the longest x1 4.87 us: per_device(): jnp.sum(jnp.transpose(weights, (0, 3, 1, 2))[..., None] * partial_value,...]
    another operation x1 -> x0, loops' own time: 5.35 us -> none  [per_device(): lax.map(one_slot, (blocks[0, 0], blocks[1, 0], codes_in))]
  transfers between devices with their start and end apart: 3 -> 14, of which waited for: 3 -> 8; matrix products, arithmetic and copies ran while one was open for 4% -> 2% of each run, Pallas kernels for 0% -> 13%
where the time goes in v5:
time: 33.7 us; the launch traced here: 33.5 us
  starting transfers between devices  16.1 us (48%)
  waiting for transfers between devices  9.12 us (27%)
  Pallas kernels  7.48 us (22%)
  local copies, waits for them, and re-layouts  0.76 us (2%)
    ppermute x14, starting transfers between devices, send(): return lax.ppermute(x, 'seq', ways[way])  16.1 us
    ppermute x14, waiting for transfers between devices, send(): return lax.ppermute(x, 'seq', ways[way])  9.12 us
    pallas_call x1, Pallas kernels, merge(): pl.pallas_call(functools.partial(merge_kernel, sources=sources), out_shap...  3.01 us
    pallas_call x1, Pallas kernels, weights(): pl.pallas_call(functools.partial(weights_kernel, sources=sources), out_sh...  2.9 us
    pallas_call x1, Pallas kernels, prepare(): pl.pallas_call(functools.partial(prepare_kernel, kv_dev=kv_dev), out_shap...  1.57 us
    unnamed x1, local copies, waits for them, and re-layouts  0.76 us
  transfers between devices with their start and end apart: 14, of which 8 were waited for; matrix products, arithmetic and copies ran while one was open for 2% of the time, Pallas kernels for 13%

profile of v5, /device:TPU:0, one launch (start us, length us, event | category | flops | bytes accessed | tf_op | source)
XLA Modules:
  0.0 33.5 jit_solution(1233483288673455388)
XLA Ops:
  0.0 3.0 %collective-permute-start = (bf16[512,128]{1,0:T(8,128)(2,1)}, bf16[512,128]{1,0:T(8,128)(2,1)S(1)}, u32[]{:S(2)}, u32[]{:S(2)}) collective-permute-start(bf16[512,128]{1,0:T(8,128)(2,1)} %bitcast.2), channel_id=1, source_target_pairs={{0,4},{4,8},{8,12},{12,14},{14,10},{10,6},{6,2},{2,0},{1,5},{5,9},... | collective-permute-start | bytes 393224 | tf_op jit(solution)/shard_map/ppermute | solution.py:194
  3.0 0.0 collective-permute-start.1
  3.0 2.0 %collective-permute-start.4 = (bf16[512,128]{1,0:T(8,128)(2,1)}, bf16[512,128]{1,0:T(8,128)(2,1)S(1)}, u32[]{:S(2)}, u32[]{:S(2)}) collective-permute-start(bf16[512,128]{1,0:T(8,128)(2,1)} %bitcast.5), channel_id=1, source_target_pairs={{0,4},{4,8},{8,12},{12,14},{14,10},{10,6},{6,2},{2,0},{1,5},{5,9},... | collective-permute-start | bytes 393224 | tf_op jit(solution)/shard_map/ppermute | solution.py:194
  5.1 0.0 collective-permute-start.5
  5.1 1.6 %prepare.1 = (bf16[4,1024,128]{2,1,0:T(8,128)(2,1)S(1)}, bf16[4,128,128]{2,1,0:T(8,128)(2,1)S(1)}, bf16[4,128,128]{2,1,0:T(8,128)(2,1)S(1)}) custom-call(bf16[128,32,128]{2,1,0:T(8,128)(2,1)} %q_hbm.1, bf16[512,128]{1,0:T(8,128)(2,1)} %bitcast.4, bf16[512,128]{1,0:T(8,128)(2,1)} %bitcast.7), custom_call_target="tpu_custom_call" | custom-call | tf_op jit(solution)/shard_map/prepare/pallas_call | solution.py:50
  6.6 0.8 %collective-permute-done.refs_0_ = bf16[512,128]{1,0:T(8,128)(2,1)S(1)} collective-permute-done((bf16[512,128]{1,0:T(8,128)(2,1)}, bf16[512,128]{1,0:T(8,128)(2,1)S(1)}, u32[]{:S(2)}, u32[]{:S(2)}) %collective-permute-start) | collective-permute-done | bytes 131104 | tf_op jit(solution)/shard_map/ppermute | solution.py:194
  7.5 2.1 %collective-permute-done.1.refs_1_ = bf16[512,128]{1,0:T(8,128)(2,1)S(1)} collective-permute-done((bf16[512,128]{1,0:T(8,128)(2,1)}, bf16[512,128]{1,0:T(8,128)(2,1)S(1)}, u32[]{:S(2)}, u32[]{:S(2)}) %collective-permute-start.1) | collective-permute-done | bytes 131104 | tf_op jit(solution)/shard_map/ppermute | solution.py:194
  9.6 1.6 %collective-permute-start.2 = (bf16[512,128]{1,0:T(8,128)(2,1)S(1)}, bf16[512,128]{1,0:T(8,128)(2,1)S(1)}, u32[]{:S(2)}, u32[]{:S(2)}) collective-permute-start(bf16[512,128]{1,0:T(8,128)(2,1)S(1)} %collective-permute-done.refs_0_), channel_id=1, source_target_pairs={{0,4},{4,8},{8,12},{12,14},{14,10},{10,6},{6,2},{2,0},{1,5},{5,9},... | collective-permute-start | bytes 393224 | tf_op jit(solution)/shard_map/ppermute | solution.py:194
  11.1 0.4 %collective-permute-start.3 = (bf16[512,128]{1,0:T(8,128)(2,1)S(1)}, bf16[512,128]{1,0:T(8,128)(2,1)S(1)}, u32[]{:S(2)}, u32[]{:S(2)}) collective-permute-start(bf16[512,128]{1,0:T(8,128)(2,1)S(1)} %collective-permute-done.1.refs_1_), channel_id=1, source_target_pairs={{0,2},{4,0},{8,4},{12,8},{14,12},{10,14},{6,10},{2,6},{1,3},{5,1},... | collective-permute-start | bytes 393224 | tf_op jit(solution)/shard_map/ppermute | solution.py:194
  11.6 0.0 collective-permute-done.4.refs_0_
  11.6 0.0 collective-permute-done.5.refs_1_
  11.6 1.6 %collective-permute-start.6 = (bf16[512,128]{1,0:T(8,128)(2,1)S(1)}, bf16[512,128]{1,0:T(8,128)(2,1)S(1)}, u32[]{:S(2)}, u32[]{:S(2)}) collective-permute-start(bf16[512,128]{1,0:T(8,128)(2,1)S(1)} %collective-permute-done.4.refs_0_), channel_id=1, source_target_pairs={{0,4},{4,8},{8,12},{12,14},{14,10},{10,6},{6,2},{2,0},{1,5},{5,9},... | collective-permute-start | bytes 393224 | tf_op jit(solution)/shard_map/ppermute | solution.py:194
  13.2 0.4 %collective-permute-start.7 = (bf16[512,128]{1,0:T(8,128)(2,1)S(1)}, bf16[512,128]{1,0:T(8,128)(2,1)S(1)}, u32[]{:S(2)}, u32[]{:S(2)}) collective-permute-start(bf16[512,128]{1,0:T(8,128)(2,1)S(1)} %collective-permute-done.5.refs_1_), channel_id=1, source_target_pairs={{0,2},{4,0},{8,4},{12,8},{14,12},{10,14},{6,10},{2,6},{1,3},{5,1},... | collective-permute-start | bytes 393224 | tf_op jit(solution)/shard_map/ppermute | solution.py:194
  13.6 1.8 %collective-permute-done.2.refs_2_ = bf16[512,128]{1,0:T(8,128)(2,1)S(1)} collective-permute-done((bf16[512,128]{1,0:T(8,128)(2,1)S(1)}, bf16[512,128]{1,0:T(8,128)(2,1)S(1)}, u32[]{:S(2)}, u32[]{:S(2)}) %collective-permute-start.2) | collective-permute-done | bytes 131104 | tf_op jit(solution)/shard_map/ppermute | solution.py:194
  15.4 1.0 %collective-permute-done.3.refs_3_ = bf16[512,128]{1,0:T(8,128)(2,1)S(1)} collective-permute-done((bf16[512,128]{1,0:T(8,128)(2,1)S(1)}, bf16[512,128]{1,0:T(8,128)(2,1)S(1)}, u32[]{:S(2)}, u32[]{:S(2)}) %collective-permute-start.3) | collective-permute-done | bytes 131104 | tf_op jit(solution)/shard_map/ppermute | solution.py:194
  16.5 1.6 %collective-permute-start.8 = (bf16[512,128]{1,0:T(8,128)(2,1)S(1)}, bf16[512,128]{1,0:T(8,128)(2,1)S(1)}, u32[]{:S(2)}, u32[]{:S(2)}) collective-permute-start(bf16[512,128]{1,0:T(8,128)(2,1)S(1)} %collective-permute-done.2.refs_2_), channel_id=1, source_target_pairs={{0,4},{4,8},{8,12},{12,14},{14,10},{10,6},{6,2},{2,0},{1,5},{5,9},... | collective-permute-start | bytes 393224 | tf_op jit(solution)/shard_map/ppermute | solution.py:194
  18.0 0.0 collective-permute-done.6.refs_2_
  18.1 0.1 collective-permute-done.7.refs_3_
  18.1 0.4 %collective-permute-start.12 = (bf16[512,128]{1,0:T(8,128)(2,1)S(1)}, bf16[512,128]{1,0:T(8,128)(2,1)S(1)}, u32[]{:S(2)}, u32[]{:S(2)}) collective-permute-start(bf16[512,128]{1,0:T(8,128)(2,1)S(1)} %collective-permute-done.7.refs_3_), channel_id=1, source_target_pairs={{0,2},{4,0},{8,4},{12,8},{14,12},{10,14},{6,10},{2,6},{1,3},{5,1},... | collective-permute-start | bytes 393224 | tf_op jit(solution)/shard_map/ppermute | solution.py:194
  18.6 1.4 %collective-permute-start.9 = (bf16[512,128]{1,0:T(8,128)(2,1)S(1)}, bf16[512,128]{1,0:T(8,128)(2,1)S(1)}, u32[]{:S(2)}, u32[]{:S(2)}) collective-permute-start(bf16[512,128]{1,0:T(8,128)(2,1)S(1)} %collective-permute-done.3.refs_3_), channel_id=1, source_target_pairs={{0,2},{4,0},{8,4},{12,8},{14,12},{10,14},{6,10},{2,6},{1,3},{5,1},... | collective-permute-start | bytes 393224 | tf_op jit(solution)/shard_map/ppermute | solution.py:194
  20.0 2.6 %collective-permute-done.8.refs_4_ = bf16[512,128]{1,0:T(8,128)(2,1)S(1)} collective-permute-done((bf16[512,128]{1,0:T(8,128)(2,1)S(1)}, bf16[512,128]{1,0:T(8,128)(2,1)S(1)}, u32[]{:S(2)}, u32[]{:S(2)}) %collective-permute-start.8) | collective-permute-done | bytes 131104 | tf_op jit(solution)/shard_map/ppermute | solution.py:194
  22.6 1.6 %collective-permute-start.10 = (bf16[512,128]{1,0:T(8,128)(2,1)S(1)}, bf16[512,128]{1,0:T(8,128)(2,1)S(1)}, u32[]{:S(2)}, u32[]{:S(2)}) collective-permute-start(bf16[512,128]{1,0:T(8,128)(2,1)S(1)} %collective-permute-done.8.refs_4_), channel_id=1, source_target_pairs={{0,4},{4,8},{8,12},{12,14},{14,10},{10,6},{6,2},{2,0},{1,5},{5,9},... | collective-permute-start | bytes 393224 | tf_op jit(solution)/shard_map/ppermute | solution.py:194
  24.1 1.4 %collective-permute-start.11 = (bf16[512,128]{1,0:T(8,128)(2,1)S(1)}, bf16[512,128]{1,0:T(8,128)(2,1)S(1)}, u32[]{:S(2)}, u32[]{:S(2)}) collective-permute-start(bf16[512,128]{1,0:T(8,128)(2,1)S(1)} %collective-permute-done.6.refs_2_), channel_id=1, source_target_pairs={{0,4},{4,8},{8,12},{12,14},{14,10},{10,6},{6,2},{2,0},{1,5},{5,9},... | collective-permute-start | bytes 393224 | tf_op jit(solution)/shard_map/ppermute | solution.py:194
  25.5 0.0 collective-permute-done.12.refs_5_
  25.5 0.6 %collective-permute-start.13 = (bf16[512,128]{1,0:T(8,128)(2,1)S(1)}, bf16[512,128]{1,0:T(8,128)(2,1)S(1)}, u32[]{:S(2)}, u32[]{:S(2)}) collective-permute-start(bf16[512,128]{1,0:T(8,128)(2,1)S(1)} %collective-permute-done.12.refs_5_), channel_id=1, source_target_pairs={{0,2},{4,0},{8,4},{12,8},{14,12},{10,14},{6,10},{2,6},{1,3},{5,1},... | collective-permute-start | bytes 393224 | tf_op jit(solution)/shard_map/ppermute | solution.py:194
  26.2 0.8 %copy.6.chosen_ref = s32[8,4]{1,0:T(8,128)S(1)} copy(s32[8,4]{0,1:T(4,128)} %param.7) | data formatting | bytes 256 | tf_op args[3]
  26.9 0.0 collective-permute-done.9.refs_5_
  26.9 0.6 %collective-permute-done.10.refs_6_ = bf16[512,128]{1,0:T(8,128)(2,1)S(1)} collective-permute-done((bf16[512,128]{1,0:T(8,128)(2,1)S(1)}, bf16[512,128]{1,0:T(8,128)(2,1)S(1)}, u32[]{:S(2)}, u32[]{:S(2)}) %collective-permute-start.10) | collective-permute-done | bytes 131104 | tf_op jit(solution)/shard_map/ppermute | solution.py:194
  27.5 2.9 %weights.1.weights_ref = bf16[4,1024,512]{2,1,0:T(8,128)(2,1)S(1)} custom-call(s32[8,4]{1,0:T(8,128)S(1)} %copy.6.chosen_ref, bf16[4,1024,128]{2,1,0:T(8,128)(2,1)S(1)} %get-tuple-element.24.q_ref, bf16[4,128,128]{2,1,0:T(8,128)(2,1)S(1)} %get-tuple-element.25.own_ref, bf16[512,128]{1,0:T(8,128)(2,1)S(1)} %collective-permute-done.refs_0_, ...), custom_call_target="tpu_custom_call" | custom-call | tf_op jit(solution)/shard_map/weights/pallas_call | solution.py:132
  30.4 0.0 collective-permute-done.11.refs_4_
  30.4 0.1 collective-permute-done.13.refs_6_
  30.5 3.0 %merge.1 = bf16[128,32,128]{2,1,0:T(8,128)(2,1)} custom-call(s32[8,4]{1,0:T(8,128)S(1)} %copy.6.chosen_ref, bf16[4,1024,512]{2,1,0:T(8,128)(2,1)S(1)} %weights.1.weights_ref, bf16[4,128,128]{2,1,0:T(8,128)(2,1)S(1)} %get-tuple-element.34.own_ref, bf16[512,128]{1,0:T(8,128)(2,1)S(1)} %collective-permute-done.4.refs_0_, ...), custom_call_target="tpu_custom_call" | custom-call | tf_op jit(solution)/shard_map/merge/pallas_call | solution.py:167
Async XLA Ops:
  0.0 7.5 %collective-permute-start = (bf16[512,128]{1,0:T(8,128)(2,1)}, bf16[512,128]{1,0:T(8,128)(2,1)S(1)}, u32[]{:S(2)}, u32[]{:S(2)}) collective-permute-start(bf16[512,128]{1,0:T(8,128)(2,1)} %bitcast.2), channel_id=1, source_target_pairs={{0,4},{4,8},{8,12},{12,14},{14,10},{10,6},{6,2},{2,0},{1,5},{5,9},... | collective-permute-start | bytes 393224 | tf_op jit(solution)/shard_map/ppermute | solution.py:194
  3.0 6.5 %collective-permute-start.1 = (bf16[512,128]{1,0:T(8,128)(2,1)}, bf16[512,128]{1,0:T(8,128)(2,1)S(1)}, u32[]{:S(2)}, u32[]{:S(2)}) collective-permute-start(bf16[512,128]{1,0:T(8,128)(2,1)} %bitcast.3), channel_id=1, source_target_pairs={{0,2},{4,0},{8,4},{12,8},{14,12},{10,14},{6,10},{2,6},{1,3},{5,1},... | collective-permute-start | bytes 393224 | tf_op jit(solution)/shard_map/ppermute | solution.py:194
  3.0 8.6 %collective-permute-start.4 = (bf16[512,128]{1,0:T(8,128)(2,1)}, bf16[512,128]{1,0:T(8,128)(2,1)S(1)}, u32[]{:S(2)}, u32[]{:S(2)}) collective-permute-start(bf16[512,128]{1,0:T(8,128)(2,1)} %bitcast.5), channel_id=1, source_target_pairs={{0,4},{4,8},{8,12},{12,14},{14,10},{10,6},{6,2},{2,0},{1,5},{5,9},... | collective-permute-start | bytes 393224 | tf_op jit(solution)/shard_map/ppermute | solution.py:194
  5.1 6.5 %collective-permute-start.5 = (bf16[512,128]{1,0:T(8,128)(2,1)}, bf16[512,128]{1,0:T(8,128)(2,1)S(1)}, u32[]{:S(2)}, u32[]{:S(2)}) collective-permute-start(bf16[512,128]{1,0:T(8,128)(2,1)} %bitcast.6), channel_id=1, source_target_pairs={{0,2},{4,0},{8,4},{12,8},{14,12},{10,14},{6,10},{2,6},{1,3},{5,1},... | collective-permute-start | bytes 393224 | tf_op jit(solution)/shard_map/ppermute | solution.py:194
  9.6 5.9 %collective-permute-start.2 = (bf16[512,128]{1,0:T(8,128)(2,1)S(1)}, bf16[512,128]{1,0:T(8,128)(2,1)S(1)}, u32[]{:S(2)}, u32[]{:S(2)}) collective-permute-start(bf16[512,128]{1,0:T(8,128)(2,1)S(1)} %collective-permute-done.refs_0_), channel_id=1, source_target_pairs={{0,4},{4,8},{8,12},{12,14},{14,10},{10,6},{6,2},{2,0},{1,5},{5,9},... | collective-permute-start | bytes 393224 | tf_op jit(solution)/shard_map/ppermute | solution.py:194
  11.1 5.3 %collective-permute-start.3 = (bf16[512,128]{1,0:T(8,128)(2,1)S(1)}, bf16[512,128]{1,0:T(8,128)(2,1)S(1)}, u32[]{:S(2)}, u32[]{:S(2)}) collective-permute-start(bf16[512,128]{1,0:T(8,128)(2,1)S(1)} %collective-permute-done.1.refs_1_), channel_id=1, source_target_pairs={{0,2},{4,0},{8,4},{12,8},{14,12},{10,14},{6,10},{2,6},{1,3},{5,1},... | collective-permute-start | bytes 393224 | tf_op jit(solution)/shard_map/ppermute | solution.py:194
  11.6 6.5 %collective-permute-start.6 = (bf16[512,128]{1,0:T(8,128)(2,1)S(1)}, bf16[512,128]{1,0:T(8,128)(2,1)S(1)}, u32[]{:S(2)}, u32[]{:S(2)}) collective-permute-start(bf16[512,128]{1,0:T(8,128)(2,1)S(1)} %collective-permute-done.4.refs_0_), channel_id=1, source_target_pairs={{0,4},{4,8},{8,12},{12,14},{14,10},{10,6},{6,2},{2,0},{1,5},{5,9},... | collective-permute-start | bytes 393224 | tf_op jit(solution)/shard_map/ppermute | solution.py:194
  13.2 5.0 %collective-permute-start.7 = (bf16[512,128]{1,0:T(8,128)(2,1)S(1)}, bf16[512,128]{1,0:T(8,128)(2,1)S(1)}, u32[]{:S(2)}, u32[]{:S(2)}) collective-permute-start(bf16[512,128]{1,0:T(8,128)(2,1)S(1)} %collective-permute-done.5.refs_1_), channel_id=1, source_target_pairs={{0,2},{4,0},{8,4},{12,8},{14,12},{10,14},{6,10},{2,6},{1,3},{5,1},... | collective-permute-start | bytes 393224 | tf_op jit(solution)/shard_map/ppermute | solution.py:194
  16.5 6.1 %collective-permute-start.8 = (bf16[512,128]{1,0:T(8,128)(2,1)S(1)}, bf16[512,128]{1,0:T(8,128)(2,1)S(1)}, u32[]{:S(2)}, u32[]{:S(2)}) collective-permute-start(bf16[512,128]{1,0:T(8,128)(2,1)S(1)} %collective-permute-done.2.refs_2_), channel_id=1, source_target_pairs={{0,4},{4,8},{8,12},{12,14},{14,10},{10,6},{6,2},{2,0},{1,5},{5,9},... | collective-permute-start | bytes 393224 | tf_op jit(solution)/shard_map/ppermute | solution.py:194
  18.1 7.4 %collective-permute-start.12 = (bf16[512,128]{1,0:T(8,128)(2,1)S(1)}, bf16[512,128]{1,0:T(8,128)(2,1)S(1)}, u32[]{:S(2)}, u32[]{:S(2)}) collective-permute-start(bf16[512,128]{1,0:T(8,128)(2,1)S(1)} %collective-permute-done.7.refs_3_), channel_id=1, source_target_pairs={{0,2},{4,0},{8,4},{12,8},{14,12},{10,14},{6,10},{2,6},{1,3},{5,1},... | collective-permute-start | bytes 393224 | tf_op jit(solution)/shard_map/ppermute | solution.py:194
  18.6 8.3 %collective-permute-start.9 = (bf16[512,128]{1,0:T(8,128)(2,1)S(1)}, bf16[512,128]{1,0:T(8,128)(2,1)S(1)}, u32[]{:S(2)}, u32[]{:S(2)}) collective-permute-start(bf16[512,128]{1,0:T(8,128)(2,1)S(1)} %collective-permute-done.3.refs_3_), channel_id=1, source_target_pairs={{0,2},{4,0},{8,4},{12,8},{14,12},{10,14},{6,10},{2,6},{1,3},{5,1},... | collective-permute-start | bytes 393224 | tf_op jit(solution)/shard_map/ppermute | solution.py:194
  22.6 5.0 %collective-permute-start.10 = (bf16[512,128]{1,0:T(8,128)(2,1)S(1)}, bf16[512,128]{1,0:T(8,128)(2,1)S(1)}, u32[]{:S(2)}, u32[]{:S(2)}) collective-permute-start(bf16[512,128]{1,0:T(8,128)(2,1)S(1)} %collective-permute-done.8.refs_4_), channel_id=1, source_target_pairs={{0,4},{4,8},{8,12},{12,14},{14,10},{10,6},{6,2},{2,0},{1,5},{5,9},... | collective-permute-start | bytes 393224 | tf_op jit(solution)/shard_map/ppermute | solution.py:194
  24.1 6.3 %collective-permute-start.11 = (bf16[512,128]{1,0:T(8,128)(2,1)S(1)}, bf16[512,128]{1,0:T(8,128)(2,1)S(1)}, u32[]{:S(2)}, u32[]{:S(2)}) collective-permute-start(bf16[512,128]{1,0:T(8,128)(2,1)S(1)} %collective-permute-done.6.refs_2_), channel_id=1, source_target_pairs={{0,4},{4,8},{8,12},{12,14},{14,10},{10,6},{6,2},{2,0},{1,5},{5,9},... | collective-permute-start | bytes 393224 | tf_op jit(solution)/shard_map/ppermute | solution.py:194
  25.5 5.0 %collective-permute-start.13 = (bf16[512,128]{1,0:T(8,128)(2,1)S(1)}, bf16[512,128]{1,0:T(8,128)(2,1)S(1)}, u32[]{:S(2)}, u32[]{:S(2)}) collective-permute-start(bf16[512,128]{1,0:T(8,128)(2,1)S(1)} %collective-permute-done.12.refs_5_), channel_id=1, source_target_pairs={{0,2},{4,0},{8,4},{12,8},{14,12},{10,14},{6,10},{2,6},{1,3},{5,1},... | collective-permute-start | bytes 393224 | tf_op jit(solution)/shard_map/ppermute | solution.py:194

commit v6 on v5

v6 whole, which is shorter than its diff:
```python
import functools
import math

import jax
import jax.numpy as jnp
from jax import lax
from jax.experimental import pallas as pl
from jax.experimental.pallas import tpu as pltpu
from jax.sharding import PartitionSpec as P

NO_KEY = -1e30
ROW_CHUNK = 256
MOST_ROUND = 16


def params():
    return pltpu.CompilerParams(vmem_limit_bytes=16 * 2**20)


def vmem():
    return pl.BlockSpec(memory_space=pltpu.VMEM)


def prepare_kernel(
    chosen_ref, q_hbm, k_hbm, v_hbm, slots_out, q_out, k_out, v_out,
    q_ref, k_ref, v_ref, k_wide, v_wide, sems, *, kv_dev, sources,
):
    copies = [
        pltpu.make_async_copy(source, here, sems.at[n])
        for n, (source, here) in enumerate(((k_hbm, k_ref), (v_hbm, v_ref), (q_hbm, q_ref)))
    ]
    for copy in copies:
        copy.start()
    target = lax.axis_index("seq").astype(jnp.int32)
    count = jnp.int32(0)
    for part, source in enumerate(sources(target)):
        is_listed = chosen_ref[target, 0] == source
        for j in range(1, chosen_ref.shape[1]):
            is_listed |= chosen_ref[target, j] == source
        slots_out[part] = jnp.where(is_listed, count, -1)
        count += is_listed.astype(jnp.int32)
    slots_out[slots_out.shape[0] - 1] = count

    tokens, heads, dim = q_ref.shape
    group = heads // kv_dev
    for copy, ref, wide, out in zip(copies, (k_ref, v_ref), (k_wide, v_wide), (k_out, v_out)):
        copy.wait()
        wide[...] = ref[...].astype(jnp.float32)
        for h in range(kv_dev):
            out[h] = wide[pl.ds(h, tokens, stride=kv_dev), :].astype(jnp.bfloat16)
    copies[2].wait()
    for h in range(kv_dev):
        q = q_ref[:, pl.ds(h * group, group), :].astype(jnp.float32)
        q_out[h] = q.reshape(tokens * group, dim).astype(jnp.bfloat16)


def prepare(chosen, queries, k_own, v_own, kv_dev, sources, parts):
    tokens, heads, dim = queries.shape
    smem = pl.BlockSpec(memory_space=pltpu.SMEM)
    operands = [pltpu.with_memory_space_constraint(x, pltpu.HBM) for x in (queries, k_own, v_own)]
    by_head = jax.ShapeDtypeStruct((kv_dev, tokens, dim), jnp.bfloat16)
    return pl.pallas_call(
        functools.partial(prepare_kernel, kv_dev=kv_dev, sources=sources),
        out_shape=(
            jax.ShapeDtypeStruct((parts + 1,), jnp.int32),
            jax.ShapeDtypeStruct((kv_dev, tokens * heads // kv_dev, dim), jnp.bfloat16),
            by_head,
            by_head,
        ),
        in_specs=[smem] + [pl.BlockSpec(memory_space=pltpu.HBM)] * 3,
        out_specs=(smem, vmem(), vmem(), vmem()),
        scratch_shapes=[
            pltpu.VMEM(queries.shape, jnp.bfloat16),
            pltpu.VMEM(k_own.shape, jnp.bfloat16),
            pltpu.VMEM(k_own.shape, jnp.bfloat16),
            pltpu.VMEM(k_own.shape, jnp.float32),
            pltpu.VMEM(k_own.shape, jnp.float32),
            pltpu.SemaphoreType.DMA((3,)),
        ],
        compiler_params=params(),
        name="prepare",
    )(chosen, *operands)


def gather_listed(slots_ref, parts, wide):
    block = parts[0].shape[0]
    count = slots_ref[len(parts)]
    for i, part in enumerate(parts):
        slot = slots_ref[i]

        @pl.when(slot >= 0)
        def _take(part=part, slot=slot):
            rows = pl.ds(pl.multiple_of(slot * block, block), block)
            wide[rows, :] = part[...].astype(jnp.float32)

    for j in range(wide.shape[0] // block):

        @pl.when(count <= j)
        def _clear(j=j):
            wide[pl.ds(j * block, block), :] = jnp.zeros((block, wide.shape[1]), jnp.float32)

    return count


def weights_kernel(slots_ref, q_ref, own_ref, *refs):
    *parts, out_ref, wide = refs
    kv_dev, tokens, dim = own_ref.shape
    rows_all = q_ref.shape[1]
    group = rows_all // tokens
    others = wide.shape[0] // (tokens * kv_dev)
    count = gather_listed(slots_ref, parts, wide)
    factor = dim ** (-0.5) * math.log2(math.e)

    def fill(bias):
        for h in range(kv_dev):
            k_h = wide[pl.ds(h, others * tokens, stride=kv_dev), :].astype(jnp.bfloat16)
            k_h = jnp.concatenate([own_ref[h], k_h], axis=0)
            for first in range(0, rows_all, ROW_CHUNK):
                rows = pl.ds(first, ROW_CHUNK)
                s = lax.dot_general(
                    q_ref[h, rows, :], k_h, (((1,), (1,)), ((), ())), preferred_element_type=jnp.float32
                )
                row = (lax.broadcasted_iota(jnp.int32, (ROW_CHUNK, tokens), 0) + first) // group
                key = lax.broadcasted_iota(jnp.int32, (ROW_CHUNK, tokens), 1)
                scores = [jnp.where(key <= row, s[:, :tokens], NO_KEY)]
                for j in range(others):
                    score = s[:, (j + 1) * tokens : (j + 2) * tokens]
                    scores.append(score if bias is None else score + bias[j])
                top = scores[0]
                for score in scores[1:]:
                    top = jnp.maximum(top, score)
                top = jnp.max(top, axis=1, keepdims=True)
                for j, score in enumerate(scores):
                    probs = jnp.exp2((score - top) * factor).astype(jnp.bfloat16)
                    out_ref[h, rows, pl.ds(j * tokens, tokens)] = probs

    @pl.when(count == others)
    def _full():
        fill(None)

    @pl.when(count < others)
    def _some():
        fill([jnp.where(count <= j, NO_KEY, 0.0).astype(jnp.float32) for j in range(others)])


def weights(listed, queries, k_own, k_parts, slots):
    kv_dev, rows, _ = queries.shape
    block, dim = k_parts[0].shape
    return pl.pallas_call(
        weights_kernel,
        out_shape=jax.ShapeDtypeStruct((kv_dev, rows, slots * block // kv_dev), jnp.bfloat16),
        in_specs=[pl.BlockSpec(memory_space=pltpu.SMEM)] + [vmem()] * (2 + len(k_parts)),
        out_specs=vmem(),
        scratch_shapes=[pltpu.VMEM(((slots - 1) * block, dim), jnp.float32)],
        compiler_params=params(),
        name="weights",
    )(listed, queries, k_own, *k_parts)


def merge_kernel(slots_ref, weights_ref, own_ref, *refs):
    *parts, out_hbm, wide, values, out_ref, sems = refs
    kv_dev, tokens, dim = own_ref.shape
    group = weights_ref.shape[1] // tokens
    others = wide.shape[0] // (tokens * kv_dev)
    gather_listed(slots_ref, parts, wide)
    ones = jnp.ones(((others + 1) * tokens, dim), jnp.bfloat16)
    for h in range(kv_dev):
        v_h = wide[pl.ds(h, others * tokens, stride=kv_dev), :].astype(jnp.bfloat16)
        v_h = jnp.concatenate([own_ref[h], v_h], axis=0)
        values[h] = jnp.concatenate([v_h, ones], axis=1)
    chunk = ROW_CHUNK // group
    copies = []
    for n in range(tokens // chunk):
        here = pl.ds(n * chunk, chunk)
        for h in range(kv_dev):
            probs = weights_ref[h, pl.ds(n * ROW_CHUNK, ROW_CHUNK), :]
            both = jnp.dot(probs, values[h], preferred_element_type=jnp.float32)
            merged = (both[:, :dim] / both[:, dim:]).reshape(chunk, group, dim)
            out_ref[here, pl.ds(h * group, group), :] = merged.astype(jnp.bfloat16)
        copy = pltpu.make_async_copy(out_ref.at[here], out_hbm.at[here], sems.at[n])
        copy.start()
        copies.append(copy)
    for copy in copies:
        copy.wait()


def merge(listed, probs, v_own, v_parts, slots):
    kv_dev, rows, keys = probs.shape
    block, dim = v_parts[0].shape
    tokens = block // kv_dev
    out = (tokens, rows * kv_dev // tokens, dim)
    return pl.pallas_call(
        merge_kernel,
        out_shape=jax.ShapeDtypeStruct(out, jnp.bfloat16),
        in_specs=[pl.BlockSpec(memory_space=pltpu.SMEM)] + [vmem()] * (2 + len(v_parts)),
        out_specs=pl.BlockSpec(memory_space=pltpu.HBM),
        scratch_shapes=[
            pltpu.VMEM(((slots - 1) * block, dim), jnp.float32),
            pltpu.VMEM((kv_dev, keys, 2 * dim), jnp.bfloat16),
            pltpu.VMEM(out, jnp.bfloat16),
            pltpu.SemaphoreType.DMA((rows // ROW_CHUNK,)),
        ],
        compiler_params=params(),
        name="merge",
    )(listed, probs, v_own, *v_parts)


def ring_at(place, members):
    back = members - 1 - place
    return jnp.where(place < members // 2, 2 * place, 2 * back + 1)


def ring_place(block, members):
    return jnp.where(block % 2 == 0, block // 2, members - 1 - block // 2)


def round_the_ring(k_own, v_own, ready, members):
    ring = list(range(0, members, 2)) + list(range(members - 1, 0, -2))
    ways = [
        [(ring[p], ring[(p + turn) % members]) for p in range(members)] for turn in (1, -1)
    ]

    def send(x, way):
        return lax.ppermute(x, "seq", ways[way])

    half = members // 2
    k_two, v_two, k_all, v_all = (k_own, k_own), (v_own, v_own), [], []
    for distance in range(1, half):
        k_two = tuple(send(x, way) for way, x in enumerate(k_two))
        v_two = tuple(send(x, way) for way, x in enumerate(v_two))
        if distance == 1:
            k_two, ready = lax.optimization_barrier((k_two, ready))
        k_two = lax.optimization_barrier(k_two)
        if distance < half - 1:
            v_two = lax.optimization_barrier(v_two)
        k_all += k_two
        v_all += v_two
    k_all.append(send(k_two[0], 0))
    v_last, _ = lax.optimization_barrier((v_two[1], k_two))
    v_all.append(send(v_last, 1))
    return k_all, v_all, ready


def ring_sources(members):
    def sources(target):
        place = ring_place(target, members)
        turns = [turn for far in range(1, members // 2) for turn in (-far, far)] + [members // 2]
        return [ring_at(lax.rem(place + turn + members, members), members) for turn in turns]

    return sources


def others(row, target):
    slots = row.shape[-1]
    own_at = jnp.argmax(row == target[..., None], axis=-1)
    j = jnp.arange(slots - 1)
    return jnp.where(j >= own_at[..., None], row[..., 1:], row[..., :-1])


def relay(k_own, v_own, chosen, members):
    block, dim = k_own.shape
    stacked = jnp.stack([k_own, v_own]).reshape(2, members, block // members, dim)
    shares = lax.all_to_all(stacked, "seq", split_axis=1, concat_axis=1, tiled=True)
    wanted = others(chosen, jnp.arange(members, dtype=jnp.int32))
    picked = jnp.take(shares, jnp.maximum(wanted, 0), axis=1)
    arrived = lax.all_to_all(picked, "seq", split_axis=1, concat_axis=3, tiled=True)
    count = wanted.shape[1]
    k_parts, v_parts = ([arrived[n, 0, j].reshape(block, dim) for j in range(count)] for n in range(2))
    return k_parts, v_parts, jnp.where(wanted < 0, -1, jnp.arange(count, dtype=jnp.int32))


def per_device(queries, keys, values, chosen):
    members = lax.axis_size("seq")
    tokens, kv_dev, dim = keys.shape
    slots = chosen.shape[1]
    k_own = keys.reshape(tokens * kv_dev, dim)
    v_own = values.reshape(tokens * kv_dev, dim)
    if members <= MOST_ROUND:
        sources = ring_sources(members)
        ready = prepare(chosen, queries, k_own, v_own, kv_dev, sources, members - 1)
        k_parts, v_parts, ready = round_the_ring(k_own, v_own, ready, members)
    else:
        k_parts, v_parts, mine = relay(k_own, v_own, chosen, members)

        def sources(_):
            return [jnp.int32(j) for j in range(slots - 1)]

        ready = prepare(mine, queries, k_own, v_own, kv_dev, sources, slots - 1)
    listed, q_ready, k_ready, v_ready = ready
    probs = weights(listed, q_ready, k_ready, k_parts, slots)
    return merge(listed, probs, v_ready, v_parts, slots)


def solution(mesh):
    rows = P(("groups", "seq"), "head", None)
    return jax.shard_map(
        per_device,
        mesh=mesh,
        in_specs=(rows, rows, rows, P("groups", None)),
        out_specs=rows,
        check_vma=False,
    )
```

time: 33.7 us -> 33.4 us (level)
  Pallas kernels: 7.48 us -> 8.29 us
  starting transfers between devices: 16.1 us -> 15.4 us
  waiting for transfers between devices: 9.12 us -> 8.74 us
    pallas_call x3, Pallas kernels: 7.48 us -> 8.29 us  [the longest x1 2.83 us: weights(): pl.pallas_call(weights_kernel, out_shape=jax.ShapeDtypeStruct((kv_dev, ro...]
    ppermute x14, starting transfers between devices: 16.1 us -> 15.4 us  [send(): return lax.ppermute(x, 'seq', ways[way])]
    ppermute x14, waiting for transfers between devices: 9.12 us -> 8.74 us  [send(): return lax.ppermute(x, 'seq', ways[way])]
  transfers between devices with their start and end apart: 14 -> 14, of which waited for: 8 -> 8; matrix products, arithmetic and copies ran while one was open for 2% -> 2% of each run, Pallas kernels for 13% -> 17%
where the time goes in v6:
time: 33.4 us; the launch traced here: 33.2 us
  starting transfers between devices  15.4 us (46%)
  waiting for transfers between devices  8.74 us (26%)
  Pallas kernels  8.29 us (25%)
  local copies, waits for them, and re-layouts  0.76 us (2%)
    ppermute x14, starting transfers between devices, send(): return lax.ppermute(x, 'seq', ways[way])  15.4 us
    ppermute x14, waiting for transfers between devices, send(): return lax.ppermute(x, 'seq', ways[way])  8.74 us
    pallas_call x1, Pallas kernels, weights(): pl.pallas_call(weights_kernel, out_shape=jax.ShapeDtypeStruct((kv_dev, ro...  2.83 us
    pallas_call x1, Pallas kernels, prepare(): pl.pallas_call(functools.partial(prepare_kernel, kv_dev=kv_dev, sources=s...  2.76 us
    pallas_call x1, Pallas kernels, merge(): pl.pallas_call(merge_kernel, out_shape=jax.ShapeDtypeStruct(out, jnp.bflo...  2.69 us
    unnamed x1, local copies, waits for them, and re-layouts  0.76 us
  transfers between devices with their start and end apart: 14, of which 8 were waited for; matrix products, arithmetic and copies ran while one was open for 2% of the time, Pallas kernels for 17%

profile of v6, /device:TPU:0, one launch (start us, length us, event | category | flops | bytes accessed | tf_op | source)
XLA Modules:
  0.0 33.2 jit_solution(10256358959614119446)
XLA Ops:
  0.0 3.0 %collective-permute-start = (bf16[512,128]{1,0:T(8,128)(2,1)}, bf16[512,128]{1,0:T(8,128)(2,1)S(1)}, u32[]{:S(2)}, u32[]{:S(2)}) collective-permute-start(bf16[512,128]{1,0:T(8,128)(2,1)} %bitcast.2), channel_id=1, source_target_pairs={{0,4},{4,8},{8,12},{12,14},{14,10},{10,6},{6,2},{2,0},{1,5},{5,9},... | collective-permute-start | bytes 393224 | tf_op jit(solution)/shard_map/ppermute | solution.py:224
  3.0 0.0 collective-permute-start.1
  3.0 2.0 %collective-permute-start.7 = (bf16[512,128]{1,0:T(8,128)(2,1)}, bf16[512,128]{1,0:T(8,128)(2,1)S(1)}, u32[]{:S(2)}, u32[]{:S(2)}) collective-permute-start(bf16[512,128]{1,0:T(8,128)(2,1)} %bitcast.5), channel_id=1, source_target_pairs={{0,4},{4,8},{8,12},{12,14},{14,10},{10,6},{6,2},{2,0},{1,5},{5,9},... | collective-permute-start | bytes 393224 | tf_op jit(solution)/shard_map/ppermute | solution.py:224
  5.1 0.0 collective-permute-start.8
  5.1 0.8 %copy.5.chosen_ref = s32[8,4]{1,0:T(8,128)S(1)} copy(s32[8,4]{0,1:T(4,128)} %param.7) | data formatting | bytes 256 | tf_op args[3]
  5.8 2.8 %prepare.1 = (s32[8]{0:T(128)S(1)}, bf16[4,1024,128]{2,1,0:T(8,128)(2,1)S(1)}, bf16[4,128,128]{2,1,0:T(8,128)(2,1)S(1)}, bf16[4,128,128]{2,1,0:T(8,128)(2,1)S(1)}) custom-call(s32[8,4]{1,0:T(8,128)S(1)} %copy.5.chosen_ref, bf16[128,32,128]{2,1,0:T(8,128)(2,1)} %q_hbm.1, bf16[512,128]{1,0:T(8,128)(2,1)} %bitcast.4, bf16[512,128]{1,0:T(8,128)(2,1)} %bitcast.7), custom_call_target="tpu_custom_call" | custom-call | tf_op jit(solution)/shard_map/prepare/pallas_call | solution.py:62
  8.6 0.0 collective-permute-done.refs_0_
  8.6 1.0 %collective-permute-done.1.refs_1_ = bf16[512,128]{1,0:T(8,128)(2,1)S(1)} collective-permute-done((bf16[512,128]{1,0:T(8,128)(2,1)}, bf16[512,128]{1,0:T(8,128)(2,1)S(1)}, u32[]{:S(2)}, u32[]{:S(2)}) %collective-permute-start.1) | collective-permute-done | bytes 131104 | tf_op jit(solution)/shard_map/ppermute | solution.py:224
  9.6 1.6 %collective-permute-start.2 = (bf16[512,128]{1,0:T(8,128)(2,1)S(1)}, bf16[512,128]{1,0:T(8,128)(2,1)S(1)}, u32[]{:S(2)}, u32[]{:S(2)}) collective-permute-start(bf16[512,128]{1,0:T(8,128)(2,1)S(1)} %collective-permute-done.refs_0_), channel_id=1, source_target_pairs={{0,4},{4,8},{8,12},{12,14},{14,10},{10,6},{6,2},{2,0},{1,5},{5,9},... | collective-permute-start | bytes 393224 | tf_op jit(solution)/shard_map/ppermute | solution.py:224
  11.2 0.4 %collective-permute-start.3 = (bf16[512,128]{1,0:T(8,128)(2,1)S(1)}, bf16[512,128]{1,0:T(8,128)(2,1)S(1)}, u32[]{:S(2)}, u32[]{:S(2)}) collective-permute-start(bf16[512,128]{1,0:T(8,128)(2,1)S(1)} %collective-permute-done.1.refs_1_), channel_id=1, source_target_pairs={{0,2},{4,0},{8,4},{12,8},{14,12},{10,14},{6,10},{2,6},{1,3},{5,1},... | collective-permute-start | bytes 393224 | tf_op jit(solution)/shard_map/ppermute | solution.py:224
  11.6 0.0 collective-permute-done.7.refs_0_
  11.6 0.0 collective-permute-done.8.refs_1_
  11.6 1.0 %collective-permute-start.10 = (bf16[512,128]{1,0:T(8,128)(2,1)S(1)}, bf16[512,128]{1,0:T(8,128)(2,1)S(1)}, u32[]{:S(2)}, u32[]{:S(2)}) collective-permute-start(bf16[512,128]{1,0:T(8,128)(2,1)S(1)} %collective-permute-done.8.refs_1_), channel_id=1, source_target_pairs={{0,2},{4,0},{8,4},{12,8},{14,12},{10,14},{6,10},{2,6},{1,3},{5,1},... | collective-permute-start | bytes 393224 | tf_op jit(solution)/shard_map/ppermute | solution.py:224
  12.6 1.0 %collective-permute-start.9 = (bf16[512,128]{1,0:T(8,128)(2,1)S(1)}, bf16[512,128]{1,0:T(8,128)(2,1)S(1)}, u32[]{:S(2)}, u32[]{:S(2)}) collective-permute-start(bf16[512,128]{1,0:T(8,128)(2,1)S(1)} %collective-permute-done.7.refs_0_), channel_id=1, source_target_pairs={{0,4},{4,8},{8,12},{12,14},{14,10},{10,6},{6,2},{2,0},{1,5},{5,9},... | collective-permute-start | bytes 393224 | tf_op jit(solution)/shard_map/ppermute | solution.py:224
  13.6 2.3 %collective-permute-done.2.refs_2_ = bf16[512,128]{1,0:T(8,128)(2,1)S(1)} collective-permute-done((bf16[512,128]{1,0:T(8,128)(2,1)S(1)}, bf16[512,128]{1,0:T(8,128)(2,1)S(1)}, u32[]{:S(2)}, u32[]{:S(2)}) %collective-permute-start.2) | collective-permute-done | bytes 131104 | tf_op jit(solution)/shard_map/ppermute | solution.py:224
  15.9 0.2 collective-permute-done.3.refs_3_
  16.1 1.6 %collective-permute-start.4 = (bf16[512,128]{1,0:T(8,128)(2,1)S(1)}, bf16[512,128]{1,0:T(8,128)(2,1)S(1)}, u32[]{:S(2)}, u32[]{:S(2)}) collective-permute-start(bf16[512,128]{1,0:T(8,128)(2,1)S(1)} %collective-permute-done.2.refs_2_), channel_id=1, source_target_pairs={{0,4},{4,8},{8,12},{12,14},{14,10},{10,6},{6,2},{2,0},{1,5},{5,9},... | collective-permute-start | bytes 393224 | tf_op jit(solution)/shard_map/ppermute | solution.py:224
  17.7 0.4 %collective-permute-start.5 = (bf16[512,128]{1,0:T(8,128)(2,1)S(1)}, bf16[512,128]{1,0:T(8,128)(2,1)S(1)}, u32[]{:S(2)}, u32[]{:S(2)}) collective-permute-start(bf16[512,128]{1,0:T(8,128)(2,1)S(1)} %collective-permute-done.3.refs_3_), channel_id=1, source_target_pairs={{0,2},{4,0},{8,4},{12,8},{14,12},{10,14},{6,10},{2,6},{1,3},{5,1},... | collective-permute-start | bytes 393224 | tf_op jit(solution)/shard_map/ppermute | solution.py:224
  18.2 0.0 collective-permute-done.10.refs_3_
  18.2 0.5 %collective-permute-done.9.refs_2_ = bf16[512,128]{1,0:T(8,128)(2,1)S(1)} collective-permute-done((bf16[512,128]{1,0:T(8,128)(2,1)S(1)}, bf16[512,128]{1,0:T(8,128)(2,1)S(1)}, u32[]{:S(2)}, u32[]{:S(2)}) %collective-permute-start.9) | collective-permute-done | bytes 131104 | tf_op jit(solution)/shard_map/ppermute | solution.py:224
  18.7 1.1 %collective-permute-start.12 = (bf16[512,128]{1,0:T(8,128)(2,1)S(1)}, bf16[512,128]{1,0:T(8,128)(2,1)S(1)}, u32[]{:S(2)}, u32[]{:S(2)}) collective-permute-start(bf16[512,128]{1,0:T(8,128)(2,1)S(1)} %collective-permute-done.10.refs_3_), channel_id=1, source_target_pairs={{0,2},{4,0},{8,4},{12,8},{14,12},{10,14},{6,10},{2,6},{1,3},{5,1},... | collective-permute-start | bytes 393224 | tf_op jit(solution)/shard_map/ppermute | solution.py:224
  19.8 1.0 %collective-permute-start.11 = (bf16[512,128]{1,0:T(8,128)(2,1)S(1)}, bf16[512,128]{1,0:T(8,128)(2,1)S(1)}, u32[]{:S(2)}, u32[]{:S(2)}) collective-permute-start(bf16[512,128]{1,0:T(8,128)(2,1)S(1)} %collective-permute-done.9.refs_2_), channel_id=1, source_target_pairs={{0,4},{4,8},{8,12},{12,14},{14,10},{10,6},{6,2},{2,0},{1,5},{5,9},... | collective-permute-start | bytes 393224 | tf_op jit(solution)/shard_map/ppermute | solution.py:224
  20.7 1.8 %collective-permute-done.4.refs_4_ = bf16[512,128]{1,0:T(8,128)(2,1)S(1)} collective-permute-done((bf16[512,128]{1,0:T(8,128)(2,1)S(1)}, bf16[512,128]{1,0:T(8,128)(2,1)S(1)}, u32[]{:S(2)}, u32[]{:S(2)}) %collective-permute-start.4) | collective-permute-done | bytes 131104 | tf_op jit(solution)/shard_map/ppermute | solution.py:224
  22.5 0.2 collective-permute-done.5.refs_5_
  22.7 1.5 %collective-permute-start.6 = (bf16[512,128]{1,0:T(8,128)(2,1)S(1)}, bf16[512,128]{1,0:T(8,128)(2,1)S(1)}, u32[]{:S(2)}, u32[]{:S(2)}) collective-permute-start(bf16[512,128]{1,0:T(8,128)(2,1)S(1)} %collective-permute-done.4.refs_4_), channel_id=1, source_target_pairs={{0,4},{4,8},{8,12},{12,14},{14,10},{10,6},{6,2},{2,0},{1,5},{5,9},... | collective-permute-start | bytes 393224 | tf_op jit(solution)/shard_map/ppermute | solution.py:224
  24.1 0.9 %collective-permute-done.12.refs_5_ = bf16[512,128]{1,0:T(8,128)(2,1)S(1)} collective-permute-done((bf16[512,128]{1,0:T(8,128)(2,1)S(1)}, bf16[512,128]{1,0:T(8,128)(2,1)S(1)}, u32[]{:S(2)}, u32[]{:S(2)}) %collective-permute-start.12) | collective-permute-done | bytes 131104 | tf_op jit(solution)/shard_map/ppermute | solution.py:224
  25.0 0.7 %collective-permute-start.13 = (bf16[512,128]{1,0:T(8,128)(2,1)S(1)}, bf16[512,128]{1,0:T(8,128)(2,1)S(1)}, u32[]{:S(2)}, u32[]{:S(2)}) collective-permute-start(bf16[512,128]{1,0:T(8,128)(2,1)S(1)} %collective-permute-done.12.refs_5_), channel_id=1, source_target_pairs={{0,2},{4,0},{8,4},{12,8},{14,12},{10,14},{6,10},{2,6},{1,3},{5,1},... | collective-permute-start | bytes 393224 | tf_op jit(solution)/shard_map/ppermute | solution.py:224
  25.8 1.9 %collective-permute-done.6.refs_6_ = bf16[512,128]{1,0:T(8,128)(2,1)S(1)} collective-permute-done((bf16[512,128]{1,0:T(8,128)(2,1)S(1)}, bf16[512,128]{1,0:T(8,128)(2,1)S(1)}, u32[]{:S(2)}, u32[]{:S(2)}) %collective-permute-start.6) | collective-permute-done | bytes 131104 | tf_op jit(solution)/shard_map/ppermute | solution.py:224
  27.6 2.8 %weights.1.weights_ref = bf16[4,1024,512]{2,1,0:T(8,128)(2,1)S(1)} custom-call(s32[8]{0:T(128)S(1)} %get-tuple-element.30.slots_ref, bf16[4,1024,128]{2,1,0:T(8,128)(2,1)S(1)} %get-tuple-element.31.q_ref, bf16[4,128,128]{2,1,0:T(8,128)(2,1)S(1)} %get-tuple-element.32.own_ref, bf16[512,128]{1,0:T(8,128)(2,1)S(1)} %collective-permute-done.refs_0_, ...), custom_call_target="tpu_custom_call" | custom-call | tf_op jit(solution)/shard_map/weights/pallas_call | solution.py:149
  30.5 0.0 collective-permute-done.11.refs_4_
  30.5 0.0 collective-permute-done.13.refs_6_
  30.5 2.7 %merge.1 = bf16[128,32,128]{2,1,0:T(8,128)(2,1)} custom-call(s32[8]{0:T(128)S(1)} %get-tuple-element.30.slots_ref, bf16[4,1024,512]{2,1,0:T(8,128)(2,1)S(1)} %weights.1.weights_ref, bf16[4,128,128]{2,1,0:T(8,128)(2,1)S(1)} %get-tuple-element.41.own_ref, bf16[512,128]{1,0:T(8,128)(2,1)S(1)} %collective-permute-done.7.refs_0_, ...), custom_call_target="tpu_custom_call" | custom-call | tf_op jit(solution)/shard_map/merge/pallas_call | solution.py:192
Async XLA Ops:
  0.0 8.6 %collective-permute-start = (bf16[512,128]{1,0:T(8,128)(2,1)}, bf16[512,128]{1,0:T(8,128)(2,1)S(1)}, u32[]{:S(2)}, u32[]{:S(2)}) collective-permute-start(bf16[512,128]{1,0:T(8,128)(2,1)} %bitcast.2), channel_id=1, source_target_pairs={{0,4},{4,8},{8,12},{12,14},{14,10},{10,6},{6,2},{2,0},{1,5},{5,9},... | collective-permute-start | bytes 393224 | tf_op jit(solution)/shard_map/ppermute | solution.py:224
  3.0 6.5 %collective-permute-start.1 = (bf16[512,128]{1,0:T(8,128)(2,1)}, bf16[512,128]{1,0:T(8,128)(2,1)S(1)}, u32[]{:S(2)}, u32[]{:S(2)}) collective-permute-start(bf16[512,128]{1,0:T(8,128)(2,1)} %bitcast.3), channel_id=1, source_target_pairs={{0,2},{4,0},{8,4},{12,8},{14,12},{10,14},{6,10},{2,6},{1,3},{5,1},... | collective-permute-start | bytes 393224 | tf_op jit(solution)/shard_map/ppermute | solution.py:224
  3.0 8.6 %collective-permute-start.7 = (bf16[512,128]{1,0:T(8,128)(2,1)}, bf16[512,128]{1,0:T(8,128)(2,1)S(1)}, u32[]{:S(2)}, u32[]{:S(2)}) collective-permute-start(bf16[512,128]{1,0:T(8,128)(2,1)} %bitcast.5), channel_id=1, source_target_pairs={{0,4},{4,8},{8,12},{12,14},{14,10},{10,6},{6,2},{2,0},{1,5},{5,9},... | collective-permute-start | bytes 393224 | tf_op jit(solution)/shard_map/ppermute | solution.py:224
  5.1 6.5 %collective-permute-start.8 = (bf16[512,128]{1,0:T(8,128)(2,1)}, bf16[512,128]{1,0:T(8,128)(2,1)S(1)}, u32[]{:S(2)}, u32[]{:S(2)}) collective-permute-start(bf16[512,128]{1,0:T(8,128)(2,1)} %bitcast.6), channel_id=1, source_target_pairs={{0,2},{4,0},{8,4},{12,8},{14,12},{10,14},{6,10},{2,6},{1,3},{5,1},... | collective-permute-start | bytes 393224 | tf_op jit(solution)/shard_map/ppermute | solution.py:224
  9.6 6.4 %collective-permute-start.2 = (bf16[512,128]{1,0:T(8,128)(2,1)S(1)}, bf16[512,128]{1,0:T(8,128)(2,1)S(1)}, u32[]{:S(2)}, u32[]{:S(2)}) collective-permute-start(bf16[512,128]{1,0:T(8,128)(2,1)S(1)} %collective-permute-done.refs_0_), channel_id=1, source_target_pairs={{0,4},{4,8},{8,12},{12,14},{14,10},{10,6},{6,2},{2,0},{1,5},{5,9},... | collective-permute-start | bytes 393224 | tf_op jit(solution)/shard_map/ppermute | solution.py:224
  11.2 5.0 %collective-permute-start.3 = (bf16[512,128]{1,0:T(8,128)(2,1)S(1)}, bf16[512,128]{1,0:T(8,128)(2,1)S(1)}, u32[]{:S(2)}, u32[]{:S(2)}) collective-permute-start(bf16[512,128]{1,0:T(8,128)(2,1)S(1)} %collective-permute-done.1.refs_1_), channel_id=1, source_target_pairs={{0,2},{4,0},{8,4},{12,8},{14,12},{10,14},{6,10},{2,6},{1,3},{5,1},... | collective-permute-start | bytes 393224 | tf_op jit(solution)/shard_map/ppermute | solution.py:224
  11.6 6.6 %collective-permute-start.10 = (bf16[512,128]{1,0:T(8,128)(2,1)S(1)}, bf16[512,128]{1,0:T(8,128)(2,1)S(1)}, u32[]{:S(2)}, u32[]{:S(2)}) collective-permute-start(bf16[512,128]{1,0:T(8,128)(2,1)S(1)} %collective-permute-done.8.refs_1_), channel_id=1, source_target_pairs={{0,2},{4,0},{8,4},{12,8},{14,12},{10,14},{6,10},{2,6},{1,3},{5,1},... | collective-permute-start | bytes 393224 | tf_op jit(solution)/shard_map/ppermute | solution.py:224
  12.6 6.1 %collective-permute-start.9 = (bf16[512,128]{1,0:T(8,128)(2,1)S(1)}, bf16[512,128]{1,0:T(8,128)(2,1)S(1)}, u32[]{:S(2)}, u32[]{:S(2)}) collective-permute-start(bf16[512,128]{1,0:T(8,128)(2,1)S(1)} %collective-permute-done.7.refs_0_), channel_id=1, source_target_pairs={{0,4},{4,8},{8,12},{12,14},{14,10},{10,6},{6,2},{2,0},{1,5},{5,9},... | collective-permute-start | bytes 393224 | tf_op jit(solution)/shard_map/ppermute | solution.py:224
  16.1 6.4 %collective-permute-start.4 = (bf16[512,128]{1,0:T(8,128)(2,1)S(1)}, bf16[512,128]{1,0:T(8,128)(2,1)S(1)}, u32[]{:S(2)}, u32[]{:S(2)}) collective-permute-start(bf16[512,128]{1,0:T(8,128)(2,1)S(1)} %collective-permute-done.2.refs_2_), channel_id=1, source_target_pairs={{0,4},{4,8},{8,12},{12,14},{14,10},{10,6},{6,2},{2,0},{1,5},{5,9},... | collective-permute-start | bytes 393224 | tf_op jit(solution)/shard_map/ppermute | solution.py:224
  17.7 5.0 %collective-permute-start.5 = (bf16[512,128]{1,0:T(8,128)(2,1)S(1)}, bf16[512,128]{1,0:T(8,128)(2,1)S(1)}, u32[]{:S(2)}, u32[]{:S(2)}) collective-permute-start(bf16[512,128]{1,0:T(8,128)(2,1)S(1)} %collective-permute-done.3.refs_3_), channel_id=1, source_target_pairs={{0,2},{4,0},{8,4},{12,8},{14,12},{10,14},{6,10},{2,6},{1,3},{5,1},... | collective-permute-start | bytes 393224 | tf_op jit(solution)/shard_map/ppermute | solution.py:224
  18.7 6.3 %collective-permute-start.12 = (bf16[512,128]{1,0:T(8,128)(2,1)S(1)}, bf16[512,128]{1,0:T(8,128)(2,1)S(1)}, u32[]{:S(2)}, u32[]{:S(2)}) collective-permute-start(bf16[512,128]{1,0:T(8,128)(2,1)S(1)} %collective-permute-done.10.refs_3_), channel_id=1, source_target_pairs={{0,2},{4,0},{8,4},{12,8},{14,12},{10,14},{6,10},{2,6},{1,3},{5,1},... | collective-permute-start | bytes 393224 | tf_op jit(solution)/shard_map/ppermute | solution.py:224
  19.8 10.7 %collective-permute-start.11 = (bf16[512,128]{1,0:T(8,128)(2,1)S(1)}, bf16[512,128]{1,0:T(8,128)(2,1)S(1)}, u32[]{:S(2)}, u32[]{:S(2)}) collective-permute-start(bf16[512,128]{1,0:T(8,128)(2,1)S(1)} %collective-permute-done.9.refs_2_), channel_id=1, source_target_pairs={{0,4},{4,8},{8,12},{12,14},{14,10},{10,6},{6,2},{2,0},{1,5},{5,9},... | collective-permute-start | bytes 393224 | tf_op jit(solution)/shard_map/ppermute | solution.py:224
  22.7 5.0 %collective-permute-start.6 = (bf16[512,128]{1,0:T(8,128)(2,1)S(1)}, bf16[512,128]{1,0:T(8,128)(2,1)S(1)}, u32[]{:S(2)}, u32[]{:S(2)}) collective-permute-start(bf16[512,128]{1,0:T(8,128)(2,1)S(1)} %collective-permute-done.4.refs_4_), channel_id=1, source_target_pairs={{0,4},{4,8},{8,12},{12,14},{14,10},{10,6},{6,2},{2,0},{1,5},{5,9},... | collective-permute-start | bytes 393224 | tf_op jit(solution)/shard_map/ppermute | solution.py:224
  25.0 5.5 %collective-permute-start.13 = (bf16[512,128]{1,0:T(8,128)(2,1)S(1)}, bf16[512,128]{1,0:T(8,128)(2,1)S(1)}, u32[]{:S(2)}, u32[]{:S(2)}) collective-permute-start(bf16[512,128]{1,0:T(8,128)(2,1)S(1)} %collective-permute-done.12.refs_5_), channel_id=1, source_target_pairs={{0,2},{4,0},{8,4},{12,8},{14,12},{10,14},{6,10},{2,6},{1,3},{5,1},... | collective-permute-start | bytes 393224 | tf_op jit(solution)/shard_map/ppermute | solution.py:224

commit v7 on v6

--- a/solution.py
+++ b/solution.py
@@ -22,25 +22,15 @@
 
 
 def prepare_kernel(
-    chosen_ref, q_hbm, k_hbm, v_hbm, slots_out, q_out, k_out, v_out,
-    q_ref, k_ref, v_ref, k_wide, v_wide, sems, *, kv_dev, sources,
+    lists_hbm, q_hbm, k_hbm, v_hbm, lists_out, q_out, k_out, v_out,
+    q_ref, k_ref, v_ref, k_wide, v_wide, sems, *, kv_dev,
 ):
+    whole = ((k_hbm, k_ref), (v_hbm, v_ref), (q_hbm, q_ref), (lists_hbm, lists_out))
     copies = [
-        pltpu.make_async_copy(source, here, sems.at[n])
-        for n, (source, here) in enumerate(((k_hbm, k_ref), (v_hbm, v_ref), (q_hbm, q_ref)))
+        pltpu.make_async_copy(source, here, sems.at[n]) for n, (source, here) in enumerate(whole)
     ]
     for copy in copies:
         copy.start()
-    target = lax.axis_index("seq").astype(jnp.int32)
-    count = jnp.int32(0)
-    for part, source in enumerate(sources(target)):
-        is_listed = chosen_ref[target, 0] == source
-        for j in range(1, chosen_ref.shape[1]):
-            is_listed |= chosen_ref[target, j] == source
-        slots_out[part] = jnp.where(is_listed, count, -1)
-        count += is_listed.astype(jnp.int32)
-    slots_out[slots_out.shape[0] - 1] = count
-
     tokens, heads, dim = q_ref.shape
     group = heads // kv_dev
     for copy, ref, wide, out in zip(copies, (k_ref, v_ref), (k_wide, v_wide), (k_out, v_out)):
@@ -52,47 +42,52 @@
     for h in range(kv_dev):
         q = q_ref[:, pl.ds(h * group, group), :].astype(jnp.float32)
         q_out[h] = q.reshape(tokens * group, dim).astype(jnp.bfloat16)
-
-
-def prepare(chosen, queries, k_own, v_own, kv_dev, sources, parts):
+    copies[3].wait()
+
+
+def prepare(lists, queries, k_own, v_own, kv_dev):
     tokens, heads, dim = queries.shape
-    smem = pl.BlockSpec(memory_space=pltpu.SMEM)
-    operands = [pltpu.with_memory_space_constraint(x, pltpu.HBM) for x in (queries, k_own, v_own)]
+    operands = [
+        pltpu.with_memory_space_constraint(x, pltpu.HBM) for x in (lists, queries, k_own, v_own)
+    ]
     by_head = jax.ShapeDtypeStruct((kv_dev, tokens, dim), jnp.bfloat16)
     return pl.pallas_call(
-        functools.partial(prepare_kernel, kv_dev=kv_dev, sources=sources),
+        functools.partial(prepare_kernel, kv_dev=kv_dev),
         out_shape=(
-            jax.ShapeDtypeStruct((parts + 1,), jnp.int32),
+            jax.ShapeDtypeStruct(lists.shape, lists.dtype),
             jax.ShapeDtypeStruct((kv_dev, tokens * heads // kv_dev, dim), jnp.bfloat16),
             by_head,
             by_head,
         ),
-        in_specs=[smem] + [pl.BlockSpec(memory_space=pltpu.HBM)] * 3,
-        out_specs=(smem, vmem(), vmem(), vmem()),
+        in_specs=[pl.BlockSpec(memory_space=pltpu.HBM)] * 4,
+        out_specs=(vmem(), vmem(), vmem(), vmem()),
         scratch_shapes=[
             pltpu.VMEM(queries.shape, jnp.bfloat16),
             pltpu.VMEM(k_own.shape, jnp.bfloat16),
             pltpu.VMEM(k_own.shape, jnp.bfloat16),
             pltpu.VMEM(k_own.shape, jnp.float32),
             pltpu.VMEM(k_own.shape, jnp.float32),
-            pltpu.SemaphoreType.DMA((3,)),
+            pltpu.SemaphoreType.DMA((4,)),
         ],
         compiler_params=params(),
         name="prepare",
-    )(chosen, *operands)
-
-
-def gather_listed(slots_ref, parts, wide):
+    )(*operands)
+
+
+def gather_listed(lists_ref, parts, wide, sources):
+    target = lax.axis_index("seq").astype(jnp.int32)
     block = parts[0].shape[0]
-    count = slots_ref[len(parts)]
-    for i, part in enumerate(parts):
-        slot = slots_ref[i]
-
-        @pl.when(slot >= 0)
-        def _take(part=part, slot=slot):
-            rows = pl.ds(pl.multiple_of(slot * block, block), block)
+    listed = [lists_ref[j, target] for j in range(lists_ref.shape[0])]
+    count = jnp.int32(0)
+    for part, source in zip(parts, sources(target)):
+        is_listed = functools.reduce(jnp.logical_or, [entry == source for entry in listed])
+
+        @pl.when(is_listed)
+        def _take(part=part, count=count):
+            rows = pl.ds(pl.multiple_of(count * block, block), block)
             wide[rows, :] = part[...].astype(jnp.float32)
 
+        count += is_listed.astype(jnp.int32)
     for j in range(wide.shape[0] // block):
 
         @pl.when(count <= j)
@@ -102,13 +97,13 @@
     return count
 
 
-def weights_kernel(slots_ref, q_ref, own_ref, *refs):
+def weights_kernel(lists_ref, q_ref, own_ref, *refs, sources):
     *parts, out_ref, wide = refs
     kv_dev, tokens, dim = own_ref.shape
     rows_all = q_ref.shape[1]
     group = rows_all // tokens
     others = wide.shape[0] // (tokens * kv_dev)
-    count = gather_listed(slots_ref, parts, wide)
+    count = gather_listed(lists_ref, parts, wide, sources)
     factor = dim ** (-0.5) * math.log2(math.e)
 
     def fill(bias):
@@ -143,26 +138,27 @@
         fill([jnp.where(count <= j, NO_KEY, 0.0).astype(jnp.float32) for j in range(others)])
 
 
-def weights(listed, queries, k_own, k_parts, slots):
+def weights(lists, queries, k_own, k_parts, sources):
+    slots = lists.shape[0]
     kv_dev, rows, _ = queries.shape
     block, dim = k_parts[0].shape
     return pl.pallas_call(
-        weights_kernel,
+        functools.partial(weights_kernel, sources=sources),
         out_shape=jax.ShapeDtypeStruct((kv_dev, rows, slots * block // kv_dev), jnp.bfloat16),
         in_specs=[pl.BlockSpec(memory_space=pltpu.SMEM)] + [vmem()] * (2 + len(k_parts)),
         out_specs=vmem(),
         scratch_shapes=[pltpu.VMEM(((slots - 1) * block, dim), jnp.float32)],
         compiler_params=params(),
         name="weights",
-    )(listed, queries, k_own, *k_parts)
-
-
-def merge_kernel(slots_ref, weights_ref, own_ref, *refs):
+    )(lists, queries, k_own, *k_parts)
+
+
+def merge_kernel(lists_ref, weights_ref, own_ref, *refs, sources):
     *parts, out_hbm, wide, values, out_ref, sems = refs
     kv_dev, tokens, dim = own_ref.shape
     group = weights_ref.shape[1] // tokens
     others = wide.shape[0] // (tokens * kv_dev)
-    gather_listed(slots_ref, parts, wide)
+    gather_listed(lists_ref, parts, wide, sources)
     ones = jnp.ones(((others + 1) * tokens, dim), jnp.bfloat16)
     for h in range(kv_dev):
         v_h = wide[pl.ds(h, others * tokens, stride=kv_dev), :].astype(jnp.bfloat16)
@@ -184,13 +180,14 @@
         copy.wait()
 
 
-def merge(listed, probs, v_own, v_parts, slots):
+def merge(lists, probs, v_own, v_parts, sources):
+    slots = lists.shape[0]
     kv_dev, rows, keys = probs.shape
     block, dim = v_parts[0].shape
     tokens = block // kv_dev
     out = (tokens, rows * kv_dev // tokens, dim)
     return pl.pallas_call(
-        merge_kernel,
+        functools.partial(merge_kernel, sources=sources),
         out_shape=jax.ShapeDtypeStruct(out, jnp.bfloat16),
         in_specs=[pl.BlockSpec(memory_space=pltpu.SMEM)] + [vmem()] * (2 + len(v_parts)),
         out_specs=pl.BlockSpec(memory_space=pltpu.HBM),
@@ -202,7 +199,7 @@
         ],
         compiler_params=params(),
         name="merge",
-    )(listed, probs, v_own, *v_parts)
+    )(lists, probs, v_own, *v_parts)
 
 
 def ring_at(place, members):
@@ -214,7 +211,7 @@
     return jnp.where(block % 2 == 0, block // 2, members - 1 - block // 2)
 
 
-def round_the_ring(k_own, v_own, ready, members):
+def round_the_ring(k_own, v_own, members):
     ring = list(range(0, members, 2)) + list(range(members - 1, 0, -2))
     ways = [
         [(ring[p], ring[(p + turn) % members]) for p in range(members)] for turn in (1, -1)
@@ -228,8 +225,6 @@
     for distance in range(1, half):
         k_two = tuple(send(x, way) for way, x in enumerate(k_two))
         v_two = tuple(send(x, way) for way, x in enumerate(v_two))
-        if distance == 1:
-            k_two, ready = lax.optimization_barrier((k_two, ready))
         k_two = lax.optimization_barrier(k_two)
         if distance < half - 1:
             v_two = lax.optimization_barrier(v_two)
@@ -238,7 +233,7 @@
     k_all.append(send(k_two[0], 0))
     v_last, _ = lax.optimization_barrier((v_two[1], k_two))
     v_all.append(send(v_last, 1))
-    return k_all, v_all, ready
+    return k_all, v_all, k_two
 
 
 def ring_sources(members):
@@ -277,18 +272,17 @@
     v_own = values.reshape(tokens * kv_dev, dim)
     if members <= MOST_ROUND:
         sources = ring_sources(members)
-        ready = prepare(chosen, queries, k_own, v_own, kv_dev, sources, members - 1)
-        k_parts, v_parts, ready = round_the_ring(k_own, v_own, ready, members)
+        k_parts, v_parts, before = round_the_ring(k_own, v_own, members)
+        queries, _ = lax.optimization_barrier((queries, before))
     else:
-        k_parts, v_parts, mine = relay(k_own, v_own, chosen, members)
+        k_parts, v_parts, chosen = relay(k_own, v_own, chosen, members)
 
         def sources(_):
             return [jnp.int32(j) for j in range(slots - 1)]
 
-        ready = prepare(mine, queries, k_own, v_own, kv_dev, sources, slots - 1)
-    listed, q_ready, k_ready, v_ready = ready
-    probs = weights(listed, q_ready, k_ready, k_parts, slots)
-    return merge(listed, probs, v_ready, v_parts, slots)
+    lists, q_ready, k_ready, v_ready = prepare(chosen.T, queries, k_own, v_own, kv_dev)
+    probs = weights(lists, q_ready, k_ready, k_parts, sources)
+    return merge(lists, probs, v_ready, v_parts, sources)
 
 
 def solution(mesh):

time: 33.4 us -> 33.5 us (level)
  waiting for transfers between devices: 8.74 us -> 10.9 us
  Pallas kernels: 8.29 us -> 7.23 us
  local copies, waits for them, and re-layouts: 0.76 us -> 0 us
    ppermute x14, waiting for transfers between devices: 8.74 us -> 10.9 us  [send(): return lax.ppermute(x, 'seq', ways[way])]
    pallas_call x3, Pallas kernels: 8.29 us -> 7.23 us  [the longest x1 2.89 us: weights(): pl.pallas_call(functools.partial(weights_kernel, sources=sources), out_sh...]
    unnamed x1 -> x0, local copies, waits for them, and re-layouts: 0.76 us -> none
  transfers between devices with their start and end apart: 14 -> 14, of which waited for: 8 -> 9; matrix products, arithmetic and copies ran while one was open for 2% -> 0% of each run, Pallas kernels for 17% -> 13%
where the time goes in v7:
time: 33.5 us; the launch traced here: 33.3 us
  starting transfers between devices  15.1 us (45%)
  waiting for transfers between devices  10.9 us (33%)
  Pallas kernels  7.23 us (22%)
    ppermute x14, starting transfers between devices, send(): return lax.ppermute(x, 'seq', ways[way])  15.1 us
    ppermute x14, waiting for transfers between devices, send(): return lax.ppermute(x, 'seq', ways[way])  10.9 us
    pallas_call x1, Pallas kernels, weights(): pl.pallas_call(functools.partial(weights_kernel, sources=sources), out_sh...  2.89 us
    pallas_call x1, Pallas kernels, merge(): pl.pallas_call(functools.partial(merge_kernel, sources=sources), out_shap...  2.76 us
    pallas_call x1, Pallas kernels, prepare(): pl.pallas_call(functools.partial(prepare_kernel, kv_dev=kv_dev), out_shap...  1.58 us
  transfers between devices with their start and end apart: 14, of which 9 were waited for; matrix products, arithmetic and copies ran while one was open for 0% of the time, Pallas kernels for 13%

profile of v7, /device:TPU:0, one launch (start us, length us, event | category | flops | bytes accessed | tf_op | source)
XLA Modules:
  0.0 33.3 jit_solution(5704602735619878717)
XLA Ops:
  0.0 3.0 %collective-permute-start = (bf16[512,128]{1,0:T(8,128)(2,1)}, bf16[512,128]{1,0:T(8,128)(2,1)S(1)}, u32[]{:S(2)}, u32[]{:S(2)}) collective-permute-start(bf16[512,128]{1,0:T(8,128)(2,1)} %bitcast.3), channel_id=1, source_target_pairs={{0,4},{4,8},{8,12},{12,14},{14,10},{10,6},{6,2},{2,0},{1,5},{5,9},... | collective-permute-start | bytes 393224 | tf_op jit(solution)/shard_map/ppermute | solution.py:221
  3.0 0.0 collective-permute-start.1
  3.0 2.0 %collective-permute-start.7 = (bf16[512,128]{1,0:T(8,128)(2,1)}, bf16[512,128]{1,0:T(8,128)(2,1)S(1)}, u32[]{:S(2)}, u32[]{:S(2)}) collective-permute-start(bf16[512,128]{1,0:T(8,128)(2,1)} %bitcast.6), channel_id=1, source_target_pairs={{0,4},{4,8},{8,12},{12,14},{14,10},{10,6},{6,2},{2,0},{1,5},{5,9},... | collective-permute-start | bytes 393224 | tf_op jit(solution)/shard_map/ppermute | solution.py:221
  5.1 0.0 collective-permute-start.8
  5.1 2.4 %collective-permute-done.refs_0_ = bf16[512,128]{1,0:T(8,128)(2,1)S(1)} collective-permute-done((bf16[512,128]{1,0:T(8,128)(2,1)}, bf16[512,128]{1,0:T(8,128)(2,1)S(1)}, u32[]{:S(2)}, u32[]{:S(2)}) %collective-permute-start) | collective-permute-done | bytes 131104 | tf_op jit(solution)/shard_map/ppermute | solution.py:221
  7.5 2.1 %collective-permute-done.1.refs_1_ = bf16[512,128]{1,0:T(8,128)(2,1)S(1)} collective-permute-done((bf16[512,128]{1,0:T(8,128)(2,1)}, bf16[512,128]{1,0:T(8,128)(2,1)S(1)}, u32[]{:S(2)}, u32[]{:S(2)}) %collective-permute-start.1) | collective-permute-done | bytes 131104 | tf_op jit(solution)/shard_map/ppermute | solution.py:221
  9.6 1.6 %collective-permute-start.2 = (bf16[512,128]{1,0:T(8,128)(2,1)S(1)}, bf16[512,128]{1,0:T(8,128)(2,1)S(1)}, u32[]{:S(2)}, u32[]{:S(2)}) collective-permute-start(bf16[512,128]{1,0:T(8,128)(2,1)S(1)} %collective-permute-done.refs_0_), channel_id=1, source_target_pairs={{0,4},{4,8},{8,12},{12,14},{14,10},{10,6},{6,2},{2,0},{1,5},{5,9},... | collective-permute-start | bytes 393224 | tf_op jit(solution)/shard_map/ppermute | solution.py:221
  11.2 0.4 %collective-permute-start.3 = (bf16[512,128]{1,0:T(8,128)(2,1)S(1)}, bf16[512,128]{1,0:T(8,128)(2,1)S(1)}, u32[]{:S(2)}, u32[]{:S(2)}) collective-permute-start(bf16[512,128]{1,0:T(8,128)(2,1)S(1)} %collective-permute-done.1.refs_1_), channel_id=1, source_target_pairs={{0,2},{4,0},{8,4},{12,8},{14,12},{10,14},{6,10},{2,6},{1,3},{5,1},... | collective-permute-start | bytes 393224 | tf_op jit(solution)/shard_map/ppermute | solution.py:221
  11.6 0.0 collective-permute-done.7.refs_0_
  11.6 0.0 collective-permute-done.8.refs_1_
  11.6 0.7 %collective-permute-start.10 = (bf16[512,128]{1,0:T(8,128)(2,1)S(1)}, bf16[512,128]{1,0:T(8,128)(2,1)S(1)}, u32[]{:S(2)}, u32[]{:S(2)}) collective-permute-start(bf16[512,128]{1,0:T(8,128)(2,1)S(1)} %collective-permute-done.8.refs_1_), channel_id=1, source_target_pairs={{0,2},{4,0},{8,4},{12,8},{14,12},{10,14},{6,10},{2,6},{1,3},{5,1},... | collective-permute-start | bytes 393224 | tf_op jit(solution)/shard_map/ppermute | solution.py:221
  12.3 1.3 %collective-permute-start.9 = (bf16[512,128]{1,0:T(8,128)(2,1)S(1)}, bf16[512,128]{1,0:T(8,128)(2,1)S(1)}, u32[]{:S(2)}, u32[]{:S(2)}) collective-permute-start(bf16[512,128]{1,0:T(8,128)(2,1)S(1)} %collective-permute-done.7.refs_0_), channel_id=1, source_target_pairs={{0,4},{4,8},{8,12},{12,14},{14,10},{10,6},{6,2},{2,0},{1,5},{5,9},... | collective-permute-start | bytes 393224 | tf_op jit(solution)/shard_map/ppermute | solution.py:221
  13.6 2.2 %collective-permute-done.2.refs_2_ = bf16[512,128]{1,0:T(8,128)(2,1)S(1)} collective-permute-done((bf16[512,128]{1,0:T(8,128)(2,1)S(1)}, bf16[512,128]{1,0:T(8,128)(2,1)S(1)}, u32[]{:S(2)}, u32[]{:S(2)}) %collective-permute-start.2) | collective-permute-done | bytes 131104 | tf_op jit(solution)/shard_map/ppermute | solution.py:221
  15.9 0.3 collective-permute-done.3.refs_3_
  16.1 1.6 %collective-permute-start.4 = (bf16[512,128]{1,0:T(8,128)(2,1)S(1)}, bf16[512,128]{1,0:T(8,128)(2,1)S(1)}, u32[]{:S(2)}, u32[]{:S(2)}) collective-permute-start(bf16[512,128]{1,0:T(8,128)(2,1)S(1)} %collective-permute-done.2.refs_2_), channel_id=1, source_target_pairs={{0,4},{4,8},{8,12},{12,14},{14,10},{10,6},{6,2},{2,0},{1,5},{5,9},... | collective-permute-start | bytes 393224 | tf_op jit(solution)/shard_map/ppermute | solution.py:221
  17.7 0.4 %collective-permute-start.5 = (bf16[512,128]{1,0:T(8,128)(2,1)S(1)}, bf16[512,128]{1,0:T(8,128)(2,1)S(1)}, u32[]{:S(2)}, u32[]{:S(2)}) collective-permute-start(bf16[512,128]{1,0:T(8,128)(2,1)S(1)} %collective-permute-done.3.refs_3_), channel_id=1, source_target_pairs={{0,2},{4,0},{8,4},{12,8},{14,12},{10,14},{6,10},{2,6},{1,3},{5,1},... | collective-permute-start | bytes 393224 | tf_op jit(solution)/shard_map/ppermute | solution.py:221
  18.2 0.7 %collective-permute-done.10.refs_3_ = bf16[512,128]{1,0:T(8,128)(2,1)S(1)} collective-permute-done((bf16[512,128]{1,0:T(8,128)(2,1)S(1)}, bf16[512,128]{1,0:T(8,128)(2,1)S(1)}, u32[]{:S(2)}, u32[]{:S(2)}) %collective-permute-start.10) | collective-permute-done | bytes 131104 | tf_op jit(solution)/shard_map/ppermute | solution.py:221
  18.9 0.0 collective-permute-done.9.refs_2_
  18.9 0.4 %collective-permute-start.12 = (bf16[512,128]{1,0:T(8,128)(2,1)S(1)}, bf16[512,128]{1,0:T(8,128)(2,1)S(1)}, u32[]{:S(2)}, u32[]{:S(2)}) collective-permute-start(bf16[512,128]{1,0:T(8,128)(2,1)S(1)} %collective-permute-done.10.refs_3_), channel_id=1, source_target_pairs={{0,2},{4,0},{8,4},{12,8},{14,12},{10,14},{6,10},{2,6},{1,3},{5,1},... | collective-permute-start | bytes 393224 | tf_op jit(solution)/shard_map/ppermute | solution.py:221
  19.3 1.6 %collective-permute-start.11 = (bf16[512,128]{1,0:T(8,128)(2,1)S(1)}, bf16[512,128]{1,0:T(8,128)(2,1)S(1)}, u32[]{:S(2)}, u32[]{:S(2)}) collective-permute-start(bf16[512,128]{1,0:T(8,128)(2,1)S(1)} %collective-permute-done.9.refs_2_), channel_id=1, source_target_pairs={{0,4},{4,8},{8,12},{12,14},{14,10},{10,6},{6,2},{2,0},{1,5},{5,9},... | collective-permute-start | bytes 393224 | tf_op jit(solution)/shard_map/ppermute | solution.py:221
  20.9 0.5 %collective-permute-done.4.refs_4_ = bf16[512,128]{1,0:T(8,128)(2,1)S(1)} collective-permute-done((bf16[512,128]{1,0:T(8,128)(2,1)S(1)}, bf16[512,128]{1,0:T(8,128)(2,1)S(1)}, u32[]{:S(2)}, u32[]{:S(2)}) %collective-permute-start.4) | collective-permute-done | bytes 131104 | tf_op jit(solution)/shard_map/ppermute | solution.py:221
  21.4 1.3 %collective-permute-done.5.refs_5_ = bf16[512,128]{1,0:T(8,128)(2,1)S(1)} collective-permute-done((bf16[512,128]{1,0:T(8,128)(2,1)S(1)}, bf16[512,128]{1,0:T(8,128)(2,1)S(1)}, u32[]{:S(2)}, u32[]{:S(2)}) %collective-permute-start.5) | collective-permute-done | bytes 131104 | tf_op jit(solution)/shard_map/ppermute | solution.py:221
  22.7 1.5 %collective-permute-start.6 = (bf16[512,128]{1,0:T(8,128)(2,1)S(1)}, bf16[512,128]{1,0:T(8,128)(2,1)S(1)}, u32[]{:S(2)}, u32[]{:S(2)}) collective-permute-start(bf16[512,128]{1,0:T(8,128)(2,1)S(1)} %collective-permute-done.4.refs_4_), channel_id=1, source_target_pairs={{0,4},{4,8},{8,12},{12,14},{14,10},{10,6},{6,2},{2,0},{1,5},{5,9},... | collective-permute-start | bytes 393224 | tf_op jit(solution)/shard_map/ppermute | solution.py:221
  24.1 0.9 %collective-permute-done.12.refs_5_ = bf16[512,128]{1,0:T(8,128)(2,1)S(1)} collective-permute-done((bf16[512,128]{1,0:T(8,128)(2,1)S(1)}, bf16[512,128]{1,0:T(8,128)(2,1)S(1)}, u32[]{:S(2)}, u32[]{:S(2)}) %collective-permute-start.12) | collective-permute-done | bytes 131104 | tf_op jit(solution)/shard_map/ppermute | solution.py:221
  25.0 0.5 %collective-permute-start.13 = (bf16[512,128]{1,0:T(8,128)(2,1)S(1)}, bf16[512,128]{1,0:T(8,128)(2,1)S(1)}, u32[]{:S(2)}, u32[]{:S(2)}) collective-permute-start(bf16[512,128]{1,0:T(8,128)(2,1)S(1)} %collective-permute-done.12.refs_5_), channel_id=1, source_target_pairs={{0,2},{4,0},{8,4},{12,8},{14,12},{10,14},{6,10},{2,6},{1,3},{5,1},... | collective-permute-start | bytes 393224 | tf_op jit(solution)/shard_map/ppermute | solution.py:221
  25.5 1.6 %prepare.1 = (s32[4,8]{1,0:T(4,128)S(1)}, bf16[4,1024,128]{2,1,0:T(8,128)(2,1)S(1)}, bf16[4,128,128]{2,1,0:T(8,128)(2,1)S(1)}, bf16[4,128,128]{2,1,0:T(8,128)(2,1)S(1)}) custom-call(s32[4,8]{1,0:T(4,128)} %bitcast.9, bf16[128,32,128]{2,1,0:T(8,128)(2,1)} %q_hbm, bf16[512,128]{1,0:T(8,128)(2,1)} %bitcast.5, bf16[512,128]{1,0:T(8,128)(2,1)} %bitcast.8), custom_call_target="tpu_custom_call" | custom-call | tf_op jit(solution)/shard_map/prepare/pallas_call | solution.py:54
  27.1 0.5 %collective-permute-done.6.refs_6_ = bf16[512,128]{1,0:T(8,128)(2,1)S(1)} collective-permute-done((bf16[512,128]{1,0:T(8,128)(2,1)S(1)}, bf16[512,128]{1,0:T(8,128)(2,1)S(1)}, u32[]{:S(2)}, u32[]{:S(2)}) %collective-permute-start.6) | collective-permute-done | bytes 131104 | tf_op jit(solution)/shard_map/ppermute | solution.py:221
  27.6 2.9 %weights.1.weights_ref = bf16[4,1024,512]{2,1,0:T(8,128)(2,1)S(1)} custom-call(s32[4,8]{1,0:T(4,128)S(1)} %get-tuple-element.28.lists_ref, bf16[4,1024,128]{2,1,0:T(8,128)(2,1)S(1)} %get-tuple-element.29.q_ref, bf16[4,128,128]{2,1,0:T(8,128)(2,1)S(1)} %get-tuple-element.30.own_ref, bf16[512,128]{1,0:T(8,128)(2,1)S(1)} %collective-permute-done.refs_0_, ...), custom_call_target="tpu_custom_call" | custom-call | tf_op jit(solution)/shard_map/weights/pallas_call | solution.py:145
  30.5 0.0 collective-permute-done.11.refs_4_
  30.5 0.0 collective-permute-done.13.refs_6_
  30.6 2.8 %merge.1 = bf16[128,32,128]{2,1,0:T(8,128)(2,1)} custom-call(s32[4,8]{1,0:T(4,128)S(1)} %get-tuple-element.28.lists_ref, bf16[4,1024,512]{2,1,0:T(8,128)(2,1)S(1)} %weights.1.weights_ref, bf16[4,128,128]{2,1,0:T(8,128)(2,1)S(1)} %get-tuple-element.31.own_ref, bf16[512,128]{1,0:T(8,128)(2,1)S(1)} %collective-permute-done.7.refs_0_, ...), custom_call_target="tpu_custom_call" | custom-call | tf_op jit(solution)/shard_map/merge/pallas_call | solution.py:189
Async XLA Ops:
  0.0 7.5 %collective-permute-start = (bf16[512,128]{1,0:T(8,128)(2,1)}, bf16[512,128]{1,0:T(8,128)(2,1)S(1)}, u32[]{:S(2)}, u32[]{:S(2)}) collective-permute-start(bf16[512,128]{1,0:T(8,128)(2,1)} %bitcast.3), channel_id=1, source_target_pairs={{0,4},{4,8},{8,12},{12,14},{14,10},{10,6},{6,2},{2,0},{1,5},{5,9},... | collective-permute-start | bytes 393224 | tf_op jit(solution)/shard_map/ppermute | solution.py:221
  3.0 6.5 %collective-permute-start.1 = (bf16[512,128]{1,0:T(8,128)(2,1)}, bf16[512,128]{1,0:T(8,128)(2,1)S(1)}, u32[]{:S(2)}, u32[]{:S(2)}) collective-permute-start(bf16[512,128]{1,0:T(8,128)(2,1)} %bitcast.4), channel_id=1, source_target_pairs={{0,2},{4,0},{8,4},{12,8},{14,12},{10,14},{6,10},{2,6},{1,3},{5,1},... | collective-permute-start | bytes 393224 | tf_op jit(solution)/shard_map/ppermute | solution.py:221
  3.0 8.6 %collective-permute-start.7 = (bf16[512,128]{1,0:T(8,128)(2,1)}, bf16[512,128]{1,0:T(8,128)(2,1)S(1)}, u32[]{:S(2)}, u32[]{:S(2)}) collective-permute-start(bf16[512,128]{1,0:T(8,128)(2,1)} %bitcast.6), channel_id=1, source_target_pairs={{0,4},{4,8},{8,12},{12,14},{14,10},{10,6},{6,2},{2,0},{1,5},{5,9},... | collective-permute-start | bytes 393224 | tf_op jit(solution)/shard_map/ppermute | solution.py:221
  5.1 6.5 %collective-permute-start.8 = (bf16[512,128]{1,0:T(8,128)(2,1)}, bf16[512,128]{1,0:T(8,128)(2,1)S(1)}, u32[]{:S(2)}, u32[]{:S(2)}) collective-permute-start(bf16[512,128]{1,0:T(8,128)(2,1)} %bitcast.7), channel_id=1, source_target_pairs={{0,2},{4,0},{8,4},{12,8},{14,12},{10,14},{6,10},{2,6},{1,3},{5,1},... | collective-permute-start | bytes 393224 | tf_op jit(solution)/shard_map/ppermute | solution.py:221
  9.6 6.3 %collective-permute-start.2 = (bf16[512,128]{1,0:T(8,128)(2,1)S(1)}, bf16[512,128]{1,0:T(8,128)(2,1)S(1)}, u32[]{:S(2)}, u32[]{:S(2)}) collective-permute-start(bf16[512,128]{1,0:T(8,128)(2,1)S(1)} %collective-permute-done.refs_0_), channel_id=1, source_target_pairs={{0,4},{4,8},{8,12},{12,14},{14,10},{10,6},{6,2},{2,0},{1,5},{5,9},... | collective-permute-start | bytes 393224 | tf_op jit(solution)/shard_map/ppermute | solution.py:221
  11.2 5.0 %collective-permute-start.3 = (bf16[512,128]{1,0:T(8,128)(2,1)S(1)}, bf16[512,128]{1,0:T(8,128)(2,1)S(1)}, u32[]{:S(2)}, u32[]{:S(2)}) collective-permute-start(bf16[512,128]{1,0:T(8,128)(2,1)S(1)} %collective-permute-done.1.refs_1_), channel_id=1, source_target_pairs={{0,2},{4,0},{8,4},{12,8},{14,12},{10,14},{6,10},{2,6},{1,3},{5,1},... | collective-permute-start | bytes 393224 | tf_op jit(solution)/shard_map/ppermute | solution.py:221
  11.6 7.3 %collective-permute-start.10 = (bf16[512,128]{1,0:T(8,128)(2,1)S(1)}, bf16[512,128]{1,0:T(8,128)(2,1)S(1)}, u32[]{:S(2)}, u32[]{:S(2)}) collective-permute-start(bf16[512,128]{1,0:T(8,128)(2,1)S(1)} %collective-permute-done.8.refs_1_), channel_id=1, source_target_pairs={{0,2},{4,0},{8,4},{12,8},{14,12},{10,14},{6,10},{2,6},{1,3},{5,1},... | collective-permute-start | bytes 393224 | tf_op jit(solution)/shard_map/ppermute | solution.py:221
  12.3 6.6 %collective-permute-start.9 = (bf16[512,128]{1,0:T(8,128)(2,1)S(1)}, bf16[512,128]{1,0:T(8,128)(2,1)S(1)}, u32[]{:S(2)}, u32[]{:S(2)}) collective-permute-start(bf16[512,128]{1,0:T(8,128)(2,1)S(1)} %collective-permute-done.7.refs_0_), channel_id=1, source_target_pairs={{0,4},{4,8},{8,12},{12,14},{14,10},{10,6},{6,2},{2,0},{1,5},{5,9},... | collective-permute-start | bytes 393224 | tf_op jit(solution)/shard_map/ppermute | solution.py:221
  16.1 5.2 %collective-permute-start.4 = (bf16[512,128]{1,0:T(8,128)(2,1)S(1)}, bf16[512,128]{1,0:T(8,128)(2,1)S(1)}, u32[]{:S(2)}, u32[]{:S(2)}) collective-permute-start(bf16[512,128]{1,0:T(8,128)(2,1)S(1)} %collective-permute-done.2.refs_2_), channel_id=1, source_target_pairs={{0,4},{4,8},{8,12},{12,14},{14,10},{10,6},{6,2},{2,0},{1,5},{5,9},... | collective-permute-start | bytes 393224 | tf_op jit(solution)/shard_map/ppermute | solution.py:221
  17.7 5.0 %collective-permute-start.5 = (bf16[512,128]{1,0:T(8,128)(2,1)S(1)}, bf16[512,128]{1,0:T(8,128)(2,1)S(1)}, u32[]{:S(2)}, u32[]{:S(2)}) collective-permute-start(bf16[512,128]{1,0:T(8,128)(2,1)S(1)} %collective-permute-done.3.refs_3_), channel_id=1, source_target_pairs={{0,2},{4,0},{8,4},{12,8},{14,12},{10,14},{6,10},{2,6},{1,3},{5,1},... | collective-permute-start | bytes 393224 | tf_op jit(solution)/shard_map/ppermute | solution.py:221
  18.9 6.2 %collective-permute-start.12 = (bf16[512,128]{1,0:T(8,128)(2,1)S(1)}, bf16[512,128]{1,0:T(8,128)(2,1)S(1)}, u32[]{:S(2)}, u32[]{:S(2)}) collective-permute-start(bf16[512,128]{1,0:T(8,128)(2,1)S(1)} %collective-permute-done.10.refs_3_), channel_id=1, source_target_pairs={{0,2},{4,0},{8,4},{12,8},{14,12},{10,14},{6,10},{2,6},{1,3},{5,1},... | collective-permute-start | bytes 393224 | tf_op jit(solution)/shard_map/ppermute | solution.py:221
  19.3 11.3 %collective-permute-start.11 = (bf16[512,128]{1,0:T(8,128)(2,1)S(1)}, bf16[512,128]{1,0:T(8,128)(2,1)S(1)}, u32[]{:S(2)}, u32[]{:S(2)}) collective-permute-start(bf16[512,128]{1,0:T(8,128)(2,1)S(1)} %collective-permute-done.9.refs_2_), channel_id=1, source_target_pairs={{0,4},{4,8},{8,12},{12,14},{14,10},{10,6},{6,2},{2,0},{1,5},{5,9},... | collective-permute-start | bytes 393224 | tf_op jit(solution)/shard_map/ppermute | solution.py:221
  22.7 5.0 %collective-permute-start.6 = (bf16[512,128]{1,0:T(8,128)(2,1)S(1)}, bf16[512,128]{1,0:T(8,128)(2,1)S(1)}, u32[]{:S(2)}, u32[]{:S(2)}) collective-permute-start(bf16[512,128]{1,0:T(8,128)(2,1)S(1)} %collective-permute-done.4.refs_4_), channel_id=1, source_target_pairs={{0,4},{4,8},{8,12},{12,14},{14,10},{10,6},{6,2},{2,0},{1,5},{5,9},... | collective-permute-start | bytes 393224 | tf_op jit(solution)/shard_map/ppermute | solution.py:221
  25.0 5.5 %collective-permute-start.13 = (bf16[512,128]{1,0:T(8,128)(2,1)S(1)}, bf16[512,128]{1,0:T(8,128)(2,1)S(1)}, u32[]{:S(2)}, u32[]{:S(2)}) collective-permute-start(bf16[512,128]{1,0:T(8,128)(2,1)S(1)} %collective-permute-done.12.refs_5_), channel_id=1, source_target_pairs={{0,2},{4,0},{8,4},{12,8},{14,12},{10,14},{6,10},{2,6},{1,3},{5,1},... | collective-permute-start | bytes 393224 | tf_op jit(solution)/shard_map/ppermute | solution.py:221

commit v8 on v7

v8 whole, which is shorter than its diff:
```python
import functools
import math

import jax
import jax.numpy as jnp
from jax import lax
from jax.experimental import pallas as pl
from jax.experimental.pallas import tpu as pltpu
from jax.sharding import PartitionSpec as P

NO_KEY = -1e30
ROW_CHUNK = 256
MOST_ROUND = 16
HEADS_OUT = 16


def params():
    return pltpu.CompilerParams(vmem_limit_bytes=16 * 2**20)


def vmem():
    return pl.BlockSpec(memory_space=pltpu.VMEM)


def prepare_kernel(
    lists_hbm, q_hbm, k_hbm, v_hbm, lists_out, q_out, k_out, v_out,
    q_ref, k_ref, v_ref, k_wide, v_wide, sems, *, kv_dev,
):
    whole = ((k_hbm, k_ref), (v_hbm, v_ref), (q_hbm, q_ref), (lists_hbm, lists_out))
    copies = [
        pltpu.make_async_copy(source, here, sems.at[n]) for n, (source, here) in enumerate(whole)
    ]
    for copy in copies:
        copy.start()
    tokens, heads, dim = q_ref.shape
    group = heads // kv_dev
    for copy, ref, wide, out in zip(copies, (k_ref, v_ref), (k_wide, v_wide), (k_out, v_out)):
        copy.wait()
        wide[...] = ref[...].astype(jnp.float32)
        for h in range(kv_dev):
            out[h] = wide[pl.ds(h, tokens, stride=kv_dev), :].astype(jnp.bfloat16)
    copies[2].wait()
    for h in range(kv_dev):
        q = q_ref[:, pl.ds(h * group, group), :].astype(jnp.float32)
        q_out[h] = q.reshape(tokens * group, dim).astype(jnp.bfloat16)
    copies[3].wait()


def prepare(lists, queries, k_own, v_own, kv_dev):
    tokens, heads, dim = queries.shape
    operands = [
        pltpu.with_memory_space_constraint(x, pltpu.HBM) for x in (lists, queries, k_own, v_own)
    ]
    by_head = jax.ShapeDtypeStruct((kv_dev, tokens, dim), jnp.bfloat16)
    return pl.pallas_call(
        functools.partial(prepare_kernel, kv_dev=kv_dev),
        out_shape=(
            jax.ShapeDtypeStruct(lists.shape, lists.dtype),
            jax.ShapeDtypeStruct((kv_dev, tokens * heads // kv_dev, dim), jnp.bfloat16),
            by_head,
            by_head,
        ),
        in_specs=[pl.BlockSpec(memory_space=pltpu.HBM)] * 4,
        out_specs=(vmem(), vmem(), vmem(), vmem()),
        scratch_shapes=[
            pltpu.VMEM(queries.shape, jnp.bfloat16),
            pltpu.VMEM(k_own.shape, jnp.bfloat16),
            pltpu.VMEM(k_own.shape, jnp.bfloat16),
            pltpu.VMEM(k_own.shape, jnp.float32),
            pltpu.VMEM(k_own.shape, jnp.float32),
            pltpu.SemaphoreType.DMA((4,)),
        ],
        compiler_params=params(),
        name="prepare",
    )(*operands)


def is_listed(lists_ref, target, source):
    same = [lists_ref[j, target] == source for j in range(lists_ref.shape[0])]
    return functools.reduce(jnp.logical_or, same)


def by_head(wide, h, kv_dev, keys):
    return wide[pl.ds(h, keys, stride=kv_dev), :].astype(jnp.bfloat16)


def with_ones(values):
    return jnp.concatenate([values, jnp.ones_like(values)], axis=1)


def put_out(out_ref, h, first, both, group):
    rows, dim = both.shape[0], both.shape[1] // 2
    merged = (both[:, :dim] / both[:, dim:]).reshape(rows // group, group, dim)
    tokens = pl.ds(first // group, rows // group)
    out_ref[tokens, pl.ds(h * group, group), :] = merged.astype(jnp.bfloat16)


def send_out(out_ref, out_hbm, sems, h, group):
    done = (h + 1) * group
    if done % HEADS_OUT:
        return []
    heads = pl.ds(done - HEADS_OUT, HEADS_OUT)
    copy = pltpu.make_async_copy(
        out_ref.at[:, heads, :], out_hbm.at[:, heads, :], sems.at[done // HEADS_OUT - 1]
    )
    copy.start()
    return [copy]


def attend_kernel(lists_ref, q_ref, k_own_ref, v_own_ref, *refs, parts, sources, last):
    k_parts, v_parts = refs[:parts], refs[parts : 2 * parts]
    out_hbm, *state, k_wide, v_wide, out_ref, sems = refs[2 * parts :]
    kv_dev, tokens, dim = k_own_ref.shape
    rows_all = q_ref.shape[1]
    group = rows_all // tokens
    block = tokens * kv_dev
    most = k_wide.shape[0] // block
    factor = dim ** (-0.5) * math.log2(math.e)
    target = lax.axis_index("seq").astype(jnp.int32)

    count = jnp.int32(0)
    for source, k_part, v_part in zip(sources(target), k_parts, v_parts):
        take = is_listed(lists_ref, target, source)

        @pl.when(take)
        def _take(k_part=k_part, v_part=v_part, count=count):
            rows = pl.ds(pl.multiple_of(count * block, block), block)
            k_wide[rows, :] = k_part[...].astype(jnp.float32)
            v_wide[rows, :] = v_part[...].astype(jnp.float32)

        count += take.astype(jnp.int32)

    def run(others, final):
        copies = []
        for h in range(kv_dev):
            k_h, v_h = k_own_ref[h], v_own_ref[h]
            if others:
                keys = others * tokens
                k_h = jnp.concatenate([k_h, by_head(k_wide, h, kv_dev, keys)], axis=0)
                v_h = jnp.concatenate([v_h, by_head(v_wide, h, kv_dev, keys)], axis=0)
            v_h = with_ones(v_h)
            for first in range(0, rows_all, ROW_CHUNK):
                rows = pl.ds(first, ROW_CHUNK)
                s = lax.dot_general(
                    q_ref[h, rows, :], k_h, (((1,), (1,)), ((), ())), preferred_element_type=jnp.float32
                )
                row = (lax.broadcasted_iota(jnp.int32, (ROW_CHUNK, tokens), 0) + first) // group
                key = lax.broadcasted_iota(jnp.int32, (ROW_CHUNK, tokens), 1)
                scores = [jnp.where(key <= row, s[:, :tokens], NO_KEY)]
                scores += [s[:, (j + 1) * tokens : (j + 2) * tokens] for j in range(others)]
                top = jnp.max(functools.reduce(jnp.maximum, scores), axis=1, keepdims=True)
                probs = [jnp.exp2((score - top) * factor).astype(jnp.bfloat16) for score in scores]
                both = jnp.dot(
                    jnp.concatenate(probs, axis=1), v_h, preferred_element_type=jnp.float32
                )
                if final:
                    put_out(out_ref, h, first, both, group)
                else:
                    state[0][h, rows, :] = jnp.broadcast_to(top, (ROW_CHUNK, dim))
                    state[1][h, rows, :] = both
            if final:
                copies += send_out(out_ref, out_hbm, sems, h, group)
        for copy in copies:
            copy.wait()

    unfinished = False if last is None else is_listed(lists_ref, target, last(target))
    for others in range(most + 1):

        @pl.when(jnp.logical_and(count == others, jnp.logical_not(unfinished)))
        def _whole(others=others):
            run(others, True)

        if last is not None and others < most:

            @pl.when(jnp.logical_and(count == others, unfinished))
            def _part(others=others):
                run(others, False)


def attend(lists, queries, k_own, v_own, k_parts, v_parts, sources, last):
    kv_dev, rows, dim = queries.shape
    tokens = k_own.shape[1]
    rest = (lists.shape[0] - 1) * tokens * kv_dev
    out = jax.ShapeDtypeStruct((tokens, rows * kv_dev // tokens, dim), jnp.bfloat16)
    state = [] if last is None else [
        jax.ShapeDtypeStruct((kv_dev, rows, wide), jnp.float32) for wide in (dim, 2 * dim)
    ]
    hbm, smem = (pl.BlockSpec(memory_space=space) for space in (pltpu.HBM, pltpu.SMEM))
    return pl.pallas_call(
        functools.partial(attend_kernel, parts=len(k_parts), sources=sources, last=last),
        out_shape=(out, *state),
        in_specs=[smem] + [vmem()] * (3 + 2 * len(k_parts)),
        out_specs=(hbm, *(vmem() for _ in state)),
        scratch_shapes=[
            pltpu.VMEM((rest, dim), jnp.float32),
            pltpu.VMEM((rest, dim), jnp.float32),
            pltpu.VMEM(out.shape, jnp.bfloat16),
            pltpu.SemaphoreType.DMA((out.shape[1] // HEADS_OUT,)),
        ],
        compiler_params=params(),
        name="attend",
    )(lists, queries, k_own, v_own, *k_parts, *v_parts)


def last_kernel(
    lists_ref, q_ref, top_ref, both_ref, k_ref, v_ref, _, out_hbm, k_wide, v_wide, out_ref, sems, *, last
):
    kv_dev, rows_all, dim = q_ref.shape
    tokens = k_ref.shape[0] // kv_dev
    group = rows_all // tokens
    factor = dim ** (-0.5) * math.log2(math.e)
    target = lax.axis_index("seq").astype(jnp.int32)

    @pl.when(is_listed(lists_ref, target, last(target)))
    def _add():
        k_wide[...] = k_ref[...].astype(jnp.float32)
        v_wide[...] = v_ref[...].astype(jnp.float32)
        copies = []
        for h in range(kv_dev):
            k_h = by_head(k_wide, h, kv_dev, tokens)
            v_h = with_ones(by_head(v_wide, h, kv_dev, tokens))
            for first in range(0, rows_all, ROW_CHUNK):
                rows = pl.ds(first, ROW_CHUNK)
                s = lax.dot_general(
                    q_ref[h, rows, :], k_h, (((1,), (1,)), ((), ())), preferred_element_type=jnp.float32
                )
                before = top_ref[h, rows, :]
                top = jnp.maximum(before, jnp.max(s, axis=1, keepdims=True))
                probs = jnp.exp2((s - top) * factor).astype(jnp.bfloat16)
                shrink = jnp.exp2((before - top) * factor)
                both = jnp.dot(probs, v_h, preferred_element_type=jnp.float32)
                both += both_ref[h, rows, :] * jnp.concatenate([shrink, shrink], axis=1)
                put_out(out_ref, h, first, both, group)
            copies += send_out(out_ref, out_hbm, sems, h, group)
        for copy in copies:
            copy.wait()


def attend_last(lists, queries, state, k_last, v_last, out, last):
    top, both = state
    hbm, smem = (pl.BlockSpec(memory_space=space) for space in (pltpu.HBM, pltpu.SMEM))
    return pl.pallas_call(
        functools.partial(last_kernel, last=last),
        out_shape=jax.ShapeDtypeStruct(out.shape, out.dtype),
        in_specs=[smem] + [vmem()] * 5 + [hbm],
        out_specs=hbm,
        input_output_aliases={6: 0},
        scratch_shapes=[
            pltpu.VMEM(k_last.shape, jnp.float32),
            pltpu.VMEM(k_last.shape, jnp.float32),
            pltpu.VMEM(out.shape, jnp.bfloat16),
            pltpu.SemaphoreType.DMA((out.shape[1] // HEADS_OUT,)),
        ],
        compiler_params=params(),
        name="attend_last",
    )(lists, queries, top, both, k_last, v_last, out)


def ring_at(place, members):
    back = members - 1 - place
    return jnp.where(place < members // 2, 2 * place, 2 * back + 1)


def ring_place(block, members):
    return jnp.where(block % 2 == 0, block // 2, members - 1 - block // 2)


def round_the_ring(k_own, v_own, ready, members):
    ring = list(range(0, members, 2)) + list(range(members - 1, 0, -2))
    ways = [
        [(ring[p], ring[(p + turn) % members]) for p in range(members)] for turn in (1, -1)
    ]

    def send(x, way):
        return lax.ppermute(x, "seq", ways[way])

    half = members // 2
    k_two, v_two, k_all, v_all = [k_own, k_own], [v_own, v_own], [], []
    for distance in range(1, half):
        ahead = send(k_two[0], 0), send(v_two[1], 1)
        behind = send(v_two[0], 0), send(k_two[1], 1)
        if distance == 1:
            ahead, ready = lax.optimization_barrier((ahead, ready))
        ahead = lax.optimization_barrier(ahead)
        behind = lax.optimization_barrier(behind)
        k_two, v_two = [ahead[0], behind[1]], [behind[0], ahead[1]]
        k_all += k_two
        v_all += v_two
    return k_all, v_all, send(k_two[0], 0), send(v_two[1], 1), ready


def ring_sources(members):
    def at(target, turn):
        place = lax.rem(ring_place(target, members) + turn + members, members)
        return ring_at(place, members)

    def sources(target):
        return [at(target, turn) for far in range(1, members // 2) for turn in (-far, far)]

    return sources, lambda target: at(target, members // 2)


def others(row, target):
    slots = row.shape[-1]
    own_at = jnp.argmax(row == target[..., None], axis=-1)
    j = jnp.arange(slots - 1)
    return jnp.where(j >= own_at[..., None], row[..., 1:], row[..., :-1])


def relay(k_own, v_own, chosen, members):
    block, dim = k_own.shape
    stacked = jnp.stack([k_own, v_own]).reshape(2, members, block // members, dim)
    shares = lax.all_to_all(stacked, "seq", split_axis=1, concat_axis=1, tiled=True)
    wanted = others(chosen, jnp.arange(members, dtype=jnp.int32))
    picked = jnp.take(shares, jnp.maximum(wanted, 0), axis=1)
    arrived = lax.all_to_all(picked, "seq", split_axis=1, concat_axis=3, tiled=True)
    count = wanted.shape[1]
    k_parts, v_parts = ([arrived[n, 0, j].reshape(block, dim) for j in range(count)] for n in range(2))
    return k_parts, v_parts, jnp.where(wanted < 0, -1, jnp.arange(count, dtype=jnp.int32))


def per_device(queries, keys, values, chosen):
    members = lax.axis_size("seq")
    tokens, kv_dev, dim = keys.shape
    k_own = keys.reshape(tokens * kv_dev, dim)
    v_own = values.reshape(tokens * kv_dev, dim)
    if members <= MOST_ROUND:
        ready = prepare(chosen.T, queries, k_own, v_own, kv_dev)
        k_parts, v_parts, k_last, v_last, ready = round_the_ring(k_own, v_own, ready, members)
        lists, q_ready, k_ready, v_ready = ready
        sources, last = ring_sources(members)
        out, *state = attend(lists, q_ready, k_ready, v_ready, k_parts, v_parts, sources, last)
        return attend_last(lists, q_ready, state, k_last, v_last, out, last)

    k_parts, v_parts, mine = relay(k_own, v_own, chosen, members)
    lists, *ready = prepare(mine.T, queries, k_own, v_own, kv_dev)

    def sources(_):
        return [jnp.int32(j) for j in range(len(k_parts))]

    lists = jnp.concatenate([lists, jnp.full_like(lists[:1], -1)])
    return attend(lists, *ready, k_parts, v_parts, sources, None)[0]


def solution(mesh):
    rows = P(("groups", "seq"), "head", None)
    return jax.shard_map(
        per_device,
        mesh=mesh,
        in_specs=(rows, rows, rows, P("groups", None)),
        out_specs=rows,
        check_vma=False,
    )
```

time: 33.5 us -> 32.9 us (0.982)
  the two profiles are of different devices: /device:TPU:0 before, /device:TPU:20 now
where the time goes in v8:
time: 32.9 us; the launch traced here: 32.8 us
  starting transfers between devices  14.3 us (43%)
  Pallas kernels  10.2 us (31%)
  waiting for transfers between devices  8.11 us (25%)
    ppermute x14, starting transfers between devices, send(): return lax.ppermute(x, 'seq', ways[way])  14.3 us
    ppermute x14, waiting for transfers between devices, send(): return lax.ppermute(x, 'seq', ways[way])  8.11 us
    pallas_call x1, Pallas kernels, attend(): pl.pallas_call(functools.partial(attend_kernel, parts=len(k_parts), sourc...  4.77 us
    pallas_call x1, Pallas kernels, attend_last(): pl.pallas_call(functools.partial(last_kernel, last=last), out_shape=jax.S...  3.88 us
    pallas_call x1, Pallas kernels, prepare(): pl.pallas_call(functools.partial(prepare_kernel, kv_dev=kv_dev), out_shap...  1.58 us
  transfers between devices with their start and end apart: 14, of which 9 were waited for; matrix products, arithmetic and copies ran while one was open for 0% of the time, Pallas kernels for 19%

profile of v8, /device:TPU:20, one launch (start us, length us, event | category | flops | bytes accessed | tf_op | source)
XLA Modules:
  0.0 32.8 jit_solution(16368781288522071632)
XLA Ops:
  0.0 1.6 %collective-permute-start = (bf16[512,128]{1,0:T(8,128)(2,1)}, bf16[512,128]{1,0:T(8,128)(2,1)S(1)}, u32[]{:S(2)}, u32[]{:S(2)}) collective-permute-start(bf16[512,128]{1,0:T(8,128)(2,1)} %bitcast.6), channel_id=1, source_target_pairs={{0,4},{4,8},{8,12},{12,14},{14,10},{10,6},{6,2},{2,0},{1,5},{5,9},... | collective-permute-start | bytes 393224 | tf_op jit(solution)/shard_map/ppermute | solution.py:275
  1.6 0.4 %collective-permute-start.1 = (bf16[512,128]{1,0:T(8,128)(2,1)}, bf16[512,128]{1,0:T(8,128)(2,1)S(1)}, u32[]{:S(2)}, u32[]{:S(2)}) collective-permute-start(bf16[512,128]{1,0:T(8,128)(2,1)} %bitcast.3), channel_id=1, source_target_pairs={{0,2},{4,0},{8,4},{12,8},{14,12},{10,14},{6,10},{2,6},{1,3},{5,1},... | collective-permute-start | bytes 393224 | tf_op jit(solution)/shard_map/ppermute | solution.py:275
  2.0 1.6 %collective-permute-start.2 = (bf16[512,128]{1,0:T(8,128)(2,1)}, bf16[512,128]{1,0:T(8,128)(2,1)S(1)}, u32[]{:S(2)}, u32[]{:S(2)}) collective-permute-start(bf16[512,128]{1,0:T(8,128)(2,1)} %bitcast.4), channel_id=1, source_target_pairs={{0,4},{4,8},{8,12},{12,14},{14,10},{10,6},{6,2},{2,0},{1,5},{5,9},... | collective-permute-start | bytes 393224 | tf_op jit(solution)/shard_map/ppermute | solution.py:275
  3.6 0.4 %collective-permute-start.3 = (bf16[512,128]{1,0:T(8,128)(2,1)}, bf16[512,128]{1,0:T(8,128)(2,1)S(1)}, u32[]{:S(2)}, u32[]{:S(2)}) collective-permute-start(bf16[512,128]{1,0:T(8,128)(2,1)} %bitcast.7), channel_id=1, source_target_pairs={{0,2},{4,0},{8,4},{12,8},{14,12},{10,14},{6,10},{2,6},{1,3},{5,1},... | collective-permute-start | bytes 393224 | tf_op jit(solution)/shard_map/ppermute | solution.py:275
  4.1 1.6 %prepare.1 = (s32[4,8]{1,0:T(4,128)S(1)}, bf16[4,1024,128]{2,1,0:T(8,128)(2,1)S(1)}, bf16[4,128,128]{2,1,0:T(8,128)(2,1)S(1)}, bf16[4,128,128]{2,1,0:T(8,128)(2,1)S(1)}) custom-call(s32[4,8]{1,0:T(4,128)} %bitcast.9, bf16[128,32,128]{2,1,0:T(8,128)(2,1)} %q_hbm.1, bf16[512,128]{1,0:T(8,128)(2,1)} %bitcast.8, bf16[512,128]{1,0:T(8,128)(2,1)} %bitcast.5), custom_call_target="tpu_custom_call" | custom-call | tf_op jit(solution)/shard_map/prepare/pallas_call | solution.py:55
  5.6 1.0 %collective-permute-done.refs_0_ = bf16[512,128]{1,0:T(8,128)(2,1)S(1)} collective-permute-done((bf16[512,128]{1,0:T(8,128)(2,1)}, bf16[512,128]{1,0:T(8,128)(2,1)S(1)}, u32[]{:S(2)}, u32[]{:S(2)}) %collective-permute-start) | collective-permute-done | bytes 131104 | tf_op jit(solution)/shard_map/ppermute | solution.py:275
  6.6 1.5 %collective-permute-done.1.refs_7_ = bf16[512,128]{1,0:T(8,128)(2,1)S(1)} collective-permute-done((bf16[512,128]{1,0:T(8,128)(2,1)}, bf16[512,128]{1,0:T(8,128)(2,1)S(1)}, u32[]{:S(2)}, u32[]{:S(2)}) %collective-permute-start.1) | collective-permute-done | bytes 131104 | tf_op jit(solution)/shard_map/ppermute | solution.py:275
  8.1 1.5 %collective-permute-start.4 = (bf16[512,128]{1,0:T(8,128)(2,1)S(1)}, bf16[512,128]{1,0:T(8,128)(2,1)S(1)}, u32[]{:S(2)}, u32[]{:S(2)}) collective-permute-start(bf16[512,128]{1,0:T(8,128)(2,1)S(1)} %collective-permute-done.refs_0_), channel_id=1, source_target_pairs={{0,4},{4,8},{8,12},{12,14},{14,10},{10,6},{6,2},{2,0},{1,5},{5,9},... | collective-permute-start | bytes 393224 | tf_op jit(solution)/shard_map/ppermute | solution.py:275
  9.6 0.5 %collective-permute-start.5 = (bf16[512,128]{1,0:T(8,128)(2,1)S(1)}, bf16[512,128]{1,0:T(8,128)(2,1)S(1)}, u32[]{:S(2)}, u32[]{:S(2)}) collective-permute-start(bf16[512,128]{1,0:T(8,128)(2,1)S(1)} %collective-permute-done.1.refs_7_), channel_id=1, source_target_pairs={{0,2},{4,0},{8,4},{12,8},{14,12},{10,14},{6,10},{2,6},{1,3},{5,1},... | collective-permute-start | bytes 393224 | tf_op jit(solution)/shard_map/ppermute | solution.py:275
  10.1 0.0 collective-permute-done.2.refs_6_
  10.1 0.0 collective-permute-done.3.refs_1_
  10.1 2.1 %collective-permute-start.6 = (bf16[512,128]{1,0:T(8,128)(2,1)S(1)}, bf16[512,128]{1,0:T(8,128)(2,1)S(1)}, u32[]{:S(2)}, u32[]{:S(2)}) collective-permute-start(bf16[512,128]{1,0:T(8,128)(2,1)S(1)} %collective-permute-done.2.refs_6_), channel_id=1, source_target_pairs={{0,4},{4,8},{8,12},{12,14},{14,10},{10,6},{6,2},{2,0},{1,5},{5,9},... | collective-permute-start | bytes 393224 | tf_op jit(solution)/shard_map/ppermute | solution.py:275
  12.2 0.0 collective-permute-start.7
  12.2 1.8 %collective-permute-done.4.refs_2_ = bf16[512,128]{1,0:T(8,128)(2,1)S(1)} collective-permute-done((bf16[512,128]{1,0:T(8,128)(2,1)S(1)}, bf16[512,128]{1,0:T(8,128)(2,1)S(1)}, u32[]{:S(2)}, u32[]{:S(2)}) %collective-permute-start.4) | collective-permute-done | bytes 131104 | tf_op jit(solution)/shard_map/ppermute | solution.py:275
  14.0 1.1 %collective-permute-done.5.refs_9_ = bf16[512,128]{1,0:T(8,128)(2,1)S(1)} collective-permute-done((bf16[512,128]{1,0:T(8,128)(2,1)S(1)}, bf16[512,128]{1,0:T(8,128)(2,1)S(1)}, u32[]{:S(2)}, u32[]{:S(2)}) %collective-permute-start.5) | collective-permute-done | bytes 131104 | tf_op jit(solution)/shard_map/ppermute | solution.py:275
  15.1 0.5 %collective-permute-start.8 = (bf16[512,128]{1,0:T(8,128)(2,1)S(1)}, bf16[512,128]{1,0:T(8,128)(2,1)S(1)}, u32[]{:S(2)}, u32[]{:S(2)}) collective-permute-start(bf16[512,128]{1,0:T(8,128)(2,1)S(1)} %collective-permute-done.4.refs_2_), channel_id=1, source_target_pairs={{0,4},{4,8},{8,12},{12,14},{14,10},{10,6},{6,2},{2,0},{1,5},{5,9},... | collective-permute-start | bytes 393224 | tf_op jit(solution)/shard_map/ppermute | solution.py:275
  15.6 1.5 %collective-permute-start.9 = (bf16[512,128]{1,0:T(8,128)(2,1)S(1)}, bf16[512,128]{1,0:T(8,128)(2,1)S(1)}, u32[]{:S(2)}, u32[]{:S(2)}) collective-permute-start(bf16[512,128]{1,0:T(8,128)(2,1)S(1)} %collective-permute-done.5.refs_9_), channel_id=1, source_target_pairs={{0,2},{4,0},{8,4},{12,8},{14,12},{10,14},{6,10},{2,6},{1,3},{5,1},... | collective-permute-start | bytes 393224 | tf_op jit(solution)/shard_map/ppermute | solution.py:275
  17.2 0.0 collective-permute-done.6.refs_8_
  17.2 1.4 %collective-permute-done.7.refs_3_ = bf16[512,128]{1,0:T(8,128)(2,1)S(1)} collective-permute-done((bf16[512,128]{1,0:T(8,128)(2,1)S(1)}, bf16[512,128]{1,0:T(8,128)(2,1)S(1)}, u32[]{:S(2)}, u32[]{:S(2)}) %collective-permute-start.7) | collective-permute-done | bytes 131104 | tf_op jit(solution)/shard_map/ppermute | solution.py:275
  18.5 0.4 %collective-permute-start.10 = (bf16[512,128]{1,0:T(8,128)(2,1)S(1)}, bf16[512,128]{1,0:T(8,128)(2,1)S(1)}, u32[]{:S(2)}, u32[]{:S(2)}) collective-permute-start(bf16[512,128]{1,0:T(8,128)(2,1)S(1)} %collective-permute-done.6.refs_8_), channel_id=1, source_target_pairs={{0,4},{4,8},{8,12},{12,14},{14,10},{10,6},{6,2},{2,0},{1,5},{5,9},... | collective-permute-start | bytes 393224 | tf_op jit(solution)/shard_map/ppermute | solution.py:275
  19.0 1.6 %collective-permute-start.11 = (bf16[512,128]{1,0:T(8,128)(2,1)S(1)}, bf16[512,128]{1,0:T(8,128)(2,1)S(1)}, u32[]{:S(2)}, u32[]{:S(2)}) collective-permute-start(bf16[512,128]{1,0:T(8,128)(2,1)S(1)} %collective-permute-done.7.refs_3_), channel_id=1, source_target_pairs={{0,2},{4,0},{8,4},{12,8},{14,12},{10,14},{6,10},{2,6},{1,3},{5,1},... | collective-permute-start | bytes 393224 | tf_op jit(solution)/shard_map/ppermute | solution.py:275
  20.6 0.1 collective-permute-done.8.refs_4_
  20.7 0.7 %collective-permute-done.9.refs_11_ = bf16[512,128]{1,0:T(8,128)(2,1)S(1)} collective-permute-done((bf16[512,128]{1,0:T(8,128)(2,1)S(1)}, bf16[512,128]{1,0:T(8,128)(2,1)S(1)}, u32[]{:S(2)}, u32[]{:S(2)}) %collective-permute-start.9) | collective-permute-done | bytes 131104 | tf_op jit(solution)/shard_map/ppermute | solution.py:275
  21.4 0.4 %collective-permute-start.12 = (bf16[512,128]{1,0:T(8,128)(2,1)S(1)}, bf16[512,128]{1,0:T(8,128)(2,1)S(1)}, u32[]{:S(2)}, u32[]{:S(2)}) collective-permute-start(bf16[512,128]{1,0:T(8,128)(2,1)S(1)} %collective-permute-done.8.refs_4_), channel_id=1, source_target_pairs={{0,4},{4,8},{8,12},{12,14},{14,10},{10,6},{6,2},{2,0},{1,5},{5,9},... | collective-permute-start | bytes 393224 | tf_op jit(solution)/shard_map/ppermute | solution.py:275
  21.8 1.6 %collective-permute-start.13 = (bf16[512,128]{1,0:T(8,128)(2,1)S(1)}, bf16[512,128]{1,0:T(8,128)(2,1)S(1)}, u32[]{:S(2)}, u32[]{:S(2)}) collective-permute-start(bf16[512,128]{1,0:T(8,128)(2,1)S(1)} %collective-permute-done.9.refs_11_), channel_id=1, source_target_pairs={{0,2},{4,0},{8,4},{12,8},{14,12},{10,14},{6,10},{2,6},{1,3},{5,1},... | collective-permute-start | bytes 393224 | tf_op jit(solution)/shard_map/ppermute | solution.py:275
  23.4 0.1 collective-permute-done.10.refs_10_
  23.5 0.4 %collective-permute-done.11.refs_5_ = bf16[512,128]{1,0:T(8,128)(2,1)S(1)} collective-permute-done((bf16[512,128]{1,0:T(8,128)(2,1)S(1)}, bf16[512,128]{1,0:T(8,128)(2,1)S(1)}, u32[]{:S(2)}, u32[]{:S(2)}) %collective-permute-start.11) | collective-permute-done | bytes 131104 | tf_op jit(solution)/shard_map/ppermute | solution.py:275
  24.0 4.8 %attend.1 = (bf16[128,32,128]{2,1,0:T(8,128)(2,1)}, f32[4,1024,128]{2,1,0:T(8,128)S(1)}, f32[4,1024,256]{2,1,0:T(8,128)S(1)}) custom-call(s32[4,8]{1,0:T(4,128)S(1)} %get-tuple-element.34.lists_ref, bf16[4,1024,128]{2,1,0:T(8,128)(2,1)S(1)} %get-tuple-element.35.q_ref, bf16[4,128,128]{2,1,0:T(8,128)(2,1)S(1)} %get-tuple-element.36.k_own_ref, ...), custom_call_target="tpu_custom_call" | custom-call | tf_op jit(solution)/shard_map/attend/pallas_call | solution.py:189
  28.7 0.0 collective-permute-done.12.k_ref
  28.7 0.0 collective-permute-done.13.v_ref
  28.8 3.9 %attend_last.1 = bf16[128,32,128]{2,1,0:T(8,128)(2,1)} custom-call(s32[4,8]{1,0:T(4,128)S(1)} %get-tuple-element.34.lists_ref, bf16[4,1024,128]{2,1,0:T(8,128)(2,1)S(1)} %get-tuple-element.35.q_ref, f32[4,1024,128]{2,1,0:T(8,128)S(1)} %get-tuple-element.52.top_ref, f32[4,1024,256]{2,1,0:T(8,128)S(1)} %get-tuple-element.53.both_ref, ...), custom_call_target="tpu_custom_call", output_to_operand_aliasing={{}: (6, {})} | custom-call | tf_op jit(solution)/shard_map/attend_last/pallas_call | solution.py:242
Async XLA Ops:
  0.0 6.6 %collective-permute-start = (bf16[512,128]{1,0:T(8,128)(2,1)}, bf16[512,128]{1,0:T(8,128)(2,1)S(1)}, u32[]{:S(2)}, u32[]{:S(2)}) collective-permute-start(bf16[512,128]{1,0:T(8,128)(2,1)} %bitcast.6), channel_id=1, source_target_pairs={{0,4},{4,8},{8,12},{12,14},{14,10},{10,6},{6,2},{2,0},{1,5},{5,9},... | collective-permute-start | bytes 393224 | tf_op jit(solution)/shard_map/ppermute | solution.py:275
  1.6 6.5 %collective-permute-start.1 = (bf16[512,128]{1,0:T(8,128)(2,1)}, bf16[512,128]{1,0:T(8,128)(2,1)S(1)}, u32[]{:S(2)}, u32[]{:S(2)}) collective-permute-start(bf16[512,128]{1,0:T(8,128)(2,1)} %bitcast.3), channel_id=1, source_target_pairs={{0,2},{4,0},{8,4},{12,8},{14,12},{10,14},{6,10},{2,6},{1,3},{5,1},... | collective-permute-start | bytes 393224 | tf_op jit(solution)/shard_map/ppermute | solution.py:275
  2.0 8.1 %collective-permute-start.2 = (bf16[512,128]{1,0:T(8,128)(2,1)}, bf16[512,128]{1,0:T(8,128)(2,1)S(1)}, u32[]{:S(2)}, u32[]{:S(2)}) collective-permute-start(bf16[512,128]{1,0:T(8,128)(2,1)} %bitcast.4), channel_id=1, source_target_pairs={{0,4},{4,8},{8,12},{12,14},{14,10},{10,6},{6,2},{2,0},{1,5},{5,9},... | collective-permute-start | bytes 393224 | tf_op jit(solution)/shard_map/ppermute | solution.py:275
  3.6 6.5 %collective-permute-start.3 = (bf16[512,128]{1,0:T(8,128)(2,1)}, bf16[512,128]{1,0:T(8,128)(2,1)S(1)}, u32[]{:S(2)}, u32[]{:S(2)}) collective-permute-start(bf16[512,128]{1,0:T(8,128)(2,1)} %bitcast.7), channel_id=1, source_target_pairs={{0,2},{4,0},{8,4},{12,8},{14,12},{10,14},{6,10},{2,6},{1,3},{5,1},... | collective-permute-start | bytes 393224 | tf_op jit(solution)/shard_map/ppermute | solution.py:275
  8.1 5.9 %collective-permute-start.4 = (bf16[512,128]{1,0:T(8,128)(2,1)S(1)}, bf16[512,128]{1,0:T(8,128)(2,1)S(1)}, u32[]{:S(2)}, u32[]{:S(2)}) collective-permute-start(bf16[512,128]{1,0:T(8,128)(2,1)S(1)} %collective-permute-done.refs_0_), channel_id=1, source_target_pairs={{0,4},{4,8},{8,12},{12,14},{14,10},{10,6},{6,2},{2,0},{1,5},{5,9},... | collective-permute-start | bytes 393224 | tf_op jit(solution)/shard_map/ppermute | solution.py:275
  9.6 5.5 %collective-permute-start.5 = (bf16[512,128]{1,0:T(8,128)(2,1)S(1)}, bf16[512,128]{1,0:T(8,128)(2,1)S(1)}, u32[]{:S(2)}, u32[]{:S(2)}) collective-permute-start(bf16[512,128]{1,0:T(8,128)(2,1)S(1)} %collective-permute-done.1.refs_7_), channel_id=1, source_target_pairs={{0,2},{4,0},{8,4},{12,8},{14,12},{10,14},{6,10},{2,6},{1,3},{5,1},... | collective-permute-start | bytes 393224 | tf_op jit(solution)/shard_map/ppermute | solution.py:275
  10.1 7.0 %collective-permute-start.6 = (bf16[512,128]{1,0:T(8,128)(2,1)S(1)}, bf16[512,128]{1,0:T(8,128)(2,1)S(1)}, u32[]{:S(2)}, u32[]{:S(2)}) collective-permute-start(bf16[512,128]{1,0:T(8,128)(2,1)S(1)} %collective-permute-done.2.refs_6_), channel_id=1, source_target_pairs={{0,4},{4,8},{8,12},{12,14},{14,10},{10,6},{6,2},{2,0},{1,5},{5,9},... | collective-permute-start | bytes 393224 | tf_op jit(solution)/shard_map/ppermute | solution.py:275
  12.2 6.3 %collective-permute-start.7 = (bf16[512,128]{1,0:T(8,128)(2,1)S(1)}, bf16[512,128]{1,0:T(8,128)(2,1)S(1)}, u32[]{:S(2)}, u32[]{:S(2)}) collective-permute-start(bf16[512,128]{1,0:T(8,128)(2,1)S(1)} %collective-permute-done.3.refs_1_), channel_id=1, source_target_pairs={{0,2},{4,0},{8,4},{12,8},{14,12},{10,14},{6,10},{2,6},{1,3},{5,1},... | collective-permute-start | bytes 393224 | tf_op jit(solution)/shard_map/ppermute | solution.py:275
  15.1 5.5 %collective-permute-start.8 = (bf16[512,128]{1,0:T(8,128)(2,1)S(1)}, bf16[512,128]{1,0:T(8,128)(2,1)S(1)}, u32[]{:S(2)}, u32[]{:S(2)}) collective-permute-start(bf16[512,128]{1,0:T(8,128)(2,1)S(1)} %collective-permute-done.4.refs_2_), channel_id=1, source_target_pairs={{0,4},{4,8},{8,12},{12,14},{14,10},{10,6},{6,2},{2,0},{1,5},{5,9},... | collective-permute-start | bytes 393224 | tf_op jit(solution)/shard_map/ppermute | solution.py:275
  15.6 5.7 %collective-permute-start.9 = (bf16[512,128]{1,0:T(8,128)(2,1)S(1)}, bf16[512,128]{1,0:T(8,128)(2,1)S(1)}, u32[]{:S(2)}, u32[]{:S(2)}) collective-permute-start(bf16[512,128]{1,0:T(8,128)(2,1)S(1)} %collective-permute-done.5.refs_9_), channel_id=1, source_target_pairs={{0,2},{4,0},{8,4},{12,8},{14,12},{10,14},{6,10},{2,6},{1,3},{5,1},... | collective-permute-start | bytes 393224 | tf_op jit(solution)/shard_map/ppermute | solution.py:275
  18.5 5.0 %collective-permute-start.10 = (bf16[512,128]{1,0:T(8,128)(2,1)S(1)}, bf16[512,128]{1,0:T(8,128)(2,1)S(1)}, u32[]{:S(2)}, u32[]{:S(2)}) collective-permute-start(bf16[512,128]{1,0:T(8,128)(2,1)S(1)} %collective-permute-done.6.refs_8_), channel_id=1, source_target_pairs={{0,4},{4,8},{8,12},{12,14},{14,10},{10,6},{6,2},{2,0},{1,5},{5,9},... | collective-permute-start | bytes 393224 | tf_op jit(solution)/shard_map/ppermute | solution.py:275
  19.0 5.0 %collective-permute-start.11 = (bf16[512,128]{1,0:T(8,128)(2,1)S(1)}, bf16[512,128]{1,0:T(8,128)(2,1)S(1)}, u32[]{:S(2)}, u32[]{:S(2)}) collective-permute-start(bf16[512,128]{1,0:T(8,128)(2,1)S(1)} %collective-permute-done.7.refs_3_), channel_id=1, source_target_pairs={{0,2},{4,0},{8,4},{12,8},{14,12},{10,14},{6,10},{2,6},{1,3},{5,1},... | collective-permute-start | bytes 393224 | tf_op jit(solution)/shard_map/ppermute | solution.py:275
  21.4 7.4 %collective-permute-start.12 = (bf16[512,128]{1,0:T(8,128)(2,1)S(1)}, bf16[512,128]{1,0:T(8,128)(2,1)S(1)}, u32[]{:S(2)}, u32[]{:S(2)}) collective-permute-start(bf16[512,128]{1,0:T(8,128)(2,1)S(1)} %collective-permute-done.8.refs_4_), channel_id=1, source_target_pairs={{0,4},{4,8},{8,12},{12,14},{14,10},{10,6},{6,2},{2,0},{1,5},{5,9},... | collective-permute-start | bytes 393224 | tf_op jit(solution)/shard_map/ppermute | solution.py:275
  21.8 7.0 %collective-permute-start.13 = (bf16[512,128]{1,0:T(8,128)(2,1)S(1)}, bf16[512,128]{1,0:T(8,128)(2,1)S(1)}, u32[]{:S(2)}, u32[]{:S(2)}) collective-permute-start(bf16[512,128]{1,0:T(8,128)(2,1)S(1)} %collective-permute-done.9.refs_11_), channel_id=1, source_target_pairs={{0,2},{4,0},{8,4},{12,8},{14,12},{10,14},{6,10},{2,6},{1,3},{5,1},... | collective-permute-start | bytes 393224 | tf_op jit(solution)/shard_map/ppermute | solution.py:275

commit v9 on v8

--- a/solution.py
+++ b/solution.py
@@ -11,7 +11,6 @@
 NO_KEY = -1e30
 ROW_CHUNK = 256
 MOST_ROUND = 16
-HEADS_OUT = 16
 
 
 def params():
@@ -88,6 +87,10 @@
     return jnp.concatenate([values, jnp.ones_like(values)], axis=1)
 
 
+def scores_of(q, keys):
+    return lax.dot_general(q, keys, (((1,), (1,)), ((), ())), preferred_element_type=jnp.float32)
+
+
 def put_out(out_ref, h, first, both, group):
     rows, dim = both.shape[0], both.shape[1] // 2
     merged = (both[:, :dim] / both[:, dim:]).reshape(rows // group, group, dim)
@@ -95,21 +98,29 @@
     out_ref[tokens, pl.ds(h * group, group), :] = merged.astype(jnp.bfloat16)
 
 
-def send_out(out_ref, out_hbm, sems, h, group):
-    done = (h + 1) * group
-    if done % HEADS_OUT:
-        return []
-    heads = pl.ds(done - HEADS_OUT, HEADS_OUT)
-    copy = pltpu.make_async_copy(
-        out_ref.at[:, heads, :], out_hbm.at[:, heads, :], sems.at[done // HEADS_OUT - 1]
-    )
-    copy.start()
-    return [copy]
+def over_rows(rows_all, body, out_ref, out_hbm, sems, sends):
+    chunks = rows_all // ROW_CHUNK
+    tokens = out_ref.shape[0] // chunks
+
+    def copy(n):
+        here = pl.ds(pl.multiple_of(n * tokens, tokens), tokens)
+        return pltpu.make_async_copy(out_ref.at[here], out_hbm.at[here], sems.at[n])
+
+    def step(n, carry):
+        body(pl.multiple_of(n * ROW_CHUNK, ROW_CHUNK))
+        if sends:
+            copy(n).start()
+        return carry
+
+    lax.fori_loop(0, chunks, step, 0)
+    if sends:
+        for n in range(chunks):
+            copy(n).wait()
 
 
 def attend_kernel(lists_ref, q_ref, k_own_ref, v_own_ref, *refs, parts, sources, last):
     k_parts, v_parts = refs[:parts], refs[parts : 2 * parts]
-    out_hbm, *state, k_wide, v_wide, out_ref, sems = refs[2 * parts :]
+    out_hbm, *state, k_wide, v_wide, k_ready, v_ready, out_ref, sems = refs[2 * parts :]
     kv_dev, tokens, dim = k_own_ref.shape
     rows_all = q_ref.shape[1]
     group = rows_all // tokens
@@ -131,37 +142,36 @@
         count += take.astype(jnp.int32)
 
     def run(others, final):
-        copies = []
+        keys = (others + 1) * tokens
         for h in range(kv_dev):
             k_h, v_h = k_own_ref[h], v_own_ref[h]
             if others:
-                keys = others * tokens
-                k_h = jnp.concatenate([k_h, by_head(k_wide, h, kv_dev, keys)], axis=0)
-                v_h = jnp.concatenate([v_h, by_head(v_wide, h, kv_dev, keys)], axis=0)
-            v_h = with_ones(v_h)
-            for first in range(0, rows_all, ROW_CHUNK):
-                rows = pl.ds(first, ROW_CHUNK)
-                s = lax.dot_general(
-                    q_ref[h, rows, :], k_h, (((1,), (1,)), ((), ())), preferred_element_type=jnp.float32
-                )
-                row = (lax.broadcasted_iota(jnp.int32, (ROW_CHUNK, tokens), 0) + first) // group
-                key = lax.broadcasted_iota(jnp.int32, (ROW_CHUNK, tokens), 1)
+                k_h = jnp.concatenate([k_h, by_head(k_wide, h, kv_dev, others * tokens)], axis=0)
+                v_h = jnp.concatenate([v_h, by_head(v_wide, h, kv_dev, others * tokens)], axis=0)
+            k_ready[h, pl.ds(0, keys), :] = k_h
+            v_ready[h, pl.ds(0, keys), :] = with_ones(v_h)
+
+        def rows_from(first):
+            rows = pl.ds(first, ROW_CHUNK)
+            row = (lax.broadcasted_iota(jnp.int32, (ROW_CHUNK, tokens), 0) + first) // group
+            key = lax.broadcasted_iota(jnp.int32, (ROW_CHUNK, tokens), 1)
+            for h in range(kv_dev):
+                s = scores_of(q_ref[h, rows, :], k_ready[h, pl.ds(0, keys), :])
                 scores = [jnp.where(key <= row, s[:, :tokens], NO_KEY)]
                 scores += [s[:, (j + 1) * tokens : (j + 2) * tokens] for j in range(others)]
                 top = jnp.max(functools.reduce(jnp.maximum, scores), axis=1, keepdims=True)
                 probs = [jnp.exp2((score - top) * factor).astype(jnp.bfloat16) for score in scores]
+                probs = jnp.concatenate(probs, axis=1)
                 both = jnp.dot(
-                    jnp.concatenate(probs, axis=1), v_h, preferred_element_type=jnp.float32
+                    probs, v_ready[h, pl.ds(0, keys), :], preferred_element_type=jnp.float32
                 )
                 if final:
                     put_out(out_ref, h, first, both, group)
                 else:
                     state[0][h, rows, :] = jnp.broadcast_to(top, (ROW_CHUNK, dim))
                     state[1][h, rows, :] = both
-            if final:
-                copies += send_out(out_ref, out_hbm, sems, h, group)
-        for copy in copies:
-            copy.wait()
+
+        over_rows(rows_all, rows_from, out_ref, out_hbm, sems, final)
 
     unfinished = False if last is None else is_listed(lists_ref, target, last(target))
     for others in range(most + 1):
@@ -180,7 +190,8 @@
 def attend(lists, queries, k_own, v_own, k_parts, v_parts, sources, last):
     kv_dev, rows, dim = queries.shape
     tokens = k_own.shape[1]
-    rest = (lists.shape[0] - 1) * tokens * kv_dev
+    slots = lists.shape[0]
+    rest = (slots - 1) * tokens * kv_dev
     out = jax.ShapeDtypeStruct((tokens, rows * kv_dev // tokens, dim), jnp.bfloat16)
     state = [] if last is None else [
         jax.ShapeDtypeStruct((kv_dev, rows, wide), jnp.float32) for wide in (dim, 2 * dim)
@@ -194,8 +205,10 @@
         scratch_shapes=[
             pltpu.VMEM((rest, dim), jnp.float32),
             pltpu.VMEM((rest, dim), jnp.float32),
+            pltpu.VMEM((kv_dev, slots * tokens, dim), jnp.bfloat16),
+            pltpu.VMEM((kv_dev, slots * tokens, 2 * dim), jnp.bfloat16),
             pltpu.VMEM(out.shape, jnp.bfloat16),
-            pltpu.SemaphoreType.DMA((out.shape[1] // HEADS_OUT,)),
+            pltpu.SemaphoreType.DMA((rows // ROW_CHUNK,)),
         ],
         compiler_params=params(),
         name="attend",
@@ -203,7 +216,8 @@
 
 
 def last_kernel(
-    lists_ref, q_ref, top_ref, both_ref, k_ref, v_ref, _, out_hbm, k_wide, v_wide, out_ref, sems, *, last
+    lists_ref, q_ref, top_ref, both_ref, k_ref, v_ref, _, out_hbm,
+    k_wide, v_wide, k_ready, v_ready, out_ref, sems, *, last,
 ):
     kv_dev, rows_all, dim = q_ref.shape
     tokens = k_ref.shape[0] // kv_dev
@@ -211,33 +225,32 @@
     factor = dim ** (-0.5) * math.log2(math.e)
     target = lax.axis_index("seq").astype(jnp.int32)
 
+    def rows_from(first):
+        rows = pl.ds(first, ROW_CHUNK)
+        for h in range(kv_dev):
+            s = scores_of(q_ref[h, rows, :], k_ready[h])
+            before = top_ref[h, rows, :]
+            top = jnp.maximum(before, jnp.max(s, axis=1, keepdims=True))
+            probs = jnp.exp2((s - top) * factor).astype(jnp.bfloat16)
+            shrink = jnp.exp2((before - top) * factor)
+            both = jnp.dot(probs, v_ready[h], preferred_element_type=jnp.float32)
+            both += both_ref[h, rows, :] * jnp.concatenate([shrink, shrink], axis=1)
+            put_out(out_ref, h, first, both, group)
+
     @pl.when(is_listed(lists_ref, target, last(target)))
     def _add():
         k_wide[...] = k_ref[...].astype(jnp.float32)
         v_wide[...] = v_ref[...].astype(jnp.float32)
-        copies = []
         for h in range(kv_dev):
-            k_h = by_head(k_wide, h, kv_dev, tokens)
-            v_h = with_ones(by_head(v_wide, h, kv_dev, tokens))
-            for first in range(0, rows_all, ROW_CHUNK):
-                rows = pl.ds(first, ROW_CHUNK)
-                s = lax.dot_general(
-                    q_ref[h, rows, :], k_h, (((1,), (1,)), ((), ())), preferred_element_type=jnp.float32
-                )
-                before = top_ref[h, rows, :]
-                top = jnp.maximum(before, jnp.max(s, axis=1, keepdims=True))
-                probs = jnp.exp2((s - top) * factor).astype(jnp.bfloat16)
-                shrink = jnp.exp2((before - top) * factor)
-                both = jnp.dot(probs, v_h, preferred_element_type=jnp.float32)
-                both += both_ref[h, rows, :] * jnp.concatenate([shrink, shrink], axis=1)
-                put_out(out_ref, h, first, both, group)
-            copies += send_out(out_ref, out_hbm, sems, h, group)
-        for copy in copies:
-            copy.wait()
+            k_ready[h] = by_head(k_wide, h, kv_dev, tokens)
+            v_ready[h] = with_ones(by_head(v_wide, h, kv_dev, tokens))
+        over_rows(rows_all, rows_from, out_ref, out_hbm, sems, True)
 
 
 def attend_last(lists, queries, state, k_last, v_last, out, last):
     top, both = state
+    kv_dev, rows, dim = queries.shape
+    tokens = out.shape[0]
     hbm, smem = (pl.BlockSpec(memory_space=space) for space in (pltpu.HBM, pltpu.SMEM))
     return pl.pallas_call(
         functools.partial(last_kernel, last=last),
@@ -248,8 +261,10 @@
         scratch_shapes=[
             pltpu.VMEM(k_last.shape, jnp.float32),
             pltpu.VMEM(k_last.shape, jnp.float32),
+            pltpu.VMEM((kv_dev, tokens, dim), jnp.bfloat16),
+            pltpu.VMEM((kv_dev, tokens, 2 * dim), jnp.bfloat16),
             pltpu.VMEM(out.shape, jnp.bfloat16),
-            pltpu.SemaphoreType.DMA((out.shape[1] // HEADS_OUT,)),
+            pltpu.SemaphoreType.DMA((rows // ROW_CHUNK,)),
         ],
         compiler_params=params(),
         name="attend_last",

time: 32.9 us -> 33.9 us (1.030)
  Pallas kernels: 10.2 us -> 11.4 us
    pallas_call x1, Pallas kernels: 3.88 us -> 4.52 us  [attend_last(): pl.pallas_call(functools.partial(last_kernel, last=last), out_shape=jax.S...]
    pallas_call x1, Pallas kernels: 4.77 us -> 5.28 us  [attend(): pl.pallas_call(functools.partial(attend_kernel, parts=len(k_parts), sourc...]
  transfers between devices with their start and end apart: 14 -> 14, of which waited for: 9 -> 9; matrix products, arithmetic and copies ran while one was open for 0% -> 0% of each run, Pallas kernels for 19% -> 20%
where the time goes in v9:
time: 33.9 us; the launch traced here: 33.8 us
  starting transfers between devices  14.3 us (42%)
  Pallas kernels  11.4 us (34%)
  waiting for transfers between devices  8.11 us (24%)
    ppermute x14, starting transfers between devices, send(): return lax.ppermute(x, 'seq', ways[way])  14.3 us
    ppermute x14, waiting for transfers between devices, send(): return lax.ppermute(x, 'seq', ways[way])  8.11 us
    pallas_call x1, Pallas kernels, attend(): pl.pallas_call(functools.partial(attend_kernel, parts=len(k_parts), sourc...  5.28 us
    pallas_call x1, Pallas kernels, attend_last(): pl.pallas_call(functools.partial(last_kernel, last=last), out_shape=jax.S...  4.52 us
    pallas_call x1, Pallas kernels, prepare(): pl.pallas_call(functools.partial(prepare_kernel, kv_dev=kv_dev), out_shap...  1.58 us
  transfers between devices with their start and end apart: 14, of which 9 were waited for; matrix products, arithmetic and copies ran while one was open for 0% of the time, Pallas kernels for 20%

profile of v9, /device:TPU:20, one launch (start us, length us, event | category | flops | bytes accessed | tf_op | source)
XLA Modules:
  0.0 33.8 jit_solution(2240999493447688750)
XLA Ops:
  0.0 1.6 %collective-permute-start = (bf16[512,128]{1,0:T(8,128)(2,1)}, bf16[512,128]{1,0:T(8,128)(2,1)S(1)}, u32[]{:S(2)}, u32[]{:S(2)}) collective-permute-start(bf16[512,128]{1,0:T(8,128)(2,1)} %bitcast.6), channel_id=1, source_target_pairs={{0,4},{4,8},{8,12},{12,14},{14,10},{10,6},{6,2},{2,0},{1,5},{5,9},... | collective-permute-start | bytes 393224 | tf_op jit(solution)/shard_map/ppermute | solution.py:290
  1.6 0.4 %collective-permute-start.1 = (bf16[512,128]{1,0:T(8,128)(2,1)}, bf16[512,128]{1,0:T(8,128)(2,1)S(1)}, u32[]{:S(2)}, u32[]{:S(2)}) collective-permute-start(bf16[512,128]{1,0:T(8,128)(2,1)} %bitcast.3), channel_id=1, source_target_pairs={{0,2},{4,0},{8,4},{12,8},{14,12},{10,14},{6,10},{2,6},{1,3},{5,1},... | collective-permute-start | bytes 393224 | tf_op jit(solution)/shard_map/ppermute | solution.py:290
  2.0 1.6 %collective-permute-start.2 = (bf16[512,128]{1,0:T(8,128)(2,1)}, bf16[512,128]{1,0:T(8,128)(2,1)S(1)}, u32[]{:S(2)}, u32[]{:S(2)}) collective-permute-start(bf16[512,128]{1,0:T(8,128)(2,1)} %bitcast.4), channel_id=1, source_target_pairs={{0,4},{4,8},{8,12},{12,14},{14,10},{10,6},{6,2},{2,0},{1,5},{5,9},... | collective-permute-start | bytes 393224 | tf_op jit(solution)/shard_map/ppermute | solution.py:290
  3.6 0.4 %collective-permute-start.3 = (bf16[512,128]{1,0:T(8,128)(2,1)}, bf16[512,128]{1,0:T(8,128)(2,1)S(1)}, u32[]{:S(2)}, u32[]{:S(2)}) collective-permute-start(bf16[512,128]{1,0:T(8,128)(2,1)} %bitcast.7), channel_id=1, source_target_pairs={{0,2},{4,0},{8,4},{12,8},{14,12},{10,14},{6,10},{2,6},{1,3},{5,1},... | collective-permute-start | bytes 393224 | tf_op jit(solution)/shard_map/ppermute | solution.py:290
  4.1 1.6 %prepare.1 = (s32[4,8]{1,0:T(4,128)S(1)}, bf16[4,1024,128]{2,1,0:T(8,128)(2,1)S(1)}, bf16[4,128,128]{2,1,0:T(8,128)(2,1)S(1)}, bf16[4,128,128]{2,1,0:T(8,128)(2,1)S(1)}) custom-call(s32[4,8]{1,0:T(4,128)} %bitcast.9, bf16[128,32,128]{2,1,0:T(8,128)(2,1)} %q_hbm.1, bf16[512,128]{1,0:T(8,128)(2,1)} %bitcast.8, bf16[512,128]{1,0:T(8,128)(2,1)} %bitcast.5), custom_call_target="tpu_custom_call" | custom-call | tf_op jit(solution)/shard_map/prepare/pallas_call | solution.py:54
  5.6 1.0 %collective-permute-done.refs_0_ = bf16[512,128]{1,0:T(8,128)(2,1)S(1)} collective-permute-done((bf16[512,128]{1,0:T(8,128)(2,1)}, bf16[512,128]{1,0:T(8,128)(2,1)S(1)}, u32[]{:S(2)}, u32[]{:S(2)}) %collective-permute-start) | collective-permute-done | bytes 131104 | tf_op jit(solution)/shard_map/ppermute | solution.py:290
  6.6 1.5 %collective-permute-done.1.refs_7_ = bf16[512,128]{1,0:T(8,128)(2,1)S(1)} collective-permute-done((bf16[512,128]{1,0:T(8,128)(2,1)}, bf16[512,128]{1,0:T(8,128)(2,1)S(1)}, u32[]{:S(2)}, u32[]{:S(2)}) %collective-permute-start.1) | collective-permute-done | bytes 131104 | tf_op jit(solution)/shard_map/ppermute | solution.py:290
  8.1 1.5 %collective-permute-start.4 = (bf16[512,128]{1,0:T(8,128)(2,1)S(1)}, bf16[512,128]{1,0:T(8,128)(2,1)S(1)}, u32[]{:S(2)}, u32[]{:S(2)}) collective-permute-start(bf16[512,128]{1,0:T(8,128)(2,1)S(1)} %collective-permute-done.refs_0_), channel_id=1, source_target_pairs={{0,4},{4,8},{8,12},{12,14},{14,10},{10,6},{6,2},{2,0},{1,5},{5,9},... | collective-permute-start | bytes 393224 | tf_op jit(solution)/shard_map/ppermute | solution.py:290
  9.6 0.5 %collective-permute-start.5 = (bf16[512,128]{1,0:T(8,128)(2,1)S(1)}, bf16[512,128]{1,0:T(8,128)(2,1)S(1)}, u32[]{:S(2)}, u32[]{:S(2)}) collective-permute-start(bf16[512,128]{1,0:T(8,128)(2,1)S(1)} %collective-permute-done.1.refs_7_), channel_id=1, source_target_pairs={{0,2},{4,0},{8,4},{12,8},{14,12},{10,14},{6,10},{2,6},{1,3},{5,1},... | collective-permute-start | bytes 393224 | tf_op jit(solution)/shard_map/ppermute | solution.py:290
  10.1 0.0 collective-permute-done.2.refs_6_
  10.1 0.0 collective-permute-done.3.refs_1_
  10.1 2.1 %collective-permute-start.6 = (bf16[512,128]{1,0:T(8,128)(2,1)S(1)}, bf16[512,128]{1,0:T(8,128)(2,1)S(1)}, u32[]{:S(2)}, u32[]{:S(2)}) collective-permute-start(bf16[512,128]{1,0:T(8,128)(2,1)S(1)} %collective-permute-done.2.refs_6_), channel_id=1, source_target_pairs={{0,4},{4,8},{8,12},{12,14},{14,10},{10,6},{6,2},{2,0},{1,5},{5,9},... | collective-permute-start | bytes 393224 | tf_op jit(solution)/shard_map/ppermute | solution.py:290
  12.2 0.0 collective-permute-start.7
  12.2 1.8 %collective-permute-done.4.refs_2_ = bf16[512,128]{1,0:T(8,128)(2,1)S(1)} collective-permute-done((bf16[512,128]{1,0:T(8,128)(2,1)S(1)}, bf16[512,128]{1,0:T(8,128)(2,1)S(1)}, u32[]{:S(2)}, u32[]{:S(2)}) %collective-permute-start.4) | collective-permute-done | bytes 131104 | tf_op jit(solution)/shard_map/ppermute | solution.py:290
  14.0 1.1 %collective-permute-done.5.refs_9_ = bf16[512,128]{1,0:T(8,128)(2,1)S(1)} collective-permute-done((bf16[512,128]{1,0:T(8,128)(2,1)S(1)}, bf16[512,128]{1,0:T(8,128)(2,1)S(1)}, u32[]{:S(2)}, u32[]{:S(2)}) %collective-permute-start.5) | collective-permute-done | bytes 131104 | tf_op jit(solution)/shard_map/ppermute | solution.py:290
  15.1 0.5 %collective-permute-start.8 = (bf16[512,128]{1,0:T(8,128)(2,1)S(1)}, bf16[512,128]{1,0:T(8,128)(2,1)S(1)}, u32[]{:S(2)}, u32[]{:S(2)}) collective-permute-start(bf16[512,128]{1,0:T(8,128)(2,1)S(1)} %collective-permute-done.4.refs_2_), channel_id=1, source_target_pairs={{0,4},{4,8},{8,12},{12,14},{14,10},{10,6},{6,2},{2,0},{1,5},{5,9},... | collective-permute-start | bytes 393224 | tf_op jit(solution)/shard_map/ppermute | solution.py:290
  15.6 1.5 %collective-permute-start.9 = (bf16[512,128]{1,0:T(8,128)(2,1)S(1)}, bf16[512,128]{1,0:T(8,128)(2,1)S(1)}, u32[]{:S(2)}, u32[]{:S(2)}) collective-permute-start(bf16[512,128]{1,0:T(8,128)(2,1)S(1)} %collective-permute-done.5.refs_9_), channel_id=1, source_target_pairs={{0,2},{4,0},{8,4},{12,8},{14,12},{10,14},{6,10},{2,6},{1,3},{5,1},... | collective-permute-start | bytes 393224 | tf_op jit(solution)/shard_map/ppermute | solution.py:290
  17.2 0.0 collective-permute-done.6.refs_8_
  17.2 1.4 %collective-permute-done.7.refs_3_ = bf16[512,128]{1,0:T(8,128)(2,1)S(1)} collective-permute-done((bf16[512,128]{1,0:T(8,128)(2,1)S(1)}, bf16[512,128]{1,0:T(8,128)(2,1)S(1)}, u32[]{:S(2)}, u32[]{:S(2)}) %collective-permute-start.7) | collective-permute-done | bytes 131104 | tf_op jit(solution)/shard_map/ppermute | solution.py:290
  18.5 0.4 %collective-permute-start.10 = (bf16[512,128]{1,0:T(8,128)(2,1)S(1)}, bf16[512,128]{1,0:T(8,128)(2,1)S(1)}, u32[]{:S(2)}, u32[]{:S(2)}) collective-permute-start(bf16[512,128]{1,0:T(8,128)(2,1)S(1)} %collective-permute-done.6.refs_8_), channel_id=1, source_target_pairs={{0,4},{4,8},{8,12},{12,14},{14,10},{10,6},{6,2},{2,0},{1,5},{5,9},... | collective-permute-start | bytes 393224 | tf_op jit(solution)/shard_map/ppermute | solution.py:290
  19.0 1.6 %collective-permute-start.11 = (bf16[512,128]{1,0:T(8,128)(2,1)S(1)}, bf16[512,128]{1,0:T(8,128)(2,1)S(1)}, u32[]{:S(2)}, u32[]{:S(2)}) collective-permute-start(bf16[512,128]{1,0:T(8,128)(2,1)S(1)} %collective-permute-done.7.refs_3_), channel_id=1, source_target_pairs={{0,2},{4,0},{8,4},{12,8},{14,12},{10,14},{6,10},{2,6},{1,3},{5,1},... | collective-permute-start | bytes 393224 | tf_op jit(solution)/shard_map/ppermute | solution.py:290
  20.6 0.1 collective-permute-done.8.refs_4_
  20.7 0.7 %collective-permute-done.9.refs_11_ = bf16[512,128]{1,0:T(8,128)(2,1)S(1)} collective-permute-done((bf16[512,128]{1,0:T(8,128)(2,1)S(1)}, bf16[512,128]{1,0:T(8,128)(2,1)S(1)}, u32[]{:S(2)}, u32[]{:S(2)}) %collective-permute-start.9) | collective-permute-done | bytes 131104 | tf_op jit(solution)/shard_map/ppermute | solution.py:290
  21.4 0.4 %collective-permute-start.12 = (bf16[512,128]{1,0:T(8,128)(2,1)S(1)}, bf16[512,128]{1,0:T(8,128)(2,1)S(1)}, u32[]{:S(2)}, u32[]{:S(2)}) collective-permute-start(bf16[512,128]{1,0:T(8,128)(2,1)S(1)} %collective-permute-done.8.refs_4_), channel_id=1, source_target_pairs={{0,4},{4,8},{8,12},{12,14},{14,10},{10,6},{6,2},{2,0},{1,5},{5,9},... | collective-permute-start | bytes 393224 | tf_op jit(solution)/shard_map/ppermute | solution.py:290
  21.8 1.6 %collective-permute-start.13 = (bf16[512,128]{1,0:T(8,128)(2,1)S(1)}, bf16[512,128]{1,0:T(8,128)(2,1)S(1)}, u32[]{:S(2)}, u32[]{:S(2)}) collective-permute-start(bf16[512,128]{1,0:T(8,128)(2,1)S(1)} %collective-permute-done.9.refs_11_), channel_id=1, source_target_pairs={{0,2},{4,0},{8,4},{12,8},{14,12},{10,14},{6,10},{2,6},{1,3},{5,1},... | collective-permute-start | bytes 393224 | tf_op jit(solution)/shard_map/ppermute | solution.py:290
  23.4 0.1 collective-permute-done.10.refs_10_
  23.5 0.4 %collective-permute-done.11.refs_5_ = bf16[512,128]{1,0:T(8,128)(2,1)S(1)} collective-permute-done((bf16[512,128]{1,0:T(8,128)(2,1)S(1)}, bf16[512,128]{1,0:T(8,128)(2,1)S(1)}, u32[]{:S(2)}, u32[]{:S(2)}) %collective-permute-start.11) | collective-permute-done | bytes 131104 | tf_op jit(solution)/shard_map/ppermute | solution.py:290
  24.0 5.3 %attend.1 = (bf16[128,32,128]{2,1,0:T(8,128)(2,1)}, f32[4,1024,128]{2,1,0:T(8,128)S(1)}, f32[4,1024,256]{2,1,0:T(8,128)S(1)}) custom-call(s32[4,8]{1,0:T(4,128)S(1)} %get-tuple-element.34.lists_ref, bf16[4,1024,128]{2,1,0:T(8,128)(2,1)S(1)} %get-tuple-element.35.q_ref, bf16[4,128,128]{2,1,0:T(8,128)(2,1)S(1)} %get-tuple-element.36.k_own_ref, ...), custom_call_target="tpu_custom_call" | custom-call | tf_op jit(solution)/shard_map/attend/pallas_call | solution.py:200
  29.2 0.0 collective-permute-done.12.k_ref
  29.3 0.0 collective-permute-done.13.v_ref
  29.3 4.5 %attend_last.1 = bf16[128,32,128]{2,1,0:T(8,128)(2,1)} custom-call(s32[4,8]{1,0:T(4,128)S(1)} %get-tuple-element.34.lists_ref, bf16[4,1024,128]{2,1,0:T(8,128)(2,1)S(1)} %get-tuple-element.35.q_ref, f32[4,1024,128]{2,1,0:T(8,128)S(1)} %get-tuple-element.52.top_ref, f32[4,1024,256]{2,1,0:T(8,128)S(1)} %get-tuple-element.53.both_ref, ...), custom_call_target="tpu_custom_call", output_to_operand_aliasing={{}: (6, {})} | custom-call | tf_op jit(solution)/shard_map/attend_last/pallas_call | solution.py:255
Async XLA Ops:
  0.0 6.6 %collective-permute-start = (bf16[512,128]{1,0:T(8,128)(2,1)}, bf16[512,128]{1,0:T(8,128)(2,1)S(1)}, u32[]{:S(2)}, u32[]{:S(2)}) collective-permute-start(bf16[512,128]{1,0:T(8,128)(2,1)} %bitcast.6), channel_id=1, source_target_pairs={{0,4},{4,8},{8,12},{12,14},{14,10},{10,6},{6,2},{2,0},{1,5},{5,9},... | collective-permute-start | bytes 393224 | tf_op jit(solution)/shard_map/ppermute | solution.py:290
  1.6 6.5 %collective-permute-start.1 = (bf16[512,128]{1,0:T(8,128)(2,1)}, bf16[512,128]{1,0:T(8,128)(2,1)S(1)}, u32[]{:S(2)}, u32[]{:S(2)}) collective-permute-start(bf16[512,128]{1,0:T(8,128)(2,1)} %bitcast.3), channel_id=1, source_target_pairs={{0,2},{4,0},{8,4},{12,8},{14,12},{10,14},{6,10},{2,6},{1,3},{5,1},... | collective-permute-start | bytes 393224 | tf_op jit(solution)/shard_map/ppermute | solution.py:290
  2.0 8.1 %collective-permute-start.2 = (bf16[512,128]{1,0:T(8,128)(2,1)}, bf16[512,128]{1,0:T(8,128)(2,1)S(1)}, u32[]{:S(2)}, u32[]{:S(2)}) collective-permute-start(bf16[512,128]{1,0:T(8,128)(2,1)} %bitcast.4), channel_id=1, source_target_pairs={{0,4},{4,8},{8,12},{12,14},{14,10},{10,6},{6,2},{2,0},{1,5},{5,9},... | collective-permute-start | bytes 393224 | tf_op jit(solution)/shard_map/ppermute | solution.py:290
  3.6 6.5 %collective-permute-start.3 = (bf16[512,128]{1,0:T(8,128)(2,1)}, bf16[512,128]{1,0:T(8,128)(2,1)S(1)}, u32[]{:S(2)}, u32[]{:S(2)}) collective-permute-start(bf16[512,128]{1,0:T(8,128)(2,1)} %bitcast.7), channel_id=1, source_target_pairs={{0,2},{4,0},{8,4},{12,8},{14,12},{10,14},{6,10},{2,6},{1,3},{5,1},... | collective-permute-start | bytes 393224 | tf_op jit(solution)/shard_map/ppermute | solution.py:290
  8.1 5.9 %collective-permute-start.4 = (bf16[512,128]{1,0:T(8,128)(2,1)S(1)}, bf16[512,128]{1,0:T(8,128)(2,1)S(1)}, u32[]{:S(2)}, u32[]{:S(2)}) collective-permute-start(bf16[512,128]{1,0:T(8,128)(2,1)S(1)} %collective-permute-done.refs_0_), channel_id=1, source_target_pairs={{0,4},{4,8},{8,12},{12,14},{14,10},{10,6},{6,2},{2,0},{1,5},{5,9},... | collective-permute-start | bytes 393224 | tf_op jit(solution)/shard_map/ppermute | solution.py:290
  9.6 5.5 %collective-permute-start.5 = (bf16[512,128]{1,0:T(8,128)(2,1)S(1)}, bf16[512,128]{1,0:T(8,128)(2,1)S(1)}, u32[]{:S(2)}, u32[]{:S(2)}) collective-permute-start(bf16[512,128]{1,0:T(8,128)(2,1)S(1)} %collective-permute-done.1.refs_7_), channel_id=1, source_target_pairs={{0,2},{4,0},{8,4},{12,8},{14,12},{10,14},{6,10},{2,6},{1,3},{5,1},... | collective-permute-start | bytes 393224 | tf_op jit(solution)/shard_map/ppermute | solution.py:290
  10.1 7.0 %collective-permute-start.6 = (bf16[512,128]{1,0:T(8,128)(2,1)S(1)}, bf16[512,128]{1,0:T(8,128)(2,1)S(1)}, u32[]{:S(2)}, u32[]{:S(2)}) collective-permute-start(bf16[512,128]{1,0:T(8,128)(2,1)S(1)} %collective-permute-done.2.refs_6_), channel_id=1, source_target_pairs={{0,4},{4,8},{8,12},{12,14},{14,10},{10,6},{6,2},{2,0},{1,5},{5,9},... | collective-permute-start | bytes 393224 | tf_op jit(solution)/shard_map/ppermute | solution.py:290
  12.2 6.3 %collective-permute-start.7 = (bf16[512,128]{1,0:T(8,128)(2,1)S(1)}, bf16[512,128]{1,0:T(8,128)(2,1)S(1)}, u32[]{:S(2)}, u32[]{:S(2)}) collective-permute-start(bf16[512,128]{1,0:T(8,128)(2,1)S(1)} %collective-permute-done.3.refs_1_), channel_id=1, source_target_pairs={{0,2},{4,0},{8,4},{12,8},{14,12},{10,14},{6,10},{2,6},{1,3},{5,1},... | collective-permute-start | bytes 393224 | tf_op jit(solution)/shard_map/ppermute | solution.py:290
  15.1 5.5 %collective-permute-start.8 = (bf16[512,128]{1,0:T(8,128)(2,1)S(1)}, bf16[512,128]{1,0:T(8,128)(2,1)S(1)}, u32[]{:S(2)}, u32[]{:S(2)}) collective-permute-start(bf16[512,128]{1,0:T(8,128)(2,1)S(1)} %collective-permute-done.4.refs_2_), channel_id=1, source_target_pairs={{0,4},{4,8},{8,12},{12,14},{14,10},{10,6},{6,2},{2,0},{1,5},{5,9},... | collective-permute-start | bytes 393224 | tf_op jit(solution)/shard_map/ppermute | solution.py:290
  15.6 5.7 %collective-permute-start.9 = (bf16[512,128]{1,0:T(8,128)(2,1)S(1)}, bf16[512,128]{1,0:T(8,128)(2,1)S(1)}, u32[]{:S(2)}, u32[]{:S(2)}) collective-permute-start(bf16[512,128]{1,0:T(8,128)(2,1)S(1)} %collective-permute-done.5.refs_9_), channel_id=1, source_target_pairs={{0,2},{4,0},{8,4},{12,8},{14,12},{10,14},{6,10},{2,6},{1,3},{5,1},... | collective-permute-start | bytes 393224 | tf_op jit(solution)/shard_map/ppermute | solution.py:290
  18.5 5.0 %collective-permute-start.10 = (bf16[512,128]{1,0:T(8,128)(2,1)S(1)}, bf16[512,128]{1,0:T(8,128)(2,1)S(1)}, u32[]{:S(2)}, u32[]{:S(2)}) collective-permute-start(bf16[512,128]{1,0:T(8,128)(2,1)S(1)} %collective-permute-done.6.refs_8_), channel_id=1, source_target_pairs={{0,4},{4,8},{8,12},{12,14},{14,10},{10,6},{6,2},{2,0},{1,5},{5,9},... | collective-permute-start | bytes 393224 | tf_op jit(solution)/shard_map/ppermute | solution.py:290
  19.0 5.0 %collective-permute-start.11 = (bf16[512,128]{1,0:T(8,128)(2,1)S(1)}, bf16[512,128]{1,0:T(8,128)(2,1)S(1)}, u32[]{:S(2)}, u32[]{:S(2)}) collective-permute-start(bf16[512,128]{1,0:T(8,128)(2,1)S(1)} %collective-permute-done.7.refs_3_), channel_id=1, source_target_pairs={{0,2},{4,0},{8,4},{12,8},{14,12},{10,14},{6,10},{2,6},{1,3},{5,1},... | collective-permute-start | bytes 393224 | tf_op jit(solution)/shard_map/ppermute | solution.py:290
  21.4 7.9 %collective-permute-start.12 = (bf16[512,128]{1,0:T(8,128)(2,1)S(1)}, bf16[512,128]{1,0:T(8,128)(2,1)S(1)}, u32[]{:S(2)}, u32[]{:S(2)}) collective-permute-start(bf16[512,128]{1,0:T(8,128)(2,1)S(1)} %collective-permute-done.8.refs_4_), channel_id=1, source_target_pairs={{0,4},{4,8},{8,12},{12,14},{14,10},{10,6},{6,2},{2,0},{1,5},{5,9},... | collective-permute-start | bytes 393224 | tf_op jit(solution)/shard_map/ppermute | solution.py:290
  21.8 7.5 %collective-permute-start.13 = (bf16[512,128]{1,0:T(8,128)(2,1)S(1)}, bf16[512,128]{1,0:T(8,128)(2,1)S(1)}, u32[]{:S(2)}, u32[]{:S(2)}) collective-permute-start(bf16[512,128]{1,0:T(8,128)(2,1)S(1)} %collective-permute-done.9.refs_11_), channel_id=1, source_target_pairs={{0,2},{4,0},{8,4},{12,8},{14,12},{10,14},{6,10},{2,6},{1,3},{5,1},... | collective-permute-start | bytes 393224 | tf_op jit(solution)/shard_map/ppermute | solution.py:290

commit v10 on v8

--- a/solution.py
+++ b/solution.py
@@ -90,7 +90,7 @@
 
 def put_out(out_ref, h, first, both, group):
     rows, dim = both.shape[0], both.shape[1] // 2
-    merged = (both[:, :dim] / both[:, dim:]).reshape(rows // group, group, dim)
+    merged = (both[:, :dim] * pl.reciprocal(both[:, dim:])).reshape(rows // group, group, dim)
     tokens = pl.ds(first // group, rows // group)
     out_ref[tokens, pl.ds(h * group, group), :] = merged.astype(jnp.bfloat16)
 
@@ -107,6 +107,24 @@
     return [copy]
 
 
+def chunks_of(kv_dev, rows_all):
+    return [(h, first) for h in range(kv_dev) for first in range(0, rows_all, ROW_CHUNK)]
+
+
+def in_turns(stages, jobs):
+    held = {}
+    for turn in range(len(jobs) + len(stages) - 1):
+        for n, stage in enumerate(stages):
+            at = turn - n
+            if 0 <= at < len(jobs):
+                held[at] = stage(jobs[at], held.get(at))
+        held.pop(turn - len(stages) + 1, None)
+
+
+def scores_of(q, keys):
+    return lax.dot_general(q, keys, (((1,), (1,)), ((), ())), preferred_element_type=jnp.float32)
+
+
 def attend_kernel(lists_ref, q_ref, k_own_ref, v_own_ref, *refs, parts, sources, last):
     k_parts, v_parts = refs[:parts], refs[parts : 2 * parts]
     out_hbm, *state, k_wide, v_wide, out_ref, sems = refs[2 * parts :]
@@ -131,35 +149,45 @@
         count += take.astype(jnp.int32)
 
     def run(others, final):
+        keys = (others + 1) * tokens
         copies = []
+        k_ready, v_ready = [], []
         for h in range(kv_dev):
             k_h, v_h = k_own_ref[h], v_own_ref[h]
             if others:
-                keys = others * tokens
-                k_h = jnp.concatenate([k_h, by_head(k_wide, h, kv_dev, keys)], axis=0)
-                v_h = jnp.concatenate([v_h, by_head(v_wide, h, kv_dev, keys)], axis=0)
-            v_h = with_ones(v_h)
-            for first in range(0, rows_all, ROW_CHUNK):
+                k_h = jnp.concatenate([k_h, by_head(k_wide, h, kv_dev, keys - tokens)], axis=0)
+                v_h = jnp.concatenate([v_h, by_head(v_wide, h, kv_dev, keys - tokens)], axis=0)
+            k_ready.append(k_h)
+            v_ready.append(with_ones(v_h))
+
+        def score(job, _):
+            h, first = job
+            return scores_of(q_ref[h, pl.ds(first, ROW_CHUNK), :], k_ready[h])
+
+        def weigh(job, s):
+            first = job[1]
+            row = (lax.broadcasted_iota(jnp.int32, (ROW_CHUNK, tokens), 0) + first) // group
+            key = lax.broadcasted_iota(jnp.int32, (ROW_CHUNK, tokens), 1)
+            scores = [jnp.where(key <= row, s[:, :tokens], NO_KEY)]
+            scores += [s[:, (j + 1) * tokens : (j + 2) * tokens] for j in range(others)]
+            top = jnp.max(functools.reduce(jnp.maximum, scores), axis=1, keepdims=True)
+            probs = [jnp.exp2((part - top) * factor).astype(jnp.bfloat16) for part in scores]
+            return jnp.concatenate(probs, axis=1), top
+
+        def add_up(job, weighed):
+            h, first = job
+            probs, top = weighed
+            both = jnp.dot(probs, v_ready[h], preferred_element_type=jnp.float32)
+            if final:
+                put_out(out_ref, h, first, both, group)
+                if first + ROW_CHUNK == rows_all:
+                    copies.extend(send_out(out_ref, out_hbm, sems, h, group))
+            else:
                 rows = pl.ds(first, ROW_CHUNK)
-                s = lax.dot_general(
-                    q_ref[h, rows, :], k_h, (((1,), (1,)), ((), ())), preferred_element_type=jnp.float32
-                )
-                row = (lax.broadcasted_iota(jnp.int32, (ROW_CHUNK, tokens), 0) + first) // group
-                key = lax.broadcasted_iota(jnp.int32, (ROW_CHUNK, tokens), 1)
-                scores = [jnp.where(key <= row, s[:, :tokens], NO_KEY)]
-                scores += [s[:, (j + 1) * tokens : (j + 2) * tokens] for j in range(others)]
-                top = jnp.max(functools.reduce(jnp.maximum, scores), axis=1, keepdims=True)
-                probs = [jnp.exp2((score - top) * factor).astype(jnp.bfloat16) for score in scores]
-                both = jnp.dot(
-                    jnp.concatenate(probs, axis=1), v_h, preferred_element_type=jnp.float32
-                )
-                if final:
-                    put_out(out_ref, h, first, both, group)
-                else:
-                    state[0][h, rows, :] = jnp.broadcast_to(top, (ROW_CHUNK, dim))
-                    state[1][h, rows, :] = both
-            if final:
-                copies += send_out(out_ref, out_hbm, sems, h, group)
+                state[0][h, rows, :] = jnp.broadcast_to(top, (ROW_CHUNK, dim))
+                state[1][h, rows, :] = both
+
+        in_turns([score, weigh, add_up], chunks_of(kv_dev, rows_all))
         for copy in copies:
             copy.wait()
 
@@ -215,23 +243,31 @@
     def _add():
         k_wide[...] = k_ref[...].astype(jnp.float32)
         v_wide[...] = v_ref[...].astype(jnp.float32)
+        k_ready = [by_head(k_wide, h, kv_dev, tokens) for h in range(kv_dev)]
+        v_ready = [with_ones(by_head(v_wide, h, kv_dev, tokens)) for h in range(kv_dev)]
         copies = []
-        for h in range(kv_dev):
-            k_h = by_head(k_wide, h, kv_dev, tokens)
-            v_h = with_ones(by_head(v_wide, h, kv_dev, tokens))
-            for first in range(0, rows_all, ROW_CHUNK):
-                rows = pl.ds(first, ROW_CHUNK)
-                s = lax.dot_general(
-                    q_ref[h, rows, :], k_h, (((1,), (1,)), ((), ())), preferred_element_type=jnp.float32
-                )
-                before = top_ref[h, rows, :]
-                top = jnp.maximum(before, jnp.max(s, axis=1, keepdims=True))
-                probs = jnp.exp2((s - top) * factor).astype(jnp.bfloat16)
-                shrink = jnp.exp2((before - top) * factor)
-                both = jnp.dot(probs, v_h, preferred_element_type=jnp.float32)
-                both += both_ref[h, rows, :] * jnp.concatenate([shrink, shrink], axis=1)
-                put_out(out_ref, h, first, both, group)
-            copies += send_out(out_ref, out_hbm, sems, h, group)
+
+        def score(job, _):
+            h, first = job
+            return scores_of(q_ref[h, pl.ds(first, ROW_CHUNK), :], k_ready[h])
+
+        def weigh(job, s):
+            h, first = job
+            before = top_ref[h, pl.ds(first, ROW_CHUNK), :]
+            top = jnp.maximum(before, jnp.max(s, axis=1, keepdims=True))
+            shrink = jnp.exp2((before - top) * factor)
+            return jnp.exp2((s - top) * factor).astype(jnp.bfloat16), shrink
+
+        def add_up(job, weighed):
+            h, first = job
+            probs, shrink = weighed
+            both = jnp.dot(probs, v_ready[h], preferred_element_type=jnp.float32)
+            both += both_ref[h, pl.ds(first, ROW_CHUNK), :] * jnp.concatenate([shrink, shrink], axis=1)
+            put_out(out_ref, h, first, both, group)
+            if first + ROW_CHUNK == rows_all:
+                copies.extend(send_out(out_ref, out_hbm, sems, h, group))
+
+        in_turns([score, weigh, add_up], chunks_of(kv_dev, rows_all))
         for copy in copies:
             copy.wait()
 

time: 32.9 us -> 31.5 us (0.957)
  the two profiles are of different devices: /device:TPU:20 before, /device:TPU:0 now
where the time goes in v10:
time: 31.5 us; the launch traced here: 31.3 us
  starting transfers between devices  15.2 us (48%)
  waiting for transfers between devices  10.7 us (34%)
  Pallas kernels  5.23 us (17%)
    ppermute x14, starting transfers between devices, send(): return lax.ppermute(x, 'seq', ways[way])  15.2 us
    ppermute x14, waiting for transfers between devices, send(): return lax.ppermute(x, 'seq', ways[way])  10.7 us
    pallas_call x1, Pallas kernels, attend(): pl.pallas_call(functools.partial(attend_kernel, parts=len(k_parts), sourc...  3.05 us
    pallas_call x1, Pallas kernels, prepare(): pl.pallas_call(functools.partial(prepare_kernel, kv_dev=kv_dev), out_shap...  1.57 us
  transfers between devices with their start and end apart: 14, of which 9 were waited for; matrix products, arithmetic and copies ran while one was open for 0% of the time, Pallas kernels for 15%

profile of v10, /device:TPU:0, one launch (start us, length us, event | category | flops | bytes accessed | tf_op | source)
XLA Modules:
  0.0 31.3 jit_solution(15799242565398272839)
XLA Ops:
  0.0 3.0 %collective-permute-start = (bf16[512,128]{1,0:T(8,128)(2,1)}, bf16[512,128]{1,0:T(8,128)(2,1)S(1)}, u32[]{:S(2)}, u32[]{:S(2)}) collective-permute-start(bf16[512,128]{1,0:T(8,128)(2,1)} %bitcast.6), channel_id=1, source_target_pairs={{0,4},{4,8},{8,12},{12,14},{14,10},{10,6},{6,2},{2,0},{1,5},{5,9},... | collective-permute-start | bytes 393224 | tf_op jit(solution)/shard_map/ppermute | solution.py:311
  3.0 0.0 collective-permute-start.1
  3.0 2.0 %collective-permute-start.2 = (bf16[512,128]{1,0:T(8,128)(2,1)}, bf16[512,128]{1,0:T(8,128)(2,1)S(1)}, u32[]{:S(2)}, u32[]{:S(2)}) collective-permute-start(bf16[512,128]{1,0:T(8,128)(2,1)} %bitcast.4), channel_id=1, source_target_pairs={{0,4},{4,8},{8,12},{12,14},{14,10},{10,6},{6,2},{2,0},{1,5},{5,9},... | collective-permute-start | bytes 393224 | tf_op jit(solution)/shard_map/ppermute | solution.py:311
  5.1 0.0 collective-permute-start.3
  5.1 1.6 %prepare.1 = (s32[4,8]{1,0:T(4,128)S(1)}, bf16[4,1024,128]{2,1,0:T(8,128)(2,1)S(1)}, bf16[4,128,128]{2,1,0:T(8,128)(2,1)S(1)}, bf16[4,128,128]{2,1,0:T(8,128)(2,1)S(1)}) custom-call(s32[4,8]{1,0:T(4,128)} %bitcast.9, bf16[128,32,128]{2,1,0:T(8,128)(2,1)} %q_hbm.1, bf16[512,128]{1,0:T(8,128)(2,1)} %bitcast.8, bf16[512,128]{1,0:T(8,128)(2,1)} %bitcast.5), custom_call_target="tpu_custom_call" | custom-call | tf_op jit(solution)/shard_map/prepare/pallas_call | solution.py:55
  6.6 0.8 %collective-permute-done.refs_0_ = bf16[512,128]{1,0:T(8,128)(2,1)S(1)} collective-permute-done((bf16[512,128]{1,0:T(8,128)(2,1)}, bf16[512,128]{1,0:T(8,128)(2,1)S(1)}, u32[]{:S(2)}, u32[]{:S(2)}) %collective-permute-start) | collective-permute-done | bytes 131104 | tf_op jit(solution)/shard_map/ppermute | solution.py:311
  7.5 2.1 %collective-permute-done.1.refs_7_ = bf16[512,128]{1,0:T(8,128)(2,1)S(1)} collective-permute-done((bf16[512,128]{1,0:T(8,128)(2,1)}, bf16[512,128]{1,0:T(8,128)(2,1)S(1)}, u32[]{:S(2)}, u32[]{:S(2)}) %collective-permute-start.1) | collective-permute-done | bytes 131104 | tf_op jit(solution)/shard_map/ppermute | solution.py:311
  9.6 1.6 %collective-permute-start.4 = (bf16[512,128]{1,0:T(8,128)(2,1)S(1)}, bf16[512,128]{1,0:T(8,128)(2,1)S(1)}, u32[]{:S(2)}, u32[]{:S(2)}) collective-permute-start(bf16[512,128]{1,0:T(8,128)(2,1)S(1)} %collective-permute-done.refs_0_), channel_id=1, source_target_pairs={{0,4},{4,8},{8,12},{12,14},{14,10},{10,6},{6,2},{2,0},{1,5},{5,9},... | collective-permute-start | bytes 393224 | tf_op jit(solution)/shard_map/ppermute | solution.py:311
  11.1 0.4 %collective-permute-start.5 = (bf16[512,128]{1,0:T(8,128)(2,1)S(1)}, bf16[512,128]{1,0:T(8,128)(2,1)S(1)}, u32[]{:S(2)}, u32[]{:S(2)}) collective-permute-start(bf16[512,128]{1,0:T(8,128)(2,1)S(1)} %collective-permute-done.1.refs_7_), channel_id=1, source_target_pairs={{0,2},{4,0},{8,4},{12,8},{14,12},{10,14},{6,10},{2,6},{1,3},{5,1},... | collective-permute-start | bytes 393224 | tf_op jit(solution)/shard_map/ppermute | solution.py:311
  11.6 0.0 collective-permute-done.2.refs_6_
  11.6 0.0 collective-permute-done.3.refs_1_
  11.6 1.6 %collective-permute-start.6 = (bf16[512,128]{1,0:T(8,128)(2,1)S(1)}, bf16[512,128]{1,0:T(8,128)(2,1)S(1)}, u32[]{:S(2)}, u32[]{:S(2)}) collective-permute-start(bf16[512,128]{1,0:T(8,128)(2,1)S(1)} %collective-permute-done.2.refs_6_), channel_id=1, source_target_pairs={{0,4},{4,8},{8,12},{12,14},{14,10},{10,6},{6,2},{2,0},{1,5},{5,9},... | collective-permute-start | bytes 393224 | tf_op jit(solution)/shard_map/ppermute | solution.py:311
  13.2 0.5 %collective-permute-start.7 = (bf16[512,128]{1,0:T(8,128)(2,1)S(1)}, bf16[512,128]{1,0:T(8,128)(2,1)S(1)}, u32[]{:S(2)}, u32[]{:S(2)}) collective-permute-start(bf16[512,128]{1,0:T(8,128)(2,1)S(1)} %collective-permute-done.3.refs_1_), channel_id=1, source_target_pairs={{0,2},{4,0},{8,4},{12,8},{14,12},{10,14},{6,10},{2,6},{1,3},{5,1},... | collective-permute-start | bytes 393224 | tf_op jit(solution)/shard_map/ppermute | solution.py:311
  13.6 1.8 %collective-permute-done.4.refs_2_ = bf16[512,128]{1,0:T(8,128)(2,1)S(1)} collective-permute-done((bf16[512,128]{1,0:T(8,128)(2,1)S(1)}, bf16[512,128]{1,0:T(8,128)(2,1)S(1)}, u32[]{:S(2)}, u32[]{:S(2)}) %collective-permute-start.4) | collective-permute-done | bytes 131104 | tf_op jit(solution)/shard_map/ppermute | solution.py:311
  15.4 1.3 %collective-permute-done.5.refs_9_ = bf16[512,128]{1,0:T(8,128)(2,1)S(1)} collective-permute-done((bf16[512,128]{1,0:T(8,128)(2,1)S(1)}, bf16[512,128]{1,0:T(8,128)(2,1)S(1)}, u32[]{:S(2)}, u32[]{:S(2)}) %collective-permute-start.5) | collective-permute-done | bytes 131104 | tf_op jit(solution)/shard_map/ppermute | solution.py:311
  16.8 1.6 %collective-permute-start.8 = (bf16[512,128]{1,0:T(8,128)(2,1)S(1)}, bf16[512,128]{1,0:T(8,128)(2,1)S(1)}, u32[]{:S(2)}, u32[]{:S(2)}) collective-permute-start(bf16[512,128]{1,0:T(8,128)(2,1)S(1)} %collective-permute-done.4.refs_2_), channel_id=1, source_target_pairs={{0,4},{4,8},{8,12},{12,14},{14,10},{10,6},{6,2},{2,0},{1,5},{5,9},... | collective-permute-start | bytes 393224 | tf_op jit(solution)/shard_map/ppermute | solution.py:311
  18.3 0.4 %collective-permute-start.9 = (bf16[512,128]{1,0:T(8,128)(2,1)S(1)}, bf16[512,128]{1,0:T(8,128)(2,1)S(1)}, u32[]{:S(2)}, u32[]{:S(2)}) collective-permute-start(bf16[512,128]{1,0:T(8,128)(2,1)S(1)} %collective-permute-done.5.refs_9_), channel_id=1, source_target_pairs={{0,2},{4,0},{8,4},{12,8},{14,12},{10,14},{6,10},{2,6},{1,3},{5,1},... | collective-permute-start | bytes 393224 | tf_op jit(solution)/shard_map/ppermute | solution.py:311
  18.8 0.0 collective-permute-done.6.refs_8_
  18.8 0.5 %collective-permute-done.7.refs_3_ = bf16[512,128]{1,0:T(8,128)(2,1)S(1)} collective-permute-done((bf16[512,128]{1,0:T(8,128)(2,1)S(1)}, bf16[512,128]{1,0:T(8,128)(2,1)S(1)}, u32[]{:S(2)}, u32[]{:S(2)}) %collective-permute-start.7) | collective-permute-done | bytes 131104 | tf_op jit(solution)/shard_map/ppermute | solution.py:311
  19.3 1.6 %collective-permute-start.10 = (bf16[512,128]{1,0:T(8,128)(2,1)S(1)}, bf16[512,128]{1,0:T(8,128)(2,1)S(1)}, u32[]{:S(2)}, u32[]{:S(2)}) collective-permute-start(bf16[512,128]{1,0:T(8,128)(2,1)S(1)} %collective-permute-done.6.refs_8_), channel_id=1, source_target_pairs={{0,4},{4,8},{8,12},{12,14},{14,10},{10,6},{6,2},{2,0},{1,5},{5,9},... | collective-permute-start | bytes 393224 | tf_op jit(solution)/shard_map/ppermute | solution.py:311
  20.9 0.4 %collective-permute-start.11 = (bf16[512,128]{1,0:T(8,128)(2,1)S(1)}, bf16[512,128]{1,0:T(8,128)(2,1)S(1)}, u32[]{:S(2)}, u32[]{:S(2)}) collective-permute-start(bf16[512,128]{1,0:T(8,128)(2,1)S(1)} %collective-permute-done.7.refs_3_), channel_id=1, source_target_pairs={{0,2},{4,0},{8,4},{12,8},{14,12},{10,14},{6,10},{2,6},{1,3},{5,1},... | collective-permute-start | bytes 393224 | tf_op jit(solution)/shard_map/ppermute | solution.py:311
  21.3 0.4 %collective-permute-done.8.refs_4_ = bf16[512,128]{1,0:T(8,128)(2,1)S(1)} collective-permute-done((bf16[512,128]{1,0:T(8,128)(2,1)S(1)}, bf16[512,128]{1,0:T(8,128)(2,1)S(1)}, u32[]{:S(2)}, u32[]{:S(2)}) %collective-permute-start.8) | collective-permute-done | bytes 131104 | tf_op jit(solution)/shard_map/ppermute | solution.py:311
  21.7 1.9 %collective-permute-done.9.refs_11_ = bf16[512,128]{1,0:T(8,128)(2,1)S(1)} collective-permute-done((bf16[512,128]{1,0:T(8,128)(2,1)S(1)}, bf16[512,128]{1,0:T(8,128)(2,1)S(1)}, u32[]{:S(2)}, u32[]{:S(2)}) %collective-permute-start.9) | collective-permute-done | bytes 131104 | tf_op jit(solution)/shard_map/ppermute | solution.py:311
  23.6 2.0 %collective-permute-start.12 = (bf16[512,128]{1,0:T(8,128)(2,1)S(1)}, bf16[512,128]{1,0:T(8,128)(2,1)S(1)}, u32[]{:S(2)}, u32[]{:S(2)}) collective-permute-start(bf16[512,128]{1,0:T(8,128)(2,1)S(1)} %collective-permute-done.8.refs_4_), channel_id=1, source_target_pairs={{0,4},{4,8},{8,12},{12,14},{14,10},{10,6},{6,2},{2,0},{1,5},{5,9},... | collective-permute-start | bytes 393224 | tf_op jit(solution)/shard_map/ppermute | solution.py:311
  25.6 0.1 collective-permute-start.13
  25.7 0.0 collective-permute-done.10.refs_10_
  25.7 0.4 %collective-permute-done.11.refs_5_ = bf16[512,128]{1,0:T(8,128)(2,1)S(1)} collective-permute-done((bf16[512,128]{1,0:T(8,128)(2,1)S(1)}, bf16[512,128]{1,0:T(8,128)(2,1)S(1)}, u32[]{:S(2)}, u32[]{:S(2)}) %collective-permute-start.11) | collective-permute-done | bytes 131104 | tf_op jit(solution)/shard_map/ppermute | solution.py:311
  26.1 3.0 %attend.1 = (bf16[128,32,128]{2,1,0:T(8,128)(2,1)}, f32[4,1024,128]{2,1,0:T(8,128)S(1)}, f32[4,1024,256]{2,1,0:T(8,128)S(1)}) custom-call(s32[4,8]{1,0:T(4,128)S(1)} %get-tuple-element.34.lists_ref, bf16[4,1024,128]{2,1,0:T(8,128)(2,1)S(1)} %get-tuple-element.35.q_ref, bf16[4,128,128]{2,1,0:T(8,128)(2,1)S(1)} %get-tuple-element.36.k_own_ref, ...), custom_call_target="tpu_custom_call" | custom-call | tf_op jit(solution)/shard_map/attend/pallas_call | solution.py:217
  29.2 0.0 collective-permute-done.12.k_ref
  29.2 1.4 %collective-permute-done.13.v_ref = bf16[512,128]{1,0:T(8,128)(2,1)S(1)} collective-permute-done((bf16[512,128]{1,0:T(8,128)(2,1)S(1)}, bf16[512,128]{1,0:T(8,128)(2,1)S(1)}, u32[]{:S(2)}, u32[]{:S(2)}) %collective-permute-start.13) | collective-permute-done | bytes 131104 | tf_op jit(solution)/shard_map/ppermute | solution.py:311
  30.5 0.6 %attend_last.1 = bf16[128,32,128]{2,1,0:T(8,128)(2,1)} custom-call(s32[4,8]{1,0:T(4,128)S(1)} %get-tuple-element.34.lists_ref, bf16[4,1024,128]{2,1,0:T(8,128)(2,1)S(1)} %get-tuple-element.35.q_ref, f32[4,1024,128]{2,1,0:T(8,128)S(1)} %get-tuple-element.52.top_ref, f32[4,1024,256]{2,1,0:T(8,128)S(1)} %get-tuple-element.53.both_ref, ...), custom_call_target="tpu_custom_call", output_to_operand_aliasing={{}: (6, {})} | custom-call | tf_op jit(solution)/shard_map/attend_last/pallas_call | solution.py:278
Async XLA Ops:
  0.0 7.5 %collective-permute-start = (bf16[512,128]{1,0:T(8,128)(2,1)}, bf16[512,128]{1,0:T(8,128)(2,1)S(1)}, u32[]{:S(2)}, u32[]{:S(2)}) collective-permute-start(bf16[512,128]{1,0:T(8,128)(2,1)} %bitcast.6), channel_id=1, source_target_pairs={{0,4},{4,8},{8,12},{12,14},{14,10},{10,6},{6,2},{2,0},{1,5},{5,9},... | collective-permute-start | bytes 393224 | tf_op jit(solution)/shard_map/ppermute | solution.py:311
  3.0 6.5 %collective-permute-start.1 = (bf16[512,128]{1,0:T(8,128)(2,1)}, bf16[512,128]{1,0:T(8,128)(2,1)S(1)}, u32[]{:S(2)}, u32[]{:S(2)}) collective-permute-start(bf16[512,128]{1,0:T(8,128)(2,1)} %bitcast.3), channel_id=1, source_target_pairs={{0,2},{4,0},{8,4},{12,8},{14,12},{10,14},{6,10},{2,6},{1,3},{5,1},... | collective-permute-start | bytes 393224 | tf_op jit(solution)/shard_map/ppermute | solution.py:311
  3.0 8.6 %collective-permute-start.2 = (bf16[512,128]{1,0:T(8,128)(2,1)}, bf16[512,128]{1,0:T(8,128)(2,1)S(1)}, u32[]{:S(2)}, u32[]{:S(2)}) collective-permute-start(bf16[512,128]{1,0:T(8,128)(2,1)} %bitcast.4), channel_id=1, source_target_pairs={{0,4},{4,8},{8,12},{12,14},{14,10},{10,6},{6,2},{2,0},{1,5},{5,9},... | collective-permute-start | bytes 393224 | tf_op jit(solution)/shard_map/ppermute | solution.py:311
  5.1 6.5 %collective-permute-start.3 = (bf16[512,128]{1,0:T(8,128)(2,1)}, bf16[512,128]{1,0:T(8,128)(2,1)S(1)}, u32[]{:S(2)}, u32[]{:S(2)}) collective-permute-start(bf16[512,128]{1,0:T(8,128)(2,1)} %bitcast.7), channel_id=1, source_target_pairs={{0,2},{4,0},{8,4},{12,8},{14,12},{10,14},{6,10},{2,6},{1,3},{5,1},... | collective-permute-start | bytes 393224 | tf_op jit(solution)/shard_map/ppermute | solution.py:311
  9.6 5.9 %collective-permute-start.4 = (bf16[512,128]{1,0:T(8,128)(2,1)S(1)}, bf16[512,128]{1,0:T(8,128)(2,1)S(1)}, u32[]{:S(2)}, u32[]{:S(2)}) collective-permute-start(bf16[512,128]{1,0:T(8,128)(2,1)S(1)} %collective-permute-done.refs_0_), channel_id=1, source_target_pairs={{0,4},{4,8},{8,12},{12,14},{14,10},{10,6},{6,2},{2,0},{1,5},{5,9},... | collective-permute-start | bytes 393224 | tf_op jit(solution)/shard_map/ppermute | solution.py:311
  11.1 5.6 %collective-permute-start.5 = (bf16[512,128]{1,0:T(8,128)(2,1)S(1)}, bf16[512,128]{1,0:T(8,128)(2,1)S(1)}, u32[]{:S(2)}, u32[]{:S(2)}) collective-permute-start(bf16[512,128]{1,0:T(8,128)(2,1)S(1)} %collective-permute-done.1.refs_7_), channel_id=1, source_target_pairs={{0,2},{4,0},{8,4},{12,8},{14,12},{10,14},{6,10},{2,6},{1,3},{5,1},... | collective-permute-start | bytes 393224 | tf_op jit(solution)/shard_map/ppermute | solution.py:311
  11.6 7.2 %collective-permute-start.6 = (bf16[512,128]{1,0:T(8,128)(2,1)S(1)}, bf16[512,128]{1,0:T(8,128)(2,1)S(1)}, u32[]{:S(2)}, u32[]{:S(2)}) collective-permute-start(bf16[512,128]{1,0:T(8,128)(2,1)S(1)} %collective-permute-done.2.refs_6_), channel_id=1, source_target_pairs={{0,4},{4,8},{8,12},{12,14},{14,10},{10,6},{6,2},{2,0},{1,5},{5,9},... | collective-permute-start | bytes 393224 | tf_op jit(solution)/shard_map/ppermute | solution.py:311
  13.2 6.1 %collective-permute-start.7 = (bf16[512,128]{1,0:T(8,128)(2,1)S(1)}, bf16[512,128]{1,0:T(8,128)(2,1)S(1)}, u32[]{:S(2)}, u32[]{:S(2)}) collective-permute-start(bf16[512,128]{1,0:T(8,128)(2,1)S(1)} %collective-permute-done.3.refs_1_), channel_id=1, source_target_pairs={{0,2},{4,0},{8,4},{12,8},{14,12},{10,14},{6,10},{2,6},{1,3},{5,1},... | collective-permute-start | bytes 393224 | tf_op jit(solution)/shard_map/ppermute | solution.py:311
  16.8 5.0 %collective-permute-start.8 = (bf16[512,128]{1,0:T(8,128)(2,1)S(1)}, bf16[512,128]{1,0:T(8,128)(2,1)S(1)}, u32[]{:S(2)}, u32[]{:S(2)}) collective-permute-start(bf16[512,128]{1,0:T(8,128)(2,1)S(1)} %collective-permute-done.4.refs_2_), channel_id=1, source_target_pairs={{0,4},{4,8},{8,12},{12,14},{14,10},{10,6},{6,2},{2,0},{1,5},{5,9},... | collective-permute-start | bytes 393224 | tf_op jit(solution)/shard_map/ppermute | solution.py:311
  18.3 5.3 %collective-permute-start.9 = (bf16[512,128]{1,0:T(8,128)(2,1)S(1)}, bf16[512,128]{1,0:T(8,128)(2,1)S(1)}, u32[]{:S(2)}, u32[]{:S(2)}) collective-permute-start(bf16[512,128]{1,0:T(8,128)(2,1)S(1)} %collective-permute-done.5.refs_9_), channel_id=1, source_target_pairs={{0,2},{4,0},{8,4},{12,8},{14,12},{10,14},{6,10},{2,6},{1,3},{5,1},... | collective-permute-start | bytes 393224 | tf_op jit(solution)/shard_map/ppermute | solution.py:311
  19.3 6.4 %collective-permute-start.10 = (bf16[512,128]{1,0:T(8,128)(2,1)S(1)}, bf16[512,128]{1,0:T(8,128)(2,1)S(1)}, u32[]{:S(2)}, u32[]{:S(2)}) collective-permute-start(bf16[512,128]{1,0:T(8,128)(2,1)S(1)} %collective-permute-done.6.refs_8_), channel_id=1, source_target_pairs={{0,4},{4,8},{8,12},{12,14},{14,10},{10,6},{6,2},{2,0},{1,5},{5,9},... | collective-permute-start | bytes 393224 | tf_op jit(solution)/shard_map/ppermute | solution.py:311
  20.9 5.2 %collective-permute-start.11 = (bf16[512,128]{1,0:T(8,128)(2,1)S(1)}, bf16[512,128]{1,0:T(8,128)(2,1)S(1)}, u32[]{:S(2)}, u32[]{:S(2)}) collective-permute-start(bf16[512,128]{1,0:T(8,128)(2,1)S(1)} %collective-permute-done.7.refs_3_), channel_id=1, source_target_pairs={{0,2},{4,0},{8,4},{12,8},{14,12},{10,14},{6,10},{2,6},{1,3},{5,1},... | collective-permute-start | bytes 393224 | tf_op jit(solution)/shard_map/ppermute | solution.py:311
  23.6 5.5 %collective-permute-start.12 = (bf16[512,128]{1,0:T(8,128)(2,1)S(1)}, bf16[512,128]{1,0:T(8,128)(2,1)S(1)}, u32[]{:S(2)}, u32[]{:S(2)}) collective-permute-start(bf16[512,128]{1,0:T(8,128)(2,1)S(1)} %collective-permute-done.8.refs_4_), channel_id=1, source_target_pairs={{0,4},{4,8},{8,12},{12,14},{14,10},{10,6},{6,2},{2,0},{1,5},{5,9},... | collective-permute-start | bytes 393224 | tf_op jit(solution)/shard_map/ppermute | solution.py:311
  25.6 5.0 %collective-permute-start.13 = (bf16[512,128]{1,0:T(8,128)(2,1)S(1)}, bf16[512,128]{1,0:T(8,128)(2,1)S(1)}, u32[]{:S(2)}, u32[]{:S(2)}) collective-permute-start(bf16[512,128]{1,0:T(8,128)(2,1)S(1)} %collective-permute-done.9.refs_11_), channel_id=1, source_target_pairs={{0,2},{4,0},{8,4},{12,8},{14,12},{10,14},{6,10},{2,6},{1,3},{5,1},... | collective-permute-start | bytes 393224 | tf_op jit(solution)/shard_map/ppermute | solution.py:311

commit v11 on v10

--- a/solution.py
+++ b/solution.py
@@ -10,7 +10,7 @@
 
 NO_KEY = -1e30
 ROW_CHUNK = 256
-MOST_ROUND = 16
+ROUND = (8, 12, 16)
 HEADS_OUT = 16
 
 
@@ -75,9 +75,16 @@
     )(*operands)
 
 
-def is_listed(lists_ref, target, source):
-    same = [lists_ref[j, target] == source for j in range(lists_ref.shape[0])]
-    return functools.reduce(jnp.logical_or, same)
+def listed_bits(lists_ref, code):
+    target = lax.axis_index("seq").astype(jnp.int32)
+    entries = lists_ref[...]
+    mine = lax.broadcasted_iota(jnp.int32, entries.shape, 1) == target
+    bits = jnp.left_shift(1, code(jnp.maximum(entries, 0), target)).astype(jnp.float32)
+    return jnp.sum(jnp.where(jnp.logical_and(mine, entries >= 0), bits, 0.0)).astype(jnp.int32)
+
+
+def has(bits, code):
+    return jnp.bitwise_and(lax.shift_right_logical(bits, jnp.int32(code)), 1) == 1
 
 
 def by_head(wide, h, kv_dev, keys):
@@ -125,7 +132,8 @@
     return lax.dot_general(q, keys, (((1,), (1,)), ((), ())), preferred_element_type=jnp.float32)
 
 
-def attend_kernel(lists_ref, q_ref, k_own_ref, v_own_ref, *refs, parts, sources, last):
+def attend_kernel(lists_ref, q_ref, k_own_ref, v_own_ref, *refs, codes, code, last):
+    parts = len(codes)
     k_parts, v_parts = refs[:parts], refs[parts : 2 * parts]
     out_hbm, *state, k_wide, v_wide, out_ref, sems = refs[2 * parts :]
     kv_dev, tokens, dim = k_own_ref.shape
@@ -134,11 +142,11 @@
     block = tokens * kv_dev
     most = k_wide.shape[0] // block
     factor = dim ** (-0.5) * math.log2(math.e)
-    target = lax.axis_index("seq").astype(jnp.int32)
-
+
+    bits = listed_bits(lists_ref, code)
     count = jnp.int32(0)
-    for source, k_part, v_part in zip(sources(target), k_parts, v_parts):
-        take = is_listed(lists_ref, target, source)
+    for part_code, k_part, v_part in zip(codes, k_parts, v_parts):
+        take = has(bits, part_code)
 
         @pl.when(take)
         def _take(k_part=k_part, v_part=v_part, count=count):
@@ -191,7 +199,7 @@
         for copy in copies:
             copy.wait()
 
-    unfinished = False if last is None else is_listed(lists_ref, target, last(target))
+    unfinished = False if last is None else has(bits, last)
     for others in range(most + 1):
 
         @pl.when(jnp.logical_and(count == others, jnp.logical_not(unfinished)))
@@ -205,7 +213,7 @@
                 run(others, False)
 
 
-def attend(lists, queries, k_own, v_own, k_parts, v_parts, sources, last):
+def attend(lists, queries, k_own, v_own, k_parts, v_parts, codes, code, last):
     kv_dev, rows, dim = queries.shape
     tokens = k_own.shape[1]
     rest = (lists.shape[0] - 1) * tokens * kv_dev
@@ -213,11 +221,11 @@
     state = [] if last is None else [
         jax.ShapeDtypeStruct((kv_dev, rows, wide), jnp.float32) for wide in (dim, 2 * dim)
     ]
-    hbm, smem = (pl.BlockSpec(memory_space=space) for space in (pltpu.HBM, pltpu.SMEM))
+    hbm = pl.BlockSpec(memory_space=pltpu.HBM)
     return pl.pallas_call(
-        functools.partial(attend_kernel, parts=len(k_parts), sources=sources, last=last),
+        functools.partial(attend_kernel, codes=codes, code=code, last=last),
         out_shape=(out, *state),
-        in_specs=[smem] + [vmem()] * (3 + 2 * len(k_parts)),
+        in_specs=[vmem()] * (4 + 2 * len(k_parts)),
         out_specs=(hbm, *(vmem() for _ in state)),
         scratch_shapes=[
             pltpu.VMEM((rest, dim), jnp.float32),
@@ -231,15 +239,14 @@
 
 
 def last_kernel(
-    lists_ref, q_ref, top_ref, both_ref, k_ref, v_ref, _, out_hbm, k_wide, v_wide, out_ref, sems, *, last
+    lists_ref, q_ref, top_ref, both_ref, k_ref, v_ref, _, out_hbm, k_wide, v_wide, out_ref, sems, *, code, last
 ):
     kv_dev, rows_all, dim = q_ref.shape
     tokens = k_ref.shape[0] // kv_dev
     group = rows_all // tokens
     factor = dim ** (-0.5) * math.log2(math.e)
-    target = lax.axis_index("seq").astype(jnp.int32)
-
-    @pl.when(is_listed(lists_ref, target, last(target)))
+
+    @pl.when(has(listed_bits(lists_ref, code), last))
     def _add():
         k_wide[...] = k_ref[...].astype(jnp.float32)
         v_wide[...] = v_ref[...].astype(jnp.float32)
@@ -272,13 +279,13 @@
             copy.wait()
 
 
-def attend_last(lists, queries, state, k_last, v_last, out, last):
+def attend_last(lists, queries, state, k_last, v_last, out, code, last):
     top, both = state
-    hbm, smem = (pl.BlockSpec(memory_space=space) for space in (pltpu.HBM, pltpu.SMEM))
+    hbm = pl.BlockSpec(memory_space=pltpu.HBM)
     return pl.pallas_call(
-        functools.partial(last_kernel, last=last),
+        functools.partial(last_kernel, code=code, last=last),
         out_shape=jax.ShapeDtypeStruct(out.shape, out.dtype),
-        in_specs=[smem] + [vmem()] * 5 + [hbm],
+        in_specs=[vmem()] * 6 + [hbm],
         out_specs=hbm,
         input_output_aliases={6: 0},
         scratch_shapes=[
@@ -292,29 +299,46 @@
     )(lists, queries, top, both, k_last, v_last, out)
 
 
-def ring_at(place, members):
-    back = members - 1 - place
-    return jnp.where(place < members // 2, 2 * place, 2 * back + 1)
-
-
 def ring_place(block, members):
-    return jnp.where(block % 2 == 0, block // 2, members - 1 - block // 2)
+    return jnp.where((block & 1) == 0, block >> 1, members - 1 - (block >> 1))
+
+
+def ring_code(members):
+    def code(block, target):
+        ahead = ring_place(block, members) - ring_place(target, members)
+        return jnp.where(ahead < 0, ahead + members, ahead)
+
+    return code
+
+
+def ring_steps(members):
+    half = members // 2
+    first, final = half // 2, half // 2 + half - 1
+    still = {p: p for p in range(members)}
+    forward = {p: (p + 1) % members for p in range(members)}
+    backward = {p: (p - 1) % members for p in range(members)}
+    forward_late = {**still, **{p: p + 1 for p in range(first - 1, final)}, final: first - 1}
+    backward_late = {**still, **{p: p - 1 for p in range(first + 2, final + 3)}}
+    backward_late.update({p: p - 1 for p in range(2, first + 2)})
+    backward_late[1] = final + 2
+    forward_last = {**still, **{p: p + 1 for p in range(first, final)}, final: first}
+    backward_last = {**still, **{p: p - 1 for p in range(first + 1, final + 1)}, first: final}
+    return (forward, backward), (forward_late, backward_late), (forward_last, backward_last)
 
 
 def round_the_ring(k_own, v_own, ready, members):
     ring = list(range(0, members, 2)) + list(range(members - 1, 0, -2))
-    ways = [
-        [(ring[p], ring[(p + turn) % members]) for p in range(members)] for turn in (1, -1)
-    ]
-
-    def send(x, way):
-        return lax.ppermute(x, "seq", ways[way])
+    steps, late, final = ring_steps(members)
+
+    def send(x, step):
+        return lax.ppermute(x, "seq", [(ring[p], ring[to]) for p, to in sorted(step.items())])
 
     half = members // 2
     k_two, v_two, k_all, v_all = [k_own, k_own], [v_own, v_own], [], []
     for distance in range(1, half):
-        ahead = send(k_two[0], 0), send(v_two[1], 1)
-        behind = send(v_two[0], 0), send(k_two[1], 1)
+        forward, backward = late if distance == half - 1 else steps
+        ahead = send(k_two[0], forward), send(v_two[1], backward)
+        behind = send(v_two[0], forward), send(k_two[1], backward)
         if distance == 1:
             ahead, ready = lax.optimization_barrier((ahead, ready))
         ahead = lax.optimization_barrier(ahead)
@@ -322,18 +346,10 @@
         k_two, v_two = [ahead[0], behind[1]], [behind[0], ahead[1]]
         k_all += k_two
         v_all += v_two
-    return k_all, v_all, send(k_two[0], 0), send(v_two[1], 1), ready
-
-
-def ring_sources(members):
-    def at(target, turn):
-        place = lax.rem(ring_place(target, members) + turn + members, members)
-        return ring_at(place, members)
-
-    def sources(target):
-        return [at(target, turn) for far in range(1, members // 2) for turn in (-far, far)]
-
-    return sources, lambda target: at(target, members // 2)
+    here = ring_place(lax.axis_index("seq").astype(jnp.int32), members)
+    k_last = jnp.where(here == half // 2 + half - 1, k_all[1], k_two[0])
+    v_last = jnp.where(here == half // 2, v_all[0], v_two[1])
+    return k_all, v_all, send(k_last, final[0]), send(v_last, final[1]), ready
 
 
 def others(row, target):
@@ -360,22 +376,22 @@
     tokens, kv_dev, dim = keys.shape
     k_own = keys.reshape(tokens * kv_dev, dim)
     v_own = values.reshape(tokens * kv_dev, dim)
-    if members <= MOST_ROUND:
+    if members in ROUND:
         ready = prepare(chosen.T, queries, k_own, v_own, kv_dev)
         k_parts, v_parts, k_last, v_last, ready = round_the_ring(k_own, v_own, ready, members)
         lists, q_ready, k_ready, v_ready = ready
-        sources, last = ring_sources(members)
-        out, *state = attend(lists, q_ready, k_ready, v_ready, k_parts, v_parts, sources, last)
-        return attend_last(lists, q_ready, state, k_last, v_last, out, last)
+        half, code = members // 2, ring_code(members)
+        codes = [turn for far in range(1, half) for turn in (members - far, far)]
+        out, *state = attend(
+            lists, q_ready, k_ready, v_ready, k_parts, v_parts, codes, code, half
+        )
+        return attend_last(lists, q_ready, state, k_last, v_last, out, code, half)
 
     k_parts, v_parts, mine = relay(k_own, v_own, chosen, members)
     lists, *ready = prepare(mine.T, queries, k_own, v_own, kv_dev)
-
-    def sources(_):
-        return [jnp.int32(j) for j in range(len(k_parts))]
-
     lists = jnp.concatenate([lists, jnp.full_like(lists[:1], -1)])
-    return attend(lists, *ready, k_parts, v_parts, sources, None)[0]
+    codes = list(range(len(k_parts)))
+    return attend(lists, *ready, k_parts, v_parts, codes, lambda block, _: block, None)[0]
 
 
 def solution(mesh):

time: 31.5 us -> 39.1 us (1.24)
  the two profiles are of different devices: /device:TPU:0 before, /device:TPU:20 now
where the time goes in v11:
time: 39.1 us; the launch traced here: 38.8 us
  starting transfers between devices  25.7 us (66%)
  Pallas kernels  7.28 us (19%)
  waiting for transfers between devices  5.52 us (14%)
    ppermute x14, starting transfers between devices, send(): lax.ppermute(x, 'seq', [(ring[p], ring[to]) for p, to in sorted(step.item...  25.7 us
    ppermute x14, waiting for transfers between devices, send(): lax.ppermute(x, 'seq', [(ring[p], ring[to]) for p, to in sorted(step.item...  5.52 us
    pallas_call x1, Pallas kernels, attend(): pl.pallas_call(functools.partial(attend_kernel, codes=codes, code=code, l...  3.02 us
    pallas_call x1, Pallas kernels, attend_last(): pl.pallas_call(functools.partial(last_kernel, code=code, last=last), out_...  2.68 us
    pallas_call x1, Pallas kernels, prepare(): pl.pallas_call(functools.partial(prepare_kernel, kv_dev=kv_dev), out_shap...  1.58 us
  transfers between devices with their start and end apart: 14, of which 5 were waited for; matrix products, arithmetic and copies ran while one was open for 0% of the time, Pallas kernels for 12%

profile of v11, /device:TPU:20, one launch (start us, length us, event | category | flops | bytes accessed | tf_op | source)
XLA Modules:
  0.0 38.8 jit_solution(1046256120197459171)
XLA Ops:
  0.0 1.6 %collective-permute-start = (bf16[512,128]{1,0:T(8,128)(2,1)}, bf16[512,128]{1,0:T(8,128)(2,1)S(1)}, u32[]{:S(2)}, u32[]{:S(2)}) collective-permute-start(bf16[512,128]{1,0:T(8,128)(2,1)} %bitcast.6), channel_id=1, source_target_pairs={{0,4},{4,8},{8,12},{12,14},{14,10},{10,6},{6,2},{2,0},{1,5},{5,9},... | collective-permute-start | bytes 393224 | tf_op jit(solution)/shard_map/ppermute | solution.py:334
  1.6 0.4 %collective-permute-start.1 = (bf16[512,128]{1,0:T(8,128)(2,1)}, bf16[512,128]{1,0:T(8,128)(2,1)S(1)}, u32[]{:S(2)}, u32[]{:S(2)}) collective-permute-start(bf16[512,128]{1,0:T(8,128)(2,1)} %bitcast.3), channel_id=1, source_target_pairs={{0,2},{4,0},{8,4},{12,8},{14,12},{10,14},{6,10},{2,6},{1,3},{5,1},... | collective-permute-start | bytes 393224 | tf_op jit(solution)/shard_map/ppermute | solution.py:334
  2.0 1.6 %collective-permute-start.2 = (bf16[512,128]{1,0:T(8,128)(2,1)}, bf16[512,128]{1,0:T(8,128)(2,1)S(1)}, u32[]{:S(2)}, u32[]{:S(2)}) collective-permute-start(bf16[512,128]{1,0:T(8,128)(2,1)} %bitcast.4), channel_id=1, source_target_pairs={{0,4},{4,8},{8,12},{12,14},{14,10},{10,6},{6,2},{2,0},{1,5},{5,9},... | collective-permute-start | bytes 393224 | tf_op jit(solution)/shard_map/ppermute | solution.py:334
  3.6 0.4 %collective-permute-start.3 = (bf16[512,128]{1,0:T(8,128)(2,1)}, bf16[512,128]{1,0:T(8,128)(2,1)S(1)}, u32[]{:S(2)}, u32[]{:S(2)}) collective-permute-start(bf16[512,128]{1,0:T(8,128)(2,1)} %bitcast.7), channel_id=1, source_target_pairs={{0,2},{4,0},{8,4},{12,8},{14,12},{10,14},{6,10},{2,6},{1,3},{5,1},... | collective-permute-start | bytes 393224 | tf_op jit(solution)/shard_map/ppermute | solution.py:334
  4.1 1.6 %prepare.1 = (s32[4,8]{1,0:T(4,128)S(1)}, bf16[4,1024,128]{2,1,0:T(8,128)(2,1)S(1)}, bf16[4,128,128]{2,1,0:T(8,128)(2,1)S(1)}, bf16[4,128,128]{2,1,0:T(8,128)(2,1)S(1)}) custom-call(s32[4,8]{1,0:T(4,128)} %bitcast.9, bf16[128,32,128]{2,1,0:T(8,128)(2,1)} %q_hbm.1, bf16[512,128]{1,0:T(8,128)(2,1)} %bitcast.8, bf16[512,128]{1,0:T(8,128)(2,1)} %bitcast.5), custom_call_target="tpu_custom_call" | custom-call | tf_op jit(solution)/shard_map/prepare/pallas_call | solution.py:55
  5.6 1.0 %collective-permute-done.refs_0_ = bf16[512,128]{1,0:T(8,128)(2,1)S(1)} collective-permute-done((bf16[512,128]{1,0:T(8,128)(2,1)}, bf16[512,128]{1,0:T(8,128)(2,1)S(1)}, u32[]{:S(2)}, u32[]{:S(2)}) %collective-permute-start) | collective-permute-done | bytes 131104 | tf_op jit(solution)/shard_map/ppermute | solution.py:334
  6.6 1.5 %collective-permute-done.1.refs_7_ = bf16[512,128]{1,0:T(8,128)(2,1)S(1)} collective-permute-done((bf16[512,128]{1,0:T(8,128)(2,1)}, bf16[512,128]{1,0:T(8,128)(2,1)S(1)}, u32[]{:S(2)}, u32[]{:S(2)}) %collective-permute-start.1) | collective-permute-done | bytes 131104 | tf_op jit(solution)/shard_map/ppermute | solution.py:334
  8.1 1.5 %collective-permute-start.4 = (bf16[512,128]{1,0:T(8,128)(2,1)S(1)}, bf16[512,128]{1,0:T(8,128)(2,1)S(1)}, u32[]{:S(2)}, u32[]{:S(2)}) collective-permute-start(bf16[512,128]{1,0:T(8,128)(2,1)S(1)} %collective-permute-done.refs_0_), channel_id=1, source_target_pairs={{0,4},{4,8},{8,12},{12,14},{14,10},{10,6},{6,2},{2,0},{1,5},{5,9},... | collective-permute-start | bytes 393224 | tf_op jit(solution)/shard_map/ppermute | solution.py:334
  9.6 0.5 %collective-permute-start.5 = (bf16[512,128]{1,0:T(8,128)(2,1)S(1)}, bf16[512,128]{1,0:T(8,128)(2,1)S(1)}, u32[]{:S(2)}, u32[]{:S(2)}) collective-permute-start(bf16[512,128]{1,0:T(8,128)(2,1)S(1)} %collective-permute-done.1.refs_7_), channel_id=1, source_target_pairs={{0,2},{4,0},{8,4},{12,8},{14,12},{10,14},{6,10},{2,6},{1,3},{5,1},... | collective-permute-start | bytes 393224 | tf_op jit(solution)/shard_map/ppermute | solution.py:334
  10.1 0.0 collective-permute-done.2.refs_6_
  10.1 0.0 collective-permute-done.3.refs_1_
  10.1 2.1 %collective-permute-start.6 = (bf16[512,128]{1,0:T(8,128)(2,1)S(1)}, bf16[512,128]{1,0:T(8,128)(2,1)S(1)}, u32[]{:S(2)}, u32[]{:S(2)}) collective-permute-start(bf16[512,128]{1,0:T(8,128)(2,1)S(1)} %collective-permute-done.2.refs_6_), channel_id=1, source_target_pairs={{0,4},{4,8},{8,12},{12,14},{14,10},{10,6},{6,2},{2,0},{1,5},{5,9},... | collective-permute-start | bytes 393224 | tf_op jit(solution)/shard_map/ppermute | solution.py:334
  12.2 0.0 collective-permute-start.7
  12.2 1.5 %collective-permute-done.4.refs_2_ = bf16[512,128]{1,0:T(8,128)(2,1)S(1)} collective-permute-done((bf16[512,128]{1,0:T(8,128)(2,1)S(1)}, bf16[512,128]{1,0:T(8,128)(2,1)S(1)}, u32[]{:S(2)}, u32[]{:S(2)}) %collective-permute-start.4) | collective-permute-done | bytes 131104 | tf_op jit(solution)/shard_map/ppermute | solution.py:334
  13.7 1.2 %collective-permute-done.5.refs_9_ = bf16[512,128]{1,0:T(8,128)(2,1)S(1)} collective-permute-done((bf16[512,128]{1,0:T(8,128)(2,1)S(1)}, bf16[512,128]{1,0:T(8,128)(2,1)S(1)}, u32[]{:S(2)}, u32[]{:S(2)}) %collective-permute-start.5) | collective-permute-done | bytes 131104 | tf_op jit(solution)/shard_map/ppermute | solution.py:334
  14.9 2.4 %collective-permute-start.8 = (bf16[512,128]{1,0:T(8,128)(2,1)S(1)}, bf16[512,128]{1,0:T(8,128)(2,1)S(1)}, u32[]{:S(2)}, u32[]{:S(2)}) collective-permute-start(bf16[512,128]{1,0:T(8,128)(2,1)S(1)} %collective-permute-done.4.refs_2_), channel_id=1, source_target_pairs={{0,0},{4,8},{8,12},{12,14},{14,10},{10,4},{6,6},{2,2},{1,1},{5,9},... | collective-permute-start | bytes 393224 | tf_op jit(solution)/shard_map/ppermute | solution.py:334
  17.3 3.5 %collective-permute-start.9 = (bf16[512,128]{1,0:T(8,128)(2,1)S(1)}, bf16[512,128]{1,0:T(8,128)(2,1)S(1)}, u32[]{:S(2)}, u32[]{:S(2)}) collective-permute-start(bf16[512,128]{1,0:T(8,128)(2,1)S(1)} %collective-permute-done.5.refs_9_), channel_id=1, source_target_pairs={{0,0},{4,2},{8,4},{12,8},{14,12},{10,14},{6,10},{2,6},{1,1},{5,3},... | collective-permute-start | bytes 393224 | tf_op jit(solution)/shard_map/ppermute | solution.py:334
  20.8 0.0 collective-permute-done.6.refs_8_
  20.8 0.0 collective-permute-done.7.refs_3_
  20.8 2.4 %collective-permute-start.10 = (bf16[512,128]{1,0:T(8,128)(2,1)S(1)}, bf16[512,128]{1,0:T(8,128)(2,1)S(1)}, u32[]{:S(2)}, u32[]{:S(2)}) collective-permute-start(bf16[512,128]{1,0:T(8,128)(2,1)S(1)} %collective-permute-done.6.refs_8_), channel_id=1, source_target_pairs={{0,0},{4,8},{8,12},{12,14},{14,10},{10,4},{6,6},{2,2},{1,1},{5,9},... | collective-permute-start | bytes 393224 | tf_op jit(solution)/shard_map/ppermute | solution.py:334
  23.2 3.5 %collective-permute-start.11 = (bf16[512,128]{1,0:T(8,128)(2,1)S(1)}, bf16[512,128]{1,0:T(8,128)(2,1)S(1)}, u32[]{:S(2)}, u32[]{:S(2)}) collective-permute-start(bf16[512,128]{1,0:T(8,128)(2,1)S(1)} %collective-permute-done.7.refs_3_), channel_id=1, source_target_pairs={{0,0},{4,2},{8,4},{12,8},{14,12},{10,14},{6,10},{2,6},{1,1},{5,3},... | collective-permute-start | bytes 393224 | tf_op jit(solution)/shard_map/ppermute | solution.py:334
  26.7 0.0 collective-permute-done.8.refs_4_
  26.7 0.0 collective-permute-done.9.refs_11_
  26.7 2.4 %collective-permute-start.12 = (bf16[512,128]{1,0:T(8,128)(2,1)S(1)}, bf16[512,128]{1,0:T(8,128)(2,1)S(1)}, u32[]{:S(2)}, u32[]{:S(2)}) collective-permute-start(bf16[512,128]{1,0:T(8,128)(2,1)S(1)} %broadcast_select_fusion.1), channel_id=1, source_target_pairs={{0,0},{4,4},{8,12},{12,14},{14,10},{10,8},{6,6},{2,2},{1,1},{5,5},... | collective-permute-start | bytes 393224 | tf_op jit(solution)/shard_map/ppermute | solution.py:334
  29.1 3.5 %collective-permute-start.13 = (bf16[512,128]{1,0:T(8,128)(2,1)S(1)}, bf16[512,128]{1,0:T(8,128)(2,1)S(1)}, u32[]{:S(2)}, u32[]{:S(2)}) collective-permute-start(bf16[512,128]{1,0:T(8,128)(2,1)S(1)} %broadcast_select_fusion), channel_id=1, source_target_pairs={{0,0},{4,4},{8,10},{12,8},{14,12},{10,14},{6,6},{2,2},{1,1},{5,5},... | collective-permute-start | bytes 393224 | tf_op jit(solution)/shard_map/ppermute | solution.py:334
  32.6 0.0 collective-permute-done.10.refs_10_
  32.6 0.0 collective-permute-done.11.refs_5_
  32.6 3.0 %attend.1 = (bf16[128,32,128]{2,1,0:T(8,128)(2,1)}, f32[4,1024,128]{2,1,0:T(8,128)S(1)}, f32[4,1024,256]{2,1,0:T(8,128)S(1)}) custom-call(s32[4,8]{1,0:T(4,128)S(1)} %get-tuple-element.34.lists_ref, bf16[4,1024,128]{2,1,0:T(8,128)(2,1)S(1)} %get-tuple-element.35.q_ref, bf16[4,128,128]{2,1,0:T(8,128)(2,1)S(1)} %get-tuple-element.36.k_own_ref, ...), custom_call_target="tpu_custom_call" | custom-call | tf_op jit(solution)/shard_map/attend/pallas_call | solution.py:225
  35.7 0.0 collective-permute-done.12.k_ref
  35.7 0.3 collective-permute-done.13.v_ref
  36.0 2.7 %attend_last.1 = bf16[128,32,128]{2,1,0:T(8,128)(2,1)} custom-call(s32[4,8]{1,0:T(4,128)S(1)} %get-tuple-element.34.lists_ref, bf16[4,1024,128]{2,1,0:T(8,128)(2,1)S(1)} %get-tuple-element.35.q_ref, f32[4,1024,128]{2,1,0:T(8,128)S(1)} %get-tuple-element.52.top_ref, f32[4,1024,256]{2,1,0:T(8,128)S(1)} %get-tuple-element.53.both_ref, ...), custom_call_target="tpu_custom_call", output_to_operand_aliasing={{}: (6, {})} | custom-call | tf_op jit(solution)/shard_map/attend_last/pallas_call | solution.py:285
  (2 shorter events, 0.0 us)
Async XLA Ops:
  0.0 6.6 %collective-permute-start = (bf16[512,128]{1,0:T(8,128)(2,1)}, bf16[512,128]{1,0:T(8,128)(2,1)S(1)}, u32[]{:S(2)}, u32[]{:S(2)}) collective-permute-start(bf16[512,128]{1,0:T(8,128)(2,1)} %bitcast.6), channel_id=1, source_target_pairs={{0,4},{4,8},{8,12},{12,14},{14,10},{10,6},{6,2},{2,0},{1,5},{5,9},... | collective-permute-start | bytes 393224 | tf_op jit(solution)/shard_map/ppermute | solution.py:334
  1.6 6.5 %collective-permute-start.1 = (bf16[512,128]{1,0:T(8,128)(2,1)}, bf16[512,128]{1,0:T(8,128)(2,1)S(1)}, u32[]{:S(2)}, u32[]{:S(2)}) collective-permute-start(bf16[512,128]{1,0:T(8,128)(2,1)} %bitcast.3), channel_id=1, source_target_pairs={{0,2},{4,0},{8,4},{12,8},{14,12},{10,14},{6,10},{2,6},{1,3},{5,1},... | collective-permute-start | bytes 393224 | tf_op jit(solution)/shard_map/ppermute | solution.py:334
  2.0 8.1 %collective-permute-start.2 = (bf16[512,128]{1,0:T(8,128)(2,1)}, bf16[512,128]{1,0:T(8,128)(2,1)S(1)}, u32[]{:S(2)}, u32[]{:S(2)}) collective-permute-start(bf16[512,128]{1,0:T(8,128)(2,1)} %bitcast.4), channel_id=1, source_target_pairs={{0,4},{4,8},{8,12},{12,14},{14,10},{10,6},{6,2},{2,0},{1,5},{5,9},... | collective-permute-start | bytes 393224 | tf_op jit(solution)/shard_map/ppermute | solution.py:334
  3.6 6.5 %collective-permute-start.3 = (bf16[512,128]{1,0:T(8,128)(2,1)}, bf16[512,128]{1,0:T(8,128)(2,1)S(1)}, u32[]{:S(2)}, u32[]{:S(2)}) collective-permute-start(bf16[512,128]{1,0:T(8,128)(2,1)} %bitcast.7), channel_id=1, source_target_pairs={{0,2},{4,0},{8,4},{12,8},{14,12},{10,14},{6,10},{2,6},{1,3},{5,1},... | collective-permute-start | bytes 393224 | tf_op jit(solution)/shard_map/ppermute | solution.py:334
  8.1 5.6 %collective-permute-start.4 = (bf16[512,128]{1,0:T(8,128)(2,1)S(1)}, bf16[512,128]{1,0:T(8,128)(2,1)S(1)}, u32[]{:S(2)}, u32[]{:S(2)}) collective-permute-start(bf16[512,128]{1,0:T(8,128)(2,1)S(1)} %collective-permute-done.refs_0_), channel_id=1, source_target_pairs={{0,4},{4,8},{8,12},{12,14},{14,10},{10,6},{6,2},{2,0},{1,5},{5,9},... | collective-permute-start | bytes 393224 | tf_op jit(solution)/shard_map/ppermute | solution.py:334
  9.6 5.3 %collective-permute-start.5 = (bf16[512,128]{1,0:T(8,128)(2,1)S(1)}, bf16[512,128]{1,0:T(8,128)(2,1)S(1)}, u32[]{:S(2)}, u32[]{:S(2)}) collective-permute-start(bf16[512,128]{1,0:T(8,128)(2,1)S(1)} %collective-permute-done.1.refs_7_), channel_id=1, source_target_pairs={{0,2},{4,0},{8,4},{12,8},{14,12},{10,14},{6,10},{2,6},{1,3},{5,1},... | collective-permute-start | bytes 393224 | tf_op jit(solution)/shard_map/ppermute | solution.py:334
  10.1 10.7 %collective-permute-start.6 = (bf16[512,128]{1,0:T(8,128)(2,1)S(1)}, bf16[512,128]{1,0:T(8,128)(2,1)S(1)}, u32[]{:S(2)}, u32[]{:S(2)}) collective-permute-start(bf16[512,128]{1,0:T(8,128)(2,1)S(1)} %collective-permute-done.2.refs_6_), channel_id=1, source_target_pairs={{0,4},{4,8},{8,12},{12,14},{14,10},{10,6},{6,2},{2,0},{1,5},{5,9},... | collective-permute-start | bytes 393224 | tf_op jit(solution)/shard_map/ppermute | solution.py:334
  12.2 8.6 %collective-permute-start.7 = (bf16[512,128]{1,0:T(8,128)(2,1)S(1)}, bf16[512,128]{1,0:T(8,128)(2,1)S(1)}, u32[]{:S(2)}, u32[]{:S(2)}) collective-permute-start(bf16[512,128]{1,0:T(8,128)(2,1)S(1)} %collective-permute-done.3.refs_1_), channel_id=1, source_target_pairs={{0,2},{4,0},{8,4},{12,8},{14,12},{10,14},{6,10},{2,6},{1,3},{5,1},... | collective-permute-start | bytes 393224 | tf_op jit(solution)/shard_map/ppermute | solution.py:334
  14.9 11.7 %collective-permute-start.8 = (bf16[512,128]{1,0:T(8,128)(2,1)S(1)}, bf16[512,128]{1,0:T(8,128)(2,1)S(1)}, u32[]{:S(2)}, u32[]{:S(2)}) collective-permute-start(bf16[512,128]{1,0:T(8,128)(2,1)S(1)} %collective-permute-done.4.refs_2_), channel_id=1, source_target_pairs={{0,0},{4,8},{8,12},{12,14},{14,10},{10,4},{6,6},{2,2},{1,1},{5,9},... | collective-permute-start | bytes 393224 | tf_op jit(solution)/shard_map/ppermute | solution.py:334
  17.3 9.4 %collective-permute-start.9 = (bf16[512,128]{1,0:T(8,128)(2,1)S(1)}, bf16[512,128]{1,0:T(8,128)(2,1)S(1)}, u32[]{:S(2)}, u32[]{:S(2)}) collective-permute-start(bf16[512,128]{1,0:T(8,128)(2,1)S(1)} %collective-permute-done.5.refs_9_), channel_id=1, source_target_pairs={{0,0},{4,2},{8,4},{12,8},{14,12},{10,14},{6,10},{2,6},{1,1},{5,3},... | collective-permute-start | bytes 393224 | tf_op jit(solution)/shard_map/ppermute | solution.py:334
  20.8 11.8 %collective-permute-start.10 = (bf16[512,128]{1,0:T(8,128)(2,1)S(1)}, bf16[512,128]{1,0:T(8,128)(2,1)S(1)}, u32[]{:S(2)}, u32[]{:S(2)}) collective-permute-start(bf16[512,128]{1,0:T(8,128)(2,1)S(1)} %collective-permute-done.6.refs_8_), channel_id=1, source_target_pairs={{0,0},{4,8},{8,12},{12,14},{14,10},{10,4},{6,6},{2,2},{1,1},{5,9},... | collective-permute-start | bytes 393224 | tf_op jit(solution)/shard_map/ppermute | solution.py:334
  23.2 9.4 %collective-permute-start.11 = (bf16[512,128]{1,0:T(8,128)(2,1)S(1)}, bf16[512,128]{1,0:T(8,128)(2,1)S(1)}, u32[]{:S(2)}, u32[]{:S(2)}) collective-permute-start(bf16[512,128]{1,0:T(8,128)(2,1)S(1)} %collective-permute-done.7.refs_3_), channel_id=1, source_target_pairs={{0,0},{4,2},{8,4},{12,8},{14,12},{10,14},{6,10},{2,6},{1,1},{5,3},... | collective-permute-start | bytes 393224 | tf_op jit(solution)/shard_map/ppermute | solution.py:334
  26.7 8.9 %collective-permute-start.12 = (bf16[512,128]{1,0:T(8,128)(2,1)S(1)}, bf16[512,128]{1,0:T(8,128)(2,1)S(1)}, u32[]{:S(2)}, u32[]{:S(2)}) collective-permute-start(bf16[512,128]{1,0:T(8,128)(2,1)S(1)} %broadcast_select_fusion.1), channel_id=1, source_target_pairs={{0,0},{4,4},{8,12},{12,14},{14,10},{10,8},{6,6},{2,2},{1,1},{5,5},... | collective-permute-start | bytes 393224 | tf_op jit(solution)/shard_map/ppermute | solution.py:334
  29.1 6.9 %collective-permute-start.13 = (bf16[512,128]{1,0:T(8,128)(2,1)S(1)}, bf16[512,128]{1,0:T(8,128)(2,1)S(1)}, u32[]{:S(2)}, u32[]{:S(2)}) collective-permute-start(bf16[512,128]{1,0:T(8,128)(2,1)S(1)} %broadcast_select_fusion), channel_id=1, source_target_pairs={{0,0},{4,4},{8,10},{12,8},{14,12},{10,14},{6,6},{2,2},{1,1},{5,5},... | collective-permute-start | bytes 393224 | tf_op jit(solution)/shard_map/ppermute | solution.py:334

commit v12 on v11

--- a/solution.py
+++ b/solution.py
@@ -10,7 +10,7 @@
 
 NO_KEY = -1e30
 ROW_CHUNK = 256
-ROUND = (8, 12, 16)
+ROUND = (8, 16)
 HEADS_OUT = 16
 
 
@@ -312,23 +312,21 @@
 
 
 def ring_steps(members):
-    half = members // 2
-    first, final = half // 2, half // 2 + half - 1
-    still = {p: p for p in range(members)}
+    first, final = members // 4, 3 * members // 4 - 1
     forward = {p: (p + 1) % members for p in range(members)}
     backward = {p: (p - 1) % members for p in range(members)}
-    forward_late = {**still, **{p: p + 1 for p in range(first - 1, final)}, final: first - 1}
-    backward_late = {**still, **{p: p - 1 for p in range(first + 2, final + 3)}}
-    backward_late.update({p: p - 1 for p in range(2, first + 2)})
-    backward_late[1] = final + 2
-    forward_last = {**still, **{p: p + 1 for p in range(first, final)}, final: first}
-    backward_last = {**still, **{p: p - 1 for p in range(first + 1, final + 1)}, first: final}
-    return (forward, backward), (forward_late, backward_late), (forward_last, backward_last)
+    low = [p for p in range(members) if not first <= p <= final]
+    last_forward = {p: members - 1 - p for p in low}
+    last_backward = {p: p ^ 1 for p in low}
+    last_forward.update({p: p + 1 for p in range(first, final)})
+    last_backward.update({p: p - 1 for p in range(first + 1, final + 1)})
+    last_forward[final], last_backward[first] = first, final
+    return forward, backward, last_forward, last_backward
 
 
 def round_the_ring(k_own, v_own, ready, members):
     ring = list(range(0, members, 2)) + list(range(members - 1, 0, -2))
-    steps, late, final = ring_steps(members)
+    forward, backward, last_forward, last_backward = ring_steps(members)
 
     def send(x, step):
         return lax.ppermute(x, "seq", [(ring[p], ring[to]) for p, to in sorted(step.items())])
@@ -336,7 +334,6 @@
     half = members // 2
     k_two, v_two, k_all, v_all = [k_own, k_own], [v_own, v_own], [], []
     for distance in range(1, half):
-        forward, backward = late if distance == half - 1 else steps
         ahead = send(k_two[0], forward), send(v_two[1], backward)
         behind = send(v_two[0], forward), send(k_two[1], backward)
         if distance == 1:
@@ -347,9 +344,9 @@
         k_all += k_two
         v_all += v_two
     here = ring_place(lax.axis_index("seq").astype(jnp.int32), members)
-    k_last = jnp.where(here == half // 2 + half - 1, k_all[1], k_two[0])
-    v_last = jnp.where(here == half // 2, v_all[0], v_two[1])
-    return k_all, v_all, send(k_last, final[0]), send(v_last, final[1]), ready
+    k_last = jnp.where(here == 3 * members // 4 - 1, k_all[1], k_two[0])
+    v_last = jnp.where(here == members // 4, v_all[0], v_two[1])
+    return k_all, v_all, send(k_last, last_forward), send(v_last, last_backward), ready
 
 
 def others(row, target):

time: 39.1 us -> 30.6 us (0.78)
  the two profiles are of different devices: /device:TPU:20 before, /device:TPU:0 now
where the time goes in v12:
time: 30.6 us; the launch traced here: 30.4 us
  starting transfers between devices  13.7 us (45%)
  waiting for transfers between devices  12.3 us (40%)
  Pallas kernels  4.26 us (14%)
    ppermute x14, starting transfers between devices, send(): lax.ppermute(x, 'seq', [(ring[p], ring[to]) for p, to in sorted(step.item...  13.7 us
    ppermute x14, waiting for transfers between devices, send(): lax.ppermute(x, 'seq', [(ring[p], ring[to]) for p, to in sorted(step.item...  12.3 us
    pallas_call x1, Pallas kernels, attend(): pl.pallas_call(functools.partial(attend_kernel, codes=codes, code=code, l...  2.53 us
    pallas_call x1, Pallas kernels, prepare(): pl.pallas_call(functools.partial(prepare_kernel, kv_dev=kv_dev), out_shap...  1.57 us
  transfers between devices with their start and end apart: 14, of which 10 were waited for; matrix products, arithmetic and copies ran while one was open for 0% of the time, Pallas kernels for 13%

profile of v12, /device:TPU:0, one launch (start us, length us, event | category | flops | bytes accessed | tf_op | source)
XLA Modules:
  0.0 30.4 jit_solution(3753395784524015923)
XLA Ops:
  0.0 3.0 %collective-permute-start = (bf16[512,128]{1,0:T(8,128)(2,1)}, bf16[512,128]{1,0:T(8,128)(2,1)S(1)}, u32[]{:S(2)}, u32[]{:S(2)}) collective-permute-start(bf16[512,128]{1,0:T(8,128)(2,1)} %bitcast.6), channel_id=1, source_target_pairs={{0,4},{4,8},{8,12},{12,14},{14,10},{10,6},{6,2},{2,0},{1,5},{5,9},... | collective-permute-start | bytes 393224 | tf_op jit(solution)/shard_map/ppermute | solution.py:332
  3.0 0.0 collective-permute-start.1
  3.0 2.0 %collective-permute-start.2 = (bf16[512,128]{1,0:T(8,128)(2,1)}, bf16[512,128]{1,0:T(8,128)(2,1)S(1)}, u32[]{:S(2)}, u32[]{:S(2)}) collective-permute-start(bf16[512,128]{1,0:T(8,128)(2,1)} %bitcast.4), channel_id=1, source_target_pairs={{0,4},{4,8},{8,12},{12,14},{14,10},{10,6},{6,2},{2,0},{1,5},{5,9},... | collective-permute-start | bytes 393224 | tf_op jit(solution)/shard_map/ppermute | solution.py:332
  5.1 0.0 collective-permute-start.3
  5.1 1.6 %prepare.1 = (s32[4,8]{1,0:T(4,128)S(1)}, bf16[4,1024,128]{2,1,0:T(8,128)(2,1)S(1)}, bf16[4,128,128]{2,1,0:T(8,128)(2,1)S(1)}, bf16[4,128,128]{2,1,0:T(8,128)(2,1)S(1)}) custom-call(s32[4,8]{1,0:T(4,128)} %bitcast.9, bf16[128,32,128]{2,1,0:T(8,128)(2,1)} %q_hbm.1, bf16[512,128]{1,0:T(8,128)(2,1)} %bitcast.8, bf16[512,128]{1,0:T(8,128)(2,1)} %bitcast.5), custom_call_target="tpu_custom_call" | custom-call | tf_op jit(solution)/shard_map/prepare/pallas_call | solution.py:55
  6.6 0.8 %collective-permute-done.refs_0_ = bf16[512,128]{1,0:T(8,128)(2,1)S(1)} collective-permute-done((bf16[512,128]{1,0:T(8,128)(2,1)}, bf16[512,128]{1,0:T(8,128)(2,1)S(1)}, u32[]{:S(2)}, u32[]{:S(2)}) %collective-permute-start) | collective-permute-done | bytes 131104 | tf_op jit(solution)/shard_map/ppermute | solution.py:332
  7.5 2.1 %collective-permute-done.1.refs_7_ = bf16[512,128]{1,0:T(8,128)(2,1)S(1)} collective-permute-done((bf16[512,128]{1,0:T(8,128)(2,1)}, bf16[512,128]{1,0:T(8,128)(2,1)S(1)}, u32[]{:S(2)}, u32[]{:S(2)}) %collective-permute-start.1) | collective-permute-done | bytes 131104 | tf_op jit(solution)/shard_map/ppermute | solution.py:332
  9.6 1.6 %collective-permute-start.4 = (bf16[512,128]{1,0:T(8,128)(2,1)S(1)}, bf16[512,128]{1,0:T(8,128)(2,1)S(1)}, u32[]{:S(2)}, u32[]{:S(2)}) collective-permute-start(bf16[512,128]{1,0:T(8,128)(2,1)S(1)} %collective-permute-done.refs_0_), channel_id=1, source_target_pairs={{0,4},{4,8},{8,12},{12,14},{14,10},{10,6},{6,2},{2,0},{1,5},{5,9},... | collective-permute-start | bytes 393224 | tf_op jit(solution)/shard_map/ppermute | solution.py:332
  11.1 0.4 %collective-permute-start.5 = (bf16[512,128]{1,0:T(8,128)(2,1)S(1)}, bf16[512,128]{1,0:T(8,128)(2,1)S(1)}, u32[]{:S(2)}, u32[]{:S(2)}) collective-permute-start(bf16[512,128]{1,0:T(8,128)(2,1)S(1)} %collective-permute-done.1.refs_7_), channel_id=1, source_target_pairs={{0,2},{4,0},{8,4},{12,8},{14,12},{10,14},{6,10},{2,6},{1,3},{5,1},... | collective-permute-start | bytes 393224 | tf_op jit(solution)/shard_map/ppermute | solution.py:332
  11.6 0.0 collective-permute-done.2.refs_6_
  11.6 0.0 collective-permute-done.3.refs_1_
  11.6 1.6 %collective-permute-start.6 = (bf16[512,128]{1,0:T(8,128)(2,1)S(1)}, bf16[512,128]{1,0:T(8,128)(2,1)S(1)}, u32[]{:S(2)}, u32[]{:S(2)}) collective-permute-start(bf16[512,128]{1,0:T(8,128)(2,1)S(1)} %collective-permute-done.2.refs_6_), channel_id=1, source_target_pairs={{0,4},{4,8},{8,12},{12,14},{14,10},{10,6},{6,2},{2,0},{1,5},{5,9},... | collective-permute-start | bytes 393224 | tf_op jit(solution)/shard_map/ppermute | solution.py:332
  13.2 0.5 %collective-permute-start.7 = (bf16[512,128]{1,0:T(8,128)(2,1)S(1)}, bf16[512,128]{1,0:T(8,128)(2,1)S(1)}, u32[]{:S(2)}, u32[]{:S(2)}) collective-permute-start(bf16[512,128]{1,0:T(8,128)(2,1)S(1)} %collective-permute-done.3.refs_1_), channel_id=1, source_target_pairs={{0,2},{4,0},{8,4},{12,8},{14,12},{10,14},{6,10},{2,6},{1,3},{5,1},... | collective-permute-start | bytes 393224 | tf_op jit(solution)/shard_map/ppermute | solution.py:332
  13.6 1.8 %collective-permute-done.4.refs_2_ = bf16[512,128]{1,0:T(8,128)(2,1)S(1)} collective-permute-done((bf16[512,128]{1,0:T(8,128)(2,1)S(1)}, bf16[512,128]{1,0:T(8,128)(2,1)S(1)}, u32[]{:S(2)}, u32[]{:S(2)}) %collective-permute-start.4) | collective-permute-done | bytes 131104 | tf_op jit(solution)/shard_map/ppermute | solution.py:332
  15.4 1.3 %collective-permute-done.5.refs_9_ = bf16[512,128]{1,0:T(8,128)(2,1)S(1)} collective-permute-done((bf16[512,128]{1,0:T(8,128)(2,1)S(1)}, bf16[512,128]{1,0:T(8,128)(2,1)S(1)}, u32[]{:S(2)}, u32[]{:S(2)}) %collective-permute-start.5) | collective-permute-done | bytes 131104 | tf_op jit(solution)/shard_map/ppermute | solution.py:332
  16.8 1.6 %collective-permute-start.8 = (bf16[512,128]{1,0:T(8,128)(2,1)S(1)}, bf16[512,128]{1,0:T(8,128)(2,1)S(1)}, u32[]{:S(2)}, u32[]{:S(2)}) collective-permute-start(bf16[512,128]{1,0:T(8,128)(2,1)S(1)} %collective-permute-done.4.refs_2_), channel_id=1, source_target_pairs={{0,4},{4,8},{8,12},{12,14},{14,10},{10,6},{6,2},{2,0},{1,5},{5,9},... | collective-permute-start | bytes 393224 | tf_op jit(solution)/shard_map/ppermute | solution.py:332
  18.3 0.4 %collective-permute-start.9 = (bf16[512,128]{1,0:T(8,128)(2,1)S(1)}, bf16[512,128]{1,0:T(8,128)(2,1)S(1)}, u32[]{:S(2)}, u32[]{:S(2)}) collective-permute-start(bf16[512,128]{1,0:T(8,128)(2,1)S(1)} %collective-permute-done.5.refs_9_), channel_id=1, source_target_pairs={{0,2},{4,0},{8,4},{12,8},{14,12},{10,14},{6,10},{2,6},{1,3},{5,1},... | collective-permute-start | bytes 393224 | tf_op jit(solution)/shard_map/ppermute | solution.py:332
  18.8 0.0 collective-permute-done.6.refs_8_
  18.8 0.5 %collective-permute-done.7.refs_3_ = bf16[512,128]{1,0:T(8,128)(2,1)S(1)} collective-permute-done((bf16[512,128]{1,0:T(8,128)(2,1)S(1)}, bf16[512,128]{1,0:T(8,128)(2,1)S(1)}, u32[]{:S(2)}, u32[]{:S(2)}) %collective-permute-start.7) | collective-permute-done | bytes 131104 | tf_op jit(solution)/shard_map/ppermute | solution.py:332
  19.3 1.6 %collective-permute-start.10 = (bf16[512,128]{1,0:T(8,128)(2,1)S(1)}, bf16[512,128]{1,0:T(8,128)(2,1)S(1)}, u32[]{:S(2)}, u32[]{:S(2)}) collective-permute-start(bf16[512,128]{1,0:T(8,128)(2,1)S(1)} %collective-permute-done.6.refs_8_), channel_id=1, source_target_pairs={{0,4},{4,8},{8,12},{12,14},{14,10},{10,6},{6,2},{2,0},{1,5},{5,9},... | collective-permute-start | bytes 393224 | tf_op jit(solution)/shard_map/ppermute | solution.py:332
  20.9 0.4 %collective-permute-start.11 = (bf16[512,128]{1,0:T(8,128)(2,1)S(1)}, bf16[512,128]{1,0:T(8,128)(2,1)S(1)}, u32[]{:S(2)}, u32[]{:S(2)}) collective-permute-start(bf16[512,128]{1,0:T(8,128)(2,1)S(1)} %collective-permute-done.7.refs_3_), channel_id=1, source_target_pairs={{0,2},{4,0},{8,4},{12,8},{14,12},{10,14},{6,10},{2,6},{1,3},{5,1},... | collective-permute-start | bytes 393224 | tf_op jit(solution)/shard_map/ppermute | solution.py:332
  21.3 0.4 %collective-permute-done.8.refs_4_ = bf16[512,128]{1,0:T(8,128)(2,1)S(1)} collective-permute-done((bf16[512,128]{1,0:T(8,128)(2,1)S(1)}, bf16[512,128]{1,0:T(8,128)(2,1)S(1)}, u32[]{:S(2)}, u32[]{:S(2)}) %collective-permute-start.8) | collective-permute-done | bytes 131104 | tf_op jit(solution)/shard_map/ppermute | solution.py:332
  21.7 2.9 %collective-permute-done.9.refs_11_ = bf16[512,128]{1,0:T(8,128)(2,1)S(1)} collective-permute-done((bf16[512,128]{1,0:T(8,128)(2,1)S(1)}, bf16[512,128]{1,0:T(8,128)(2,1)S(1)}, u32[]{:S(2)}, u32[]{:S(2)}) %collective-permute-start.9) | collective-permute-done | bytes 131104 | tf_op jit(solution)/shard_map/ppermute | solution.py:332
  24.6 0.4 %collective-permute-start.12 = (bf16[512,128]{1,0:T(8,128)(2,1)S(1)}, bf16[512,128]{1,0:T(8,128)(2,1)S(1)}, u32[]{:S(2)}, u32[]{:S(2)}) collective-permute-start(bf16[512,128]{1,0:T(8,128)(2,1)S(1)} %broadcast_select_fusion.1), channel_id=1, source_target_pairs={{0,2},{4,6},{8,12},{12,14},{14,10},{10,8},{6,4},{2,0},{1,3},{5,7},... | collective-permute-start | bytes 393224 | tf_op jit(solution)/shard_map/ppermute | solution.py:332
  25.1 0.0 collective-permute-start.13
  25.1 0.0 collective-permute-done.10.refs_10_
  25.2 1.0 %collective-permute-done.11.refs_5_ = bf16[512,128]{1,0:T(8,128)(2,1)S(1)} collective-permute-done((bf16[512,128]{1,0:T(8,128)(2,1)S(1)}, bf16[512,128]{1,0:T(8,128)(2,1)S(1)}, u32[]{:S(2)}, u32[]{:S(2)}) %collective-permute-start.11) | collective-permute-done | bytes 131104 | tf_op jit(solution)/shard_map/ppermute | solution.py:332
  26.1 2.5 %attend.1 = (bf16[128,32,128]{2,1,0:T(8,128)(2,1)}, f32[4,1024,128]{2,1,0:T(8,128)S(1)}, f32[4,1024,256]{2,1,0:T(8,128)S(1)}) custom-call(s32[4,8]{1,0:T(4,128)S(1)} %get-tuple-element.34.lists_ref, bf16[4,1024,128]{2,1,0:T(8,128)(2,1)S(1)} %get-tuple-element.35.q_ref, bf16[4,128,128]{2,1,0:T(8,128)(2,1)S(1)} %get-tuple-element.36.k_own_ref, ...), custom_call_target="tpu_custom_call" | custom-call | tf_op jit(solution)/shard_map/attend/pallas_call | solution.py:225
  28.6 1.0 %collective-permute-done.12.k_ref = bf16[512,128]{1,0:T(8,128)(2,1)S(1)} collective-permute-done((bf16[512,128]{1,0:T(8,128)(2,1)S(1)}, bf16[512,128]{1,0:T(8,128)(2,1)S(1)}, u32[]{:S(2)}, u32[]{:S(2)}) %collective-permute-start.12) | collective-permute-done | bytes 131104 | tf_op jit(solution)/shard_map/ppermute | solution.py:332
  29.6 0.5 %collective-permute-done.13.v_ref = bf16[512,128]{1,0:T(8,128)(2,1)S(1)} collective-permute-done((bf16[512,128]{1,0:T(8,128)(2,1)S(1)}, bf16[512,128]{1,0:T(8,128)(2,1)S(1)}, u32[]{:S(2)}, u32[]{:S(2)}) %collective-permute-start.13) | collective-permute-done | bytes 131104 | tf_op jit(solution)/shard_map/ppermute | solution.py:332
  30.1 0.2 attend_last.1
  (2 shorter events, 0.0 us)
Async XLA Ops:
  0.0 7.5 %collective-permute-start = (bf16[512,128]{1,0:T(8,128)(2,1)}, bf16[512,128]{1,0:T(8,128)(2,1)S(1)}, u32[]{:S(2)}, u32[]{:S(2)}) collective-permute-start(bf16[512,128]{1,0:T(8,128)(2,1)} %bitcast.6), channel_id=1, source_target_pairs={{0,4},{4,8},{8,12},{12,14},{14,10},{10,6},{6,2},{2,0},{1,5},{5,9},... | collective-permute-start | bytes 393224 | tf_op jit(solution)/shard_map/ppermute | solution.py:332
  3.0 6.5 %collective-permute-start.1 = (bf16[512,128]{1,0:T(8,128)(2,1)}, bf16[512,128]{1,0:T(8,128)(2,1)S(1)}, u32[]{:S(2)}, u32[]{:S(2)}) collective-permute-start(bf16[512,128]{1,0:T(8,128)(2,1)} %bitcast.3), channel_id=1, source_target_pairs={{0,2},{4,0},{8,4},{12,8},{14,12},{10,14},{6,10},{2,6},{1,3},{5,1},... | collective-permute-start | bytes 393224 | tf_op jit(solution)/shard_map/ppermute | solution.py:332
  3.0 8.6 %collective-permute-start.2 = (bf16[512,128]{1,0:T(8,128)(2,1)}, bf16[512,128]{1,0:T(8,128)(2,1)S(1)}, u32[]{:S(2)}, u32[]{:S(2)}) collective-permute-start(bf16[512,128]{1,0:T(8,128)(2,1)} %bitcast.4), channel_id=1, source_target_pairs={{0,4},{4,8},{8,12},{12,14},{14,10},{10,6},{6,2},{2,0},{1,5},{5,9},... | collective-permute-start | bytes 393224 | tf_op jit(solution)/shard_map/ppermute | solution.py:332
  5.1 6.5 %collective-permute-start.3 = (bf16[512,128]{1,0:T(8,128)(2,1)}, bf16[512,128]{1,0:T(8,128)(2,1)S(1)}, u32[]{:S(2)}, u32[]{:S(2)}) collective-permute-start(bf16[512,128]{1,0:T(8,128)(2,1)} %bitcast.7), channel_id=1, source_target_pairs={{0,2},{4,0},{8,4},{12,8},{14,12},{10,14},{6,10},{2,6},{1,3},{5,1},... | collective-permute-start | bytes 393224 | tf_op jit(solution)/shard_map/ppermute | solution.py:332
  9.6 5.9 %collective-permute-start.4 = (bf16[512,128]{1,0:T(8,128)(2,1)S(1)}, bf16[512,128]{1,0:T(8,128)(2,1)S(1)}, u32[]{:S(2)}, u32[]{:S(2)}) collective-permute-start(bf16[512,128]{1,0:T(8,128)(2,1)S(1)} %collective-permute-done.refs_0_), channel_id=1, source_target_pairs={{0,4},{4,8},{8,12},{12,14},{14,10},{10,6},{6,2},{2,0},{1,5},{5,9},... | collective-permute-start | bytes 393224 | tf_op jit(solution)/shard_map/ppermute | solution.py:332
  11.1 5.6 %collective-permute-start.5 = (bf16[512,128]{1,0:T(8,128)(2,1)S(1)}, bf16[512,128]{1,0:T(8,128)(2,1)S(1)}, u32[]{:S(2)}, u32[]{:S(2)}) collective-permute-start(bf16[512,128]{1,0:T(8,128)(2,1)S(1)} %collective-permute-done.1.refs_7_), channel_id=1, source_target_pairs={{0,2},{4,0},{8,4},{12,8},{14,12},{10,14},{6,10},{2,6},{1,3},{5,1},... | collective-permute-start | bytes 393224 | tf_op jit(solution)/shard_map/ppermute | solution.py:332
  11.6 7.2 %collective-permute-start.6 = (bf16[512,128]{1,0:T(8,128)(2,1)S(1)}, bf16[512,128]{1,0:T(8,128)(2,1)S(1)}, u32[]{:S(2)}, u32[]{:S(2)}) collective-permute-start(bf16[512,128]{1,0:T(8,128)(2,1)S(1)} %collective-permute-done.2.refs_6_), channel_id=1, source_target_pairs={{0,4},{4,8},{8,12},{12,14},{14,10},{10,6},{6,2},{2,0},{1,5},{5,9},... | collective-permute-start | bytes 393224 | tf_op jit(solution)/shard_map/ppermute | solution.py:332
  13.2 6.1 %collective-permute-start.7 = (bf16[512,128]{1,0:T(8,128)(2,1)S(1)}, bf16[512,128]{1,0:T(8,128)(2,1)S(1)}, u32[]{:S(2)}, u32[]{:S(2)}) collective-permute-start(bf16[512,128]{1,0:T(8,128)(2,1)S(1)} %collective-permute-done.3.refs_1_), channel_id=1, source_target_pairs={{0,2},{4,0},{8,4},{12,8},{14,12},{10,14},{6,10},{2,6},{1,3},{5,1},... | collective-permute-start | bytes 393224 | tf_op jit(solution)/shard_map/ppermute | solution.py:332
  16.8 5.0 %collective-permute-start.8 = (bf16[512,128]{1,0:T(8,128)(2,1)S(1)}, bf16[512,128]{1,0:T(8,128)(2,1)S(1)}, u32[]{:S(2)}, u32[]{:S(2)}) collective-permute-start(bf16[512,128]{1,0:T(8,128)(2,1)S(1)} %collective-permute-done.4.refs_2_), channel_id=1, source_target_pairs={{0,4},{4,8},{8,12},{12,14},{14,10},{10,6},{6,2},{2,0},{1,5},{5,9},... | collective-permute-start | bytes 393224 | tf_op jit(solution)/shard_map/ppermute | solution.py:332
  18.3 6.3 %collective-permute-start.9 = (bf16[512,128]{1,0:T(8,128)(2,1)S(1)}, bf16[512,128]{1,0:T(8,128)(2,1)S(1)}, u32[]{:S(2)}, u32[]{:S(2)}) collective-permute-start(bf16[512,128]{1,0:T(8,128)(2,1)S(1)} %collective-permute-done.5.refs_9_), channel_id=1, source_target_pairs={{0,2},{4,0},{8,4},{12,8},{14,12},{10,14},{6,10},{2,6},{1,3},{5,1},... | collective-permute-start | bytes 393224 | tf_op jit(solution)/shard_map/ppermute | solution.py:332
  19.3 5.9 %collective-permute-start.10 = (bf16[512,128]{1,0:T(8,128)(2,1)S(1)}, bf16[512,128]{1,0:T(8,128)(2,1)S(1)}, u32[]{:S(2)}, u32[]{:S(2)}) collective-permute-start(bf16[512,128]{1,0:T(8,128)(2,1)S(1)} %collective-permute-done.6.refs_8_), channel_id=1, source_target_pairs={{0,4},{4,8},{8,12},{12,14},{14,10},{10,6},{6,2},{2,0},{1,5},{5,9},... | collective-permute-start | bytes 393224 | tf_op jit(solution)/shard_map/ppermute | solution.py:332
  20.9 5.2 %collective-permute-start.11 = (bf16[512,128]{1,0:T(8,128)(2,1)S(1)}, bf16[512,128]{1,0:T(8,128)(2,1)S(1)}, u32[]{:S(2)}, u32[]{:S(2)}) collective-permute-start(bf16[512,128]{1,0:T(8,128)(2,1)S(1)} %collective-permute-done.7.refs_3_), channel_id=1, source_target_pairs={{0,2},{4,0},{8,4},{12,8},{14,12},{10,14},{6,10},{2,6},{1,3},{5,1},... | collective-permute-start | bytes 393224 | tf_op jit(solution)/shard_map/ppermute | solution.py:332
  24.6 5.0 %collective-permute-start.12 = (bf16[512,128]{1,0:T(8,128)(2,1)S(1)}, bf16[512,128]{1,0:T(8,128)(2,1)S(1)}, u32[]{:S(2)}, u32[]{:S(2)}) collective-permute-start(bf16[512,128]{1,0:T(8,128)(2,1)S(1)} %broadcast_select_fusion.1), channel_id=1, source_target_pairs={{0,2},{4,6},{8,12},{12,14},{14,10},{10,8},{6,4},{2,0},{1,3},{5,7},... | collective-permute-start | bytes 393224 | tf_op jit(solution)/shard_map/ppermute | solution.py:332
  25.1 5.0 %collective-permute-start.13 = (bf16[512,128]{1,0:T(8,128)(2,1)S(1)}, bf16[512,128]{1,0:T(8,128)(2,1)S(1)}, u32[]{:S(2)}, u32[]{:S(2)}) collective-permute-start(bf16[512,128]{1,0:T(8,128)(2,1)S(1)} %broadcast_select_fusion), channel_id=1, source_target_pairs={{0,4},{4,0},{8,10},{12,8},{14,12},{10,14},{6,2},{2,6},{1,5},{5,1},... | collective-permute-start | bytes 393224 | tf_op jit(solution)/shard_map/ppermute | solution.py:332

commit v13 on v12

--- a/solution.py
+++ b/solution.py
@@ -9,7 +9,7 @@
 from jax.sharding import PartitionSpec as P
 
 NO_KEY = -1e30
-ROW_CHUNK = 256
+ROW_CHUNK = 512
 ROUND = (8, 16)
 HEADS_OUT = 16
 

time: 30.6 us -> 30.6 us (level)
  Pallas kernels: 4.26 us -> 3.89 us
    ppermute x14, waiting for transfers between devices: 12.3 us -> 12.6 us  [send(): lax.ppermute(x, 'seq', [(ring[p], ring[to]) for p, to in sorted(step.item...]
    pallas_call x1, Pallas kernels: 2.53 us -> 2.17 us  [attend(): pl.pallas_call(functools.partial(attend_kernel, codes=codes, code=code, l...]
  transfers between devices with their start and end apart: 14 -> 14, of which waited for: 10 -> 10; matrix products, arithmetic and copies ran while one was open for 0% -> 0% of each run, Pallas kernels for 13% -> 12%
where the time goes in v13:
time: 30.6 us; the launch traced here: 30.4 us
  starting transfers between devices  13.7 us (45%)
  waiting for transfers between devices  12.6 us (41%)
  Pallas kernels  3.89 us (13%)
    ppermute x14, starting transfers between devices, send(): lax.ppermute(x, 'seq', [(ring[p], ring[to]) for p, to in sorted(step.item...  13.7 us
    ppermute x14, waiting for transfers between devices, send(): lax.ppermute(x, 'seq', [(ring[p], ring[to]) for p, to in sorted(step.item...  12.6 us
    pallas_call x1, Pallas kernels, attend(): pl.pallas_call(functools.partial(attend_kernel, codes=codes, code=code, l...  2.17 us
    pallas_call x1, Pallas kernels, prepare(): pl.pallas_call(functools.partial(prepare_kernel, kv_dev=kv_dev), out_shap...  1.57 us
  transfers between devices with their start and end apart: 14, of which 10 were waited for; matrix products, arithmetic and copies ran while one was open for 0% of the time, Pallas kernels for 12%

profile of v13, /device:TPU:0, one launch (start us, length us, event | category | flops | bytes accessed | tf_op | source)
XLA Modules:
  0.0 30.4 jit_solution(7710497367779782288)
XLA Ops:
  0.0 3.0 %collective-permute-start = (bf16[512,128]{1,0:T(8,128)(2,1)}, bf16[512,128]{1,0:T(8,128)(2,1)S(1)}, u32[]{:S(2)}, u32[]{:S(2)}) collective-permute-start(bf16[512,128]{1,0:T(8,128)(2,1)} %bitcast.6), channel_id=1, source_target_pairs={{0,4},{4,8},{8,12},{12,14},{14,10},{10,6},{6,2},{2,0},{1,5},{5,9},... | collective-permute-start | bytes 393224 | tf_op jit(solution)/shard_map/ppermute | solution.py:332
  3.0 0.0 collective-permute-start.1
  3.0 2.0 %collective-permute-start.2 = (bf16[512,128]{1,0:T(8,128)(2,1)}, bf16[512,128]{1,0:T(8,128)(2,1)S(1)}, u32[]{:S(2)}, u32[]{:S(2)}) collective-permute-start(bf16[512,128]{1,0:T(8,128)(2,1)} %bitcast.4), channel_id=1, source_target_pairs={{0,4},{4,8},{8,12},{12,14},{14,10},{10,6},{6,2},{2,0},{1,5},{5,9},... | collective-permute-start | bytes 393224 | tf_op jit(solution)/shard_map/ppermute | solution.py:332
  5.1 0.0 collective-permute-start.3
  5.1 1.6 %prepare.1 = (s32[4,8]{1,0:T(4,128)S(1)}, bf16[4,1024,128]{2,1,0:T(8,128)(2,1)S(1)}, bf16[4,128,128]{2,1,0:T(8,128)(2,1)S(1)}, bf16[4,128,128]{2,1,0:T(8,128)(2,1)S(1)}) custom-call(s32[4,8]{1,0:T(4,128)} %bitcast.9, bf16[128,32,128]{2,1,0:T(8,128)(2,1)} %q_hbm.1, bf16[512,128]{1,0:T(8,128)(2,1)} %bitcast.8, bf16[512,128]{1,0:T(8,128)(2,1)} %bitcast.5), custom_call_target="tpu_custom_call" | custom-call | tf_op jit(solution)/shard_map/prepare/pallas_call | solution.py:55
  6.6 0.8 %collective-permute-done.refs_0_ = bf16[512,128]{1,0:T(8,128)(2,1)S(1)} collective-permute-done((bf16[512,128]{1,0:T(8,128)(2,1)}, bf16[512,128]{1,0:T(8,128)(2,1)S(1)}, u32[]{:S(2)}, u32[]{:S(2)}) %collective-permute-start) | collective-permute-done | bytes 131104 | tf_op jit(solution)/shard_map/ppermute | solution.py:332
  7.5 2.1 %collective-permute-done.1.refs_7_ = bf16[512,128]{1,0:T(8,128)(2,1)S(1)} collective-permute-done((bf16[512,128]{1,0:T(8,128)(2,1)}, bf16[512,128]{1,0:T(8,128)(2,1)S(1)}, u32[]{:S(2)}, u32[]{:S(2)}) %collective-permute-start.1) | collective-permute-done | bytes 131104 | tf_op jit(solution)/shard_map/ppermute | solution.py:332
  9.6 1.6 %collective-permute-start.4 = (bf16[512,128]{1,0:T(8,128)(2,1)S(1)}, bf16[512,128]{1,0:T(8,128)(2,1)S(1)}, u32[]{:S(2)}, u32[]{:S(2)}) collective-permute-start(bf16[512,128]{1,0:T(8,128)(2,1)S(1)} %collective-permute-done.refs_0_), channel_id=1, source_target_pairs={{0,4},{4,8},{8,12},{12,14},{14,10},{10,6},{6,2},{2,0},{1,5},{5,9},... | collective-permute-start | bytes 393224 | tf_op jit(solution)/shard_map/ppermute | solution.py:332
  11.1 0.4 %collective-permute-start.5 = (bf16[512,128]{1,0:T(8,128)(2,1)S(1)}, bf16[512,128]{1,0:T(8,128)(2,1)S(1)}, u32[]{:S(2)}, u32[]{:S(2)}) collective-permute-start(bf16[512,128]{1,0:T(8,128)(2,1)S(1)} %collective-permute-done.1.refs_7_), channel_id=1, source_target_pairs={{0,2},{4,0},{8,4},{12,8},{14,12},{10,14},{6,10},{2,6},{1,3},{5,1},... | collective-permute-start | bytes 393224 | tf_op jit(solution)/shard_map/ppermute | solution.py:332
  11.6 0.0 collective-permute-done.2.refs_6_
  11.6 0.0 collective-permute-done.3.refs_1_
  11.6 1.6 %collective-permute-start.6 = (bf16[512,128]{1,0:T(8,128)(2,1)S(1)}, bf16[512,128]{1,0:T(8,128)(2,1)S(1)}, u32[]{:S(2)}, u32[]{:S(2)}) collective-permute-start(bf16[512,128]{1,0:T(8,128)(2,1)S(1)} %collective-permute-done.2.refs_6_), channel_id=1, source_target_pairs={{0,4},{4,8},{8,12},{12,14},{14,10},{10,6},{6,2},{2,0},{1,5},{5,9},... | collective-permute-start | bytes 393224 | tf_op jit(solution)/shard_map/ppermute | solution.py:332
  13.2 0.5 %collective-permute-start.7 = (bf16[512,128]{1,0:T(8,128)(2,1)S(1)}, bf16[512,128]{1,0:T(8,128)(2,1)S(1)}, u32[]{:S(2)}, u32[]{:S(2)}) collective-permute-start(bf16[512,128]{1,0:T(8,128)(2,1)S(1)} %collective-permute-done.3.refs_1_), channel_id=1, source_target_pairs={{0,2},{4,0},{8,4},{12,8},{14,12},{10,14},{6,10},{2,6},{1,3},{5,1},... | collective-permute-start | bytes 393224 | tf_op jit(solution)/shard_map/ppermute | solution.py:332
  13.6 1.8 %collective-permute-done.4.refs_2_ = bf16[512,128]{1,0:T(8,128)(2,1)S(1)} collective-permute-done((bf16[512,128]{1,0:T(8,128)(2,1)S(1)}, bf16[512,128]{1,0:T(8,128)(2,1)S(1)}, u32[]{:S(2)}, u32[]{:S(2)}) %collective-permute-start.4) | collective-permute-done | bytes 131104 | tf_op jit(solution)/shard_map/ppermute | solution.py:332
  15.4 1.3 %collective-permute-done.5.refs_9_ = bf16[512,128]{1,0:T(8,128)(2,1)S(1)} collective-permute-done((bf16[512,128]{1,0:T(8,128)(2,1)S(1)}, bf16[512,128]{1,0:T(8,128)(2,1)S(1)}, u32[]{:S(2)}, u32[]{:S(2)}) %collective-permute-start.5) | collective-permute-done | bytes 131104 | tf_op jit(solution)/shard_map/ppermute | solution.py:332
  16.8 1.6 %collective-permute-start.8 = (bf16[512,128]{1,0:T(8,128)(2,1)S(1)}, bf16[512,128]{1,0:T(8,128)(2,1)S(1)}, u32[]{:S(2)}, u32[]{:S(2)}) collective-permute-start(bf16[512,128]{1,0:T(8,128)(2,1)S(1)} %collective-permute-done.4.refs_2_), channel_id=1, source_target_pairs={{0,4},{4,8},{8,12},{12,14},{14,10},{10,6},{6,2},{2,0},{1,5},{5,9},... | collective-permute-start | bytes 393224 | tf_op jit(solution)/shard_map/ppermute | solution.py:332
  18.3 0.4 %collective-permute-start.9 = (bf16[512,128]{1,0:T(8,128)(2,1)S(1)}, bf16[512,128]{1,0:T(8,128)(2,1)S(1)}, u32[]{:S(2)}, u32[]{:S(2)}) collective-permute-start(bf16[512,128]{1,0:T(8,128)(2,1)S(1)} %collective-permute-done.5.refs_9_), channel_id=1, source_target_pairs={{0,2},{4,0},{8,4},{12,8},{14,12},{10,14},{6,10},{2,6},{1,3},{5,1},... | collective-permute-start | bytes 393224 | tf_op jit(solution)/shard_map/ppermute | solution.py:332
  18.8 0.0 collective-permute-done.6.refs_8_
  18.8 0.5 %collective-permute-done.7.refs_3_ = bf16[512,128]{1,0:T(8,128)(2,1)S(1)} collective-permute-done((bf16[512,128]{1,0:T(8,128)(2,1)S(1)}, bf16[512,128]{1,0:T(8,128)(2,1)S(1)}, u32[]{:S(2)}, u32[]{:S(2)}) %collective-permute-start.7) | collective-permute-done | bytes 131104 | tf_op jit(solution)/shard_map/ppermute | solution.py:332
  19.3 1.6 %collective-permute-start.10 = (bf16[512,128]{1,0:T(8,128)(2,1)S(1)}, bf16[512,128]{1,0:T(8,128)(2,1)S(1)}, u32[]{:S(2)}, u32[]{:S(2)}) collective-permute-start(bf16[512,128]{1,0:T(8,128)(2,1)S(1)} %collective-permute-done.6.refs_8_), channel_id=1, source_target_pairs={{0,4},{4,8},{8,12},{12,14},{14,10},{10,6},{6,2},{2,0},{1,5},{5,9},... | collective-permute-start | bytes 393224 | tf_op jit(solution)/shard_map/ppermute | solution.py:332
  20.9 0.4 %collective-permute-start.11 = (bf16[512,128]{1,0:T(8,128)(2,1)S(1)}, bf16[512,128]{1,0:T(8,128)(2,1)S(1)}, u32[]{:S(2)}, u32[]{:S(2)}) collective-permute-start(bf16[512,128]{1,0:T(8,128)(2,1)S(1)} %collective-permute-done.7.refs_3_), channel_id=1, source_target_pairs={{0,2},{4,0},{8,4},{12,8},{14,12},{10,14},{6,10},{2,6},{1,3},{5,1},... | collective-permute-start | bytes 393224 | tf_op jit(solution)/shard_map/ppermute | solution.py:332
  21.3 0.4 %collective-permute-done.8.refs_4_ = bf16[512,128]{1,0:T(8,128)(2,1)S(1)} collective-permute-done((bf16[512,128]{1,0:T(8,128)(2,1)S(1)}, bf16[512,128]{1,0:T(8,128)(2,1)S(1)}, u32[]{:S(2)}, u32[]{:S(2)}) %collective-permute-start.8) | collective-permute-done | bytes 131104 | tf_op jit(solution)/shard_map/ppermute | solution.py:332
  21.7 2.9 %collective-permute-done.9.refs_11_ = bf16[512,128]{1,0:T(8,128)(2,1)S(1)} collective-permute-done((bf16[512,128]{1,0:T(8,128)(2,1)S(1)}, bf16[512,128]{1,0:T(8,128)(2,1)S(1)}, u32[]{:S(2)}, u32[]{:S(2)}) %collective-permute-start.9) | collective-permute-done | bytes 131104 | tf_op jit(solution)/shard_map/ppermute | solution.py:332
  24.6 0.4 %collective-permute-start.12 = (bf16[512,128]{1,0:T(8,128)(2,1)S(1)}, bf16[512,128]{1,0:T(8,128)(2,1)S(1)}, u32[]{:S(2)}, u32[]{:S(2)}) collective-permute-start(bf16[512,128]{1,0:T(8,128)(2,1)S(1)} %broadcast_select_fusion.1), channel_id=1, source_target_pairs={{0,2},{4,6},{8,12},{12,14},{14,10},{10,8},{6,4},{2,0},{1,3},{5,7},... | collective-permute-start | bytes 393224 | tf_op jit(solution)/shard_map/ppermute | solution.py:332
  25.1 0.0 collective-permute-start.13
  25.1 0.0 collective-permute-done.10.refs_10_
  25.2 1.0 %collective-permute-done.11.refs_5_ = bf16[512,128]{1,0:T(8,128)(2,1)S(1)} collective-permute-done((bf16[512,128]{1,0:T(8,128)(2,1)S(1)}, bf16[512,128]{1,0:T(8,128)(2,1)S(1)}, u32[]{:S(2)}, u32[]{:S(2)}) %collective-permute-start.11) | collective-permute-done | bytes 131104 | tf_op jit(solution)/shard_map/ppermute | solution.py:332
  26.1 2.2 %attend.1 = (bf16[128,32,128]{2,1,0:T(8,128)(2,1)}, f32[4,1024,128]{2,1,0:T(8,128)S(1)}, f32[4,1024,256]{2,1,0:T(8,128)S(1)}) custom-call(s32[4,8]{1,0:T(4,128)S(1)} %get-tuple-element.34.lists_ref, bf16[4,1024,128]{2,1,0:T(8,128)(2,1)S(1)} %get-tuple-element.35.q_ref, bf16[4,128,128]{2,1,0:T(8,128)(2,1)S(1)} %get-tuple-element.36.k_own_ref, ...), custom_call_target="tpu_custom_call" | custom-call | tf_op jit(solution)/shard_map/attend/pallas_call | solution.py:225
  28.3 1.4 %collective-permute-done.12.k_ref = bf16[512,128]{1,0:T(8,128)(2,1)S(1)} collective-permute-done((bf16[512,128]{1,0:T(8,128)(2,1)S(1)}, bf16[512,128]{1,0:T(8,128)(2,1)S(1)}, u32[]{:S(2)}, u32[]{:S(2)}) %collective-permute-start.12) | collective-permute-done | bytes 131104 | tf_op jit(solution)/shard_map/ppermute | solution.py:332
  29.6 0.5 %collective-permute-done.13.v_ref = bf16[512,128]{1,0:T(8,128)(2,1)S(1)} collective-permute-done((bf16[512,128]{1,0:T(8,128)(2,1)S(1)}, bf16[512,128]{1,0:T(8,128)(2,1)S(1)}, u32[]{:S(2)}, u32[]{:S(2)}) %collective-permute-start.13) | collective-permute-done | bytes 131104 | tf_op jit(solution)/shard_map/ppermute | solution.py:332
  30.1 0.2 attend_last.1
  (2 shorter events, 0.0 us)
Async XLA Ops:
  0.0 7.5 %collective-permute-start = (bf16[512,128]{1,0:T(8,128)(2,1)}, bf16[512,128]{1,0:T(8,128)(2,1)S(1)}, u32[]{:S(2)}, u32[]{:S(2)}) collective-permute-start(bf16[512,128]{1,0:T(8,128)(2,1)} %bitcast.6), channel_id=1, source_target_pairs={{0,4},{4,8},{8,12},{12,14},{14,10},{10,6},{6,2},{2,0},{1,5},{5,9},... | collective-permute-start | bytes 393224 | tf_op jit(solution)/shard_map/ppermute | solution.py:332
  3.0 6.5 %collective-permute-start.1 = (bf16[512,128]{1,0:T(8,128)(2,1)}, bf16[512,128]{1,0:T(8,128)(2,1)S(1)}, u32[]{:S(2)}, u32[]{:S(2)}) collective-permute-start(bf16[512,128]{1,0:T(8,128)(2,1)} %bitcast.3), channel_id=1, source_target_pairs={{0,2},{4,0},{8,4},{12,8},{14,12},{10,14},{6,10},{2,6},{1,3},{5,1},... | collective-permute-start | bytes 393224 | tf_op jit(solution)/shard_map/ppermute | solution.py:332
  3.0 8.6 %collective-permute-start.2 = (bf16[512,128]{1,0:T(8,128)(2,1)}, bf16[512,128]{1,0:T(8,128)(2,1)S(1)}, u32[]{:S(2)}, u32[]{:S(2)}) collective-permute-start(bf16[512,128]{1,0:T(8,128)(2,1)} %bitcast.4), channel_id=1, source_target_pairs={{0,4},{4,8},{8,12},{12,14},{14,10},{10,6},{6,2},{2,0},{1,5},{5,9},... | collective-permute-start | bytes 393224 | tf_op jit(solution)/shard_map/ppermute | solution.py:332
  5.1 6.5 %collective-permute-start.3 = (bf16[512,128]{1,0:T(8,128)(2,1)}, bf16[512,128]{1,0:T(8,128)(2,1)S(1)}, u32[]{:S(2)}, u32[]{:S(2)}) collective-permute-start(bf16[512,128]{1,0:T(8,128)(2,1)} %bitcast.7), channel_id=1, source_target_pairs={{0,2},{4,0},{8,4},{12,8},{14,12},{10,14},{6,10},{2,6},{1,3},{5,1},... | collective-permute-start | bytes 393224 | tf_op jit(solution)/shard_map/ppermute | solution.py:332
  9.6 5.9 %collective-permute-start.4 = (bf16[512,128]{1,0:T(8,128)(2,1)S(1)}, bf16[512,128]{1,0:T(8,128)(2,1)S(1)}, u32[]{:S(2)}, u32[]{:S(2)}) collective-permute-start(bf16[512,128]{1,0:T(8,128)(2,1)S(1)} %collective-permute-done.refs_0_), channel_id=1, source_target_pairs={{0,4},{4,8},{8,12},{12,14},{14,10},{10,6},{6,2},{2,0},{1,5},{5,9},... | collective-permute-start | bytes 393224 | tf_op jit(solution)/shard_map/ppermute | solution.py:332
  11.1 5.6 %collective-permute-start.5 = (bf16[512,128]{1,0:T(8,128)(2,1)S(1)}, bf16[512,128]{1,0:T(8,128)(2,1)S(1)}, u32[]{:S(2)}, u32[]{:S(2)}) collective-permute-start(bf16[512,128]{1,0:T(8,128)(2,1)S(1)} %collective-permute-done.1.refs_7_), channel_id=1, source_target_pairs={{0,2},{4,0},{8,4},{12,8},{14,12},{10,14},{6,10},{2,6},{1,3},{5,1},... | collective-permute-start | bytes 393224 | tf_op jit(solution)/shard_map/ppermute | solution.py:332
  11.6 7.2 %collective-permute-start.6 = (bf16[512,128]{1,0:T(8,128)(2,1)S(1)}, bf16[512,128]{1,0:T(8,128)(2,1)S(1)}, u32[]{:S(2)}, u32[]{:S(2)}) collective-permute-start(bf16[512,128]{1,0:T(8,128)(2,1)S(1)} %collective-permute-done.2.refs_6_), channel_id=1, source_target_pairs={{0,4},{4,8},{8,12},{12,14},{14,10},{10,6},{6,2},{2,0},{1,5},{5,9},... | collective-permute-start | bytes 393224 | tf_op jit(solution)/shard_map/ppermute | solution.py:332
  13.2 6.1 %collective-permute-start.7 = (bf16[512,128]{1,0:T(8,128)(2,1)S(1)}, bf16[512,128]{1,0:T(8,128)(2,1)S(1)}, u32[]{:S(2)}, u32[]{:S(2)}) collective-permute-start(bf16[512,128]{1,0:T(8,128)(2,1)S(1)} %collective-permute-done.3.refs_1_), channel_id=1, source_target_pairs={{0,2},{4,0},{8,4},{12,8},{14,12},{10,14},{6,10},{2,6},{1,3},{5,1},... | collective-permute-start | bytes 393224 | tf_op jit(solution)/shard_map/ppermute | solution.py:332
  16.8 5.0 %collective-permute-start.8 = (bf16[512,128]{1,0:T(8,128)(2,1)S(1)}, bf16[512,128]{1,0:T(8,128)(2,1)S(1)}, u32[]{:S(2)}, u32[]{:S(2)}) collective-permute-start(bf16[512,128]{1,0:T(8,128)(2,1)S(1)} %collective-permute-done.4.refs_2_), channel_id=1, source_target_pairs={{0,4},{4,8},{8,12},{12,14},{14,10},{10,6},{6,2},{2,0},{1,5},{5,9},... | collective-permute-start | bytes 393224 | tf_op jit(solution)/shard_map/ppermute | solution.py:332
  18.3 6.3 %collective-permute-start.9 = (bf16[512,128]{1,0:T(8,128)(2,1)S(1)}, bf16[512,128]{1,0:T(8,128)(2,1)S(1)}, u32[]{:S(2)}, u32[]{:S(2)}) collective-permute-start(bf16[512,128]{1,0:T(8,128)(2,1)S(1)} %collective-permute-done.5.refs_9_), channel_id=1, source_target_pairs={{0,2},{4,0},{8,4},{12,8},{14,12},{10,14},{6,10},{2,6},{1,3},{5,1},... | collective-permute-start | bytes 393224 | tf_op jit(solution)/shard_map/ppermute | solution.py:332
  19.3 5.9 %collective-permute-start.10 = (bf16[512,128]{1,0:T(8,128)(2,1)S(1)}, bf16[512,128]{1,0:T(8,128)(2,1)S(1)}, u32[]{:S(2)}, u32[]{:S(2)}) collective-permute-start(bf16[512,128]{1,0:T(8,128)(2,1)S(1)} %collective-permute-done.6.refs_8_), channel_id=1, source_target_pairs={{0,4},{4,8},{8,12},{12,14},{14,10},{10,6},{6,2},{2,0},{1,5},{5,9},... | collective-permute-start | bytes 393224 | tf_op jit(solution)/shard_map/ppermute | solution.py:332
  20.9 5.2 %collective-permute-start.11 = (bf16[512,128]{1,0:T(8,128)(2,1)S(1)}, bf16[512,128]{1,0:T(8,128)(2,1)S(1)}, u32[]{:S(2)}, u32[]{:S(2)}) collective-permute-start(bf16[512,128]{1,0:T(8,128)(2,1)S(1)} %collective-permute-done.7.refs_3_), channel_id=1, source_target_pairs={{0,2},{4,0},{8,4},{12,8},{14,12},{10,14},{6,10},{2,6},{1,3},{5,1},... | collective-permute-start | bytes 393224 | tf_op jit(solution)/shard_map/ppermute | solution.py:332
  24.6 5.0 %collective-permute-start.12 = (bf16[512,128]{1,0:T(8,128)(2,1)S(1)}, bf16[512,128]{1,0:T(8,128)(2,1)S(1)}, u32[]{:S(2)}, u32[]{:S(2)}) collective-permute-start(bf16[512,128]{1,0:T(8,128)(2,1)S(1)} %broadcast_select_fusion.1), channel_id=1, source_target_pairs={{0,2},{4,6},{8,12},{12,14},{14,10},{10,8},{6,4},{2,0},{1,3},{5,7},... | collective-permute-start | bytes 393224 | tf_op jit(solution)/shard_map/ppermute | solution.py:332
  25.1 5.0 %collective-permute-start.13 = (bf16[512,128]{1,0:T(8,128)(2,1)S(1)}, bf16[512,128]{1,0:T(8,128)(2,1)S(1)}, u32[]{:S(2)}, u32[]{:S(2)}) collective-permute-start(bf16[512,128]{1,0:T(8,128)(2,1)S(1)} %broadcast_select_fusion), channel_id=1, source_target_pairs={{0,4},{4,0},{8,10},{12,8},{14,12},{10,14},{6,2},{2,6},{1,5},{5,1},... | collective-permute-start | bytes 393224 | tf_op jit(solution)/shard_map/ppermute | solution.py:332

commit v14 on v13

v14 whole, which is shorter than its diff:
```python
import functools
import math

import jax
import jax.numpy as jnp
from jax import lax
from jax.experimental import pallas as pl
from jax.experimental.pallas import tpu as pltpu
from jax.sharding import PartitionSpec as P

NO_KEY = -1e30
ROW_CHUNK = 512
LARGEST = 64.0
ROUND = (8, 16)
HEADS_OUT = 16


def params():
    return pltpu.CompilerParams(vmem_limit_bytes=16 * 2**20)


def vmem():
    return pl.BlockSpec(memory_space=pltpu.VMEM)


def listed_bits(lists_ref, code):
    target = lax.axis_index("seq").astype(jnp.int32)
    entries = lists_ref[...]
    mine = lax.broadcasted_iota(jnp.int32, entries.shape, 1) == target
    bits = jnp.left_shift(1, code(jnp.maximum(entries, 0), target)).astype(jnp.float32)
    return jnp.sum(jnp.where(jnp.logical_and(mine, entries >= 0), bits, 0.0)).astype(jnp.int32)


def has(bits, code):
    return jnp.bitwise_and(lax.shift_right_logical(bits, jnp.int32(code)), 1) == 1


def by_head(wide, h, kv_dev, keys):
    return wide[pl.ds(h, keys, stride=kv_dev), :].astype(jnp.bfloat16)


def with_ones(values):
    return jnp.concatenate([values, jnp.ones_like(values)], axis=1)


def put_out(out_ref, h, first, both, group):
    rows, dim = both.shape[0], both.shape[1] // 2
    merged = (both[:, :dim] * pl.reciprocal(both[:, dim:])).reshape(rows // group, group, dim)
    tokens = pl.ds(first // group, rows // group)
    out_ref[tokens, pl.ds(h * group, group), :] = merged.astype(jnp.bfloat16)


def send_out(out_ref, out_hbm, sems, h, group):
    done = (h + 1) * group
    if done % HEADS_OUT:
        return []
    heads = pl.ds(done - HEADS_OUT, HEADS_OUT)
    copy = pltpu.make_async_copy(
        out_ref.at[:, heads, :], out_hbm.at[:, heads, :], sems.at[done // HEADS_OUT - 1]
    )
    copy.start()
    return [copy]


def chunks_of(kv_dev, rows_all):
    return [(h, first) for h in range(kv_dev) for first in range(0, rows_all, ROW_CHUNK)]


def in_turns(stages, jobs):
    held = {}
    for turn in range(len(jobs) + len(stages) - 1):
        for n, stage in enumerate(stages):
            at = turn - n
            if 0 <= at < len(jobs):
                held[at] = stage(jobs[at], held.get(at))
        held.pop(turn - len(stages) + 1, None)


def scores_of(q, keys):
    return lax.dot_general(q, keys, (((1,), (1,)), ((), ())), preferred_element_type=jnp.float32)


def own_kernel(
    lists_hbm, q_hbm, k_hbm, v_hbm, lists_out, q_out, top_out, both_out,
    q_ref, k_ref, v_ref, k_wide, v_wide, sems, *, kv_dev,
):
    whole = ((k_hbm, k_ref), (v_hbm, v_ref), (q_hbm, q_ref), (lists_hbm, lists_out))
    copies = [
        pltpu.make_async_copy(source, here, sems.at[n]) for n, (source, here) in enumerate(whole)
    ]
    for copy in copies:
        copy.start()
    tokens, heads, dim = q_ref.shape
    group = heads // kv_dev
    factor = dim ** (-0.5) * math.log2(math.e)
    copies[0].wait()
    k_wide[...] = k_ref[...].astype(jnp.float32)
    copies[1].wait()
    v_wide[...] = v_ref[...].astype(jnp.float32)
    k_ready = [by_head(k_wide, h, kv_dev, tokens) for h in range(kv_dev)]
    v_ready = [with_ones(by_head(v_wide, h, kv_dev, tokens)) for h in range(kv_dev)]
    copies[2].wait()

    def score(job, _):
        h, first = job
        here = pl.ds(first // group, ROW_CHUNK // group)
        q = q_ref[here, pl.ds(h * group, group), :].astype(jnp.float32)
        q = q.reshape(ROW_CHUNK, dim).astype(jnp.bfloat16)
        q_out[h, pl.ds(first, ROW_CHUNK), :] = q
        return scores_of(q, k_ready[h])

    def weigh(job, s):
        row = (lax.broadcasted_iota(jnp.int32, s.shape, 0) + job[1]) // group
        s = jnp.where(lax.broadcasted_iota(jnp.int32, s.shape, 1) <= row, s, NO_KEY)
        top = jnp.max(s, axis=1, keepdims=True)
        return jnp.exp2((s - top) * factor).astype(jnp.bfloat16), top

    def add_up(job, weighed):
        h, first = job
        probs, top = weighed
        rows = pl.ds(first, ROW_CHUNK)
        top_out[h, rows, :] = jnp.broadcast_to(top, (ROW_CHUNK, dim))
        both_out[h, rows, :] = jnp.dot(probs, v_ready[h], preferred_element_type=jnp.float32)

    in_turns([score, weigh, add_up], chunks_of(kv_dev, tokens * group))
    copies[3].wait()


def attend_own(lists, queries, k_own, v_own, kv_dev):
    tokens, heads, dim = queries.shape
    rows = tokens * heads // kv_dev
    operands = [
        pltpu.with_memory_space_constraint(x, pltpu.HBM) for x in (lists, queries, k_own, v_own)
    ]
    return pl.pallas_call(
        functools.partial(own_kernel, kv_dev=kv_dev),
        out_shape=(
            jax.ShapeDtypeStruct(lists.shape, lists.dtype),
            jax.ShapeDtypeStruct((kv_dev, rows, dim), jnp.bfloat16),
            jax.ShapeDtypeStruct((kv_dev, rows, dim), jnp.float32),
            jax.ShapeDtypeStruct((kv_dev, rows, 2 * dim), jnp.float32),
        ),
        in_specs=[pl.BlockSpec(memory_space=pltpu.HBM)] * 4,
        out_specs=(vmem(), vmem(), vmem(), vmem()),
        scratch_shapes=[
            pltpu.VMEM(queries.shape, jnp.bfloat16),
            pltpu.VMEM(k_own.shape, jnp.bfloat16),
            pltpu.VMEM(k_own.shape, jnp.bfloat16),
            pltpu.VMEM(k_own.shape, jnp.float32),
            pltpu.VMEM(k_own.shape, jnp.float32),
            pltpu.SemaphoreType.DMA((4,)),
        ],
        compiler_params=params(),
        name="attend_own",
    )(*operands)


def listed_kernel(lists_ref, q_ref, top_ref, both_ref, *refs, codes, code, last, done):
    parts = len(codes)
    k_parts, v_parts = refs[:parts], refs[parts : 2 * parts]
    outs = refs[2 * parts + done :]
    out_hbm, *state, k_wide, v_wide, out_ref, sems = outs
    kv_dev, rows_all, dim = q_ref.shape
    block = k_parts[0].shape[0]
    tokens = block // kv_dev
    group = rows_all // tokens
    most = k_wide.shape[0] // block
    factor = dim ** (-0.5) * math.log2(math.e)

    bits = listed_bits(lists_ref, code)
    count = jnp.int32(0)
    for part_code, k_part, v_part in zip(codes, k_parts, v_parts):
        take = has(bits, part_code)

        @pl.when(take)
        def _take(k_part=k_part, v_part=v_part, count=count):
            rows = pl.ds(pl.multiple_of(count * block, block), block)
            k_wide[rows, :] = k_part[...].astype(jnp.float32)
            v_wide[rows, :] = v_part[...].astype(jnp.float32)

        count += take.astype(jnp.int32)

    def keep(h, first, top, both):
        rows = pl.ds(first, ROW_CHUNK)
        state[0][h, rows, :] = top
        state[1][h, rows, :] = both

    def run(others, final):
        keys = others * tokens
        copies, shifts = [], []
        k_ready = [by_head(k_wide, h, kv_dev, keys) for h in range(kv_dev if others else 0)]
        v_ready = [with_ones(by_head(v_wide, h, kv_dev, keys)) for h in range(kv_dev if others else 0)]

        def blocks_of(s):
            return [s[:, j * tokens : (j + 1) * tokens] for j in range(others)]

        def score(job, _):
            h, first = job
            return scores_of(q_ref[h, pl.ds(first, ROW_CHUNK), :], k_ready[h]) if others else None

        def weigh(job, s):
            if not others:
                return None
            h, first = job
            top = top_ref[h, pl.ds(first, ROW_CHUNK), :]
            shifted = [(part - top) * factor for part in blocks_of(s)]
            largest = functools.reduce(jnp.maximum, shifted)
            shifts.append(jnp.max(largest.reshape(ROW_CHUNK // 8, 8, tokens), axis=0))
            return jnp.concatenate([jnp.exp2(part).astype(jnp.bfloat16) for part in shifted], axis=1)

        def add_up(job, probs):
            h, first = job
            rows = pl.ds(first, ROW_CHUNK)
            both = both_ref[h, rows, :]
            if others:
                both += jnp.dot(probs, v_ready[h], preferred_element_type=jnp.float32)
            if not final:
                keep(h, first, top_ref[h, rows, :], both)
                return
            put_out(out_ref, h, first, both, group)
            if first + ROW_CHUNK == rows_all:
                copies.extend(send_out(out_ref, out_hbm, sems, h, group))

        in_turns([score, weigh, add_up], chunks_of(kv_dev, rows_all))
        for copy in copies:
            copy.wait()
        if not others:
            return

        @pl.when(jnp.max(functools.reduce(jnp.maximum, shifts)) > LARGEST)
        def _rescale():
            def chunk(n, carry):
                first = pl.multiple_of(n * ROW_CHUNK, ROW_CHUNK)
                rows = pl.ds(first, ROW_CHUNK)
                for h in range(kv_dev):
                    scores = blocks_of(scores_of(q_ref[h, rows, :], k_ready[h]))
                    before = top_ref[h, rows, :]
                    top = jnp.max(functools.reduce(jnp.maximum, scores), axis=1, keepdims=True)
                    top = jnp.maximum(before, top)
                    probs = [jnp.exp2((part - top) * factor).astype(jnp.bfloat16) for part in scores]
                    shrink = jnp.exp2((before - top) * factor)
                    both = both_ref[h, rows, :] * jnp.concatenate([shrink, shrink], axis=1)
                    both += jnp.dot(
                        jnp.concatenate(probs, axis=1), v_ready[h], preferred_element_type=jnp.float32
                    )
                    if final:
                        put_out(out_ref, h, first, both, group)
                    else:
                        keep(h, first, top, both)
                return carry

            lax.fori_loop(0, rows_all // ROW_CHUNK, chunk, 0)
            if final:
                for h in range(kv_dev):
                    for copy in send_out(out_ref, out_hbm, sems, h, group):
                        copy.wait()

    unfinished = False if last is None else has(bits, last)
    for others in range(int(done), most + 1):

        @pl.when(jnp.logical_and(count == others, jnp.logical_not(unfinished)))
        def _whole(others=others):
            run(others, True)

        if last is not None and others < most:

            @pl.when(jnp.logical_and(count == others, unfinished))
            def _part(others=others):
                run(others, False)


def attend_listed(lists, queries, state, k_parts, v_parts, codes, code, last=None, out=None):
    kv_dev, rows, dim = queries.shape
    block = k_parts[0].shape[0]
    most = min(len(codes), lists.shape[0] - 1)
    made = jax.ShapeDtypeStruct((block // kv_dev, rows * kv_dev**2 // block, dim), jnp.bfloat16)
    kept = [] if last is None else [jax.ShapeDtypeStruct(x.shape, x.dtype) for x in state]
    done = [] if out is None else [out]
    hbm = pl.BlockSpec(memory_space=pltpu.HBM)
    operands = [lists, queries, *state, *k_parts, *v_parts]
    return pl.pallas_call(
        functools.partial(listed_kernel, codes=codes, code=code, last=last, done=bool(done)),
        out_shape=(made, *kept),
        in_specs=[vmem()] * len(operands) + [hbm] * len(done),
        out_specs=(hbm, *(vmem() for _ in kept)),
        input_output_aliases={len(operands): 0} if done else {},
        scratch_shapes=[
            pltpu.VMEM((most * block, dim), jnp.float32),
            pltpu.VMEM((most * block, dim), jnp.float32),
            pltpu.VMEM(made.shape, jnp.bfloat16),
            pltpu.SemaphoreType.DMA((made.shape[1] // HEADS_OUT,)),
        ],
        compiler_params=params(),
        name="attend_last" if done else "attend_listed",
    )(*operands, *done)


def ring_place(block, members):
    return jnp.where((block & 1) == 0, block >> 1, members - 1 - (block >> 1))


def ring_code(members):
    def code(block, target):
        ahead = ring_place(block, members) - ring_place(target, members)
        return jnp.where(ahead < 0, ahead + members, ahead)

    return code


def ring_steps(members):
    first, final = members // 4, 3 * members // 4 - 1
    forward = {p: (p + 1) % members for p in range(members)}
    backward = {p: (p - 1) % members for p in range(members)}
    low = [p for p in range(members) if not first <= p <= final]
    last_forward = {p: members - 1 - p for p in low}
    last_backward = {p: p ^ 1 for p in low}
    last_forward.update({p: p + 1 for p in range(first, final)})
    last_backward.update({p: p - 1 for p in range(first + 1, final + 1)})
    last_forward[final], last_backward[first] = first, final
    return forward, backward, last_forward, last_backward


def round_the_ring(k_own, v_own, ready, members):
    ring = list(range(0, members, 2)) + list(range(members - 1, 0, -2))
    forward, backward, last_forward, last_backward = ring_steps(members)

    def send(x, step):
        return lax.ppermute(x, "seq", [(ring[p], ring[to]) for p, to in sorted(step.items())])

    half = members // 2
    k_two, v_two, k_all, v_all = [k_own, k_own], [v_own, v_own], [], []
    for distance in range(1, half):
        ahead = send(k_two[0], forward), send(v_two[1], backward)
        behind = send(v_two[0], forward), send(k_two[1], backward)
        if distance == 1:
            ahead, ready = lax.optimization_barrier((ahead, ready))
        if distance < half - 1:
            ahead = lax.optimization_barrier(ahead)
        behind = lax.optimization_barrier(behind)
        k_two, v_two = [ahead[0], behind[1]], [behind[0], ahead[1]]
        k_all += k_two
        v_all += v_two
    here = ring_place(lax.axis_index("seq").astype(jnp.int32), members)
    k_last = jnp.where(here == 3 * members // 4 - 1, k_all[1], k_two[0])
    v_last = jnp.where(here == members // 4, v_all[0], v_two[1])
    return k_all, v_all, send(k_last, last_forward), send(v_last, last_backward), ready


def others(row, target):
    slots = row.shape[-1]
    own_at = jnp.argmax(row == target[..., None], axis=-1)
    j = jnp.arange(slots - 1)
    return jnp.where(j >= own_at[..., None], row[..., 1:], row[..., :-1])


def relay(k_own, v_own, chosen, members):
    block, dim = k_own.shape
    stacked = jnp.stack([k_own, v_own]).reshape(2, members, block // members, dim)
    shares = lax.all_to_all(stacked, "seq", split_axis=1, concat_axis=1, tiled=True)
    wanted = others(chosen, jnp.arange(members, dtype=jnp.int32))
    picked = jnp.take(shares, jnp.maximum(wanted, 0), axis=1)
    arrived = lax.all_to_all(picked, "seq", split_axis=1, concat_axis=3, tiled=True)
    count = wanted.shape[1]
    k_parts, v_parts = ([arrived[n, 0, j].reshape(block, dim) for j in range(count)] for n in range(2))
    return k_parts, v_parts, jnp.where(wanted < 0, -1, jnp.arange(count, dtype=jnp.int32))


def per_device(queries, keys, values, chosen):
    members = lax.axis_size("seq")
    tokens, kv_dev, dim = keys.shape
    k_own = keys.reshape(tokens * kv_dev, dim)
    v_own = values.reshape(tokens * kv_dev, dim)
    if members in ROUND:
        ready = attend_own(chosen.T, queries, k_own, v_own, kv_dev)
        k_parts, v_parts, k_last, v_last, ready = round_the_ring(k_own, v_own, ready, members)
        lists, queries, *state = ready
        half, code = members // 2, ring_code(members)
        codes = [turn for far in range(1, half) for turn in (members - far, far)]
        out, *state = attend_listed(lists, queries, state, k_parts, v_parts, codes, code, last=half)
        return attend_listed(lists, queries, state, [k_last], [v_last], [half], code, out=out)[0]

    k_parts, v_parts, mine = relay(k_own, v_own, chosen, members)
    lists, queries, *state = attend_own(mine.T, queries, k_own, v_own, kv_dev)
    lists = jnp.concatenate([lists, jnp.full_like(lists[:1], -1)])
    codes = list(range(len(k_parts)))
    return attend_listed(
        lists, queries, state, k_parts, v_parts, codes, lambda block, _: block
    )[0]


def solution(mesh):
    rows = P(("groups", "seq"), "head", None)
    return jax.shard_map(
        per_device,
        mesh=mesh,
        in_specs=(rows, rows, rows, P("groups", None)),
        out_specs=rows,
        check_vma=False,
    )
```

time: 30.6 us -> 37.2 us (1.22)
  the two profiles are of different devices: /device:TPU:0 before, /device:TPU:20 now
where the time goes in v14:
time: 37.2 us; the launch traced here: 37 us
  starting transfers between devices  14.7 us (40%)
  local copies, waits for them, and re-layouts  8.78 us (24%)
  Pallas kernels  7.67 us (21%)
  waiting for transfers between devices  5.59 us (15%)
    ppermute x14, starting transfers between devices, send(): lax.ppermute(x, 'seq', [(ring[p], ring[to]) for p, to in sorted(step.item...  14.7 us
    unnamed x16, local copies, waits for them, and re-layouts  8.78 us
    ppermute x14, waiting for transfers between devices, send(): lax.ppermute(x, 'seq', [(ring[p], ring[to]) for p, to in sorted(step.item...  5.59 us
    pallas_call x2, Pallas kernels, attend_listed(): pl.pallas_call(functools.partial(listed_kernel, codes=codes, code=code, l...  5.04 us
    pallas_call x1, Pallas kernels, attend_own(): pl.pallas_call(functools.partial(own_kernel, kv_dev=kv_dev), out_shape=(j...  2.63 us
  transfers between devices with their start and end apart: 14, of which 4 were waited for; matrix products, arithmetic and copies ran while one was open for 0% of the time, Pallas kernels for 15%

profile of v14, /device:TPU:20, one launch (start us, length us, event | category | flops | bytes accessed | tf_op | source)
XLA Modules:
  0.0 37.0 jit_solution(10845239872781013442)
XLA Ops:
  0.0 1.6 %collective-permute-start = (bf16[512,128]{1,0:T(8,128)(2,1)}, bf16[512,128]{1,0:T(8,128)(2,1)S(1)}, u32[]{:S(2)}, u32[]{:S(2)}) collective-permute-start(bf16[512,128]{1,0:T(8,128)(2,1)} %bitcast.6), channel_id=1, source_target_pairs={{0,4},{4,8},{8,12},{12,14},{14,10},{10,6},{6,2},{2,0},{1,5},{5,9},... | collective-permute-start | bytes 393224 | tf_op jit(solution)/shard_map/ppermute | solution.py:328
  1.6 0.4 %collective-permute-start.1 = (bf16[512,128]{1,0:T(8,128)(2,1)}, bf16[512,128]{1,0:T(8,128)(2,1)S(1)}, u32[]{:S(2)}, u32[]{:S(2)}) collective-permute-start(bf16[512,128]{1,0:T(8,128)(2,1)} %bitcast.3), channel_id=1, source_target_pairs={{0,2},{4,0},{8,4},{12,8},{14,12},{10,14},{6,10},{2,6},{1,3},{5,1},... | collective-permute-start | bytes 393224 | tf_op jit(solution)/shard_map/ppermute | solution.py:328
  2.0 1.6 %collective-permute-start.2 = (bf16[512,128]{1,0:T(8,128)(2,1)}, bf16[512,128]{1,0:T(8,128)(2,1)S(1)}, u32[]{:S(2)}, u32[]{:S(2)}) collective-permute-start(bf16[512,128]{1,0:T(8,128)(2,1)} %bitcast.4), channel_id=1, source_target_pairs={{0,4},{4,8},{8,12},{12,14},{14,10},{10,6},{6,2},{2,0},{1,5},{5,9},... | collective-permute-start | bytes 393224 | tf_op jit(solution)/shard_map/ppermute | solution.py:328
  3.6 0.4 %collective-permute-start.3 = (bf16[512,128]{1,0:T(8,128)(2,1)}, bf16[512,128]{1,0:T(8,128)(2,1)S(1)}, u32[]{:S(2)}, u32[]{:S(2)}) collective-permute-start(bf16[512,128]{1,0:T(8,128)(2,1)} %bitcast.7), channel_id=1, source_target_pairs={{0,2},{4,0},{8,4},{12,8},{14,12},{10,14},{6,10},{2,6},{1,3},{5,1},... | collective-permute-start | bytes 393224 | tf_op jit(solution)/shard_map/ppermute | solution.py:328
  4.1 2.6 %attend_own.1 = (s32[4,8]{1,0:T(4,128)S(1)}, bf16[4,1024,128]{2,1,0:T(8,128)(2,1)S(1)}, f32[4,1024,128]{2,1,0:T(8,128)S(1)}, f32[4,1024,256]{2,1,0:T(8,128)S(1)}) custom-call(s32[4,8]{1,0:T(4,128)} %bitcast.9, bf16[128,32,128]{2,1,0:T(8,128)(2,1)} %q_hbm.1, bf16[512,128]{1,0:T(8,128)(2,1)} %bitcast.8, bf16[512,128]{1,0:T(8,128)(2,1)} %bitcast.5), custom_call_target="tpu_custom_call" | custom-call | tf_op jit(solution)/shard_map/attend_own/pallas_call | solution.py:135
  6.7 0.0 copy-start
  6.7 1.9 %copy-done = f32[4,1024,256]{2,1,0:T(8,128)} copy-done((f32[4,1024,256]{2,1,0:T(8,128)}, f32[4,1024,256]{2,1,0:T(8,128)S(1)}, u32[]{:S(2)}) %copy-start) | copy-done | bytes 4194328
  8.6 0.0 collective-permute-done.refs_0_
  8.6 0.0 collective-permute-done.1.refs_7_
  8.6 1.6 %collective-permute-start.4 = (bf16[512,128]{1,0:T(8,128)(2,1)S(1)}, bf16[512,128]{1,0:T(8,128)(2,1)}, u32[]{:S(2)}, u32[]{:S(2)}) collective-permute-start(bf16[512,128]{1,0:T(8,128)(2,1)S(1)} %collective-permute-done.refs_0_), channel_id=1, source_target_pairs={{0,4},{4,8},{8,12},{12,14},{14,10},{10,6},{6,2},{2,0},{1,5},{5,9},... | collective-permute-start | bytes 393224 | tf_op jit(solution)/shard_map/ppermute | solution.py:328
  10.2 0.0 copy-start.2
  10.2 0.7 %copy-done.2 = bf16[512,128]{1,0:T(8,128)(2,1)} copy-done((bf16[512,128]{1,0:T(8,128)(2,1)}, bf16[512,128]{1,0:T(8,128)(2,1)S(1)}, u32[]{:S(2)}) %copy-start.2) | copy-done | bytes 131096
  10.9 0.4 %collective-permute-start.5 = (bf16[512,128]{1,0:T(8,128)(2,1)S(1)}, bf16[512,128]{1,0:T(8,128)(2,1)S(1)}, u32[]{:S(2)}, u32[]{:S(2)}) collective-permute-start(bf16[512,128]{1,0:T(8,128)(2,1)S(1)} %collective-permute-done.1.refs_7_), channel_id=1, source_target_pairs={{0,2},{4,0},{8,4},{12,8},{14,12},{10,14},{6,10},{2,6},{1,3},{5,1},... | collective-permute-start | bytes 393224 | tf_op jit(solution)/shard_map/ppermute | solution.py:328
  11.3 0.0 copy-start.4
  11.3 0.6 %copy-done.4 = bf16[512,128]{1,0:T(8,128)(2,1)} copy-done((bf16[512,128]{1,0:T(8,128)(2,1)}, bf16[512,128]{1,0:T(8,128)(2,1)S(1)}, u32[]{:S(2)}) %copy-start.4) | copy-done | bytes 131096
  12.0 0.0 collective-permute-done.2.refs_6_
  12.0 0.0 collective-permute-done.3.refs_1_
  12.0 1.6 %collective-permute-start.6 = (bf16[512,128]{1,0:T(8,128)(2,1)S(1)}, bf16[512,128]{1,0:T(8,128)(2,1)}, u32[]{:S(2)}, u32[]{:S(2)}) collective-permute-start(bf16[512,128]{1,0:T(8,128)(2,1)S(1)} %collective-permute-done.2.refs_6_), channel_id=1, source_target_pairs={{0,4},{4,8},{8,12},{12,14},{14,10},{10,6},{6,2},{2,0},{1,5},{5,9},... | collective-permute-start | bytes 393224 | tf_op jit(solution)/shard_map/ppermute | solution.py:328
  13.6 0.4 %collective-permute-start.7 = (bf16[512,128]{1,0:T(8,128)(2,1)S(1)}, bf16[512,128]{1,0:T(8,128)(2,1)}, u32[]{:S(2)}, u32[]{:S(2)}) collective-permute-start(bf16[512,128]{1,0:T(8,128)(2,1)S(1)} %collective-permute-done.3.refs_1_), channel_id=1, source_target_pairs={{0,2},{4,0},{8,4},{12,8},{14,12},{10,14},{6,10},{2,6},{1,3},{5,1},... | collective-permute-start | bytes 393224 | tf_op jit(solution)/shard_map/ppermute | solution.py:328
  14.0 0.7 %collective-permute-done.4.refs_2_ = bf16[512,128]{1,0:T(8,128)(2,1)} collective-permute-done((bf16[512,128]{1,0:T(8,128)(2,1)S(1)}, bf16[512,128]{1,0:T(8,128)(2,1)}, u32[]{:S(2)}, u32[]{:S(2)}) %collective-permute-start.4) | collective-permute-done | bytes 131104 | tf_op jit(solution)/shard_map/ppermute | solution.py:328
  14.7 2.2 %collective-permute-done.5.refs_9_ = bf16[512,128]{1,0:T(8,128)(2,1)S(1)} collective-permute-done((bf16[512,128]{1,0:T(8,128)(2,1)S(1)}, bf16[512,128]{1,0:T(8,128)(2,1)S(1)}, u32[]{:S(2)}, u32[]{:S(2)}) %collective-permute-start.5) | collective-permute-done | bytes 131104 | tf_op jit(solution)/shard_map/ppermute | solution.py:328
  16.8 0.0 copy-start.6
  16.8 0.7 %copy-done.6 = bf16[512,128]{1,0:T(8,128)(2,1)} copy-done((bf16[512,128]{1,0:T(8,128)(2,1)}, bf16[512,128]{1,0:T(8,128)(2,1)S(1)}, u32[]{:S(2)}) %copy-start.6) | copy-done | bytes 131096
  17.5 1.5 %collective-permute-start.8 = (bf16[512,128]{1,0:T(8,128)(2,1)}, bf16[512,128]{1,0:T(8,128)(2,1)S(1)}, u32[]{:S(2)}, u32[]{:S(2)}) collective-permute-start(bf16[512,128]{1,0:T(8,128)(2,1)} %collective-permute-done.4.refs_2_), channel_id=1, source_target_pairs={{0,4},{4,8},{8,12},{12,14},{14,10},{10,6},{6,2},{2,0},{1,5},{5,9},... | collective-permute-start | bytes 393224 | tf_op jit(solution)/shard_map/ppermute | solution.py:328
  19.0 0.5 %collective-permute-start.11 = (bf16[512,128]{1,0:T(8,128)(2,1)}, bf16[512,128]{1,0:T(8,128)(2,1)S(1)}, u32[]{:S(2)}, u32[]{:S(2)}) collective-permute-start(bf16[512,128]{1,0:T(8,128)(2,1)} %copy-done.6), channel_id=1, source_target_pairs={{0,2},{4,0},{8,4},{12,8},{14,12},{10,14},{6,10},{2,6},{1,3},{5,1},... | collective-permute-start | bytes 393224 | tf_op jit(solution)/shard_map/ppermute | solution.py:328
  19.5 0.0 collective-permute-done.6.refs_8_
  19.5 0.0 collective-permute-done.7.refs_3_
  19.5 0.5 %collective-permute-start.10 = (bf16[512,128]{1,0:T(8,128)(2,1)}, bf16[512,128]{1,0:T(8,128)(2,1)S(1)}, u32[]{:S(2)}, u32[]{:S(2)}) collective-permute-start(bf16[512,128]{1,0:T(8,128)(2,1)} %collective-permute-done.7.refs_3_), channel_id=1, source_target_pairs={{0,2},{4,0},{8,4},{12,8},{14,12},{10,14},{6,10},{2,6},{1,3},{5,1},... | collective-permute-start | bytes 393224 | tf_op jit(solution)/shard_map/ppermute | solution.py:328
  20.0 1.6 %collective-permute-start.9 = (bf16[512,128]{1,0:T(8,128)(2,1)}, bf16[512,128]{1,0:T(8,128)(2,1)S(1)}, u32[]{:S(2)}, u32[]{:S(2)}) collective-permute-start(bf16[512,128]{1,0:T(8,128)(2,1)} %collective-permute-done.6.refs_8_), channel_id=1, source_target_pairs={{0,4},{4,8},{8,12},{12,14},{14,10},{10,6},{6,2},{2,0},{1,5},{5,9},... | collective-permute-start | bytes 393224 | tf_op jit(solution)/shard_map/ppermute | solution.py:328
  21.5 1.6 %collective-permute-done.8.refs_4_ = bf16[512,128]{1,0:T(8,128)(2,1)S(1)} collective-permute-done((bf16[512,128]{1,0:T(8,128)(2,1)}, bf16[512,128]{1,0:T(8,128)(2,1)S(1)}, u32[]{:S(2)}, u32[]{:S(2)}) %collective-permute-start.8) | collective-permute-done | bytes 131104 | tf_op jit(solution)/shard_map/ppermute | solution.py:328
  23.1 2.5 %collective-permute-start.12 = (bf16[512,128]{1,0:T(8,128)(2,1)S(1)}, bf16[512,128]{1,0:T(8,128)(2,1)S(1)}, u32[]{:S(2)}, u32[]{:S(2)}) collective-permute-start(bf16[512,128]{1,0:T(8,128)(2,1)S(1)} %broadcast_select_fusion.1), channel_id=1, source_target_pairs={{0,2},{4,6},{8,12},{12,14},{14,10},{10,8},{6,4},{2,0},{1,3},{5,7},... | collective-permute-start | bytes 393224 | tf_op jit(solution)/shard_map/ppermute | solution.py:328
  25.6 0.0 collective-permute-done.11.refs_11_
  25.6 0.1 collective-permute-start.13
  25.7 1.2 %collective-permute-done.10.refs_5_ = bf16[512,128]{1,0:T(8,128)(2,1)S(1)} collective-permute-done((bf16[512,128]{1,0:T(8,128)(2,1)}, bf16[512,128]{1,0:T(8,128)(2,1)S(1)}, u32[]{:S(2)}, u32[]{:S(2)}) %collective-permute-start.10) | collective-permute-done | bytes 131104 | tf_op jit(solution)/shard_map/ppermute | solution.py:328
  26.9 0.0 collective-permute-done.9.refs_10_
  26.9 0.0 copy-start.1
  26.9 2.2 %copy-done.1 = f32[4,1024,256]{2,1,0:T(8,128)S(1)} copy-done((f32[4,1024,256]{2,1,0:T(8,128)S(1)}, f32[4,1024,256]{2,1,0:T(8,128)}, u32[]{:S(2)}) %copy-start.1) | copy-done | bytes 4194328
  29.1 0.0 copy-start.3
  29.1 0.9 %copy-done.3 = bf16[512,128]{1,0:T(8,128)(2,1)S(1)} copy-done((bf16[512,128]{1,0:T(8,128)(2,1)S(1)}, bf16[512,128]{1,0:T(8,128)(2,1)}, u32[]{:S(2)}) %copy-start.3) | copy-done | bytes 131096
  30.0 0.0 copy-start.5
  30.0 0.9 %copy-done.5 = bf16[512,128]{1,0:T(8,128)(2,1)S(1)} copy-done((bf16[512,128]{1,0:T(8,128)(2,1)S(1)}, bf16[512,128]{1,0:T(8,128)(2,1)}, u32[]{:S(2)}) %copy-start.5) | copy-done | bytes 131096
  30.9 0.0 copy-start.7
  30.9 0.9 %copy-done.7 = bf16[512,128]{1,0:T(8,128)(2,1)S(1)} copy-done((bf16[512,128]{1,0:T(8,128)(2,1)S(1)}, bf16[512,128]{1,0:T(8,128)(2,1)}, u32[]{:S(2)}) %copy-start.7) | copy-done | bytes 131096
  31.8 2.9 %attend_listed.1 = (bf16[128,32,128]{2,1,0:T(8,128)(2,1)}, f32[4,1024,128]{2,1,0:T(8,128)S(1)}, f32[4,1024,256]{2,1,0:T(8,128)S(1)}) custom-call(s32[4,8]{1,0:T(4,128)S(1)} %get-tuple-element.32.lists_ref, bf16[4,1024,128]{2,1,0:T(8,128)(2,1)S(1)} %get-tuple-element.33.q_ref, f32[4,1024,128]{2,1,0:T(8,128)S(1)} %get-tuple-element.34.top_ref, ...), custom_call_target="tpu_custom_call" | custom-call | tf_op jit(solution)/shard_map/attend_listed/pallas_call | solution.py:281
  34.6 0.0 collective-permute-done.12.refs_0_
  34.6 0.0 collective-permute-done.13.refs_1_
  34.7 2.2 %attend_last.1 = bf16[128,32,128]{2,1,0:T(8,128)(2,1)} custom-call(s32[4,8]{1,0:T(4,128)S(1)} %get-tuple-element.32.lists_ref, bf16[4,1024,128]{2,1,0:T(8,128)(2,1)S(1)} %get-tuple-element.33.q_ref, f32[4,1024,128]{2,1,0:T(8,128)S(1)} %get-tuple-element.48.top_ref, f32[4,1024,256]{2,1,0:T(8,128)S(1)} %get-tuple-element.49.both_ref, ...), custom_call_target="tpu_custom_call", output_to_operand_aliasing={{}: (6, {})} | custom-call | tf_op jit(solution)/shard_map/attend_last/pallas_call | solution.py:281
  (2 shorter events, 0.0 us)
Async XLA Ops:
  0.0 8.6 %collective-permute-start = (bf16[512,128]{1,0:T(8,128)(2,1)}, bf16[512,128]{1,0:T(8,128)(2,1)S(1)}, u32[]{:S(2)}, u32[]{:S(2)}) collective-permute-start(bf16[512,128]{1,0:T(8,128)(2,1)} %bitcast.6), channel_id=1, source_target_pairs={{0,4},{4,8},{8,12},{12,14},{14,10},{10,6},{6,2},{2,0},{1,5},{5,9},... | collective-permute-start | bytes 393224 | tf_op jit(solution)/shard_map/ppermute | solution.py:328
  1.6 7.1 %collective-permute-start.1 = (bf16[512,128]{1,0:T(8,128)(2,1)}, bf16[512,128]{1,0:T(8,128)(2,1)S(1)}, u32[]{:S(2)}, u32[]{:S(2)}) collective-permute-start(bf16[512,128]{1,0:T(8,128)(2,1)} %bitcast.3), channel_id=1, source_target_pairs={{0,2},{4,0},{8,4},{12,8},{14,12},{10,14},{6,10},{2,6},{1,3},{5,1},... | collective-permute-start | bytes 393224 | tf_op jit(solution)/shard_map/ppermute | solution.py:328
  2.0 9.9 %collective-permute-start.2 = (bf16[512,128]{1,0:T(8,128)(2,1)}, bf16[512,128]{1,0:T(8,128)(2,1)S(1)}, u32[]{:S(2)}, u32[]{:S(2)}) collective-permute-start(bf16[512,128]{1,0:T(8,128)(2,1)} %bitcast.4), channel_id=1, source_target_pairs={{0,4},{4,8},{8,12},{12,14},{14,10},{10,6},{6,2},{2,0},{1,5},{5,9},... | collective-permute-start | bytes 393224 | tf_op jit(solution)/shard_map/ppermute | solution.py:328
  3.6 8.4 %collective-permute-start.3 = (bf16[512,128]{1,0:T(8,128)(2,1)}, bf16[512,128]{1,0:T(8,128)(2,1)S(1)}, u32[]{:S(2)}, u32[]{:S(2)}) collective-permute-start(bf16[512,128]{1,0:T(8,128)(2,1)} %bitcast.7), channel_id=1, source_target_pairs={{0,2},{4,0},{8,4},{12,8},{14,12},{10,14},{6,10},{2,6},{1,3},{5,1},... | collective-permute-start | bytes 393224 | tf_op jit(solution)/shard_map/ppermute | solution.py:328
  6.7 1.9 %copy-start = (f32[4,1024,256]{2,1,0:T(8,128)}, f32[4,1024,256]{2,1,0:T(8,128)S(1)}, u32[]{:S(2)}) copy-start(f32[4,1024,256]{2,1,0:T(8,128)S(1)} %get-tuple-element.35.both_ref) | copy-start | bytes 12582916
  8.6 6.0 %collective-permute-start.4 = (bf16[512,128]{1,0:T(8,128)(2,1)S(1)}, bf16[512,128]{1,0:T(8,128)(2,1)}, u32[]{:S(2)}, u32[]{:S(2)}) collective-permute-start(bf16[512,128]{1,0:T(8,128)(2,1)S(1)} %collective-permute-done.refs_0_), channel_id=1, source_target_pairs={{0,4},{4,8},{8,12},{12,14},{14,10},{10,6},{6,2},{2,0},{1,5},{5,9},... | collective-permute-start | bytes 393224 | tf_op jit(solution)/shard_map/ppermute | solution.py:328
  10.2 0.7 %copy-start.2 = (bf16[512,128]{1,0:T(8,128)(2,1)}, bf16[512,128]{1,0:T(8,128)(2,1)S(1)}, u32[]{:S(2)}) copy-start(bf16[512,128]{1,0:T(8,128)(2,1)S(1)} %collective-permute-done.refs_0_) | copy-start | bytes 393220
  10.9 6.0 %collective-permute-start.5 = (bf16[512,128]{1,0:T(8,128)(2,1)S(1)}, bf16[512,128]{1,0:T(8,128)(2,1)S(1)}, u32[]{:S(2)}, u32[]{:S(2)}) collective-permute-start(bf16[512,128]{1,0:T(8,128)(2,1)S(1)} %collective-permute-done.1.refs_7_), channel_id=1, source_target_pairs={{0,2},{4,0},{8,4},{12,8},{14,12},{10,14},{6,10},{2,6},{1,3},{5,1},... | collective-permute-start | bytes 393224 | tf_op jit(solution)/shard_map/ppermute | solution.py:328
  11.3 0.7 %copy-start.4 = (bf16[512,128]{1,0:T(8,128)(2,1)}, bf16[512,128]{1,0:T(8,128)(2,1)S(1)}, u32[]{:S(2)}) copy-start(bf16[512,128]{1,0:T(8,128)(2,1)S(1)} %collective-permute-done.1.refs_7_) | copy-start | bytes 393220
  12.0 7.5 %collective-permute-start.6 = (bf16[512,128]{1,0:T(8,128)(2,1)S(1)}, bf16[512,128]{1,0:T(8,128)(2,1)}, u32[]{:S(2)}, u32[]{:S(2)}) collective-permute-start(bf16[512,128]{1,0:T(8,128)(2,1)S(1)} %collective-permute-done.2.refs_6_), channel_id=1, source_target_pairs={{0,4},{4,8},{8,12},{12,14},{14,10},{10,6},{6,2},{2,0},{1,5},{5,9},... | collective-permute-start | bytes 393224 | tf_op jit(solution)/shard_map/ppermute | solution.py:328
  13.6 6.0 %collective-permute-start.7 = (bf16[512,128]{1,0:T(8,128)(2,1)S(1)}, bf16[512,128]{1,0:T(8,128)(2,1)}, u32[]{:S(2)}, u32[]{:S(2)}) collective-permute-start(bf16[512,128]{1,0:T(8,128)(2,1)S(1)} %collective-permute-done.3.refs_1_), channel_id=1, source_target_pairs={{0,2},{4,0},{8,4},{12,8},{14,12},{10,14},{6,10},{2,6},{1,3},{5,1},... | collective-permute-start | bytes 393224 | tf_op jit(solution)/shard_map/ppermute | solution.py:328
  16.8 0.7 %copy-start.6 = (bf16[512,128]{1,0:T(8,128)(2,1)}, bf16[512,128]{1,0:T(8,128)(2,1)S(1)}, u32[]{:S(2)}) copy-start(bf16[512,128]{1,0:T(8,128)(2,1)S(1)} %collective-permute-done.5.refs_9_) | copy-start | bytes 393220
  17.5 5.6 %collective-permute-start.8 = (bf16[512,128]{1,0:T(8,128)(2,1)}, bf16[512,128]{1,0:T(8,128)(2,1)S(1)}, u32[]{:S(2)}, u32[]{:S(2)}) collective-permute-start(bf16[512,128]{1,0:T(8,128)(2,1)} %collective-permute-done.4.refs_2_), channel_id=1, source_target_pairs={{0,4},{4,8},{8,12},{12,14},{14,10},{10,6},{6,2},{2,0},{1,5},{5,9},... | collective-permute-start | bytes 393224 | tf_op jit(solution)/shard_map/ppermute | solution.py:328
  19.0 6.6 %collective-permute-start.11 = (bf16[512,128]{1,0:T(8,128)(2,1)}, bf16[512,128]{1,0:T(8,128)(2,1)S(1)}, u32[]{:S(2)}, u32[]{:S(2)}) collective-permute-start(bf16[512,128]{1,0:T(8,128)(2,1)} %copy-done.6), channel_id=1, source_target_pairs={{0,2},{4,0},{8,4},{12,8},{14,12},{10,14},{6,10},{2,6},{1,3},{5,1},... | collective-permute-start | bytes 393224 | tf_op jit(solution)/shard_map/ppermute | solution.py:328
  19.5 7.3 %collective-permute-start.10 = (bf16[512,128]{1,0:T(8,128)(2,1)}, bf16[512,128]{1,0:T(8,128)(2,1)S(1)}, u32[]{:S(2)}, u32[]{:S(2)}) collective-permute-start(bf16[512,128]{1,0:T(8,128)(2,1)} %collective-permute-done.7.refs_3_), channel_id=1, source_target_pairs={{0,2},{4,0},{8,4},{12,8},{14,12},{10,14},{6,10},{2,6},{1,3},{5,1},... | collective-permute-start | bytes 393224 | tf_op jit(solution)/shard_map/ppermute | solution.py:328
  20.0 6.9 %collective-permute-start.9 = (bf16[512,128]{1,0:T(8,128)(2,1)}, bf16[512,128]{1,0:T(8,128)(2,1)S(1)}, u32[]{:S(2)}, u32[]{:S(2)}) collective-permute-start(bf16[512,128]{1,0:T(8,128)(2,1)} %collective-permute-done.6.refs_8_), channel_id=1, source_target_pairs={{0,4},{4,8},{8,12},{12,14},{14,10},{10,6},{6,2},{2,0},{1,5},{5,9},... | collective-permute-start | bytes 393224 | tf_op jit(solution)/shard_map/ppermute | solution.py:328
  23.1 11.5 %collective-permute-start.12 = (bf16[512,128]{1,0:T(8,128)(2,1)S(1)}, bf16[512,128]{1,0:T(8,128)(2,1)S(1)}, u32[]{:S(2)}, u32[]{:S(2)}) collective-permute-start(bf16[512,128]{1,0:T(8,128)(2,1)S(1)} %broadcast_select_fusion.1), channel_id=1, source_target_pairs={{0,2},{4,6},{8,12},{12,14},{14,10},{10,8},{6,4},{2,0},{1,3},{5,7},... | collective-permute-start | bytes 393224 | tf_op jit(solution)/shard_map/ppermute | solution.py:328
  25.6 9.1 %collective-permute-start.13 = (bf16[512,128]{1,0:T(8,128)(2,1)S(1)}, bf16[512,128]{1,0:T(8,128)(2,1)S(1)}, u32[]{:S(2)}, u32[]{:S(2)}) collective-permute-start(bf16[512,128]{1,0:T(8,128)(2,1)S(1)} %broadcast_select_fusion), channel_id=1, source_target_pairs={{0,4},{4,0},{8,10},{12,8},{14,12},{10,14},{6,2},{2,6},{1,5},{5,1},... | collective-permute-start | bytes 393224 | tf_op jit(solution)/shard_map/ppermute | solution.py:328
  26.9 2.2 %copy-start.1 = (f32[4,1024,256]{2,1,0:T(8,128)S(1)}, f32[4,1024,256]{2,1,0:T(8,128)}, u32[]{:S(2)}) copy-start(f32[4,1024,256]{2,1,0:T(8,128)} %copy-done) | copy-start | bytes 12582916
  29.1 0.9 %copy-start.3 = (bf16[512,128]{1,0:T(8,128)(2,1)S(1)}, bf16[512,128]{1,0:T(8,128)(2,1)}, u32[]{:S(2)}) copy-start(bf16[512,128]{1,0:T(8,128)(2,1)} %copy-done.2) | copy-start | bytes 393220
  30.0 0.9 %copy-start.5 = (bf16[512,128]{1,0:T(8,128)(2,1)S(1)}, bf16[512,128]{1,0:T(8,128)(2,1)}, u32[]{:S(2)}) copy-start(bf16[512,128]{1,0:T(8,128)(2,1)} %copy-done.4) | copy-start | bytes 393220
  30.9 0.9 %copy-start.7 = (bf16[512,128]{1,0:T(8,128)(2,1)S(1)}, bf16[512,128]{1,0:T(8,128)(2,1)}, u32[]{:S(2)}) copy-start(bf16[512,128]{1,0:T(8,128)(2,1)} %copy-done.6) | copy-start | bytes 393220

commit v15 on v12

--- a/solution.py
+++ b/solution.py
@@ -10,8 +10,8 @@
 
 NO_KEY = -1e30
 ROW_CHUNK = 256
+LARGEST = 64.0
 ROUND = (8, 16)
-HEADS_OUT = 16
 
 
 def params():
@@ -95,27 +95,37 @@
     return jnp.concatenate([values, jnp.ones_like(values)], axis=1)
 
 
-def put_out(out_ref, h, first, both, group):
-    rows, dim = both.shape[0], both.shape[1] // 2
-    merged = (both[:, :dim] * pl.reciprocal(both[:, dim:])).reshape(rows // group, group, dim)
-    tokens = pl.ds(first // group, rows // group)
-    out_ref[tokens, pl.ds(h * group, group), :] = merged.astype(jnp.bfloat16)
-
-
-def send_out(out_ref, out_hbm, sems, h, group):
-    done = (h + 1) * group
-    if done % HEADS_OUT:
-        return []
-    heads = pl.ds(done - HEADS_OUT, HEADS_OUT)
-    copy = pltpu.make_async_copy(
-        out_ref.at[:, heads, :], out_hbm.at[:, heads, :], sems.at[done // HEADS_OUT - 1]
-    )
-    copy.start()
-    return [copy]
+class Output:
+    def __init__(self, out_ref, out_hbm, sems, kv_dev, group):
+        self.out_ref, self.out_hbm, self.sems = out_ref, out_hbm, sems
+        self.kv_dev, self.group, self.copies, self.before = kv_dev, group, [], None
+
+    def put(self, h, first, both):
+        rows, dim = both.shape[0], both.shape[1] // 2
+        merged = both[:, :dim] * pl.reciprocal(both[:, dim:])
+        merged = merged.reshape(rows // self.group, self.group, dim)
+        if h % 2 == 0:
+            self.before = merged
+            return
+        here = pl.ds(first // self.group, rows // self.group)
+        heads = pl.ds((h - 1) * self.group, 2 * self.group)
+        two = jnp.concatenate([self.before, merged], axis=1)
+        self.out_ref[here, heads, :] = two.astype(jnp.bfloat16)
+        if h + 1 == self.kv_dev:
+            self.copies.append(
+                pltpu.make_async_copy(
+                    self.out_ref.at[here], self.out_hbm.at[here], self.sems.at[len(self.copies)]
+                )
+            )
+            self.copies[-1].start()
+
+    def wait(self):
+        for copy in self.copies:
+            copy.wait()
 
 
 def chunks_of(kv_dev, rows_all):
-    return [(h, first) for h in range(kv_dev) for first in range(0, rows_all, ROW_CHUNK)]
+    return [(h, first) for first in range(0, rows_all, ROW_CHUNK) for h in range(kv_dev)]
 
 
 def in_turns(stages, jobs):
@@ -158,7 +168,7 @@
 
     def run(others, final):
         keys = (others + 1) * tokens
-        copies = []
+        output = Output(out_ref, out_hbm, sems, kv_dev, group)
         k_ready, v_ready = [], []
         for h in range(kv_dev):
             k_h, v_h = k_own_ref[h], v_own_ref[h]
@@ -187,17 +197,14 @@
             probs, top = weighed
             both = jnp.dot(probs, v_ready[h], preferred_element_type=jnp.float32)
             if final:
-                put_out(out_ref, h, first, both, group)
-                if first + ROW_CHUNK == rows_all:
-                    copies.extend(send_out(out_ref, out_hbm, sems, h, group))
+                output.put(h, first, both)
             else:
                 rows = pl.ds(first, ROW_CHUNK)
                 state[0][h, rows, :] = jnp.broadcast_to(top, (ROW_CHUNK, dim))
                 state[1][h, rows, :] = both
 
         in_turns([score, weigh, add_up], chunks_of(kv_dev, rows_all))
-        for copy in copies:
-            copy.wait()
+        output.wait()
 
     unfinished = False if last is None else has(bits, last)
     for others in range(most + 1):
@@ -231,7 +238,7 @@
             pltpu.VMEM((rest, dim), jnp.float32),
             pltpu.VMEM((rest, dim), jnp.float32),
             pltpu.VMEM(out.shape, jnp.bfloat16),
-            pltpu.SemaphoreType.DMA((out.shape[1] // HEADS_OUT,)),
+            pltpu.SemaphoreType.DMA((rows // ROW_CHUNK,)),
         ],
         compiler_params=params(),
         name="attend",
@@ -252,7 +259,9 @@
         v_wide[...] = v_ref[...].astype(jnp.float32)
         k_ready = [by_head(k_wide, h, kv_dev, tokens) for h in range(kv_dev)]
         v_ready = [with_ones(by_head(v_wide, h, kv_dev, tokens)) for h in range(kv_dev)]
-        copies = []
+        jobs = chunks_of(kv_dev, rows_all)
+        output = Output(out_ref, out_hbm, sems, kv_dev, group)
+        shifts = []
 
         def score(job, _):
             h, first = job
@@ -260,23 +269,32 @@
 
         def weigh(job, s):
             h, first = job
-            before = top_ref[h, pl.ds(first, ROW_CHUNK), :]
-            top = jnp.maximum(before, jnp.max(s, axis=1, keepdims=True))
-            shrink = jnp.exp2((before - top) * factor)
-            return jnp.exp2((s - top) * factor).astype(jnp.bfloat16), shrink
-
-        def add_up(job, weighed):
+            shifted = (s - top_ref[h, pl.ds(first, ROW_CHUNK), :]) * factor
+            shifts.append(jnp.max(shifted.reshape(ROW_CHUNK // 8, 8, tokens), axis=0))
+            return jnp.exp2(shifted).astype(jnp.bfloat16)
+
+        def add_up(job, probs):
             h, first = job
-            probs, shrink = weighed
             both = jnp.dot(probs, v_ready[h], preferred_element_type=jnp.float32)
-            both += both_ref[h, pl.ds(first, ROW_CHUNK), :] * jnp.concatenate([shrink, shrink], axis=1)
-            put_out(out_ref, h, first, both, group)
-            if first + ROW_CHUNK == rows_all:
-                copies.extend(send_out(out_ref, out_hbm, sems, h, group))
-
-        in_turns([score, weigh, add_up], chunks_of(kv_dev, rows_all))
-        for copy in copies:
-            copy.wait()
+            output.put(h, first, both + both_ref[h, pl.ds(first, ROW_CHUNK), :])
+
+        in_turns([score, weigh, add_up], jobs)
+        output.wait()
+
+        @pl.when(jnp.max(functools.reduce(jnp.maximum, shifts)) > LARGEST)
+        def _rescale():
+            again = Output(out_ref, out_hbm, sems, kv_dev, group)
+            for h, first in jobs:
+                rows = pl.ds(first, ROW_CHUNK)
+                s = scores_of(q_ref[h, rows, :], k_ready[h])
+                before = top_ref[h, rows, :]
+                top = jnp.maximum(before, jnp.max(s, axis=1, keepdims=True))
+                probs = jnp.exp2((s - top) * factor).astype(jnp.bfloat16)
+                shrink = jnp.exp2((before - top) * factor)
+                both = both_ref[h, rows, :] * jnp.concatenate([shrink, shrink], axis=1)
+                both += jnp.dot(probs, v_ready[h], preferred_element_type=jnp.float32)
+                again.put(h, first, both)
+            again.wait()
 
 
 def attend_last(lists, queries, state, k_last, v_last, out, code, last):
@@ -292,7 +310,7 @@
             pltpu.VMEM(k_last.shape, jnp.float32),
             pltpu.VMEM(k_last.shape, jnp.float32),
             pltpu.VMEM(out.shape, jnp.bfloat16),
-            pltpu.SemaphoreType.DMA((out.shape[1] // HEADS_OUT,)),
+            pltpu.SemaphoreType.DMA((queries.shape[1] // ROW_CHUNK,)),
         ],
         compiler_params=params(),
         name="attend_last",
@@ -338,7 +356,8 @@
         behind = send(v_two[0], forward), send(k_two[1], backward)
         if distance == 1:
             ahead, ready = lax.optimization_barrier((ahead, ready))
-        ahead = lax.optimization_barrier(ahead)
+        if distance < half - 1:
+            ahead = lax.optimization_barrier(ahead)
         behind = lax.optimization_barrier(behind)
         k_two, v_two = [ahead[0], behind[1]], [behind[0], ahead[1]]
         k_all += k_two

time: 30.6 us -> 30.1 us (0.984)
  transfers between devices with their start and end apart: 14 -> 14, of which waited for: 10 -> 9; matrix products, arithmetic and copies ran while one was open for 0% -> 0% of each run, Pallas kernels for 13% -> 14%
where the time goes in v15:
time: 30.1 us; the launch traced here: 29.9 us
  starting transfers between devices  13.4 us (45%)
  waiting for transfers between devices  12.1 us (40%)
  Pallas kernels  4.22 us (14%)
    ppermute x14, starting transfers between devices, send(): lax.ppermute(x, 'seq', [(ring[p], ring[to]) for p, to in sorted(step.item...  13.4 us
    ppermute x14, waiting for transfers between devices, send(): lax.ppermute(x, 'seq', [(ring[p], ring[to]) for p, to in sorted(step.item...  12.1 us
    pallas_call x1, Pallas kernels, attend(): pl.pallas_call(functools.partial(attend_kernel, codes=codes, code=code, l...  2.47 us
    pallas_call x1, Pallas kernels, prepare(): pl.pallas_call(functools.partial(prepare_kernel, kv_dev=kv_dev), out_shap...  1.57 us
  transfers between devices with their start and end apart: 14, of which 9 were waited for; matrix products, arithmetic and copies ran while one was open for 0% of the time, Pallas kernels for 14%

profile of v15, /device:TPU:0, one launch (start us, length us, event | category | flops | bytes accessed | tf_op | source)
XLA Modules:
  0.0 29.9 jit_solution(9178352967568052395)
XLA Ops:
  0.0 3.0 %collective-permute-start = (bf16[512,128]{1,0:T(8,128)(2,1)}, bf16[512,128]{1,0:T(8,128)(2,1)S(1)}, u32[]{:S(2)}, u32[]{:S(2)}) collective-permute-start(bf16[512,128]{1,0:T(8,128)(2,1)} %bitcast.6), channel_id=1, source_target_pairs={{0,4},{4,8},{8,12},{12,14},{14,10},{10,6},{6,2},{2,0},{1,5},{5,9},... | collective-permute-start | bytes 393224 | tf_op jit(solution)/shard_map/ppermute | solution.py:350
  3.0 0.0 collective-permute-start.1
  3.0 2.0 %collective-permute-start.2 = (bf16[512,128]{1,0:T(8,128)(2,1)}, bf16[512,128]{1,0:T(8,128)(2,1)S(1)}, u32[]{:S(2)}, u32[]{:S(2)}) collective-permute-start(bf16[512,128]{1,0:T(8,128)(2,1)} %bitcast.4), channel_id=1, source_target_pairs={{0,4},{4,8},{8,12},{12,14},{14,10},{10,6},{6,2},{2,0},{1,5},{5,9},... | collective-permute-start | bytes 393224 | tf_op jit(solution)/shard_map/ppermute | solution.py:350
  5.1 0.0 collective-permute-start.3
  5.1 1.6 %prepare.1 = (s32[4,8]{1,0:T(4,128)S(1)}, bf16[4,1024,128]{2,1,0:T(8,128)(2,1)S(1)}, bf16[4,128,128]{2,1,0:T(8,128)(2,1)S(1)}, bf16[4,128,128]{2,1,0:T(8,128)(2,1)S(1)}) custom-call(s32[4,8]{1,0:T(4,128)} %bitcast.9, bf16[128,32,128]{2,1,0:T(8,128)(2,1)} %q_hbm.1, bf16[512,128]{1,0:T(8,128)(2,1)} %bitcast.8, bf16[512,128]{1,0:T(8,128)(2,1)} %bitcast.5), custom_call_target="tpu_custom_call" | custom-call | tf_op jit(solution)/shard_map/prepare/pallas_call | solution.py:55
  6.6 0.8 %collective-permute-done.refs_0_ = bf16[512,128]{1,0:T(8,128)(2,1)S(1)} collective-permute-done((bf16[512,128]{1,0:T(8,128)(2,1)}, bf16[512,128]{1,0:T(8,128)(2,1)S(1)}, u32[]{:S(2)}, u32[]{:S(2)}) %collective-permute-start) | collective-permute-done | bytes 131104 | tf_op jit(solution)/shard_map/ppermute | solution.py:350
  7.5 2.1 %collective-permute-done.1.refs_7_ = bf16[512,128]{1,0:T(8,128)(2,1)S(1)} collective-permute-done((bf16[512,128]{1,0:T(8,128)(2,1)}, bf16[512,128]{1,0:T(8,128)(2,1)S(1)}, u32[]{:S(2)}, u32[]{:S(2)}) %collective-permute-start.1) | collective-permute-done | bytes 131104 | tf_op jit(solution)/shard_map/ppermute | solution.py:350
  9.6 1.6 %collective-permute-start.4 = (bf16[512,128]{1,0:T(8,128)(2,1)S(1)}, bf16[512,128]{1,0:T(8,128)(2,1)S(1)}, u32[]{:S(2)}, u32[]{:S(2)}) collective-permute-start(bf16[512,128]{1,0:T(8,128)(2,1)S(1)} %collective-permute-done.refs_0_), channel_id=1, source_target_pairs={{0,4},{4,8},{8,12},{12,14},{14,10},{10,6},{6,2},{2,0},{1,5},{5,9},... | collective-permute-start | bytes 393224 | tf_op jit(solution)/shard_map/ppermute | solution.py:350
  11.1 0.4 %collective-permute-start.5 = (bf16[512,128]{1,0:T(8,128)(2,1)S(1)}, bf16[512,128]{1,0:T(8,128)(2,1)S(1)}, u32[]{:S(2)}, u32[]{:S(2)}) collective-permute-start(bf16[512,128]{1,0:T(8,128)(2,1)S(1)} %collective-permute-done.1.refs_7_), channel_id=1, source_target_pairs={{0,2},{4,0},{8,4},{12,8},{14,12},{10,14},{6,10},{2,6},{1,3},{5,1},... | collective-permute-start | bytes 393224 | tf_op jit(solution)/shard_map/ppermute | solution.py:350
  11.6 0.0 collective-permute-done.2.refs_6_
  11.6 0.0 collective-permute-done.3.refs_1_
  11.6 1.6 %collective-permute-start.6 = (bf16[512,128]{1,0:T(8,128)(2,1)S(1)}, bf16[512,128]{1,0:T(8,128)(2,1)S(1)}, u32[]{:S(2)}, u32[]{:S(2)}) collective-permute-start(bf16[512,128]{1,0:T(8,128)(2,1)S(1)} %collective-permute-done.2.refs_6_), channel_id=1, source_target_pairs={{0,4},{4,8},{8,12},{12,14},{14,10},{10,6},{6,2},{2,0},{1,5},{5,9},... | collective-permute-start | bytes 393224 | tf_op jit(solution)/shard_map/ppermute | solution.py:350
  13.2 0.5 %collective-permute-start.7 = (bf16[512,128]{1,0:T(8,128)(2,1)S(1)}, bf16[512,128]{1,0:T(8,128)(2,1)S(1)}, u32[]{:S(2)}, u32[]{:S(2)}) collective-permute-start(bf16[512,128]{1,0:T(8,128)(2,1)S(1)} %collective-permute-done.3.refs_1_), channel_id=1, source_target_pairs={{0,2},{4,0},{8,4},{12,8},{14,12},{10,14},{6,10},{2,6},{1,3},{5,1},... | collective-permute-start | bytes 393224 | tf_op jit(solution)/shard_map/ppermute | solution.py:350
  13.6 1.8 %collective-permute-done.4.refs_2_ = bf16[512,128]{1,0:T(8,128)(2,1)S(1)} collective-permute-done((bf16[512,128]{1,0:T(8,128)(2,1)S(1)}, bf16[512,128]{1,0:T(8,128)(2,1)S(1)}, u32[]{:S(2)}, u32[]{:S(2)}) %collective-permute-start.4) | collective-permute-done | bytes 131104 | tf_op jit(solution)/shard_map/ppermute | solution.py:350
  15.4 1.3 %collective-permute-done.5.refs_9_ = bf16[512,128]{1,0:T(8,128)(2,1)S(1)} collective-permute-done((bf16[512,128]{1,0:T(8,128)(2,1)S(1)}, bf16[512,128]{1,0:T(8,128)(2,1)S(1)}, u32[]{:S(2)}, u32[]{:S(2)}) %collective-permute-start.5) | collective-permute-done | bytes 131104 | tf_op jit(solution)/shard_map/ppermute | solution.py:350
  16.8 1.6 %collective-permute-start.8 = (bf16[512,128]{1,0:T(8,128)(2,1)S(1)}, bf16[512,128]{1,0:T(8,128)(2,1)S(1)}, u32[]{:S(2)}, u32[]{:S(2)}) collective-permute-start(bf16[512,128]{1,0:T(8,128)(2,1)S(1)} %collective-permute-done.4.refs_2_), channel_id=1, source_target_pairs={{0,4},{4,8},{8,12},{12,14},{14,10},{10,6},{6,2},{2,0},{1,5},{5,9},... | collective-permute-start | bytes 393224 | tf_op jit(solution)/shard_map/ppermute | solution.py:350
  18.3 0.4 %collective-permute-start.11 = (bf16[512,128]{1,0:T(8,128)(2,1)S(1)}, bf16[512,128]{1,0:T(8,128)(2,1)S(1)}, u32[]{:S(2)}, u32[]{:S(2)}) collective-permute-start(bf16[512,128]{1,0:T(8,128)(2,1)S(1)} %collective-permute-done.5.refs_9_), channel_id=1, source_target_pairs={{0,2},{4,0},{8,4},{12,8},{14,12},{10,14},{6,10},{2,6},{1,3},{5,1},... | collective-permute-start | bytes 393224 | tf_op jit(solution)/shard_map/ppermute | solution.py:350
  18.8 0.0 collective-permute-done.6.refs_8_
  18.8 0.8 %collective-permute-done.7.refs_3_ = bf16[512,128]{1,0:T(8,128)(2,1)S(1)} collective-permute-done((bf16[512,128]{1,0:T(8,128)(2,1)S(1)}, bf16[512,128]{1,0:T(8,128)(2,1)S(1)}, u32[]{:S(2)}, u32[]{:S(2)}) %collective-permute-start.7) | collective-permute-done | bytes 131104 | tf_op jit(solution)/shard_map/ppermute | solution.py:350
  19.6 0.4 %collective-permute-start.10 = (bf16[512,128]{1,0:T(8,128)(2,1)S(1)}, bf16[512,128]{1,0:T(8,128)(2,1)S(1)}, u32[]{:S(2)}, u32[]{:S(2)}) collective-permute-start(bf16[512,128]{1,0:T(8,128)(2,1)S(1)} %collective-permute-done.7.refs_3_), channel_id=1, source_target_pairs={{0,2},{4,0},{8,4},{12,8},{14,12},{10,14},{6,10},{2,6},{1,3},{5,1},... | collective-permute-start | bytes 393224 | tf_op jit(solution)/shard_map/ppermute | solution.py:350
  20.0 1.6 %collective-permute-start.9 = (bf16[512,128]{1,0:T(8,128)(2,1)S(1)}, bf16[512,128]{1,0:T(8,128)(2,1)S(1)}, u32[]{:S(2)}, u32[]{:S(2)}) collective-permute-start(bf16[512,128]{1,0:T(8,128)(2,1)S(1)} %collective-permute-done.6.refs_8_), channel_id=1, source_target_pairs={{0,4},{4,8},{8,12},{12,14},{14,10},{10,6},{6,2},{2,0},{1,5},{5,9},... | collective-permute-start | bytes 393224 | tf_op jit(solution)/shard_map/ppermute | solution.py:350
  21.6 1.4 %collective-permute-done.8.refs_4_ = bf16[512,128]{1,0:T(8,128)(2,1)S(1)} collective-permute-done((bf16[512,128]{1,0:T(8,128)(2,1)S(1)}, bf16[512,128]{1,0:T(8,128)(2,1)S(1)}, u32[]{:S(2)}, u32[]{:S(2)}) %collective-permute-start.8) | collective-permute-done | bytes 131104 | tf_op jit(solution)/shard_map/ppermute | solution.py:350
  23.0 0.0 collective-permute-start.12
  23.0 1.5 %collective-permute-done.11.refs_11_ = bf16[512,128]{1,0:T(8,128)(2,1)S(1)} collective-permute-done((bf16[512,128]{1,0:T(8,128)(2,1)S(1)}, bf16[512,128]{1,0:T(8,128)(2,1)S(1)}, u32[]{:S(2)}, u32[]{:S(2)}) %collective-permute-start.11) | collective-permute-done | bytes 131104 | tf_op jit(solution)/shard_map/ppermute | solution.py:350
  24.6 0.2 collective-permute-start.13
  24.8 1.2 %collective-permute-done.10.refs_5_ = bf16[512,128]{1,0:T(8,128)(2,1)S(1)} collective-permute-done((bf16[512,128]{1,0:T(8,128)(2,1)S(1)}, bf16[512,128]{1,0:T(8,128)(2,1)S(1)}, u32[]{:S(2)}, u32[]{:S(2)}) %collective-permute-start.10) | collective-permute-done | bytes 131104 | tf_op jit(solution)/shard_map/ppermute | solution.py:350
  26.0 0.0 collective-permute-done.9.refs_10_
  26.0 2.5 %attend.1 = (bf16[128,32,128]{2,1,0:T(8,128)(2,1)}, f32[4,1024,128]{2,1,0:T(8,128)S(1)}, f32[4,1024,256]{2,1,0:T(8,128)S(1)}) custom-call(s32[4,8]{1,0:T(4,128)S(1)} %get-tuple-element.32.lists_ref, bf16[4,1024,128]{2,1,0:T(8,128)(2,1)S(1)} %get-tuple-element.33.q_ref, bf16[4,128,128]{2,1,0:T(8,128)(2,1)S(1)} %get-tuple-element.34.k_own_ref, ...), custom_call_target="tpu_custom_call" | custom-call | tf_op jit(solution)/shard_map/attend/pallas_call | solution.py:232
  28.5 0.0 collective-permute-done.12.k_ref
  28.5 1.1 %collective-permute-done.13.v_ref = bf16[512,128]{1,0:T(8,128)(2,1)S(1)} collective-permute-done((bf16[512,128]{1,0:T(8,128)(2,1)S(1)}, bf16[512,128]{1,0:T(8,128)(2,1)S(1)}, u32[]{:S(2)}, u32[]{:S(2)}) %collective-permute-start.13) | collective-permute-done | bytes 131104 | tf_op jit(solution)/shard_map/ppermute | solution.py:350
  29.6 0.2 attend_last.1
  (2 shorter events, 0.0 us)
Async XLA Ops:
  0.0 7.5 %collective-permute-start = (bf16[512,128]{1,0:T(8,128)(2,1)}, bf16[512,128]{1,0:T(8,128)(2,1)S(1)}, u32[]{:S(2)}, u32[]{:S(2)}) collective-permute-start(bf16[512,128]{1,0:T(8,128)(2,1)} %bitcast.6), channel_id=1, source_target_pairs={{0,4},{4,8},{8,12},{12,14},{14,10},{10,6},{6,2},{2,0},{1,5},{5,9},... | collective-permute-start | bytes 393224 | tf_op jit(solution)/shard_map/ppermute | solution.py:350
  3.0 6.5 %collective-permute-start.1 = (bf16[512,128]{1,0:T(8,128)(2,1)}, bf16[512,128]{1,0:T(8,128)(2,1)S(1)}, u32[]{:S(2)}, u32[]{:S(2)}) collective-permute-start(bf16[512,128]{1,0:T(8,128)(2,1)} %bitcast.3), channel_id=1, source_target_pairs={{0,2},{4,0},{8,4},{12,8},{14,12},{10,14},{6,10},{2,6},{1,3},{5,1},... | collective-permute-start | bytes 393224 | tf_op jit(solution)/shard_map/ppermute | solution.py:350
  3.0 8.6 %collective-permute-start.2 = (bf16[512,128]{1,0:T(8,128)(2,1)}, bf16[512,128]{1,0:T(8,128)(2,1)S(1)}, u32[]{:S(2)}, u32[]{:S(2)}) collective-permute-start(bf16[512,128]{1,0:T(8,128)(2,1)} %bitcast.4), channel_id=1, source_target_pairs={{0,4},{4,8},{8,12},{12,14},{14,10},{10,6},{6,2},{2,0},{1,5},{5,9},... | collective-permute-start | bytes 393224 | tf_op jit(solution)/shard_map/ppermute | solution.py:350
  5.1 6.5 %collective-permute-start.3 = (bf16[512,128]{1,0:T(8,128)(2,1)}, bf16[512,128]{1,0:T(8,128)(2,1)S(1)}, u32[]{:S(2)}, u32[]{:S(2)}) collective-permute-start(bf16[512,128]{1,0:T(8,128)(2,1)} %bitcast.7), channel_id=1, source_target_pairs={{0,2},{4,0},{8,4},{12,8},{14,12},{10,14},{6,10},{2,6},{1,3},{5,1},... | collective-permute-start | bytes 393224 | tf_op jit(solution)/shard_map/ppermute | solution.py:350
  9.6 5.9 %collective-permute-start.4 = (bf16[512,128]{1,0:T(8,128)(2,1)S(1)}, bf16[512,128]{1,0:T(8,128)(2,1)S(1)}, u32[]{:S(2)}, u32[]{:S(2)}) collective-permute-start(bf16[512,128]{1,0:T(8,128)(2,1)S(1)} %collective-permute-done.refs_0_), channel_id=1, source_target_pairs={{0,4},{4,8},{8,12},{12,14},{14,10},{10,6},{6,2},{2,0},{1,5},{5,9},... | collective-permute-start | bytes 393224 | tf_op jit(solution)/shard_map/ppermute | solution.py:350
  11.1 5.6 %collective-permute-start.5 = (bf16[512,128]{1,0:T(8,128)(2,1)S(1)}, bf16[512,128]{1,0:T(8,128)(2,1)S(1)}, u32[]{:S(2)}, u32[]{:S(2)}) collective-permute-start(bf16[512,128]{1,0:T(8,128)(2,1)S(1)} %collective-permute-done.1.refs_7_), channel_id=1, source_target_pairs={{0,2},{4,0},{8,4},{12,8},{14,12},{10,14},{6,10},{2,6},{1,3},{5,1},... | collective-permute-start | bytes 393224 | tf_op jit(solution)/shard_map/ppermute | solution.py:350
  11.6 7.2 %collective-permute-start.6 = (bf16[512,128]{1,0:T(8,128)(2,1)S(1)}, bf16[512,128]{1,0:T(8,128)(2,1)S(1)}, u32[]{:S(2)}, u32[]{:S(2)}) collective-permute-start(bf16[512,128]{1,0:T(8,128)(2,1)S(1)} %collective-permute-done.2.refs_6_), channel_id=1, source_target_pairs={{0,4},{4,8},{8,12},{12,14},{14,10},{10,6},{6,2},{2,0},{1,5},{5,9},... | collective-permute-start | bytes 393224 | tf_op jit(solution)/shard_map/ppermute | solution.py:350
  13.2 6.4 %collective-permute-start.7 = (bf16[512,128]{1,0:T(8,128)(2,1)S(1)}, bf16[512,128]{1,0:T(8,128)(2,1)S(1)}, u32[]{:S(2)}, u32[]{:S(2)}) collective-permute-start(bf16[512,128]{1,0:T(8,128)(2,1)S(1)} %collective-permute-done.3.refs_1_), channel_id=1, source_target_pairs={{0,2},{4,0},{8,4},{12,8},{14,12},{10,14},{6,10},{2,6},{1,3},{5,1},... | collective-permute-start | bytes 393224 | tf_op jit(solution)/shard_map/ppermute | solution.py:350
  16.8 6.2 %collective-permute-start.8 = (bf16[512,128]{1,0:T(8,128)(2,1)S(1)}, bf16[512,128]{1,0:T(8,128)(2,1)S(1)}, u32[]{:S(2)}, u32[]{:S(2)}) collective-permute-start(bf16[512,128]{1,0:T(8,128)(2,1)S(1)} %collective-permute-done.4.refs_2_), channel_id=1, source_target_pairs={{0,4},{4,8},{8,12},{12,14},{14,10},{10,6},{6,2},{2,0},{1,5},{5,9},... | collective-permute-start | bytes 393224 | tf_op jit(solution)/shard_map/ppermute | solution.py:350
  18.3 6.2 %collective-permute-start.11 = (bf16[512,128]{1,0:T(8,128)(2,1)S(1)}, bf16[512,128]{1,0:T(8,128)(2,1)S(1)}, u32[]{:S(2)}, u32[]{:S(2)}) collective-permute-start(bf16[512,128]{1,0:T(8,128)(2,1)S(1)} %collective-permute-done.5.refs_9_), channel_id=1, source_target_pairs={{0,2},{4,0},{8,4},{12,8},{14,12},{10,14},{6,10},{2,6},{1,3},{5,1},... | collective-permute-start | bytes 393224 | tf_op jit(solution)/shard_map/ppermute | solution.py:350
  19.6 6.4 %collective-permute-start.10 = (bf16[512,128]{1,0:T(8,128)(2,1)S(1)}, bf16[512,128]{1,0:T(8,128)(2,1)S(1)}, u32[]{:S(2)}, u32[]{:S(2)}) collective-permute-start(bf16[512,128]{1,0:T(8,128)(2,1)S(1)} %collective-permute-done.7.refs_3_), channel_id=1, source_target_pairs={{0,2},{4,0},{8,4},{12,8},{14,12},{10,14},{6,10},{2,6},{1,3},{5,1},... | collective-permute-start | bytes 393224 | tf_op jit(solution)/shard_map/ppermute | solution.py:350
  20.0 6.0 %collective-permute-start.9 = (bf16[512,128]{1,0:T(8,128)(2,1)S(1)}, bf16[512,128]{1,0:T(8,128)(2,1)S(1)}, u32[]{:S(2)}, u32[]{:S(2)}) collective-permute-start(bf16[512,128]{1,0:T(8,128)(2,1)S(1)} %collective-permute-done.6.refs_8_), channel_id=1, source_target_pairs={{0,4},{4,8},{8,12},{12,14},{14,10},{10,6},{6,2},{2,0},{1,5},{5,9},... | collective-permute-start | bytes 393224 | tf_op jit(solution)/shard_map/ppermute | solution.py:350
  23.0 5.5 %collective-permute-start.12 = (bf16[512,128]{1,0:T(8,128)(2,1)S(1)}, bf16[512,128]{1,0:T(8,128)(2,1)S(1)}, u32[]{:S(2)}, u32[]{:S(2)}) collective-permute-start(bf16[512,128]{1,0:T(8,128)(2,1)S(1)} %broadcast_select_fusion.1), channel_id=1, source_target_pairs={{0,2},{4,6},{8,12},{12,14},{14,10},{10,8},{6,4},{2,0},{1,3},{5,7},... | collective-permute-start | bytes 393224 | tf_op jit(solution)/shard_map/ppermute | solution.py:350
  24.6 5.0 %collective-permute-start.13 = (bf16[512,128]{1,0:T(8,128)(2,1)S(1)}, bf16[512,128]{1,0:T(8,128)(2,1)S(1)}, u32[]{:S(2)}, u32[]{:S(2)}) collective-permute-start(bf16[512,128]{1,0:T(8,128)(2,1)S(1)} %broadcast_select_fusion), channel_id=1, source_target_pairs={{0,4},{4,0},{8,10},{12,8},{14,12},{10,14},{6,2},{2,6},{1,5},{5,1},... | collective-permute-start | bytes 393224 | tf_op jit(solution)/shard_map/ppermute | solution.py:350

commit v16 on v15

--- a/solution.py
+++ b/solution.py
@@ -22,45 +22,64 @@
     return pl.BlockSpec(memory_space=pltpu.VMEM)
 
 
-def prepare_kernel(
-    lists_hbm, q_hbm, k_hbm, v_hbm, lists_out, q_out, k_out, v_out,
-    q_ref, k_ref, v_ref, k_wide, v_wide, sems, *, kv_dev,
-):
-    whole = ((k_hbm, k_ref), (v_hbm, v_ref), (q_hbm, q_ref), (lists_hbm, lists_out))
-    copies = [
-        pltpu.make_async_copy(source, here, sems.at[n]) for n, (source, here) in enumerate(whole)
-    ]
-    for copy in copies:
-        copy.start()
-    tokens, heads, dim = q_ref.shape
-    group = heads // kv_dev
-    for copy, ref, wide, out in zip(copies, (k_ref, v_ref), (k_wide, v_wide), (k_out, v_out)):
-        copy.wait()
-        wide[...] = ref[...].astype(jnp.float32)
+def prepare_kernel(*refs, kv_dev, turn):
+    n_in = 4
+    lists_hbm, q_hbm, k_hbm, v_hbm = refs[:n_in]
+    rest = refs[n_in:]
+    made = rest[: len(rest) - 10]
+    outs = rest[len(made) : len(made) + 4]
+    lists_out, q_out, k_out, v_out = outs
+    q_ref, k_ref, v_ref, k_wide, v_wide, sems = rest[len(made) + 4 :]
+
+    def work():
+        whole = ((k_hbm, k_ref), (v_hbm, v_ref), (q_hbm, q_ref), (lists_hbm, lists_out))
+        copies = [
+            pltpu.make_async_copy(source, here, sems.at[n])
+            for n, (source, here) in enumerate(whole)
+        ]
+        for copy in copies:
+            copy.start()
+        tokens, heads, dim = q_ref.shape
+        group = heads // kv_dev
+        for copy, ref, wide, out in zip(copies, (k_ref, v_ref), (k_wide, v_wide), (k_out, v_out)):
+            copy.wait()
+            wide[...] = ref[...].astype(jnp.float32)
+            for h in range(kv_dev):
+                out[h] = wide[pl.ds(h, tokens, stride=kv_dev), :].astype(jnp.bfloat16)
+        copies[2].wait()
         for h in range(kv_dev):
-            out[h] = wide[pl.ds(h, tokens, stride=kv_dev), :].astype(jnp.bfloat16)
-    copies[2].wait()
-    for h in range(kv_dev):
-        q = q_ref[:, pl.ds(h * group, group), :].astype(jnp.float32)
-        q_out[h] = q.reshape(tokens * group, dim).astype(jnp.bfloat16)
-    copies[3].wait()
-
-
-def prepare(lists, queries, k_own, v_own, kv_dev):
+            q = q_ref[:, pl.ds(h * group, group), :].astype(jnp.float32)
+            q_out[h] = q.reshape(tokens * group, dim).astype(jnp.bfloat16)
+        copies[3].wait()
+
+    if turn is None:
+        work()
+        return
+    mine = lax.rem(lax.axis_index("head"), turn[1]) == turn[0]
+    pl.when(mine)(work)
+    if made:
+
+        @pl.when(jnp.logical_not(mine))
+        def _take_over():
+            for before, out in zip(made, outs):
+                out[...] = before[...]
+
+
+def prepare(lists, queries, k_own, v_own, kv_dev, turn=None, made=()):
     tokens, heads, dim = queries.shape
     operands = [
         pltpu.with_memory_space_constraint(x, pltpu.HBM) for x in (lists, queries, k_own, v_own)
     ]
     by_head = jax.ShapeDtypeStruct((kv_dev, tokens, dim), jnp.bfloat16)
     return pl.pallas_call(
-        functools.partial(prepare_kernel, kv_dev=kv_dev),
+        functools.partial(prepare_kernel, kv_dev=kv_dev, turn=turn),
         out_shape=(
             jax.ShapeDtypeStruct(lists.shape, lists.dtype),
             jax.ShapeDtypeStruct((kv_dev, tokens * heads // kv_dev, dim), jnp.bfloat16),
             by_head,
             by_head,
         ),
-        in_specs=[pl.BlockSpec(memory_space=pltpu.HBM)] * 4,
+        in_specs=[pl.BlockSpec(memory_space=pltpu.HBM)] * 4 + [vmem()] * len(made),
         out_specs=(vmem(), vmem(), vmem(), vmem()),
         scratch_shapes=[
             pltpu.VMEM(queries.shape, jnp.bfloat16),
@@ -72,7 +91,7 @@
         ],
         compiler_params=params(),
         name="prepare",
-    )(*operands)
+    )(*operands, *made)
 
 
 def listed_bits(lists_ref, code):
@@ -393,7 +412,10 @@
     k_own = keys.reshape(tokens * kv_dev, dim)
     v_own = values.reshape(tokens * kv_dev, dim)
     if members in ROUND:
-        ready = prepare(chosen.T, queries, k_own, v_own, kv_dev)
+        own = chosen.T, queries, k_own, v_own, kv_dev
+        made = prepare(*own, turn=(1, 2))
+        k_own, v_own, made = lax.optimization_barrier((k_own, v_own, made))
+        ready = prepare(*own, turn=(0, 2), made=made)
         k_parts, v_parts, k_last, v_last, ready = round_the_ring(k_own, v_own, ready, members)
         lists, q_ready, k_ready, v_ready = ready
         half, code = members // 2, ring_code(members)

time: 30.1 us -> 33 us (1.096); the launches traced: 29.9 us -> 32.3 us
  starting transfers between devices: 13.4 us -> 15.4 us
  waiting for transfers between devices: 12.1 us -> 12.5 us
    ppermute x14, starting transfers between devices: 13.4 us -> 15.4 us  [send(): lax.ppermute(x, 'seq', [(ring[p], ring[to]) for p, to in sorted(step.item...]
    ppermute x14, waiting for transfers between devices: 12.1 us -> 12.5 us  [send(): lax.ppermute(x, 'seq', [(ring[p], ring[to]) for p, to in sorted(step.item...]
    pallas_call x1 -> x2, Pallas kernels: 1.57 us -> 1.61 us  [prepare(): pl.pallas_call(functools.partial(prepare_kernel, kv_dev=kv_dev, turn=turn...]
  transfers between devices with their start and end apart: 14 -> 14, of which waited for: 9 -> 9; matrix products, arithmetic and copies ran while one was open for 0% -> 0% of each run, Pallas kernels for 14% -> 13%
where the time goes in v16:
time: 33 us; the launch traced here: 32.3 us
  starting transfers between devices  15.4 us (47%)
  waiting for transfers between devices  12.5 us (38%)
  Pallas kernels  4.25 us (13%)
    ppermute x14, starting transfers between devices, send(): lax.ppermute(x, 'seq', [(ring[p], ring[to]) for p, to in sorted(step.item...  15.4 us
    ppermute x14, waiting for transfers between devices, send(): lax.ppermute(x, 'seq', [(ring[p], ring[to]) for p, to in sorted(step.item...  12.5 us
    pallas_call x1, Pallas kernels, attend(): pl.pallas_call(functools.partial(attend_kernel, codes=codes, code=code, l...  2.47 us
    pallas_call x2, Pallas kernels, prepare(): pl.pallas_call(functools.partial(prepare_kernel, kv_dev=kv_dev, turn=turn...  1.61 us
  transfers between devices with their start and end apart: 14, of which 9 were waited for; matrix products, arithmetic and copies ran while one was open for 0% of the time, Pallas kernels for 13%

profile of v16, /device:TPU:0, one launch (start us, length us, event | category | flops | bytes accessed | tf_op | source)
XLA Modules:
  0.0 32.3 jit_solution(2167337786471318920)
XLA Ops:
  0.0 3.1 %collective-permute-start = (bf16[512,128]{1,0:T(8,128)(2,1)}, bf16[512,128]{1,0:T(8,128)(2,1)S(1)}, u32[]{:S(2)}, u32[]{:S(2)}) collective-permute-start(bf16[512,128]{1,0:T(8,128)(2,1)} %bitcast.8), channel_id=1, source_target_pairs={{0,4},{4,8},{8,12},{12,14},{14,10},{10,6},{6,2},{2,0},{1,5},{5,9},... | collective-permute-start | bytes 393224 | tf_op jit(solution)/shard_map/ppermute | solution.py:369
  3.1 0.0 collective-permute-start.1
  3.1 2.0 %collective-permute-start.2 = (bf16[512,128]{1,0:T(8,128)(2,1)}, bf16[512,128]{1,0:T(8,128)(2,1)S(1)}, u32[]{:S(2)}, u32[]{:S(2)}) collective-permute-start(bf16[512,128]{1,0:T(8,128)(2,1)} %bitcast.5), channel_id=1, source_target_pairs={{0,4},{4,8},{8,12},{12,14},{14,10},{10,6},{6,2},{2,0},{1,5},{5,9},... | collective-permute-start | bytes 393224 | tf_op jit(solution)/shard_map/ppermute | solution.py:369
  5.1 0.0 collective-permute-start.3
  5.2 1.6 %prepare.3 = (s32[4,8]{1,0:T(4,128)S(1)}, bf16[4,1024,128]{2,1,0:T(8,128)(2,1)S(1)}, bf16[4,128,128]{2,1,0:T(8,128)(2,1)S(1)}, bf16[4,128,128]{2,1,0:T(8,128)(2,1)S(1)}) custom-call(s32[4,8]{1,0:T(4,128)} %bitcast.12, bf16[128,32,128]{2,1,0:T(8,128)(2,1)} %refs_1_.3, bf16[512,128]{1,0:T(8,128)(2,1)} %bitcast.10, bf16[512,128]{1,0:T(8,128)(2,1)} %bitcast.6, ...), custom_call_target="tpu_custom_call" | custom-call | tf_op jit(solution)/shard_map/prepare/pallas_call | solution.py:74
  6.7 0.3 collective-permute-done.refs_0_
  7.0 2.6 %collective-permute-done.1.refs_7_ = bf16[512,128]{1,0:T(8,128)(2,1)S(1)} collective-permute-done((bf16[512,128]{1,0:T(8,128)(2,1)}, bf16[512,128]{1,0:T(8,128)(2,1)S(1)}, u32[]{:S(2)}, u32[]{:S(2)}) %collective-permute-start.1) | collective-permute-done | bytes 131104 | tf_op jit(solution)/shard_map/ppermute | solution.py:369
  9.6 1.6 %collective-permute-start.4 = (bf16[512,128]{1,0:T(8,128)(2,1)S(1)}, bf16[512,128]{1,0:T(8,128)(2,1)S(1)}, u32[]{:S(2)}, u32[]{:S(2)}) collective-permute-start(bf16[512,128]{1,0:T(8,128)(2,1)S(1)} %collective-permute-done.refs_0_), channel_id=1, source_target_pairs={{0,4},{4,8},{8,12},{12,14},{14,10},{10,6},{6,2},{2,0},{1,5},{5,9},... | collective-permute-start | bytes 393224 | tf_op jit(solution)/shard_map/ppermute | solution.py:369
  11.2 0.4 %collective-permute-start.5 = (bf16[512,128]{1,0:T(8,128)(2,1)S(1)}, bf16[512,128]{1,0:T(8,128)(2,1)S(1)}, u32[]{:S(2)}, u32[]{:S(2)}) collective-permute-start(bf16[512,128]{1,0:T(8,128)(2,1)S(1)} %collective-permute-done.1.refs_7_), channel_id=1, source_target_pairs={{0,2},{4,0},{8,4},{12,8},{14,12},{10,14},{6,10},{2,6},{1,3},{5,1},... | collective-permute-start | bytes 393224 | tf_op jit(solution)/shard_map/ppermute | solution.py:369
  11.6 0.0 collective-permute-done.2.refs_6_
  11.6 0.8 %collective-permute-done.3.refs_1_ = bf16[512,128]{1,0:T(8,128)(2,1)S(1)} collective-permute-done((bf16[512,128]{1,0:T(8,128)(2,1)}, bf16[512,128]{1,0:T(8,128)(2,1)S(1)}, u32[]{:S(2)}, u32[]{:S(2)}) %collective-permute-start.3) | collective-permute-done | bytes 131104 | tf_op jit(solution)/shard_map/ppermute | solution.py:369
  12.4 1.6 %collective-permute-start.6 = (bf16[512,128]{1,0:T(8,128)(2,1)S(1)}, bf16[512,128]{1,0:T(8,128)(2,1)S(1)}, u32[]{:S(2)}, u32[]{:S(2)}) collective-permute-start(bf16[512,128]{1,0:T(8,128)(2,1)S(1)} %collective-permute-done.2.refs_6_), channel_id=1, source_target_pairs={{0,4},{4,8},{8,12},{12,14},{14,10},{10,6},{6,2},{2,0},{1,5},{5,9},... | collective-permute-start | bytes 393224 | tf_op jit(solution)/shard_map/ppermute | solution.py:369
  14.0 0.4 %collective-permute-start.7 = (bf16[512,128]{1,0:T(8,128)(2,1)S(1)}, bf16[512,128]{1,0:T(8,128)(2,1)S(1)}, u32[]{:S(2)}, u32[]{:S(2)}) collective-permute-start(bf16[512,128]{1,0:T(8,128)(2,1)S(1)} %collective-permute-done.3.refs_1_), channel_id=1, source_target_pairs={{0,2},{4,0},{8,4},{12,8},{14,12},{10,14},{6,10},{2,6},{1,3},{5,1},... | collective-permute-start | bytes 393224 | tf_op jit(solution)/shard_map/ppermute | solution.py:369
  14.4 1.1 %collective-permute-done.4.refs_2_ = bf16[512,128]{1,0:T(8,128)(2,1)S(1)} collective-permute-done((bf16[512,128]{1,0:T(8,128)(2,1)S(1)}, bf16[512,128]{1,0:T(8,128)(2,1)S(1)}, u32[]{:S(2)}, u32[]{:S(2)}) %collective-permute-start.4) | collective-permute-done | bytes 131104 | tf_op jit(solution)/shard_map/ppermute | solution.py:369
  15.5 1.3 %collective-permute-done.5.refs_9_ = bf16[512,128]{1,0:T(8,128)(2,1)S(1)} collective-permute-done((bf16[512,128]{1,0:T(8,128)(2,1)S(1)}, bf16[512,128]{1,0:T(8,128)(2,1)S(1)}, u32[]{:S(2)}, u32[]{:S(2)}) %collective-permute-start.5) | collective-permute-done | bytes 131104 | tf_op jit(solution)/shard_map/ppermute | solution.py:369
  16.8 1.6 %collective-permute-start.8 = (bf16[512,128]{1,0:T(8,128)(2,1)S(1)}, bf16[512,128]{1,0:T(8,128)(2,1)S(1)}, u32[]{:S(2)}, u32[]{:S(2)}) collective-permute-start(bf16[512,128]{1,0:T(8,128)(2,1)S(1)} %collective-permute-done.4.refs_2_), channel_id=1, source_target_pairs={{0,4},{4,8},{8,12},{12,14},{14,10},{10,6},{6,2},{2,0},{1,5},{5,9},... | collective-permute-start | bytes 393224 | tf_op jit(solution)/shard_map/ppermute | solution.py:369
  18.4 0.0 collective-permute-done.6.refs_8_
  18.4 1.0 %collective-permute-done.7.refs_3_ = bf16[512,128]{1,0:T(8,128)(2,1)S(1)} collective-permute-done((bf16[512,128]{1,0:T(8,128)(2,1)S(1)}, bf16[512,128]{1,0:T(8,128)(2,1)S(1)}, u32[]{:S(2)}, u32[]{:S(2)}) %collective-permute-start.7) | collective-permute-done | bytes 131104 | tf_op jit(solution)/shard_map/ppermute | solution.py:369
  19.5 0.4 %collective-permute-start.10 = (bf16[512,128]{1,0:T(8,128)(2,1)S(1)}, bf16[512,128]{1,0:T(8,128)(2,1)S(1)}, u32[]{:S(2)}, u32[]{:S(2)}) collective-permute-start(bf16[512,128]{1,0:T(8,128)(2,1)S(1)} %collective-permute-done.7.refs_3_), channel_id=1, source_target_pairs={{0,2},{4,0},{8,4},{12,8},{14,12},{10,14},{6,10},{2,6},{1,3},{5,1},... | collective-permute-start | bytes 393224 | tf_op jit(solution)/shard_map/ppermute | solution.py:369
  19.9 1.6 %collective-permute-start.9 = (bf16[512,128]{1,0:T(8,128)(2,1)S(1)}, bf16[512,128]{1,0:T(8,128)(2,1)S(1)}, u32[]{:S(2)}, u32[]{:S(2)}) collective-permute-start(bf16[512,128]{1,0:T(8,128)(2,1)S(1)} %collective-permute-done.6.refs_8_), channel_id=1, source_target_pairs={{0,4},{4,8},{8,12},{12,14},{14,10},{10,6},{6,2},{2,0},{1,5},{5,9},... | collective-permute-start | bytes 393224 | tf_op jit(solution)/shard_map/ppermute | solution.py:369
  21.5 0.4 %collective-permute-start.11 = (bf16[512,128]{1,0:T(8,128)(2,1)S(1)}, bf16[512,128]{1,0:T(8,128)(2,1)S(1)}, u32[]{:S(2)}, u32[]{:S(2)}) collective-permute-start(bf16[512,128]{1,0:T(8,128)(2,1)S(1)} %collective-permute-done.5.refs_9_), channel_id=1, source_target_pairs={{0,2},{4,0},{8,4},{12,8},{14,12},{10,14},{6,10},{2,6},{1,3},{5,1},... | collective-permute-start | bytes 393224 | tf_op jit(solution)/shard_map/ppermute | solution.py:369
  21.9 0.2 collective-permute-done.8.refs_4_
  22.2 0.5 %collective-permute-start.12 = (bf16[512,128]{1,0:T(8,128)(2,1)S(1)}, bf16[512,128]{1,0:T(8,128)(2,1)S(1)}, u32[]{:S(2)}, u32[]{:S(2)}) collective-permute-start(bf16[512,128]{1,0:T(8,128)(2,1)S(1)} %broadcast_select_fusion.1), channel_id=1, source_target_pairs={{0,2},{4,6},{8,12},{12,14},{14,10},{10,8},{6,4},{2,0},{1,3},{5,7},... | collective-permute-start | bytes 393224 | tf_op jit(solution)/shard_map/ppermute | solution.py:369
  22.7 4.3 %collective-permute-done.11.refs_11_ = bf16[512,128]{1,0:T(8,128)(2,1)S(1)} collective-permute-done((bf16[512,128]{1,0:T(8,128)(2,1)S(1)}, bf16[512,128]{1,0:T(8,128)(2,1)S(1)}, u32[]{:S(2)}, u32[]{:S(2)}) %collective-permute-start.11) | collective-permute-done | bytes 131104 | tf_op jit(solution)/shard_map/ppermute | solution.py:369
  27.0 1.6 %collective-permute-start.13 = (bf16[512,128]{1,0:T(8,128)(2,1)S(1)}, bf16[512,128]{1,0:T(8,128)(2,1)S(1)}, u32[]{:S(2)}, u32[]{:S(2)}) collective-permute-start(bf16[512,128]{1,0:T(8,128)(2,1)S(1)} %broadcast_select_fusion), channel_id=1, source_target_pairs={{0,4},{4,0},{8,10},{12,8},{14,12},{10,14},{6,2},{2,6},{1,5},{5,1},... | collective-permute-start | bytes 393224 | tf_op jit(solution)/shard_map/ppermute | solution.py:369
  28.6 0.0 collective-permute-done.10.refs_5_
  28.6 0.0 collective-permute-done.9.refs_10_
  28.6 2.5 %attend.1 = (bf16[128,32,128]{2,1,0:T(8,128)(2,1)}, f32[4,1024,128]{2,1,0:T(8,128)S(1)}, f32[4,1024,256]{2,1,0:T(8,128)S(1)}) custom-call(s32[4,8]{1,0:T(4,128)S(1)} %get-tuple-element.52.lists_ref, bf16[4,1024,128]{2,1,0:T(8,128)(2,1)S(1)} %get-tuple-element.53.q_ref, bf16[4,128,128]{2,1,0:T(8,128)(2,1)S(1)} %get-tuple-element.54.k_own_ref, ...), custom_call_target="tpu_custom_call" | custom-call | tf_op jit(solution)/shard_map/attend/pallas_call | solution.py:251
  31.1 0.0 collective-permute-done.12.k_ref
  31.1 0.9 %collective-permute-done.13.v_ref = bf16[512,128]{1,0:T(8,128)(2,1)S(1)} collective-permute-done((bf16[512,128]{1,0:T(8,128)(2,1)S(1)}, bf16[512,128]{1,0:T(8,128)(2,1)S(1)}, u32[]{:S(2)}, u32[]{:S(2)}) %collective-permute-start.13) | collective-permute-done | bytes 131104 | tf_op jit(solution)/shard_map/ppermute | solution.py:369
  32.0 0.2 attend_last.1
  (3 shorter events, 0.1 us)
Async XLA Ops:
  0.0 7.0 %collective-permute-start = (bf16[512,128]{1,0:T(8,128)(2,1)}, bf16[512,128]{1,0:T(8,128)(2,1)S(1)}, u32[]{:S(2)}, u32[]{:S(2)}) collective-permute-start(bf16[512,128]{1,0:T(8,128)(2,1)} %bitcast.8), channel_id=1, source_target_pairs={{0,4},{4,8},{8,12},{12,14},{14,10},{10,6},{6,2},{2,0},{1,5},{5,9},... | collective-permute-start | bytes 393224 | tf_op jit(solution)/shard_map/ppermute | solution.py:369
  3.1 6.5 %collective-permute-start.1 = (bf16[512,128]{1,0:T(8,128)(2,1)}, bf16[512,128]{1,0:T(8,128)(2,1)S(1)}, u32[]{:S(2)}, u32[]{:S(2)}) collective-permute-start(bf16[512,128]{1,0:T(8,128)(2,1)} %bitcast.4), channel_id=1, source_target_pairs={{0,2},{4,0},{8,4},{12,8},{14,12},{10,14},{6,10},{2,6},{1,3},{5,1},... | collective-permute-start | bytes 393224 | tf_op jit(solution)/shard_map/ppermute | solution.py:369
  3.1 8.5 %collective-permute-start.2 = (bf16[512,128]{1,0:T(8,128)(2,1)}, bf16[512,128]{1,0:T(8,128)(2,1)S(1)}, u32[]{:S(2)}, u32[]{:S(2)}) collective-permute-start(bf16[512,128]{1,0:T(8,128)(2,1)} %bitcast.5), channel_id=1, source_target_pairs={{0,4},{4,8},{8,12},{12,14},{14,10},{10,6},{6,2},{2,0},{1,5},{5,9},... | collective-permute-start | bytes 393224 | tf_op jit(solution)/shard_map/ppermute | solution.py:369
  5.1 7.2 %collective-permute-start.3 = (bf16[512,128]{1,0:T(8,128)(2,1)}, bf16[512,128]{1,0:T(8,128)(2,1)S(1)}, u32[]{:S(2)}, u32[]{:S(2)}) collective-permute-start(bf16[512,128]{1,0:T(8,128)(2,1)} %bitcast.9), channel_id=1, source_target_pairs={{0,2},{4,0},{8,4},{12,8},{14,12},{10,14},{6,10},{2,6},{1,3},{5,1},... | collective-permute-start | bytes 393224 | tf_op jit(solution)/shard_map/ppermute | solution.py:369
  9.6 6.0 %collective-permute-start.4 = (bf16[512,128]{1,0:T(8,128)(2,1)S(1)}, bf16[512,128]{1,0:T(8,128)(2,1)S(1)}, u32[]{:S(2)}, u32[]{:S(2)}) collective-permute-start(bf16[512,128]{1,0:T(8,128)(2,1)S(1)} %collective-permute-done.refs_0_), channel_id=1, source_target_pairs={{0,4},{4,8},{8,12},{12,14},{14,10},{10,6},{6,2},{2,0},{1,5},{5,9},... | collective-permute-start | bytes 393224 | tf_op jit(solution)/shard_map/ppermute | solution.py:369
  11.2 5.7 %collective-permute-start.5 = (bf16[512,128]{1,0:T(8,128)(2,1)S(1)}, bf16[512,128]{1,0:T(8,128)(2,1)S(1)}, u32[]{:S(2)}, u32[]{:S(2)}) collective-permute-start(bf16[512,128]{1,0:T(8,128)(2,1)S(1)} %collective-permute-done.1.refs_7_), channel_id=1, source_target_pairs={{0,2},{4,0},{8,4},{12,8},{14,12},{10,14},{6,10},{2,6},{1,3},{5,1},... | collective-permute-start | bytes 393224 | tf_op jit(solution)/shard_map/ppermute | solution.py:369
  12.4 6.0 %collective-permute-start.6 = (bf16[512,128]{1,0:T(8,128)(2,1)S(1)}, bf16[512,128]{1,0:T(8,128)(2,1)S(1)}, u32[]{:S(2)}, u32[]{:S(2)}) collective-permute-start(bf16[512,128]{1,0:T(8,128)(2,1)S(1)} %collective-permute-done.2.refs_6_), channel_id=1, source_target_pairs={{0,4},{4,8},{8,12},{12,14},{14,10},{10,6},{6,2},{2,0},{1,5},{5,9},... | collective-permute-start | bytes 393224 | tf_op jit(solution)/shard_map/ppermute | solution.py:369
  14.0 5.5 %collective-permute-start.7 = (bf16[512,128]{1,0:T(8,128)(2,1)S(1)}, bf16[512,128]{1,0:T(8,128)(2,1)S(1)}, u32[]{:S(2)}, u32[]{:S(2)}) collective-permute-start(bf16[512,128]{1,0:T(8,128)(2,1)S(1)} %collective-permute-done.3.refs_1_), channel_id=1, source_target_pairs={{0,2},{4,0},{8,4},{12,8},{14,12},{10,14},{6,10},{2,6},{1,3},{5,1},... | collective-permute-start | bytes 393224 | tf_op jit(solution)/shard_map/ppermute | solution.py:369
  16.8 5.3 %collective-permute-start.8 = (bf16[512,128]{1,0:T(8,128)(2,1)S(1)}, bf16[512,128]{1,0:T(8,128)(2,1)S(1)}, u32[]{:S(2)}, u32[]{:S(2)}) collective-permute-start(bf16[512,128]{1,0:T(8,128)(2,1)S(1)} %collective-permute-done.4.refs_2_), channel_id=1, source_target_pairs={{0,4},{4,8},{8,12},{12,14},{14,10},{10,6},{6,2},{2,0},{1,5},{5,9},... | collective-permute-start | bytes 393224 | tf_op jit(solution)/shard_map/ppermute | solution.py:369
  19.5 9.1 %collective-permute-start.10 = (bf16[512,128]{1,0:T(8,128)(2,1)S(1)}, bf16[512,128]{1,0:T(8,128)(2,1)S(1)}, u32[]{:S(2)}, u32[]{:S(2)}) collective-permute-start(bf16[512,128]{1,0:T(8,128)(2,1)S(1)} %collective-permute-done.7.refs_3_), channel_id=1, source_target_pairs={{0,2},{4,0},{8,4},{12,8},{14,12},{10,14},{6,10},{2,6},{1,3},{5,1},... | collective-permute-start | bytes 393224 | tf_op jit(solution)/shard_map/ppermute | solution.py:369
  19.9 8.7 %collective-permute-start.9 = (bf16[512,128]{1,0:T(8,128)(2,1)S(1)}, bf16[512,128]{1,0:T(8,128)(2,1)S(1)}, u32[]{:S(2)}, u32[]{:S(2)}) collective-permute-start(bf16[512,128]{1,0:T(8,128)(2,1)S(1)} %collective-permute-done.6.refs_8_), channel_id=1, source_target_pairs={{0,4},{4,8},{8,12},{12,14},{14,10},{10,6},{6,2},{2,0},{1,5},{5,9},... | collective-permute-start | bytes 393224 | tf_op jit(solution)/shard_map/ppermute | solution.py:369
  21.5 5.5 %collective-permute-start.11 = (bf16[512,128]{1,0:T(8,128)(2,1)S(1)}, bf16[512,128]{1,0:T(8,128)(2,1)S(1)}, u32[]{:S(2)}, u32[]{:S(2)}) collective-permute-start(bf16[512,128]{1,0:T(8,128)(2,1)S(1)} %collective-permute-done.5.refs_9_), channel_id=1, source_target_pairs={{0,2},{4,0},{8,4},{12,8},{14,12},{10,14},{6,10},{2,6},{1,3},{5,1},... | collective-permute-start | bytes 393224 | tf_op jit(solution)/shard_map/ppermute | solution.py:369
  22.2 8.9 %collective-permute-start.12 = (bf16[512,128]{1,0:T(8,128)(2,1)S(1)}, bf16[512,128]{1,0:T(8,128)(2,1)S(1)}, u32[]{:S(2)}, u32[]{:S(2)}) collective-permute-start(bf16[512,128]{1,0:T(8,128)(2,1)S(1)} %broadcast_select_fusion.1), channel_id=1, source_target_pairs={{0,2},{4,6},{8,12},{12,14},{14,10},{10,8},{6,4},{2,0},{1,3},{5,7},... | collective-permute-start | bytes 393224 | tf_op jit(solution)/shard_map/ppermute | solution.py:369
  27.0 5.0 %collective-permute-start.13 = (bf16[512,128]{1,0:T(8,128)(2,1)S(1)}, bf16[512,128]{1,0:T(8,128)(2,1)S(1)}, u32[]{:S(2)}, u32[]{:S(2)}) collective-permute-start(bf16[512,128]{1,0:T(8,128)(2,1)S(1)} %broadcast_select_fusion), channel_id=1, source_target_pairs={{0,4},{4,0},{8,10},{12,8},{14,12},{10,14},{6,2},{2,6},{1,5},{5,1},... | collective-permute-start | bytes 393224 | tf_op jit(solution)/shard_map/ppermute | solution.py:369

commit v17 on v15

--- a/solution.py
+++ b/solution.py
@@ -11,7 +11,7 @@
 NO_KEY = -1e30
 ROW_CHUNK = 256
 LARGEST = 64.0
-ROUND = (8, 16)
+ROUND = (8,)
 
 
 def params():
@@ -329,31 +329,35 @@
     return code
 
 
-def ring_steps(members):
-    first, final = members // 4, 3 * members // 4 - 1
-    forward = {p: (p + 1) % members for p in range(members)}
-    backward = {p: (p - 1) % members for p in range(members)}
-    low = [p for p in range(members) if not first <= p <= final]
-    last_forward = {p: members - 1 - p for p in low}
-    last_backward = {p: p ^ 1 for p in low}
-    last_forward.update({p: p + 1 for p in range(first, final)})
-    last_backward.update({p: p - 1 for p in range(first + 1, final + 1)})
-    last_forward[final], last_backward[first] = first, final
-    return forward, backward, last_forward, last_backward
+LAST_KEYS = {1: 3, 2: 5, 3: 4, 4: 6, 5: 2, 6: 1}, {1: 2, 2: 0, 3: 4, 5: 1}
+LAST_VALUES = {1: 6, 2: 5, 3: 1, 4: 3, 5: 2, 6: 4}, {2: 0, 4: 4, 5: 1, 6: 3}
 
 
 def round_the_ring(k_own, v_own, ready, members):
     ring = list(range(0, members, 2)) + list(range(members - 1, 0, -2))
-    forward, backward, last_forward, last_backward = ring_steps(members)
-
-    def send(x, step):
-        return lax.ppermute(x, "seq", [(ring[p], ring[to]) for p, to in sorted(step.items())])
+    cores = lax.axis_size("head")
+    here = ring_place(lax.axis_index("seq").astype(jnp.int32), members)
+
+    def send(x, turn):
+        return lax.ppermute(x, "seq", [(ring[p], ring[(p + turn) % members]) for p in range(members)])
+
+    def send_last(parts, plan):
+        steps, whats = plan
+        x = parts[-1]
+        for place, what in whats.items():
+            x = jnp.where(here == place, parts[what], x)
+        pairs = []
+        for p in range(members):
+            for core in range(cores):
+                to = (steps[p], core) if p in steps else (p, (core + 1) % cores)
+                pairs.append((ring[p] * cores + core, ring[to[0]] * cores + to[1]))
+        return lax.ppermute(x, ("seq", "head"), pairs)
 
     half = members // 2
     k_two, v_two, k_all, v_all = [k_own, k_own], [v_own, v_own], [], []
     for distance in range(1, half):
-        ahead = send(k_two[0], forward), send(v_two[1], backward)
-        behind = send(v_two[0], forward), send(k_two[1], backward)
+        ahead = send(k_two[0], 1), send(v_two[1], -1)
+        behind = send(v_two[0], 1), send(k_two[1], -1)
         if distance == 1:
             ahead, ready = lax.optimization_barrier((ahead, ready))
         if distance < half - 1:
@@ -362,10 +366,9 @@
         k_two, v_two = [ahead[0], behind[1]], [behind[0], ahead[1]]
         k_all += k_two
         v_all += v_two
-    here = ring_place(lax.axis_index("seq").astype(jnp.int32), members)
-    k_last = jnp.where(here == 3 * members // 4 - 1, k_all[1], k_two[0])
-    v_last = jnp.where(here == members // 4, v_all[0], v_two[1])
-    return k_all, v_all, send(k_last, last_forward), send(v_last, last_backward), ready
+    k_last = send_last(k_all[:-1], LAST_KEYS)
+    v_last = send_last(v_all[:-2] + v_all[-1:], LAST_VALUES)
+    return k_all, v_all, k_last, v_last, ready
 
 
 def others(row, target):

time: 30.1 us -> 29.6 us (0.983)
  the two profiles are of different devices: /device:TPU:0 before, /device:TPU:20 now
where the time goes in v17:
time: 29.6 us; the launch traced here: 29.4 us
  starting transfers between devices  14.4 us (49%)
  waiting for transfers between devices  8.13 us (27%)
  Pallas kernels  6.69 us (23%)
    ppermute x12, starting transfers between devices, send(): lax.ppermute(x, 'seq', [(ring[p], ring[(p + turn) % members]) for p in ra...  12.2 us
    ppermute x12, waiting for transfers between devices, send(): lax.ppermute(x, 'seq', [(ring[p], ring[(p + turn) % members]) for p in ra...  7.81 us
    pallas_call x1, Pallas kernels, attend(): pl.pallas_call(functools.partial(attend_kernel, codes=codes, code=code, l...  2.95 us
    pallas_call x1, Pallas kernels, attend_last(): pl.pallas_call(functools.partial(last_kernel, code=code, last=last), out_...  2.17 us
    ppermute x2, starting transfers between devices, send_last(): return lax.ppermute(x, ('seq', 'head'), pairs)  2.12 us
    pallas_call x1, Pallas kernels, prepare(): pl.pallas_call(functools.partial(prepare_kernel, kv_dev=kv_dev), out_shap...  1.58 us
  transfers between devices with their start and end apart: 14, of which 7 were waited for; matrix products, arithmetic and copies ran while one was open for 0% of the time, Pallas kernels for 15%

profile of v17, /device:TPU:20, one launch (start us, length us, event | category | flops | bytes accessed | tf_op | source)
XLA Modules:
  0.0 29.4 jit_solution(17275245914838751146)
XLA Ops:
  0.0 1.6 %collective-permute-start = (bf16[512,128]{1,0:T(8,128)(2,1)}, bf16[512,128]{1,0:T(8,128)(2,1)S(1)}, u32[]{:S(2)}, u32[]{:S(2)}) collective-permute-start(bf16[512,128]{1,0:T(8,128)(2,1)} %bitcast.6), channel_id=1, source_target_pairs={{0,4},{4,8},{8,12},{12,14},{14,10},{10,6},{6,2},{2,0},{1,5},{5,9},... | collective-permute-start | bytes 393224 | tf_op jit(solution)/shard_map/ppermute | solution.py:342
  1.6 0.4 %collective-permute-start.1 = (bf16[512,128]{1,0:T(8,128)(2,1)}, bf16[512,128]{1,0:T(8,128)(2,1)S(1)}, u32[]{:S(2)}, u32[]{:S(2)}) collective-permute-start(bf16[512,128]{1,0:T(8,128)(2,1)} %bitcast.3), channel_id=1, source_target_pairs={{0,2},{4,0},{8,4},{12,8},{14,12},{10,14},{6,10},{2,6},{1,3},{5,1},... | collective-permute-start | bytes 393224 | tf_op jit(solution)/shard_map/ppermute | solution.py:342
  2.0 1.6 %collective-permute-start.2 = (bf16[512,128]{1,0:T(8,128)(2,1)}, bf16[512,128]{1,0:T(8,128)(2,1)S(1)}, u32[]{:S(2)}, u32[]{:S(2)}) collective-permute-start(bf16[512,128]{1,0:T(8,128)(2,1)} %bitcast.4), channel_id=1, source_target_pairs={{0,4},{4,8},{8,12},{12,14},{14,10},{10,6},{6,2},{2,0},{1,5},{5,9},... | collective-permute-start | bytes 393224 | tf_op jit(solution)/shard_map/ppermute | solution.py:342
  3.6 0.4 %collective-permute-start.3 = (bf16[512,128]{1,0:T(8,128)(2,1)}, bf16[512,128]{1,0:T(8,128)(2,1)S(1)}, u32[]{:S(2)}, u32[]{:S(2)}) collective-permute-start(bf16[512,128]{1,0:T(8,128)(2,1)} %bitcast.7), channel_id=1, source_target_pairs={{0,2},{4,0},{8,4},{12,8},{14,12},{10,14},{6,10},{2,6},{1,3},{5,1},... | collective-permute-start | bytes 393224 | tf_op jit(solution)/shard_map/ppermute | solution.py:342
  4.1 1.6 %prepare.1 = (s32[4,8]{1,0:T(4,128)S(1)}, bf16[4,1024,128]{2,1,0:T(8,128)(2,1)S(1)}, bf16[4,128,128]{2,1,0:T(8,128)(2,1)S(1)}, bf16[4,128,128]{2,1,0:T(8,128)(2,1)S(1)}) custom-call(s32[4,8]{1,0:T(4,128)} %bitcast.9, bf16[128,32,128]{2,1,0:T(8,128)(2,1)} %q_hbm.1, bf16[512,128]{1,0:T(8,128)(2,1)} %bitcast.8, bf16[512,128]{1,0:T(8,128)(2,1)} %bitcast.5), custom_call_target="tpu_custom_call" | custom-call | tf_op jit(solution)/shard_map/prepare/pallas_call | solution.py:55
  5.6 1.0 %collective-permute-done.refs_0_ = bf16[512,128]{1,0:T(8,128)(2,1)S(1)} collective-permute-done((bf16[512,128]{1,0:T(8,128)(2,1)}, bf16[512,128]{1,0:T(8,128)(2,1)S(1)}, u32[]{:S(2)}, u32[]{:S(2)}) %collective-permute-start) | collective-permute-done | bytes 131104 | tf_op jit(solution)/shard_map/ppermute | solution.py:342
  6.6 1.5 %collective-permute-done.1.refs_7_ = bf16[512,128]{1,0:T(8,128)(2,1)S(1)} collective-permute-done((bf16[512,128]{1,0:T(8,128)(2,1)}, bf16[512,128]{1,0:T(8,128)(2,1)S(1)}, u32[]{:S(2)}, u32[]{:S(2)}) %collective-permute-start.1) | collective-permute-done | bytes 131104 | tf_op jit(solution)/shard_map/ppermute | solution.py:342
  8.1 1.5 %collective-permute-start.4 = (bf16[512,128]{1,0:T(8,128)(2,1)S(1)}, bf16[512,128]{1,0:T(8,128)(2,1)S(1)}, u32[]{:S(2)}, u32[]{:S(2)}) collective-permute-start(bf16[512,128]{1,0:T(8,128)(2,1)S(1)} %collective-permute-done.refs_0_), channel_id=1, source_target_pairs={{0,4},{4,8},{8,12},{12,14},{14,10},{10,6},{6,2},{2,0},{1,5},{5,9},... | collective-permute-start | bytes 393224 | tf_op jit(solution)/shard_map/ppermute | solution.py:342
  9.6 0.5 %collective-permute-start.5 = (bf16[512,128]{1,0:T(8,128)(2,1)S(1)}, bf16[512,128]{1,0:T(8,128)(2,1)S(1)}, u32[]{:S(2)}, u32[]{:S(2)}) collective-permute-start(bf16[512,128]{1,0:T(8,128)(2,1)S(1)} %collective-permute-done.1.refs_7_), channel_id=1, source_target_pairs={{0,2},{4,0},{8,4},{12,8},{14,12},{10,14},{6,10},{2,6},{1,3},{5,1},... | collective-permute-start | bytes 393224 | tf_op jit(solution)/shard_map/ppermute | solution.py:342
  10.1 0.0 collective-permute-done.2.refs_6_
  10.1 0.0 collective-permute-done.3.refs_1_
  10.1 2.1 %collective-permute-start.6 = (bf16[512,128]{1,0:T(8,128)(2,1)S(1)}, bf16[512,128]{1,0:T(8,128)(2,1)S(1)}, u32[]{:S(2)}, u32[]{:S(2)}) collective-permute-start(bf16[512,128]{1,0:T(8,128)(2,1)S(1)} %collective-permute-done.2.refs_6_), channel_id=1, source_target_pairs={{0,4},{4,8},{8,12},{12,14},{14,10},{10,6},{6,2},{2,0},{1,5},{5,9},... | collective-permute-start | bytes 393224 | tf_op jit(solution)/shard_map/ppermute | solution.py:342
  12.2 0.0 collective-permute-start.7
  12.2 1.8 %collective-permute-done.4.refs_2_ = bf16[512,128]{1,0:T(8,128)(2,1)S(1)} collective-permute-done((bf16[512,128]{1,0:T(8,128)(2,1)S(1)}, bf16[512,128]{1,0:T(8,128)(2,1)S(1)}, u32[]{:S(2)}, u32[]{:S(2)}) %collective-permute-start.4) | collective-permute-done | bytes 131104 | tf_op jit(solution)/shard_map/ppermute | solution.py:342
  14.0 1.1 %collective-permute-done.5.refs_9_ = bf16[512,128]{1,0:T(8,128)(2,1)S(1)} collective-permute-done((bf16[512,128]{1,0:T(8,128)(2,1)S(1)}, bf16[512,128]{1,0:T(8,128)(2,1)S(1)}, u32[]{:S(2)}, u32[]{:S(2)}) %collective-permute-start.5) | collective-permute-done | bytes 131104 | tf_op jit(solution)/shard_map/ppermute | solution.py:342
  15.1 0.5 %collective-permute-start.8 = (bf16[512,128]{1,0:T(8,128)(2,1)S(1)}, bf16[512,128]{1,0:T(8,128)(2,1)S(1)}, u32[]{:S(2)}, u32[]{:S(2)}) collective-permute-start(bf16[512,128]{1,0:T(8,128)(2,1)S(1)} %collective-permute-done.4.refs_2_), channel_id=1, source_target_pairs={{0,4},{4,8},{8,12},{12,14},{14,10},{10,6},{6,2},{2,0},{1,5},{5,9},... | collective-permute-start | bytes 393224 | tf_op jit(solution)/shard_map/ppermute | solution.py:342
  15.6 1.5 %collective-permute-start.11 = (bf16[512,128]{1,0:T(8,128)(2,1)S(1)}, bf16[512,128]{1,0:T(8,128)(2,1)S(1)}, u32[]{:S(2)}, u32[]{:S(2)}) collective-permute-start(bf16[512,128]{1,0:T(8,128)(2,1)S(1)} %collective-permute-done.5.refs_9_), channel_id=1, source_target_pairs={{0,2},{4,0},{8,4},{12,8},{14,12},{10,14},{6,10},{2,6},{1,3},{5,1},... | collective-permute-start | bytes 393224 | tf_op jit(solution)/shard_map/ppermute | solution.py:342
  17.2 0.0 collective-permute-done.6.refs_8_
  17.2 1.4 %collective-permute-done.7.refs_3_ = bf16[512,128]{1,0:T(8,128)(2,1)S(1)} collective-permute-done((bf16[512,128]{1,0:T(8,128)(2,1)S(1)}, bf16[512,128]{1,0:T(8,128)(2,1)S(1)}, u32[]{:S(2)}, u32[]{:S(2)}) %collective-permute-start.7) | collective-permute-done | bytes 131104 | tf_op jit(solution)/shard_map/ppermute | solution.py:342
  18.6 0.0 collective-permute-start.10
  18.6 2.0 %collective-permute-start.9 = (bf16[512,128]{1,0:T(8,128)(2,1)S(1)}, bf16[512,128]{1,0:T(8,128)(2,1)S(1)}, u32[]{:S(2)}, u32[]{:S(2)}) collective-permute-start(bf16[512,128]{1,0:T(8,128)(2,1)S(1)} %collective-permute-done.6.refs_8_), channel_id=1, source_target_pairs={{0,4},{4,8},{8,12},{12,14},{14,10},{10,6},{6,2},{2,0},{1,5},{5,9},... | collective-permute-start | bytes 393224 | tf_op jit(solution)/shard_map/ppermute | solution.py:342
  20.6 0.0 collective-permute-done.8.refs_4_
  20.7 0.2 collective-permute-start.12
  20.9 0.0 collective-permute-done.11.refs_11_
  20.9 1.9 %collective-permute-start.13 = (bf16[512,128]{1,0:T(8,128)(2,1)S(1)}, bf16[512,128]{1,0:T(8,128)(2,1)S(1)}, u32[]{:S(2)}, u32[]{:S(2)}) collective-permute-start(bf16[512,128]{1,0:T(8,128)(2,1)S(1)} %fusion.1), channel_id=1, source_target_pairs={{0,1},{1,0},{4,6},{5,7},{8,10},{9,11},{12,4},{13,5},{14,12},{15,13... | collective-permute-start | bytes 393224 | tf_op jit(solution)/shard_map/ppermute | solution.py:354
  22.8 1.0 %collective-permute-done.10.refs_5_ = bf16[512,128]{1,0:T(8,128)(2,1)S(1)} collective-permute-done((bf16[512,128]{1,0:T(8,128)(2,1)S(1)}, bf16[512,128]{1,0:T(8,128)(2,1)S(1)}, u32[]{:S(2)}, u32[]{:S(2)}) %collective-permute-start.10) | collective-permute-done | bytes 131104 | tf_op jit(solution)/shard_map/ppermute | solution.py:342
  23.8 0.0 collective-permute-done.9.refs_10_
  23.8 2.9 %attend.1 = (bf16[128,32,128]{2,1,0:T(8,128)(2,1)}, f32[4,1024,128]{2,1,0:T(8,128)S(1)}, f32[4,1024,256]{2,1,0:T(8,128)S(1)}) custom-call(s32[4,8]{1,0:T(4,128)S(1)} %get-tuple-element.32.lists_ref, bf16[4,1024,128]{2,1,0:T(8,128)(2,1)S(1)} %get-tuple-element.33.q_ref, bf16[4,128,128]{2,1,0:T(8,128)(2,1)S(1)} %get-tuple-element.34.k_own_ref, ...), custom_call_target="tpu_custom_call" | custom-call | tf_op jit(solution)/shard_map/attend/pallas_call | solution.py:232
  26.8 0.0 collective-permute-done.12.k_ref
  26.8 0.3 %collective-permute-done.13.v_ref = bf16[512,128]{1,0:T(8,128)(2,1)S(1)} collective-permute-done((bf16[512,128]{1,0:T(8,128)(2,1)S(1)}, bf16[512,128]{1,0:T(8,128)(2,1)S(1)}, u32[]{:S(2)}, u32[]{:S(2)}) %collective-permute-start.13) | collective-permute-done | bytes 131104 | tf_op jit(solution)/shard_map/ppermute | solution.py:354
  27.1 2.2 %attend_last.1 = bf16[128,32,128]{2,1,0:T(8,128)(2,1)} custom-call(s32[4,8]{1,0:T(4,128)S(1)} %get-tuple-element.32.lists_ref, bf16[4,1024,128]{2,1,0:T(8,128)(2,1)S(1)} %get-tuple-element.33.q_ref, f32[4,1024,128]{2,1,0:T(8,128)S(1)} %get-tuple-element.48.top_ref, f32[4,1024,256]{2,1,0:T(8,128)S(1)} %get-tuple-element.49.both_ref, ...), custom_call_target="tpu_custom_call", output_to_operand_aliasing={{}: (6, {})} | custom-call | tf_op jit(solution)/shard_map/attend_last/pallas_call | solution.py:303
  (2 shorter events, 0.1 us)
Async XLA Ops:
  0.0 6.6 %collective-permute-start = (bf16[512,128]{1,0:T(8,128)(2,1)}, bf16[512,128]{1,0:T(8,128)(2,1)S(1)}, u32[]{:S(2)}, u32[]{:S(2)}) collective-permute-start(bf16[512,128]{1,0:T(8,128)(2,1)} %bitcast.6), channel_id=1, source_target_pairs={{0,4},{4,8},{8,12},{12,14},{14,10},{10,6},{6,2},{2,0},{1,5},{5,9},... | collective-permute-start | bytes 393224 | tf_op jit(solution)/shard_map/ppermute | solution.py:342
  1.6 6.5 %collective-permute-start.1 = (bf16[512,128]{1,0:T(8,128)(2,1)}, bf16[512,128]{1,0:T(8,128)(2,1)S(1)}, u32[]{:S(2)}, u32[]{:S(2)}) collective-permute-start(bf16[512,128]{1,0:T(8,128)(2,1)} %bitcast.3), channel_id=1, source_target_pairs={{0,2},{4,0},{8,4},{12,8},{14,12},{10,14},{6,10},{2,6},{1,3},{5,1},... | collective-permute-start | bytes 393224 | tf_op jit(solution)/shard_map/ppermute | solution.py:342
  2.0 8.1 %collective-permute-start.2 = (bf16[512,128]{1,0:T(8,128)(2,1)}, bf16[512,128]{1,0:T(8,128)(2,1)S(1)}, u32[]{:S(2)}, u32[]{:S(2)}) collective-permute-start(bf16[512,128]{1,0:T(8,128)(2,1)} %bitcast.4), channel_id=1, source_target_pairs={{0,4},{4,8},{8,12},{12,14},{14,10},{10,6},{6,2},{2,0},{1,5},{5,9},... | collective-permute-start | bytes 393224 | tf_op jit(solution)/shard_map/ppermute | solution.py:342
  3.6 6.5 %collective-permute-start.3 = (bf16[512,128]{1,0:T(8,128)(2,1)}, bf16[512,128]{1,0:T(8,128)(2,1)S(1)}, u32[]{:S(2)}, u32[]{:S(2)}) collective-permute-start(bf16[512,128]{1,0:T(8,128)(2,1)} %bitcast.7), channel_id=1, source_target_pairs={{0,2},{4,0},{8,4},{12,8},{14,12},{10,14},{6,10},{2,6},{1,3},{5,1},... | collective-permute-start | bytes 393224 | tf_op jit(solution)/shard_map/ppermute | solution.py:342
  8.1 5.9 %collective-permute-start.4 = (bf16[512,128]{1,0:T(8,128)(2,1)S(1)}, bf16[512,128]{1,0:T(8,128)(2,1)S(1)}, u32[]{:S(2)}, u32[]{:S(2)}) collective-permute-start(bf16[512,128]{1,0:T(8,128)(2,1)S(1)} %collective-permute-done.refs_0_), channel_id=1, source_target_pairs={{0,4},{4,8},{8,12},{12,14},{14,10},{10,6},{6,2},{2,0},{1,5},{5,9},... | collective-permute-start | bytes 393224 | tf_op jit(solution)/shard_map/ppermute | solution.py:342
  9.6 5.5 %collective-permute-start.5 = (bf16[512,128]{1,0:T(8,128)(2,1)S(1)}, bf16[512,128]{1,0:T(8,128)(2,1)S(1)}, u32[]{:S(2)}, u32[]{:S(2)}) collective-permute-start(bf16[512,128]{1,0:T(8,128)(2,1)S(1)} %collective-permute-done.1.refs_7_), channel_id=1, source_target_pairs={{0,2},{4,0},{8,4},{12,8},{14,12},{10,14},{6,10},{2,6},{1,3},{5,1},... | collective-permute-start | bytes 393224 | tf_op jit(solution)/shard_map/ppermute | solution.py:342
  10.1 7.0 %collective-permute-start.6 = (bf16[512,128]{1,0:T(8,128)(2,1)S(1)}, bf16[512,128]{1,0:T(8,128)(2,1)S(1)}, u32[]{:S(2)}, u32[]{:S(2)}) collective-permute-start(bf16[512,128]{1,0:T(8,128)(2,1)S(1)} %collective-permute-done.2.refs_6_), channel_id=1, source_target_pairs={{0,4},{4,8},{8,12},{12,14},{14,10},{10,6},{6,2},{2,0},{1,5},{5,9},... | collective-permute-start | bytes 393224 | tf_op jit(solution)/shard_map/ppermute | solution.py:342
  12.2 6.4 %collective-permute-start.7 = (bf16[512,128]{1,0:T(8,128)(2,1)S(1)}, bf16[512,128]{1,0:T(8,128)(2,1)S(1)}, u32[]{:S(2)}, u32[]{:S(2)}) collective-permute-start(bf16[512,128]{1,0:T(8,128)(2,1)S(1)} %collective-permute-done.3.refs_1_), channel_id=1, source_target_pairs={{0,2},{4,0},{8,4},{12,8},{14,12},{10,14},{6,10},{2,6},{1,3},{5,1},... | collective-permute-start | bytes 393224 | tf_op jit(solution)/shard_map/ppermute | solution.py:342
  15.1 5.5 %collective-permute-start.8 = (bf16[512,128]{1,0:T(8,128)(2,1)S(1)}, bf16[512,128]{1,0:T(8,128)(2,1)S(1)}, u32[]{:S(2)}, u32[]{:S(2)}) collective-permute-start(bf16[512,128]{1,0:T(8,128)(2,1)S(1)} %collective-permute-done.4.refs_2_), channel_id=1, source_target_pairs={{0,4},{4,8},{8,12},{12,14},{14,10},{10,6},{6,2},{2,0},{1,5},{5,9},... | collective-permute-start | bytes 393224 | tf_op jit(solution)/shard_map/ppermute | solution.py:342
  15.6 5.3 %collective-permute-start.11 = (bf16[512,128]{1,0:T(8,128)(2,1)S(1)}, bf16[512,128]{1,0:T(8,128)(2,1)S(1)}, u32[]{:S(2)}, u32[]{:S(2)}) collective-permute-start(bf16[512,128]{1,0:T(8,128)(2,1)S(1)} %collective-permute-done.5.refs_9_), channel_id=1, source_target_pairs={{0,2},{4,0},{8,4},{12,8},{14,12},{10,14},{6,10},{2,6},{1,3},{5,1},... | collective-permute-start | bytes 393224 | tf_op jit(solution)/shard_map/ppermute | solution.py:342
  18.6 5.2 %collective-permute-start.10 = (bf16[512,128]{1,0:T(8,128)(2,1)S(1)}, bf16[512,128]{1,0:T(8,128)(2,1)S(1)}, u32[]{:S(2)}, u32[]{:S(2)}) collective-permute-start(bf16[512,128]{1,0:T(8,128)(2,1)S(1)} %collective-permute-done.7.refs_3_), channel_id=1, source_target_pairs={{0,2},{4,0},{8,4},{12,8},{14,12},{10,14},{6,10},{2,6},{1,3},{5,1},... | collective-permute-start | bytes 393224 | tf_op jit(solution)/shard_map/ppermute | solution.py:342
  18.6 5.2 %collective-permute-start.9 = (bf16[512,128]{1,0:T(8,128)(2,1)S(1)}, bf16[512,128]{1,0:T(8,128)(2,1)S(1)}, u32[]{:S(2)}, u32[]{:S(2)}) collective-permute-start(bf16[512,128]{1,0:T(8,128)(2,1)S(1)} %collective-permute-done.6.refs_8_), channel_id=1, source_target_pairs={{0,4},{4,8},{8,12},{12,14},{14,10},{10,6},{6,2},{2,0},{1,5},{5,9},... | collective-permute-start | bytes 393224 | tf_op jit(solution)/shard_map/ppermute | solution.py:342
  20.7 6.1 %collective-permute-start.12 = (bf16[512,128]{1,0:T(8,128)(2,1)S(1)}, bf16[512,128]{1,0:T(8,128)(2,1)S(1)}, u32[]{:S(2)}, u32[]{:S(2)}) collective-permute-start(bf16[512,128]{1,0:T(8,128)(2,1)S(1)} %select_select_fusion.1), channel_id=1, source_target_pairs={{0,1},{1,0},{4,12},{5,13},{8,10},{9,11},{12,14},{13,15},{14,6},{15... | collective-permute-start | bytes 393224 | tf_op jit(solution)/shard_map/ppermute | solution.py:354
  20.9 6.2 %collective-permute-start.13 = (bf16[512,128]{1,0:T(8,128)(2,1)S(1)}, bf16[512,128]{1,0:T(8,128)(2,1)S(1)}, u32[]{:S(2)}, u32[]{:S(2)}) collective-permute-start(bf16[512,128]{1,0:T(8,128)(2,1)S(1)} %fusion.1), channel_id=1, source_target_pairs={{0,1},{1,0},{4,6},{5,7},{8,10},{9,11},{12,4},{13,5},{14,12},{15,13... | collective-permute-start | bytes 393224 | tf_op jit(solution)/shard_map/ppermute | solution.py:354

commit v18 on v17

--- a/solution.py
+++ b/solution.py
@@ -178,15 +178,16 @@
             k_ready.append(k_h)
             v_ready.append(with_ones(v_h))
 
+        past = lax.broadcasted_iota(jnp.int32, (ROW_CHUNK, tokens), 0)
+        past -= group * lax.broadcasted_iota(jnp.int32, (ROW_CHUNK, tokens), 1)
+
         def score(job, _):
             h, first = job
             return scores_of(q_ref[h, pl.ds(first, ROW_CHUNK), :], k_ready[h])
 
         def weigh(job, s):
             first = job[1]
-            row = (lax.broadcasted_iota(jnp.int32, (ROW_CHUNK, tokens), 0) + first) // group
-            key = lax.broadcasted_iota(jnp.int32, (ROW_CHUNK, tokens), 1)
-            scores = [jnp.where(key <= row, s[:, :tokens], NO_KEY)]
+            scores = [jnp.where(past >= -first, s[:, :tokens], NO_KEY)]
             scores += [s[:, (j + 1) * tokens : (j + 2) * tokens] for j in range(others)]
             top = jnp.max(functools.reduce(jnp.maximum, scores), axis=1, keepdims=True)
             probs = [jnp.exp2((part - top) * factor).astype(jnp.bfloat16) for part in scores]
@@ -329,7 +330,7 @@
     return code
 
 
-LAST_KEYS = {1: 3, 2: 5, 3: 4, 4: 6, 5: 2, 6: 1}, {1: 2, 2: 0, 3: 4, 5: 1}
+LAST_KEYS = {1: 2, 2: 3, 3: 4, 4: 5, 5: 6, 6: 1}, {}
 LAST_VALUES = {1: 6, 2: 5, 3: 1, 4: 3, 5: 2, 6: 4}, {2: 0, 4: 4, 5: 1, 6: 3}
 
 

time: 29.6 us -> 28.9 us (0.976)
  starting transfers between devices: 14.4 us -> 13.9 us
    ppermute x2, starting transfers between devices: 2.12 us -> 1.74 us  [send_last(): return lax.ppermute(x, ('seq', 'head'), pairs)]
    ppermute x2, waiting for transfers between devices: 0.32 us -> 0.01 us  [send_last(): return lax.ppermute(x, ('seq', 'head'), pairs)]
  transfers between devices with their start and end apart: 14 -> 14, of which waited for: 7 -> 9; matrix products, arithmetic and copies ran while one was open for 0% -> 0% of each run, Pallas kernels for 15% -> 16%
where the time goes in v18:
time: 28.9 us; the launch traced here: 28.8 us
  starting transfers between devices  13.9 us (48%)
  waiting for transfers between devices  7.95 us (28%)
  Pallas kernels  6.69 us (23%)
    ppermute x12, starting transfers between devices, send(): lax.ppermute(x, 'seq', [(ring[p], ring[(p + turn) % members]) for p in ra...  12.2 us
    ppermute x12, waiting for transfers between devices, send(): lax.ppermute(x, 'seq', [(ring[p], ring[(p + turn) % members]) for p in ra...  7.94 us
    pallas_call x1, Pallas kernels, attend(): pl.pallas_call(functools.partial(attend_kernel, codes=codes, code=code, l...  2.93 us
    pallas_call x1, Pallas kernels, attend_last(): pl.pallas_call(functools.partial(last_kernel, code=code, last=last), out_...  2.19 us
    ppermute x2, starting transfers between devices, send_last(): return lax.ppermute(x, ('seq', 'head'), pairs)  1.74 us
    pallas_call x1, Pallas kernels, prepare(): pl.pallas_call(functools.partial(prepare_kernel, kv_dev=kv_dev), out_shap...  1.58 us
  transfers between devices with their start and end apart: 14, of which 9 were waited for; matrix products, arithmetic and copies ran while one was open for 0% of the time, Pallas kernels for 16%

profile of v18, /device:TPU:20, one launch (start us, length us, event | category | flops | bytes accessed | tf_op | source)
XLA Modules:
  0.0 28.8 jit_solution(10082502113190223769)
XLA Ops:
  0.0 1.6 %collective-permute-start = (bf16[512,128]{1,0:T(8,128)(2,1)}, bf16[512,128]{1,0:T(8,128)(2,1)S(1)}, u32[]{:S(2)}, u32[]{:S(2)}) collective-permute-start(bf16[512,128]{1,0:T(8,128)(2,1)} %bitcast.6), channel_id=1, source_target_pairs={{0,4},{4,8},{8,12},{12,14},{14,10},{10,6},{6,2},{2,0},{1,5},{5,9},... | collective-permute-start | bytes 393224 | tf_op jit(solution)/shard_map/ppermute | solution.py:343
  1.6 0.4 %collective-permute-start.1 = (bf16[512,128]{1,0:T(8,128)(2,1)}, bf16[512,128]{1,0:T(8,128)(2,1)S(1)}, u32[]{:S(2)}, u32[]{:S(2)}) collective-permute-start(bf16[512,128]{1,0:T(8,128)(2,1)} %bitcast.3), channel_id=1, source_target_pairs={{0,2},{4,0},{8,4},{12,8},{14,12},{10,14},{6,10},{2,6},{1,3},{5,1},... | collective-permute-start | bytes 393224 | tf_op jit(solution)/shard_map/ppermute | solution.py:343
  2.0 1.6 %collective-permute-start.2 = (bf16[512,128]{1,0:T(8,128)(2,1)}, bf16[512,128]{1,0:T(8,128)(2,1)S(1)}, u32[]{:S(2)}, u32[]{:S(2)}) collective-permute-start(bf16[512,128]{1,0:T(8,128)(2,1)} %bitcast.4), channel_id=1, source_target_pairs={{0,4},{4,8},{8,12},{12,14},{14,10},{10,6},{6,2},{2,0},{1,5},{5,9},... | collective-permute-start | bytes 393224 | tf_op jit(solution)/shard_map/ppermute | solution.py:343
  3.6 0.4 %collective-permute-start.3 = (bf16[512,128]{1,0:T(8,128)(2,1)}, bf16[512,128]{1,0:T(8,128)(2,1)S(1)}, u32[]{:S(2)}, u32[]{:S(2)}) collective-permute-start(bf16[512,128]{1,0:T(8,128)(2,1)} %bitcast.7), channel_id=1, source_target_pairs={{0,2},{4,0},{8,4},{12,8},{14,12},{10,14},{6,10},{2,6},{1,3},{5,1},... | collective-permute-start | bytes 393224 | tf_op jit(solution)/shard_map/ppermute | solution.py:343
  4.1 1.6 %prepare.1 = (s32[4,8]{1,0:T(4,128)S(1)}, bf16[4,1024,128]{2,1,0:T(8,128)(2,1)S(1)}, bf16[4,128,128]{2,1,0:T(8,128)(2,1)S(1)}, bf16[4,128,128]{2,1,0:T(8,128)(2,1)S(1)}) custom-call(s32[4,8]{1,0:T(4,128)} %bitcast.9, bf16[128,32,128]{2,1,0:T(8,128)(2,1)} %q_hbm.1, bf16[512,128]{1,0:T(8,128)(2,1)} %bitcast.8, bf16[512,128]{1,0:T(8,128)(2,1)} %bitcast.5), custom_call_target="tpu_custom_call" | custom-call | tf_op jit(solution)/shard_map/prepare/pallas_call | solution.py:55
  5.6 1.0 %collective-permute-done.refs_0_ = bf16[512,128]{1,0:T(8,128)(2,1)S(1)} collective-permute-done((bf16[512,128]{1,0:T(8,128)(2,1)}, bf16[512,128]{1,0:T(8,128)(2,1)S(1)}, u32[]{:S(2)}, u32[]{:S(2)}) %collective-permute-start) | collective-permute-done | bytes 131104 | tf_op jit(solution)/shard_map/ppermute | solution.py:343
  6.6 1.5 %collective-permute-done.1.refs_7_ = bf16[512,128]{1,0:T(8,128)(2,1)S(1)} collective-permute-done((bf16[512,128]{1,0:T(8,128)(2,1)}, bf16[512,128]{1,0:T(8,128)(2,1)S(1)}, u32[]{:S(2)}, u32[]{:S(2)}) %collective-permute-start.1) | collective-permute-done | bytes 131104 | tf_op jit(solution)/shard_map/ppermute | solution.py:343
  8.1 0.4 %collective-permute-start.5 = (bf16[512,128]{1,0:T(8,128)(2,1)S(1)}, bf16[512,128]{1,0:T(8,128)(2,1)S(1)}, u32[]{:S(2)}, u32[]{:S(2)}) collective-permute-start(bf16[512,128]{1,0:T(8,128)(2,1)S(1)} %collective-permute-done.1.refs_7_), channel_id=1, source_target_pairs={{0,2},{4,0},{8,4},{12,8},{14,12},{10,14},{6,10},{2,6},{1,3},{5,1},... | collective-permute-start | bytes 393224 | tf_op jit(solution)/shard_map/ppermute | solution.py:343
  8.6 1.6 %collective-permute-start.4 = (bf16[512,128]{1,0:T(8,128)(2,1)S(1)}, bf16[512,128]{1,0:T(8,128)(2,1)S(1)}, u32[]{:S(2)}, u32[]{:S(2)}) collective-permute-start(bf16[512,128]{1,0:T(8,128)(2,1)S(1)} %collective-permute-done.refs_0_), channel_id=1, source_target_pairs={{0,4},{4,8},{8,12},{12,14},{14,10},{10,6},{6,2},{2,0},{1,5},{5,9},... | collective-permute-start | bytes 393224 | tf_op jit(solution)/shard_map/ppermute | solution.py:343
  10.1 0.0 collective-permute-done.2.refs_6_
  10.1 0.8 %collective-permute-done.3.refs_1_ = bf16[512,128]{1,0:T(8,128)(2,1)S(1)} collective-permute-done((bf16[512,128]{1,0:T(8,128)(2,1)}, bf16[512,128]{1,0:T(8,128)(2,1)S(1)}, u32[]{:S(2)}, u32[]{:S(2)}) %collective-permute-start.3) | collective-permute-done | bytes 131104 | tf_op jit(solution)/shard_map/ppermute | solution.py:343
  10.9 1.5 %collective-permute-start.6 = (bf16[512,128]{1,0:T(8,128)(2,1)S(1)}, bf16[512,128]{1,0:T(8,128)(2,1)S(1)}, u32[]{:S(2)}, u32[]{:S(2)}) collective-permute-start(bf16[512,128]{1,0:T(8,128)(2,1)S(1)} %collective-permute-done.2.refs_6_), channel_id=1, source_target_pairs={{0,4},{4,8},{8,12},{12,14},{14,10},{10,6},{6,2},{2,0},{1,5},{5,9},... | collective-permute-start | bytes 393224 | tf_op jit(solution)/shard_map/ppermute | solution.py:343
  12.4 0.5 %collective-permute-start.7 = (bf16[512,128]{1,0:T(8,128)(2,1)S(1)}, bf16[512,128]{1,0:T(8,128)(2,1)S(1)}, u32[]{:S(2)}, u32[]{:S(2)}) collective-permute-start(bf16[512,128]{1,0:T(8,128)(2,1)S(1)} %collective-permute-done.3.refs_1_), channel_id=1, source_target_pairs={{0,2},{4,0},{8,4},{12,8},{14,12},{10,14},{6,10},{2,6},{1,3},{5,1},... | collective-permute-start | bytes 393224 | tf_op jit(solution)/shard_map/ppermute | solution.py:343
  12.9 1.1 %collective-permute-done.5.refs_9_ = bf16[512,128]{1,0:T(8,128)(2,1)S(1)} collective-permute-done((bf16[512,128]{1,0:T(8,128)(2,1)S(1)}, bf16[512,128]{1,0:T(8,128)(2,1)S(1)}, u32[]{:S(2)}, u32[]{:S(2)}) %collective-permute-start.5) | collective-permute-done | bytes 131104 | tf_op jit(solution)/shard_map/ppermute | solution.py:343
  14.1 0.0 collective-permute-done.4.refs_2_
  14.1 0.4 %collective-permute-start.11 = (bf16[512,128]{1,0:T(8,128)(2,1)S(1)}, bf16[512,128]{1,0:T(8,128)(2,1)S(1)}, u32[]{:S(2)}, u32[]{:S(2)}) collective-permute-start(bf16[512,128]{1,0:T(8,128)(2,1)S(1)} %collective-permute-done.5.refs_9_), channel_id=1, source_target_pairs={{0,2},{4,0},{8,4},{12,8},{14,12},{10,14},{6,10},{2,6},{1,3},{5,1},... | collective-permute-start | bytes 393224 | tf_op jit(solution)/shard_map/ppermute | solution.py:343
  14.4 1.7 %collective-permute-start.8 = (bf16[512,128]{1,0:T(8,128)(2,1)S(1)}, bf16[512,128]{1,0:T(8,128)(2,1)S(1)}, u32[]{:S(2)}, u32[]{:S(2)}) collective-permute-start(bf16[512,128]{1,0:T(8,128)(2,1)S(1)} %collective-permute-done.4.refs_2_), channel_id=1, source_target_pairs={{0,4},{4,8},{8,12},{12,14},{14,10},{10,6},{6,2},{2,0},{1,5},{5,9},... | collective-permute-start | bytes 393224 | tf_op jit(solution)/shard_map/ppermute | solution.py:343
  16.1 0.5 %collective-permute-done.6.refs_8_ = bf16[512,128]{1,0:T(8,128)(2,1)S(1)} collective-permute-done((bf16[512,128]{1,0:T(8,128)(2,1)S(1)}, bf16[512,128]{1,0:T(8,128)(2,1)S(1)}, u32[]{:S(2)}, u32[]{:S(2)}) %collective-permute-start.6) | collective-permute-done | bytes 131104 | tf_op jit(solution)/shard_map/ppermute | solution.py:343
  16.6 1.3 %collective-permute-done.7.refs_3_ = bf16[512,128]{1,0:T(8,128)(2,1)S(1)} collective-permute-done((bf16[512,128]{1,0:T(8,128)(2,1)S(1)}, bf16[512,128]{1,0:T(8,128)(2,1)S(1)}, u32[]{:S(2)}, u32[]{:S(2)}) %collective-permute-start.7) | collective-permute-done | bytes 131104 | tf_op jit(solution)/shard_map/ppermute | solution.py:343
  17.9 0.6 %collective-permute-start.10 = (bf16[512,128]{1,0:T(8,128)(2,1)S(1)}, bf16[512,128]{1,0:T(8,128)(2,1)S(1)}, u32[]{:S(2)}, u32[]{:S(2)}) collective-permute-start(bf16[512,128]{1,0:T(8,128)(2,1)S(1)} %collective-permute-done.7.refs_3_), channel_id=1, source_target_pairs={{0,2},{4,0},{8,4},{12,8},{14,12},{10,14},{6,10},{2,6},{1,3},{5,1},... | collective-permute-start | bytes 393224 | tf_op jit(solution)/shard_map/ppermute | solution.py:343
  18.5 1.4 %collective-permute-start.9 = (bf16[512,128]{1,0:T(8,128)(2,1)S(1)}, bf16[512,128]{1,0:T(8,128)(2,1)S(1)}, u32[]{:S(2)}, u32[]{:S(2)}) collective-permute-start(bf16[512,128]{1,0:T(8,128)(2,1)S(1)} %collective-permute-done.6.refs_8_), channel_id=1, source_target_pairs={{0,4},{4,8},{8,12},{12,14},{14,10},{10,6},{6,2},{2,0},{1,5},{5,9},... | collective-permute-start | bytes 393224 | tf_op jit(solution)/shard_map/ppermute | solution.py:343
  19.9 0.8 %collective-permute-done.11.refs_11_ = bf16[512,128]{1,0:T(8,128)(2,1)S(1)} collective-permute-done((bf16[512,128]{1,0:T(8,128)(2,1)S(1)}, bf16[512,128]{1,0:T(8,128)(2,1)S(1)}, u32[]{:S(2)}, u32[]{:S(2)}) %collective-permute-start.11) | collective-permute-done | bytes 131104 | tf_op jit(solution)/shard_map/ppermute | solution.py:343
  20.7 0.1 collective-permute-start.13
  20.8 0.0 collective-permute-done.8.refs_4_
  20.8 1.7 %collective-permute-start.12 = (bf16[512,128]{1,0:T(8,128)(2,1)S(1)}, bf16[512,128]{1,0:T(8,128)(2,1)S(1)}, u32[]{:S(2)}, u32[]{:S(2)}) collective-permute-start(bf16[512,128]{1,0:T(8,128)(2,1)S(1)} %collective-permute-done.8.refs_4_), channel_id=1, source_target_pairs={{0,1},{1,0},{4,8},{5,9},{8,12},{9,13},{12,14},{13,15},{14,10},{15,... | collective-permute-start | bytes 393224 | tf_op jit(solution)/shard_map/ppermute | solution.py:355
  22.5 0.5 %collective-permute-done.10.refs_5_ = bf16[512,128]{1,0:T(8,128)(2,1)S(1)} collective-permute-done((bf16[512,128]{1,0:T(8,128)(2,1)S(1)}, bf16[512,128]{1,0:T(8,128)(2,1)S(1)}, u32[]{:S(2)}, u32[]{:S(2)}) %collective-permute-start.10) | collective-permute-done | bytes 131104 | tf_op jit(solution)/shard_map/ppermute | solution.py:343
  23.0 0.5 %collective-permute-done.9.refs_10_ = bf16[512,128]{1,0:T(8,128)(2,1)S(1)} collective-permute-done((bf16[512,128]{1,0:T(8,128)(2,1)S(1)}, bf16[512,128]{1,0:T(8,128)(2,1)S(1)}, u32[]{:S(2)}, u32[]{:S(2)}) %collective-permute-start.9) | collective-permute-done | bytes 131104 | tf_op jit(solution)/shard_map/ppermute | solution.py:343
  23.5 2.9 %attend.1 = (bf16[128,32,128]{2,1,0:T(8,128)(2,1)}, f32[4,1024,128]{2,1,0:T(8,128)S(1)}, f32[4,1024,256]{2,1,0:T(8,128)S(1)}) custom-call(s32[4,8]{1,0:T(4,128)S(1)} %get-tuple-element.32.lists_ref, bf16[4,1024,128]{2,1,0:T(8,128)(2,1)S(1)} %get-tuple-element.33.q_ref, bf16[4,128,128]{2,1,0:T(8,128)(2,1)S(1)} %get-tuple-element.34.k_own_ref, ...), custom_call_target="tpu_custom_call" | custom-call | tf_op jit(solution)/shard_map/attend/pallas_call | solution.py:233
  26.4 0.0 collective-permute-done.13.v_ref
  26.4 0.0 collective-permute-done.12.k_ref
  26.4 2.2 %attend_last.1 = bf16[128,32,128]{2,1,0:T(8,128)(2,1)} custom-call(s32[4,8]{1,0:T(4,128)S(1)} %get-tuple-element.32.lists_ref, bf16[4,1024,128]{2,1,0:T(8,128)(2,1)S(1)} %get-tuple-element.33.q_ref, f32[4,1024,128]{2,1,0:T(8,128)S(1)} %get-tuple-element.48.top_ref, f32[4,1024,256]{2,1,0:T(8,128)S(1)} %get-tuple-element.49.both_ref, ...), custom_call_target="tpu_custom_call", output_to_operand_aliasing={{}: (6, {})} | custom-call | tf_op jit(solution)/shard_map/attend_last/pallas_call | solution.py:304
  (1 shorter events, 0.0 us)
Async XLA Ops:
  0.0 6.6 %collective-permute-start = (bf16[512,128]{1,0:T(8,128)(2,1)}, bf16[512,128]{1,0:T(8,128)(2,1)S(1)}, u32[]{:S(2)}, u32[]{:S(2)}) collective-permute-start(bf16[512,128]{1,0:T(8,128)(2,1)} %bitcast.6), channel_id=1, source_target_pairs={{0,4},{4,8},{8,12},{12,14},{14,10},{10,6},{6,2},{2,0},{1,5},{5,9},... | collective-permute-start | bytes 393224 | tf_op jit(solution)/shard_map/ppermute | solution.py:343
  1.6 6.5 %collective-permute-start.1 = (bf16[512,128]{1,0:T(8,128)(2,1)}, bf16[512,128]{1,0:T(8,128)(2,1)S(1)}, u32[]{:S(2)}, u32[]{:S(2)}) collective-permute-start(bf16[512,128]{1,0:T(8,128)(2,1)} %bitcast.3), channel_id=1, source_target_pairs={{0,2},{4,0},{8,4},{12,8},{14,12},{10,14},{6,10},{2,6},{1,3},{5,1},... | collective-permute-start | bytes 393224 | tf_op jit(solution)/shard_map/ppermute | solution.py:343
  2.0 8.1 %collective-permute-start.2 = (bf16[512,128]{1,0:T(8,128)(2,1)}, bf16[512,128]{1,0:T(8,128)(2,1)S(1)}, u32[]{:S(2)}, u32[]{:S(2)}) collective-permute-start(bf16[512,128]{1,0:T(8,128)(2,1)} %bitcast.4), channel_id=1, source_target_pairs={{0,4},{4,8},{8,12},{12,14},{14,10},{10,6},{6,2},{2,0},{1,5},{5,9},... | collective-permute-start | bytes 393224 | tf_op jit(solution)/shard_map/ppermute | solution.py:343
  3.6 7.3 %collective-permute-start.3 = (bf16[512,128]{1,0:T(8,128)(2,1)}, bf16[512,128]{1,0:T(8,128)(2,1)S(1)}, u32[]{:S(2)}, u32[]{:S(2)}) collective-permute-start(bf16[512,128]{1,0:T(8,128)(2,1)} %bitcast.7), channel_id=1, source_target_pairs={{0,2},{4,0},{8,4},{12,8},{14,12},{10,14},{6,10},{2,6},{1,3},{5,1},... | collective-permute-start | bytes 393224 | tf_op jit(solution)/shard_map/ppermute | solution.py:343
  8.1 6.0 %collective-permute-start.5 = (bf16[512,128]{1,0:T(8,128)(2,1)S(1)}, bf16[512,128]{1,0:T(8,128)(2,1)S(1)}, u32[]{:S(2)}, u32[]{:S(2)}) collective-permute-start(bf16[512,128]{1,0:T(8,128)(2,1)S(1)} %collective-permute-done.1.refs_7_), channel_id=1, source_target_pairs={{0,2},{4,0},{8,4},{12,8},{14,12},{10,14},{6,10},{2,6},{1,3},{5,1},... | collective-permute-start | bytes 393224 | tf_op jit(solution)/shard_map/ppermute | solution.py:343
  8.6 5.5 %collective-permute-start.4 = (bf16[512,128]{1,0:T(8,128)(2,1)S(1)}, bf16[512,128]{1,0:T(8,128)(2,1)S(1)}, u32[]{:S(2)}, u32[]{:S(2)}) collective-permute-start(bf16[512,128]{1,0:T(8,128)(2,1)S(1)} %collective-permute-done.refs_0_), channel_id=1, source_target_pairs={{0,4},{4,8},{8,12},{12,14},{14,10},{10,6},{6,2},{2,0},{1,5},{5,9},... | collective-permute-start | bytes 393224 | tf_op jit(solution)/shard_map/ppermute | solution.py:343
  10.9 5.7 %collective-permute-start.6 = (bf16[512,128]{1,0:T(8,128)(2,1)S(1)}, bf16[512,128]{1,0:T(8,128)(2,1)S(1)}, u32[]{:S(2)}, u32[]{:S(2)}) collective-permute-start(bf16[512,128]{1,0:T(8,128)(2,1)S(1)} %collective-permute-done.2.refs_6_), channel_id=1, source_target_pairs={{0,4},{4,8},{8,12},{12,14},{14,10},{10,6},{6,2},{2,0},{1,5},{5,9},... | collective-permute-start | bytes 393224 | tf_op jit(solution)/shard_map/ppermute | solution.py:343
  12.4 5.5 %collective-permute-start.7 = (bf16[512,128]{1,0:T(8,128)(2,1)S(1)}, bf16[512,128]{1,0:T(8,128)(2,1)S(1)}, u32[]{:S(2)}, u32[]{:S(2)}) collective-permute-start(bf16[512,128]{1,0:T(8,128)(2,1)S(1)} %collective-permute-done.3.refs_1_), channel_id=1, source_target_pairs={{0,2},{4,0},{8,4},{12,8},{14,12},{10,14},{6,10},{2,6},{1,3},{5,1},... | collective-permute-start | bytes 393224 | tf_op jit(solution)/shard_map/ppermute | solution.py:343
  14.1 6.6 %collective-permute-start.11 = (bf16[512,128]{1,0:T(8,128)(2,1)S(1)}, bf16[512,128]{1,0:T(8,128)(2,1)S(1)}, u32[]{:S(2)}, u32[]{:S(2)}) collective-permute-start(bf16[512,128]{1,0:T(8,128)(2,1)S(1)} %collective-permute-done.5.refs_9_), channel_id=1, source_target_pairs={{0,2},{4,0},{8,4},{12,8},{14,12},{10,14},{6,10},{2,6},{1,3},{5,1},... | collective-permute-start | bytes 393224 | tf_op jit(solution)/shard_map/ppermute | solution.py:343
  14.4 6.4 %collective-permute-start.8 = (bf16[512,128]{1,0:T(8,128)(2,1)S(1)}, bf16[512,128]{1,0:T(8,128)(2,1)S(1)}, u32[]{:S(2)}, u32[]{:S(2)}) collective-permute-start(bf16[512,128]{1,0:T(8,128)(2,1)S(1)} %collective-permute-done.4.refs_2_), channel_id=1, source_target_pairs={{0,4},{4,8},{8,12},{12,14},{14,10},{10,6},{6,2},{2,0},{1,5},{5,9},... | collective-permute-start | bytes 393224 | tf_op jit(solution)/shard_map/ppermute | solution.py:343
  17.9 5.1 %collective-permute-start.10 = (bf16[512,128]{1,0:T(8,128)(2,1)S(1)}, bf16[512,128]{1,0:T(8,128)(2,1)S(1)}, u32[]{:S(2)}, u32[]{:S(2)}) collective-permute-start(bf16[512,128]{1,0:T(8,128)(2,1)S(1)} %collective-permute-done.7.refs_3_), channel_id=1, source_target_pairs={{0,2},{4,0},{8,4},{12,8},{14,12},{10,14},{6,10},{2,6},{1,3},{5,1},... | collective-permute-start | bytes 393224 | tf_op jit(solution)/shard_map/ppermute | solution.py:343
  18.5 5.0 %collective-permute-start.9 = (bf16[512,128]{1,0:T(8,128)(2,1)S(1)}, bf16[512,128]{1,0:T(8,128)(2,1)S(1)}, u32[]{:S(2)}, u32[]{:S(2)}) collective-permute-start(bf16[512,128]{1,0:T(8,128)(2,1)S(1)} %collective-permute-done.6.refs_8_), channel_id=1, source_target_pairs={{0,4},{4,8},{8,12},{12,14},{14,10},{10,6},{6,2},{2,0},{1,5},{5,9},... | collective-permute-start | bytes 393224 | tf_op jit(solution)/shard_map/ppermute | solution.py:343
  20.7 5.7 %collective-permute-start.13 = (bf16[512,128]{1,0:T(8,128)(2,1)S(1)}, bf16[512,128]{1,0:T(8,128)(2,1)S(1)}, u32[]{:S(2)}, u32[]{:S(2)}) collective-permute-start(bf16[512,128]{1,0:T(8,128)(2,1)S(1)} %fusion.1), channel_id=1, source_target_pairs={{0,1},{1,0},{4,6},{5,7},{8,10},{9,11},{12,4},{13,5},{14,12},{15,13... | collective-permute-start | bytes 393224 | tf_op jit(solution)/shard_map/ppermute | solution.py:355
  20.8 5.6 %collective-permute-start.12 = (bf16[512,128]{1,0:T(8,128)(2,1)S(1)}, bf16[512,128]{1,0:T(8,128)(2,1)S(1)}, u32[]{:S(2)}, u32[]{:S(2)}) collective-permute-start(bf16[512,128]{1,0:T(8,128)(2,1)S(1)} %collective-permute-done.8.refs_4_), channel_id=1, source_target_pairs={{0,1},{1,0},{4,8},{5,9},{8,12},{9,13},{12,14},{13,15},{14,10},{15,... | collective-permute-start | bytes 393224 | tf_op jit(solution)/shard_map/ppermute | solution.py:355

commit v19 on v18

--- a/solution.py
+++ b/solution.py
@@ -358,11 +358,10 @@
     k_two, v_two, k_all, v_all = [k_own, k_own], [v_own, v_own], [], []
     for distance in range(1, half):
         ahead = send(k_two[0], 1), send(v_two[1], -1)
+        if distance == 1:
+            k_two[1], v_two[0], ready = lax.optimization_barrier((k_two[1], v_two[0], ready))
         behind = send(v_two[0], 1), send(k_two[1], -1)
-        if distance == 1:
-            ahead, ready = lax.optimization_barrier((ahead, ready))
-        if distance < half - 1:
-            ahead = lax.optimization_barrier(ahead)
+        ahead = lax.optimization_barrier(ahead)
         behind = lax.optimization_barrier(behind)
         k_two, v_two = [ahead[0], behind[1]], [behind[0], ahead[1]]
         k_all += k_two

time: 28.9 us -> 28.9 us (level)
  the two profiles are of different devices: /device:TPU:20 before, /device:TPU:0 now
where the time goes in v19:
time: 28.9 us; the launch traced here: 28.6 us
  starting transfers between devices  13.8 us (48%)
  waiting for transfers between devices  10.4 us (36%)
  Pallas kernels  4.22 us (15%)
    ppermute x12, starting transfers between devices, send(): lax.ppermute(x, 'seq', [(ring[p], ring[(p + turn) % members]) for p in ra...  13.2 us
    ppermute x12, waiting for transfers between devices, send(): lax.ppermute(x, 'seq', [(ring[p], ring[(p + turn) % members]) for p in ra...  10.4 us
    pallas_call x1, Pallas kernels, attend(): pl.pallas_call(functools.partial(attend_kernel, codes=codes, code=code, l...  2.47 us
    pallas_call x1, Pallas kernels, prepare(): pl.pallas_call(functools.partial(prepare_kernel, kv_dev=kv_dev), out_shap...  1.58 us
  transfers between devices with their start and end apart: 14, of which 8 were waited for; matrix products, arithmetic and copies ran while one was open for 0% of the time, Pallas kernels for 14%

profile of v19, /device:TPU:0, one launch (start us, length us, event | category | flops | bytes accessed | tf_op | source)
XLA Modules:
  0.0 28.6 jit_solution(17310996234274434439)
XLA Ops:
  0.0 3.0 %collective-permute-start = (bf16[512,128]{1,0:T(8,128)(2,1)}, bf16[512,128]{1,0:T(8,128)(2,1)S(1)}, u32[]{:S(2)}, u32[]{:S(2)}) collective-permute-start(bf16[512,128]{1,0:T(8,128)(2,1)} %bitcast.6), channel_id=1, source_target_pairs={{0,4},{4,8},{8,12},{12,14},{14,10},{10,6},{6,2},{2,0},{1,5},{5,9},... | collective-permute-start | bytes 393224 | tf_op jit(solution)/shard_map/ppermute | solution.py:343
  3.0 0.0 collective-permute-start.1
  3.0 1.6 %prepare.1 = (s32[4,8]{1,0:T(4,128)S(1)}, bf16[4,1024,128]{2,1,0:T(8,128)(2,1)S(1)}, bf16[4,128,128]{2,1,0:T(8,128)(2,1)S(1)}, bf16[4,128,128]{2,1,0:T(8,128)(2,1)S(1)}) custom-call(s32[4,8]{1,0:T(4,128)} %bitcast.9, bf16[128,32,128]{2,1,0:T(8,128)(2,1)} %q_hbm.1, bf16[512,128]{1,0:T(8,128)(2,1)} %bitcast.7, bf16[512,128]{1,0:T(8,128)(2,1)} %bitcast.4), custom_call_target="tpu_custom_call" | custom-call | tf_op jit(solution)/shard_map/prepare/pallas_call | solution.py:55
  4.6 2.1 %collective-permute-start.2 = (bf16[512,128]{1,0:T(8,128)(2,1)}, bf16[512,128]{1,0:T(8,128)(2,1)S(1)}, u32[]{:S(2)}, u32[]{:S(2)}) collective-permute-start(bf16[512,128]{1,0:T(8,128)(2,1)} %bitcast.5), channel_id=1, source_target_pairs={{0,4},{4,8},{8,12},{12,14},{14,10},{10,6},{6,2},{2,0},{1,5},{5,9},... | collective-permute-start | bytes 393224 | tf_op jit(solution)/shard_map/ppermute | solution.py:343
  6.7 0.0 collective-permute-start.3
  6.7 0.0 collective-permute-done.refs_0_
  6.7 1.5 %collective-permute-done.1.refs_7_ = bf16[512,128]{1,0:T(8,128)(2,1)S(1)} collective-permute-done((bf16[512,128]{1,0:T(8,128)(2,1)}, bf16[512,128]{1,0:T(8,128)(2,1)S(1)}, u32[]{:S(2)}, u32[]{:S(2)}) %collective-permute-start.1) | collective-permute-done | bytes 131104 | tf_op jit(solution)/shard_map/ppermute | solution.py:343
  8.2 0.4 %collective-permute-start.5 = (bf16[512,128]{1,0:T(8,128)(2,1)S(1)}, bf16[512,128]{1,0:T(8,128)(2,1)S(1)}, u32[]{:S(2)}, u32[]{:S(2)}) collective-permute-start(bf16[512,128]{1,0:T(8,128)(2,1)S(1)} %collective-permute-done.1.refs_7_), channel_id=1, source_target_pairs={{0,2},{4,0},{8,4},{12,8},{14,12},{10,14},{6,10},{2,6},{1,3},{5,1},... | collective-permute-start | bytes 393224 | tf_op jit(solution)/shard_map/ppermute | solution.py:343
  8.6 1.6 %collective-permute-start.4 = (bf16[512,128]{1,0:T(8,128)(2,1)S(1)}, bf16[512,128]{1,0:T(8,128)(2,1)S(1)}, u32[]{:S(2)}, u32[]{:S(2)}) collective-permute-start(bf16[512,128]{1,0:T(8,128)(2,1)S(1)} %collective-permute-done.refs_0_), channel_id=1, source_target_pairs={{0,4},{4,8},{8,12},{12,14},{14,10},{10,6},{6,2},{2,0},{1,5},{5,9},... | collective-permute-start | bytes 393224 | tf_op jit(solution)/shard_map/ppermute | solution.py:343
  10.2 0.1 collective-permute-done.2.refs_6_
  10.3 2.4 %collective-permute-done.3.refs_1_ = bf16[512,128]{1,0:T(8,128)(2,1)S(1)} collective-permute-done((bf16[512,128]{1,0:T(8,128)(2,1)}, bf16[512,128]{1,0:T(8,128)(2,1)S(1)}, u32[]{:S(2)}, u32[]{:S(2)}) %collective-permute-start.3) | collective-permute-done | bytes 131104 | tf_op jit(solution)/shard_map/ppermute | solution.py:343
  12.7 1.6 %collective-permute-start.6 = (bf16[512,128]{1,0:T(8,128)(2,1)S(1)}, bf16[512,128]{1,0:T(8,128)(2,1)S(1)}, u32[]{:S(2)}, u32[]{:S(2)}) collective-permute-start(bf16[512,128]{1,0:T(8,128)(2,1)S(1)} %collective-permute-done.2.refs_6_), channel_id=1, source_target_pairs={{0,4},{4,8},{8,12},{12,14},{14,10},{10,6},{6,2},{2,0},{1,5},{5,9},... | collective-permute-start | bytes 393224 | tf_op jit(solution)/shard_map/ppermute | solution.py:343
  14.3 0.4 %collective-permute-start.7 = (bf16[512,128]{1,0:T(8,128)(2,1)S(1)}, bf16[512,128]{1,0:T(8,128)(2,1)S(1)}, u32[]{:S(2)}, u32[]{:S(2)}) collective-permute-start(bf16[512,128]{1,0:T(8,128)(2,1)S(1)} %collective-permute-done.3.refs_1_), channel_id=1, source_target_pairs={{0,2},{4,0},{8,4},{12,8},{14,12},{10,14},{6,10},{2,6},{1,3},{5,1},... | collective-permute-start | bytes 393224 | tf_op jit(solution)/shard_map/ppermute | solution.py:343
  14.7 0.0 collective-permute-done.5.refs_9_
  14.7 0.0 collective-permute-done.4.refs_2_
  14.7 1.3 %collective-permute-start.9 = (bf16[512,128]{1,0:T(8,128)(2,1)S(1)}, bf16[512,128]{1,0:T(8,128)(2,1)S(1)}, u32[]{:S(2)}, u32[]{:S(2)}) collective-permute-start(bf16[512,128]{1,0:T(8,128)(2,1)S(1)} %collective-permute-done.5.refs_9_), channel_id=1, source_target_pairs={{0,2},{4,0},{8,4},{12,8},{14,12},{10,14},{6,10},{2,6},{1,3},{5,1},... | collective-permute-start | bytes 393224 | tf_op jit(solution)/shard_map/ppermute | solution.py:343
  16.0 0.8 %collective-permute-start.8 = (bf16[512,128]{1,0:T(8,128)(2,1)S(1)}, bf16[512,128]{1,0:T(8,128)(2,1)S(1)}, u32[]{:S(2)}, u32[]{:S(2)}) collective-permute-start(bf16[512,128]{1,0:T(8,128)(2,1)S(1)} %collective-permute-done.4.refs_2_), channel_id=1, source_target_pairs={{0,4},{4,8},{8,12},{12,14},{14,10},{10,6},{6,2},{2,0},{1,5},{5,9},... | collective-permute-start | bytes 393224 | tf_op jit(solution)/shard_map/ppermute | solution.py:343
  16.8 2.1 %collective-permute-done.6.refs_8_ = bf16[512,128]{1,0:T(8,128)(2,1)S(1)} collective-permute-done((bf16[512,128]{1,0:T(8,128)(2,1)S(1)}, bf16[512,128]{1,0:T(8,128)(2,1)S(1)}, u32[]{:S(2)}, u32[]{:S(2)}) %collective-permute-start.6) | collective-permute-done | bytes 131104 | tf_op jit(solution)/shard_map/ppermute | solution.py:343
  18.9 0.4 %collective-permute-done.7.refs_3_ = bf16[512,128]{1,0:T(8,128)(2,1)S(1)} collective-permute-done((bf16[512,128]{1,0:T(8,128)(2,1)S(1)}, bf16[512,128]{1,0:T(8,128)(2,1)S(1)}, u32[]{:S(2)}, u32[]{:S(2)}) %collective-permute-start.7) | collective-permute-done | bytes 131104 | tf_op jit(solution)/shard_map/ppermute | solution.py:343
  19.3 1.6 %collective-permute-start.10 = (bf16[512,128]{1,0:T(8,128)(2,1)S(1)}, bf16[512,128]{1,0:T(8,128)(2,1)S(1)}, u32[]{:S(2)}, u32[]{:S(2)}) collective-permute-start(bf16[512,128]{1,0:T(8,128)(2,1)S(1)} %collective-permute-done.6.refs_8_), channel_id=1, source_target_pairs={{0,4},{4,8},{8,12},{12,14},{14,10},{10,6},{6,2},{2,0},{1,5},{5,9},... | collective-permute-start | bytes 393224 | tf_op jit(solution)/shard_map/ppermute | solution.py:343
  20.8 0.4 %collective-permute-start.11 = (bf16[512,128]{1,0:T(8,128)(2,1)S(1)}, bf16[512,128]{1,0:T(8,128)(2,1)S(1)}, u32[]{:S(2)}, u32[]{:S(2)}) collective-permute-start(bf16[512,128]{1,0:T(8,128)(2,1)S(1)} %collective-permute-done.7.refs_3_), channel_id=1, source_target_pairs={{0,2},{4,0},{8,4},{12,8},{14,12},{10,14},{6,10},{2,6},{1,3},{5,1},... | collective-permute-start | bytes 393224 | tf_op jit(solution)/shard_map/ppermute | solution.py:343
  21.3 0.8 %collective-permute-done.9.refs_11_ = bf16[512,128]{1,0:T(8,128)(2,1)S(1)} collective-permute-done((bf16[512,128]{1,0:T(8,128)(2,1)S(1)}, bf16[512,128]{1,0:T(8,128)(2,1)S(1)}, u32[]{:S(2)}, u32[]{:S(2)}) %collective-permute-start.9) | collective-permute-done | bytes 131104 | tf_op jit(solution)/shard_map/ppermute | solution.py:343
  22.0 0.0 collective-permute-done.8.refs_4_
  22.1 0.1 collective-permute-start.13
  22.1 0.5 %collective-permute-start.12 = (bf16[512,128]{1,0:T(8,128)(2,1)S(1)}, bf16[512,128]{1,0:T(8,128)(2,1)S(1)}, u32[]{:S(2)}, u32[]{:S(2)}) collective-permute-start(bf16[512,128]{1,0:T(8,128)(2,1)S(1)} %collective-permute-done.8.refs_4_), channel_id=1, source_target_pairs={{0,1},{1,0},{4,8},{5,9},{8,12},{9,13},{12,14},{13,15},{14,10},{15,... | collective-permute-start | bytes 393224 | tf_op jit(solution)/shard_map/ppermute | solution.py:355
  22.6 1.6 %collective-permute-done.10.refs_10_ = bf16[512,128]{1,0:T(8,128)(2,1)S(1)} collective-permute-done((bf16[512,128]{1,0:T(8,128)(2,1)S(1)}, bf16[512,128]{1,0:T(8,128)(2,1)S(1)}, u32[]{:S(2)}, u32[]{:S(2)}) %collective-permute-start.10) | collective-permute-done | bytes 131104 | tf_op jit(solution)/shard_map/ppermute | solution.py:343
  24.2 1.6 %collective-permute-done.11.refs_5_ = bf16[512,128]{1,0:T(8,128)(2,1)S(1)} collective-permute-done((bf16[512,128]{1,0:T(8,128)(2,1)S(1)}, bf16[512,128]{1,0:T(8,128)(2,1)S(1)}, u32[]{:S(2)}, u32[]{:S(2)}) %collective-permute-start.11) | collective-permute-done | bytes 131104 | tf_op jit(solution)/shard_map/ppermute | solution.py:343
  25.8 2.5 %attend.1 = (bf16[128,32,128]{2,1,0:T(8,128)(2,1)}, f32[4,1024,128]{2,1,0:T(8,128)S(1)}, f32[4,1024,256]{2,1,0:T(8,128)S(1)}) custom-call(s32[4,8]{1,0:T(4,128)S(1)} %get-tuple-element.34.lists_ref, bf16[4,1024,128]{2,1,0:T(8,128)(2,1)S(1)} %get-tuple-element.35.q_ref, bf16[4,128,128]{2,1,0:T(8,128)(2,1)S(1)} %get-tuple-element.36.k_own_ref, ...), custom_call_target="tpu_custom_call" | custom-call | tf_op jit(solution)/shard_map/attend/pallas_call | solution.py:233
  28.3 0.0 collective-permute-done.13.v_ref
  28.3 0.0 collective-permute-done.12.k_ref
  28.3 0.2 attend_last.1
  (1 shorter events, 0.0 us)
Async XLA Ops:
  0.0 6.7 %collective-permute-start = (bf16[512,128]{1,0:T(8,128)(2,1)}, bf16[512,128]{1,0:T(8,128)(2,1)S(1)}, u32[]{:S(2)}, u32[]{:S(2)}) collective-permute-start(bf16[512,128]{1,0:T(8,128)(2,1)} %bitcast.6), channel_id=1, source_target_pairs={{0,4},{4,8},{8,12},{12,14},{14,10},{10,6},{6,2},{2,0},{1,5},{5,9},... | collective-permute-start | bytes 393224 | tf_op jit(solution)/shard_map/ppermute | solution.py:343
  3.0 5.2 %collective-permute-start.1 = (bf16[512,128]{1,0:T(8,128)(2,1)}, bf16[512,128]{1,0:T(8,128)(2,1)S(1)}, u32[]{:S(2)}, u32[]{:S(2)}) collective-permute-start(bf16[512,128]{1,0:T(8,128)(2,1)} %bitcast.3), channel_id=1, source_target_pairs={{0,2},{4,0},{8,4},{12,8},{14,12},{10,14},{6,10},{2,6},{1,3},{5,1},... | collective-permute-start | bytes 393224 | tf_op jit(solution)/shard_map/ppermute | solution.py:343
  4.6 5.7 %collective-permute-start.2 = (bf16[512,128]{1,0:T(8,128)(2,1)}, bf16[512,128]{1,0:T(8,128)(2,1)S(1)}, u32[]{:S(2)}, u32[]{:S(2)}) collective-permute-start(bf16[512,128]{1,0:T(8,128)(2,1)} %bitcast.5), channel_id=1, source_target_pairs={{0,4},{4,8},{8,12},{12,14},{14,10},{10,6},{6,2},{2,0},{1,5},{5,9},... | collective-permute-start | bytes 393224 | tf_op jit(solution)/shard_map/ppermute | solution.py:343
  6.7 6.0 %collective-permute-start.3 = (bf16[512,128]{1,0:T(8,128)(2,1)}, bf16[512,128]{1,0:T(8,128)(2,1)S(1)}, u32[]{:S(2)}, u32[]{:S(2)}) collective-permute-start(bf16[512,128]{1,0:T(8,128)(2,1)} %bitcast.8), channel_id=1, source_target_pairs={{0,2},{4,0},{8,4},{12,8},{14,12},{10,14},{6,10},{2,6},{1,3},{5,1},... | collective-permute-start | bytes 393224 | tf_op jit(solution)/shard_map/ppermute | solution.py:343
  8.2 6.5 %collective-permute-start.5 = (bf16[512,128]{1,0:T(8,128)(2,1)S(1)}, bf16[512,128]{1,0:T(8,128)(2,1)S(1)}, u32[]{:S(2)}, u32[]{:S(2)}) collective-permute-start(bf16[512,128]{1,0:T(8,128)(2,1)S(1)} %collective-permute-done.1.refs_7_), channel_id=1, source_target_pairs={{0,2},{4,0},{8,4},{12,8},{14,12},{10,14},{6,10},{2,6},{1,3},{5,1},... | collective-permute-start | bytes 393224 | tf_op jit(solution)/shard_map/ppermute | solution.py:343
  8.6 6.1 %collective-permute-start.4 = (bf16[512,128]{1,0:T(8,128)(2,1)S(1)}, bf16[512,128]{1,0:T(8,128)(2,1)S(1)}, u32[]{:S(2)}, u32[]{:S(2)}) collective-permute-start(bf16[512,128]{1,0:T(8,128)(2,1)S(1)} %collective-permute-done.refs_0_), channel_id=1, source_target_pairs={{0,4},{4,8},{8,12},{12,14},{14,10},{10,6},{6,2},{2,0},{1,5},{5,9},... | collective-permute-start | bytes 393224 | tf_op jit(solution)/shard_map/ppermute | solution.py:343
  12.7 6.2 %collective-permute-start.6 = (bf16[512,128]{1,0:T(8,128)(2,1)S(1)}, bf16[512,128]{1,0:T(8,128)(2,1)S(1)}, u32[]{:S(2)}, u32[]{:S(2)}) collective-permute-start(bf16[512,128]{1,0:T(8,128)(2,1)S(1)} %collective-permute-done.2.refs_6_), channel_id=1, source_target_pairs={{0,4},{4,8},{8,12},{12,14},{14,10},{10,6},{6,2},{2,0},{1,5},{5,9},... | collective-permute-start | bytes 393224 | tf_op jit(solution)/shard_map/ppermute | solution.py:343
  14.3 5.0 %collective-permute-start.7 = (bf16[512,128]{1,0:T(8,128)(2,1)S(1)}, bf16[512,128]{1,0:T(8,128)(2,1)S(1)}, u32[]{:S(2)}, u32[]{:S(2)}) collective-permute-start(bf16[512,128]{1,0:T(8,128)(2,1)S(1)} %collective-permute-done.3.refs_1_), channel_id=1, source_target_pairs={{0,2},{4,0},{8,4},{12,8},{14,12},{10,14},{6,10},{2,6},{1,3},{5,1},... | collective-permute-start | bytes 393224 | tf_op jit(solution)/shard_map/ppermute | solution.py:343
  14.7 7.3 %collective-permute-start.9 = (bf16[512,128]{1,0:T(8,128)(2,1)S(1)}, bf16[512,128]{1,0:T(8,128)(2,1)S(1)}, u32[]{:S(2)}, u32[]{:S(2)}) collective-permute-start(bf16[512,128]{1,0:T(8,128)(2,1)S(1)} %collective-permute-done.5.refs_9_), channel_id=1, source_target_pairs={{0,2},{4,0},{8,4},{12,8},{14,12},{10,14},{6,10},{2,6},{1,3},{5,1},... | collective-permute-start | bytes 393224 | tf_op jit(solution)/shard_map/ppermute | solution.py:343
  16.0 6.0 %collective-permute-start.8 = (bf16[512,128]{1,0:T(8,128)(2,1)S(1)}, bf16[512,128]{1,0:T(8,128)(2,1)S(1)}, u32[]{:S(2)}, u32[]{:S(2)}) collective-permute-start(bf16[512,128]{1,0:T(8,128)(2,1)S(1)} %collective-permute-done.4.refs_2_), channel_id=1, source_target_pairs={{0,4},{4,8},{8,12},{12,14},{14,10},{10,6},{6,2},{2,0},{1,5},{5,9},... | collective-permute-start | bytes 393224 | tf_op jit(solution)/shard_map/ppermute | solution.py:343
  19.3 5.0 %collective-permute-start.10 = (bf16[512,128]{1,0:T(8,128)(2,1)S(1)}, bf16[512,128]{1,0:T(8,128)(2,1)S(1)}, u32[]{:S(2)}, u32[]{:S(2)}) collective-permute-start(bf16[512,128]{1,0:T(8,128)(2,1)S(1)} %collective-permute-done.6.refs_8_), channel_id=1, source_target_pairs={{0,4},{4,8},{8,12},{12,14},{14,10},{10,6},{6,2},{2,0},{1,5},{5,9},... | collective-permute-start | bytes 393224 | tf_op jit(solution)/shard_map/ppermute | solution.py:343
  20.8 5.0 %collective-permute-start.11 = (bf16[512,128]{1,0:T(8,128)(2,1)S(1)}, bf16[512,128]{1,0:T(8,128)(2,1)S(1)}, u32[]{:S(2)}, u32[]{:S(2)}) collective-permute-start(bf16[512,128]{1,0:T(8,128)(2,1)S(1)} %collective-permute-done.7.refs_3_), channel_id=1, source_target_pairs={{0,2},{4,0},{8,4},{12,8},{14,12},{10,14},{6,10},{2,6},{1,3},{5,1},... | collective-permute-start | bytes 393224 | tf_op jit(solution)/shard_map/ppermute | solution.py:343
  22.1 6.2 %collective-permute-start.13 = (bf16[512,128]{1,0:T(8,128)(2,1)S(1)}, bf16[512,128]{1,0:T(8,128)(2,1)S(1)}, u32[]{:S(2)}, u32[]{:S(2)}) collective-permute-start(bf16[512,128]{1,0:T(8,128)(2,1)S(1)} %fusion.1), channel_id=1, source_target_pairs={{0,1},{1,0},{4,6},{5,7},{8,10},{9,11},{12,4},{13,5},{14,12},{15,13... | collective-permute-start | bytes 393224 | tf_op jit(solution)/shard_map/ppermute | solution.py:355
  22.1 6.2 %collective-permute-start.12 = (bf16[512,128]{1,0:T(8,128)(2,1)S(1)}, bf16[512,128]{1,0:T(8,128)(2,1)S(1)}, u32[]{:S(2)}, u32[]{:S(2)}) collective-permute-start(bf16[512,128]{1,0:T(8,128)(2,1)S(1)} %collective-permute-done.8.refs_4_), channel_id=1, source_target_pairs={{0,1},{1,0},{4,8},{5,9},{8,12},{9,13},{12,14},{13,15},{14,10},{15,... | collective-permute-start | bytes 393224 | tf_op jit(solution)/shard_map/ppermute | solution.py:355

commit v20 on v19

--- a/solution.py
+++ b/solution.py
@@ -9,7 +9,7 @@
 from jax.sharding import PartitionSpec as P
 
 NO_KEY = -1e30
-ROW_CHUNK = 256
+ROW_CHUNK = 128
 LARGEST = 64.0
 ROUND = (8,)
 
@@ -95,6 +95,16 @@
     return jnp.concatenate([values, jnp.ones_like(values)], axis=1)
 
 
+class Once(dict):
+    def __init__(self, make):
+        super().__init__()
+        self.make = make
+
+    def __missing__(self, h):
+        self[h] = self.make(h)
+        return self[h]
+
+
 class Output:
     def __init__(self, out_ref, out_hbm, sems, kv_dev, group):
         self.out_ref, self.out_hbm, self.sems = out_ref, out_hbm, sems
@@ -169,15 +179,19 @@
     def run(others, final):
         keys = (others + 1) * tokens
         output = Output(out_ref, out_hbm, sems, kv_dev, group)
-        k_ready, v_ready = [], []
-        for h in range(kv_dev):
-            k_h, v_h = k_own_ref[h], v_own_ref[h]
-            if others:
-                k_h = jnp.concatenate([k_h, by_head(k_wide, h, kv_dev, keys - tokens)], axis=0)
-                v_h = jnp.concatenate([v_h, by_head(v_wide, h, kv_dev, keys - tokens)], axis=0)
-            k_ready.append(k_h)
-            v_ready.append(with_ones(v_h))
-
+
+        def keys_of(h):
+            if not others:
+                return k_own_ref[h]
+            return jnp.concatenate([k_own_ref[h], by_head(k_wide, h, kv_dev, keys - tokens)], axis=0)
+
+        def values_of(h):
+            if not others:
+                return with_ones(v_own_ref[h])
+            rest = by_head(v_wide, h, kv_dev, keys - tokens)
+            return with_ones(jnp.concatenate([v_own_ref[h], rest], axis=0))
+
+        k_ready, v_ready = Once(keys_of), Once(values_of)
         past = lax.broadcasted_iota(jnp.int32, (ROW_CHUNK, tokens), 0)
         past -= group * lax.broadcasted_iota(jnp.int32, (ROW_CHUNK, tokens), 1)
 
@@ -258,8 +272,8 @@
     def _add():
         k_wide[...] = k_ref[...].astype(jnp.float32)
         v_wide[...] = v_ref[...].astype(jnp.float32)
-        k_ready = [by_head(k_wide, h, kv_dev, tokens) for h in range(kv_dev)]
-        v_ready = [with_ones(by_head(v_wide, h, kv_dev, tokens)) for h in range(kv_dev)]
+        k_ready = Once(lambda h: by_head(k_wide, h, kv_dev, tokens))
+        v_ready = Once(lambda h: with_ones(by_head(v_wide, h, kv_dev, tokens)))
         jobs = chunks_of(kv_dev, rows_all)
         output = Output(out_ref, out_hbm, sems, kv_dev, group)
         shifts = []

time: 28.9 us -> 30.2 us (1.045)
  Pallas kernels: 4.22 us -> 5.62 us
    pallas_call x1, Pallas kernels: 2.47 us -> 3.82 us  [attend(): pl.pallas_call(functools.partial(attend_kernel, codes=codes, code=code, l...]
  transfers between devices with their start and end apart: 14 -> 14, of which waited for: 8 -> 8; matrix products, arithmetic and copies ran while one was open for 0% -> 0% of each run, Pallas kernels for 14% -> 18%
where the time goes in v20:
time: 30.2 us; the launch traced here: 30 us
  starting transfers between devices  13.8 us (46%)
  waiting for transfers between devices  10.4 us (34%)
  Pallas kernels  5.62 us (19%)
    ppermute x12, starting transfers between devices, send(): lax.ppermute(x, 'seq', [(ring[p], ring[(p + turn) % members]) for p in ra...  13.2 us
    ppermute x12, waiting for transfers between devices, send(): lax.ppermute(x, 'seq', [(ring[p], ring[(p + turn) % members]) for p in ra...  10.4 us
    pallas_call x1, Pallas kernels, attend(): pl.pallas_call(functools.partial(attend_kernel, codes=codes, code=code, l...  3.82 us
    pallas_call x1, Pallas kernels, prepare(): pl.pallas_call(functools.partial(prepare_kernel, kv_dev=kv_dev), out_shap...  1.58 us
  transfers between devices with their start and end apart: 14, of which 8 were waited for; matrix products, arithmetic and copies ran while one was open for 0% of the time, Pallas kernels for 18%

profile of v20, /device:TPU:0, one launch (start us, length us, event | category | flops | bytes accessed | tf_op | source)
XLA Modules:
  0.0 30.0 jit_solution(16344634717439200431)
XLA Ops:
  0.0 3.0 %collective-permute-start = (bf16[512,128]{1,0:T(8,128)(2,1)}, bf16[512,128]{1,0:T(8,128)(2,1)S(1)}, u32[]{:S(2)}, u32[]{:S(2)}) collective-permute-start(bf16[512,128]{1,0:T(8,128)(2,1)} %bitcast.6), channel_id=1, source_target_pairs={{0,4},{4,8},{8,12},{12,14},{14,10},{10,6},{6,2},{2,0},{1,5},{5,9},... | collective-permute-start | bytes 393224 | tf_op jit(solution)/shard_map/ppermute | solution.py:357
  3.0 0.0 collective-permute-start.1
  3.0 1.6 %prepare.1 = (s32[4,8]{1,0:T(4,128)S(1)}, bf16[4,1024,128]{2,1,0:T(8,128)(2,1)S(1)}, bf16[4,128,128]{2,1,0:T(8,128)(2,1)S(1)}, bf16[4,128,128]{2,1,0:T(8,128)(2,1)S(1)}) custom-call(s32[4,8]{1,0:T(4,128)} %bitcast.9, bf16[128,32,128]{2,1,0:T(8,128)(2,1)} %q_hbm.1, bf16[512,128]{1,0:T(8,128)(2,1)} %bitcast.7, bf16[512,128]{1,0:T(8,128)(2,1)} %bitcast.4), custom_call_target="tpu_custom_call" | custom-call | tf_op jit(solution)/shard_map/prepare/pallas_call | solution.py:55
  4.6 2.1 %collective-permute-start.2 = (bf16[512,128]{1,0:T(8,128)(2,1)}, bf16[512,128]{1,0:T(8,128)(2,1)S(1)}, u32[]{:S(2)}, u32[]{:S(2)}) collective-permute-start(bf16[512,128]{1,0:T(8,128)(2,1)} %bitcast.5), channel_id=1, source_target_pairs={{0,4},{4,8},{8,12},{12,14},{14,10},{10,6},{6,2},{2,0},{1,5},{5,9},... | collective-permute-start | bytes 393224 | tf_op jit(solution)/shard_map/ppermute | solution.py:357
  6.7 0.0 collective-permute-start.3
  6.7 0.0 collective-permute-done.refs_0_
  6.7 1.5 %collective-permute-done.1.refs_7_ = bf16[512,128]{1,0:T(8,128)(2,1)S(1)} collective-permute-done((bf16[512,128]{1,0:T(8,128)(2,1)}, bf16[512,128]{1,0:T(8,128)(2,1)S(1)}, u32[]{:S(2)}, u32[]{:S(2)}) %collective-permute-start.1) | collective-permute-done | bytes 131104 | tf_op jit(solution)/shard_map/ppermute | solution.py:357
  8.2 0.4 %collective-permute-start.5 = (bf16[512,128]{1,0:T(8,128)(2,1)S(1)}, bf16[512,128]{1,0:T(8,128)(2,1)S(1)}, u32[]{:S(2)}, u32[]{:S(2)}) collective-permute-start(bf16[512,128]{1,0:T(8,128)(2,1)S(1)} %collective-permute-done.1.refs_7_), channel_id=1, source_target_pairs={{0,2},{4,0},{8,4},{12,8},{14,12},{10,14},{6,10},{2,6},{1,3},{5,1},... | collective-permute-start | bytes 393224 | tf_op jit(solution)/shard_map/ppermute | solution.py:357
  8.6 1.6 %collective-permute-start.4 = (bf16[512,128]{1,0:T(8,128)(2,1)S(1)}, bf16[512,128]{1,0:T(8,128)(2,1)S(1)}, u32[]{:S(2)}, u32[]{:S(2)}) collective-permute-start(bf16[512,128]{1,0:T(8,128)(2,1)S(1)} %collective-permute-done.refs_0_), channel_id=1, source_target_pairs={{0,4},{4,8},{8,12},{12,14},{14,10},{10,6},{6,2},{2,0},{1,5},{5,9},... | collective-permute-start | bytes 393224 | tf_op jit(solution)/shard_map/ppermute | solution.py:357
  10.2 0.1 collective-permute-done.2.refs_6_
  10.3 2.4 %collective-permute-done.3.refs_1_ = bf16[512,128]{1,0:T(8,128)(2,1)S(1)} collective-permute-done((bf16[512,128]{1,0:T(8,128)(2,1)}, bf16[512,128]{1,0:T(8,128)(2,1)S(1)}, u32[]{:S(2)}, u32[]{:S(2)}) %collective-permute-start.3) | collective-permute-done | bytes 131104 | tf_op jit(solution)/shard_map/ppermute | solution.py:357
  12.7 1.6 %collective-permute-start.6 = (bf16[512,128]{1,0:T(8,128)(2,1)S(1)}, bf16[512,128]{1,0:T(8,128)(2,1)S(1)}, u32[]{:S(2)}, u32[]{:S(2)}) collective-permute-start(bf16[512,128]{1,0:T(8,128)(2,1)S(1)} %collective-permute-done.2.refs_6_), channel_id=1, source_target_pairs={{0,4},{4,8},{8,12},{12,14},{14,10},{10,6},{6,2},{2,0},{1,5},{5,9},... | collective-permute-start | bytes 393224 | tf_op jit(solution)/shard_map/ppermute | solution.py:357
  14.3 0.4 %collective-permute-start.7 = (bf16[512,128]{1,0:T(8,128)(2,1)S(1)}, bf16[512,128]{1,0:T(8,128)(2,1)S(1)}, u32[]{:S(2)}, u32[]{:S(2)}) collective-permute-start(bf16[512,128]{1,0:T(8,128)(2,1)S(1)} %collective-permute-done.3.refs_1_), channel_id=1, source_target_pairs={{0,2},{4,0},{8,4},{12,8},{14,12},{10,14},{6,10},{2,6},{1,3},{5,1},... | collective-permute-start | bytes 393224 | tf_op jit(solution)/shard_map/ppermute | solution.py:357
  14.7 0.0 collective-permute-done.5.refs_9_
  14.7 0.0 collective-permute-done.4.refs_2_
  14.7 1.3 %collective-permute-start.9 = (bf16[512,128]{1,0:T(8,128)(2,1)S(1)}, bf16[512,128]{1,0:T(8,128)(2,1)S(1)}, u32[]{:S(2)}, u32[]{:S(2)}) collective-permute-start(bf16[512,128]{1,0:T(8,128)(2,1)S(1)} %collective-permute-done.5.refs_9_), channel_id=1, source_target_pairs={{0,2},{4,0},{8,4},{12,8},{14,12},{10,14},{6,10},{2,6},{1,3},{5,1},... | collective-permute-start | bytes 393224 | tf_op jit(solution)/shard_map/ppermute | solution.py:357
  16.0 0.8 %collective-permute-start.8 = (bf16[512,128]{1,0:T(8,128)(2,1)S(1)}, bf16[512,128]{1,0:T(8,128)(2,1)S(1)}, u32[]{:S(2)}, u32[]{:S(2)}) collective-permute-start(bf16[512,128]{1,0:T(8,128)(2,1)S(1)} %collective-permute-done.4.refs_2_), channel_id=1, source_target_pairs={{0,4},{4,8},{8,12},{12,14},{14,10},{10,6},{6,2},{2,0},{1,5},{5,9},... | collective-permute-start | bytes 393224 | tf_op jit(solution)/shard_map/ppermute | solution.py:357
  16.8 2.1 %collective-permute-done.6.refs_8_ = bf16[512,128]{1,0:T(8,128)(2,1)S(1)} collective-permute-done((bf16[512,128]{1,0:T(8,128)(2,1)S(1)}, bf16[512,128]{1,0:T(8,128)(2,1)S(1)}, u32[]{:S(2)}, u32[]{:S(2)}) %collective-permute-start.6) | collective-permute-done | bytes 131104 | tf_op jit(solution)/shard_map/ppermute | solution.py:357
  18.9 0.4 %collective-permute-done.7.refs_3_ = bf16[512,128]{1,0:T(8,128)(2,1)S(1)} collective-permute-done((bf16[512,128]{1,0:T(8,128)(2,1)S(1)}, bf16[512,128]{1,0:T(8,128)(2,1)S(1)}, u32[]{:S(2)}, u32[]{:S(2)}) %collective-permute-start.7) | collective-permute-done | bytes 131104 | tf_op jit(solution)/shard_map/ppermute | solution.py:357
  19.3 1.6 %collective-permute-start.10 = (bf16[512,128]{1,0:T(8,128)(2,1)S(1)}, bf16[512,128]{1,0:T(8,128)(2,1)S(1)}, u32[]{:S(2)}, u32[]{:S(2)}) collective-permute-start(bf16[512,128]{1,0:T(8,128)(2,1)S(1)} %collective-permute-done.6.refs_8_), channel_id=1, source_target_pairs={{0,4},{4,8},{8,12},{12,14},{14,10},{10,6},{6,2},{2,0},{1,5},{5,9},... | collective-permute-start | bytes 393224 | tf_op jit(solution)/shard_map/ppermute | solution.py:357
  20.8 0.4 %collective-permute-start.11 = (bf16[512,128]{1,0:T(8,128)(2,1)S(1)}, bf16[512,128]{1,0:T(8,128)(2,1)S(1)}, u32[]{:S(2)}, u32[]{:S(2)}) collective-permute-start(bf16[512,128]{1,0:T(8,128)(2,1)S(1)} %collective-permute-done.7.refs_3_), channel_id=1, source_target_pairs={{0,2},{4,0},{8,4},{12,8},{14,12},{10,14},{6,10},{2,6},{1,3},{5,1},... | collective-permute-start | bytes 393224 | tf_op jit(solution)/shard_map/ppermute | solution.py:357
  21.3 0.8 %collective-permute-done.9.refs_11_ = bf16[512,128]{1,0:T(8,128)(2,1)S(1)} collective-permute-done((bf16[512,128]{1,0:T(8,128)(2,1)S(1)}, bf16[512,128]{1,0:T(8,128)(2,1)S(1)}, u32[]{:S(2)}, u32[]{:S(2)}) %collective-permute-start.9) | collective-permute-done | bytes 131104 | tf_op jit(solution)/shard_map/ppermute | solution.py:357
  22.0 0.0 collective-permute-done.8.refs_4_
  22.1 0.1 collective-permute-start.13
  22.1 0.5 %collective-permute-start.12 = (bf16[512,128]{1,0:T(8,128)(2,1)S(1)}, bf16[512,128]{1,0:T(8,128)(2,1)S(1)}, u32[]{:S(2)}, u32[]{:S(2)}) collective-permute-start(bf16[512,128]{1,0:T(8,128)(2,1)S(1)} %collective-permute-done.8.refs_4_), channel_id=1, source_target_pairs={{0,1},{1,0},{4,8},{5,9},{8,12},{9,13},{12,14},{13,15},{14,10},{15,... | collective-permute-start | bytes 393224 | tf_op jit(solution)/shard_map/ppermute | solution.py:369
  22.6 1.6 %collective-permute-done.10.refs_10_ = bf16[512,128]{1,0:T(8,128)(2,1)S(1)} collective-permute-done((bf16[512,128]{1,0:T(8,128)(2,1)S(1)}, bf16[512,128]{1,0:T(8,128)(2,1)S(1)}, u32[]{:S(2)}, u32[]{:S(2)}) %collective-permute-start.10) | collective-permute-done | bytes 131104 | tf_op jit(solution)/shard_map/ppermute | solution.py:357
  24.2 1.6 %collective-permute-done.11.refs_5_ = bf16[512,128]{1,0:T(8,128)(2,1)S(1)} collective-permute-done((bf16[512,128]{1,0:T(8,128)(2,1)S(1)}, bf16[512,128]{1,0:T(8,128)(2,1)S(1)}, u32[]{:S(2)}, u32[]{:S(2)}) %collective-permute-start.11) | collective-permute-done | bytes 131104 | tf_op jit(solution)/shard_map/ppermute | solution.py:357
  25.8 3.8 %attend.1 = (bf16[128,32,128]{2,1,0:T(8,128)(2,1)}, f32[4,1024,128]{2,1,0:T(8,128)S(1)}, f32[4,1024,256]{2,1,0:T(8,128)S(1)}) custom-call(s32[4,8]{1,0:T(4,128)S(1)} %get-tuple-element.34.lists_ref, bf16[4,1024,128]{2,1,0:T(8,128)(2,1)S(1)} %get-tuple-element.35.q_ref, bf16[4,128,128]{2,1,0:T(8,128)(2,1)S(1)} %get-tuple-element.36.k_own_ref, ...), custom_call_target="tpu_custom_call" | custom-call | tf_op jit(solution)/shard_map/attend/pallas_call | solution.py:247
  29.6 0.0 collective-permute-done.13.v_ref
  29.6 0.0 collective-permute-done.12.k_ref
  29.6 0.2 attend_last.1
  (1 shorter events, 0.0 us)
Async XLA Ops:
  0.0 6.7 %collective-permute-start = (bf16[512,128]{1,0:T(8,128)(2,1)}, bf16[512,128]{1,0:T(8,128)(2,1)S(1)}, u32[]{:S(2)}, u32[]{:S(2)}) collective-permute-start(bf16[512,128]{1,0:T(8,128)(2,1)} %bitcast.6), channel_id=1, source_target_pairs={{0,4},{4,8},{8,12},{12,14},{14,10},{10,6},{6,2},{2,0},{1,5},{5,9},... | collective-permute-start | bytes 393224 | tf_op jit(solution)/shard_map/ppermute | solution.py:357
  3.0 5.2 %collective-permute-start.1 = (bf16[512,128]{1,0:T(8,128)(2,1)}, bf16[512,128]{1,0:T(8,128)(2,1)S(1)}, u32[]{:S(2)}, u32[]{:S(2)}) collective-permute-start(bf16[512,128]{1,0:T(8,128)(2,1)} %bitcast.3), channel_id=1, source_target_pairs={{0,2},{4,0},{8,4},{12,8},{14,12},{10,14},{6,10},{2,6},{1,3},{5,1},... | collective-permute-start | bytes 393224 | tf_op jit(solution)/shard_map/ppermute | solution.py:357
  4.6 5.7 %collective-permute-start.2 = (bf16[512,128]{1,0:T(8,128)(2,1)}, bf16[512,128]{1,0:T(8,128)(2,1)S(1)}, u32[]{:S(2)}, u32[]{:S(2)}) collective-permute-start(bf16[512,128]{1,0:T(8,128)(2,1)} %bitcast.5), channel_id=1, source_target_pairs={{0,4},{4,8},{8,12},{12,14},{14,10},{10,6},{6,2},{2,0},{1,5},{5,9},... | collective-permute-start | bytes 393224 | tf_op jit(solution)/shard_map/ppermute | solution.py:357
  6.7 6.0 %collective-permute-start.3 = (bf16[512,128]{1,0:T(8,128)(2,1)}, bf16[512,128]{1,0:T(8,128)(2,1)S(1)}, u32[]{:S(2)}, u32[]{:S(2)}) collective-permute-start(bf16[512,128]{1,0:T(8,128)(2,1)} %bitcast.8), channel_id=1, source_target_pairs={{0,2},{4,0},{8,4},{12,8},{14,12},{10,14},{6,10},{2,6},{1,3},{5,1},... | collective-permute-start | bytes 393224 | tf_op jit(solution)/shard_map/ppermute | solution.py:357
  8.2 6.5 %collective-permute-start.5 = (bf16[512,128]{1,0:T(8,128)(2,1)S(1)}, bf16[512,128]{1,0:T(8,128)(2,1)S(1)}, u32[]{:S(2)}, u32[]{:S(2)}) collective-permute-start(bf16[512,128]{1,0:T(8,128)(2,1)S(1)} %collective-permute-done.1.refs_7_), channel_id=1, source_target_pairs={{0,2},{4,0},{8,4},{12,8},{14,12},{10,14},{6,10},{2,6},{1,3},{5,1},... | collective-permute-start | bytes 393224 | tf_op jit(solution)/shard_map/ppermute | solution.py:357
  8.6 6.1 %collective-permute-start.4 = (bf16[512,128]{1,0:T(8,128)(2,1)S(1)}, bf16[512,128]{1,0:T(8,128)(2,1)S(1)}, u32[]{:S(2)}, u32[]{:S(2)}) collective-permute-start(bf16[512,128]{1,0:T(8,128)(2,1)S(1)} %collective-permute-done.refs_0_), channel_id=1, source_target_pairs={{0,4},{4,8},{8,12},{12,14},{14,10},{10,6},{6,2},{2,0},{1,5},{5,9},... | collective-permute-start | bytes 393224 | tf_op jit(solution)/shard_map/ppermute | solution.py:357
  12.7 6.2 %collective-permute-start.6 = (bf16[512,128]{1,0:T(8,128)(2,1)S(1)}, bf16[512,128]{1,0:T(8,128)(2,1)S(1)}, u32[]{:S(2)}, u32[]{:S(2)}) collective-permute-start(bf16[512,128]{1,0:T(8,128)(2,1)S(1)} %collective-permute-done.2.refs_6_), channel_id=1, source_target_pairs={{0,4},{4,8},{8,12},{12,14},{14,10},{10,6},{6,2},{2,0},{1,5},{5,9},... | collective-permute-start | bytes 393224 | tf_op jit(solution)/shard_map/ppermute | solution.py:357
  14.3 5.0 %collective-permute-start.7 = (bf16[512,128]{1,0:T(8,128)(2,1)S(1)}, bf16[512,128]{1,0:T(8,128)(2,1)S(1)}, u32[]{:S(2)}, u32[]{:S(2)}) collective-permute-start(bf16[512,128]{1,0:T(8,128)(2,1)S(1)} %collective-permute-done.3.refs_1_), channel_id=1, source_target_pairs={{0,2},{4,0},{8,4},{12,8},{14,12},{10,14},{6,10},{2,6},{1,3},{5,1},... | collective-permute-start | bytes 393224 | tf_op jit(solution)/shard_map/ppermute | solution.py:357
  14.7 7.3 %collective-permute-start.9 = (bf16[512,128]{1,0:T(8,128)(2,1)S(1)}, bf16[512,128]{1,0:T(8,128)(2,1)S(1)}, u32[]{:S(2)}, u32[]{:S(2)}) collective-permute-start(bf16[512,128]{1,0:T(8,128)(2,1)S(1)} %collective-permute-done.5.refs_9_), channel_id=1, source_target_pairs={{0,2},{4,0},{8,4},{12,8},{14,12},{10,14},{6,10},{2,6},{1,3},{5,1},... | collective-permute-start | bytes 393224 | tf_op jit(solution)/shard_map/ppermute | solution.py:357
  16.0 6.0 %collective-permute-start.8 = (bf16[512,128]{1,0:T(8,128)(2,1)S(1)}, bf16[512,128]{1,0:T(8,128)(2,1)S(1)}, u32[]{:S(2)}, u32[]{:S(2)}) collective-permute-start(bf16[512,128]{1,0:T(8,128)(2,1)S(1)} %collective-permute-done.4.refs_2_), channel_id=1, source_target_pairs={{0,4},{4,8},{8,12},{12,14},{14,10},{10,6},{6,2},{2,0},{1,5},{5,9},... | collective-permute-start | bytes 393224 | tf_op jit(solution)/shard_map/ppermute | solution.py:357
  19.3 5.0 %collective-permute-start.10 = (bf16[512,128]{1,0:T(8,128)(2,1)S(1)}, bf16[512,128]{1,0:T(8,128)(2,1)S(1)}, u32[]{:S(2)}, u32[]{:S(2)}) collective-permute-start(bf16[512,128]{1,0:T(8,128)(2,1)S(1)} %collective-permute-done.6.refs_8_), channel_id=1, source_target_pairs={{0,4},{4,8},{8,12},{12,14},{14,10},{10,6},{6,2},{2,0},{1,5},{5,9},... | collective-permute-start | bytes 393224 | tf_op jit(solution)/shard_map/ppermute | solution.py:357
  20.8 5.0 %collective-permute-start.11 = (bf16[512,128]{1,0:T(8,128)(2,1)S(1)}, bf16[512,128]{1,0:T(8,128)(2,1)S(1)}, u32[]{:S(2)}, u32[]{:S(2)}) collective-permute-start(bf16[512,128]{1,0:T(8,128)(2,1)S(1)} %collective-permute-done.7.refs_3_), channel_id=1, source_target_pairs={{0,2},{4,0},{8,4},{12,8},{14,12},{10,14},{6,10},{2,6},{1,3},{5,1},... | collective-permute-start | bytes 393224 | tf_op jit(solution)/shard_map/ppermute | solution.py:357
  22.1 7.6 %collective-permute-start.13 = (bf16[512,128]{1,0:T(8,128)(2,1)S(1)}, bf16[512,128]{1,0:T(8,128)(2,1)S(1)}, u32[]{:S(2)}, u32[]{:S(2)}) collective-permute-start(bf16[512,128]{1,0:T(8,128)(2,1)S(1)} %fusion.1), channel_id=1, source_target_pairs={{0,1},{1,0},{4,6},{5,7},{8,10},{9,11},{12,4},{13,5},{14,12},{15,13... | collective-permute-start | bytes 393224 | tf_op jit(solution)/shard_map/ppermute | solution.py:369
  22.1 7.5 %collective-permute-start.12 = (bf16[512,128]{1,0:T(8,128)(2,1)S(1)}, bf16[512,128]{1,0:T(8,128)(2,1)S(1)}, u32[]{:S(2)}, u32[]{:S(2)}) collective-permute-start(bf16[512,128]{1,0:T(8,128)(2,1)S(1)} %collective-permute-done.8.refs_4_), channel_id=1, source_target_pairs={{0,1},{1,0},{4,8},{5,9},{8,12},{9,13},{12,14},{13,15},{14,10},{15,... | collective-permute-start | bytes 393224 | tf_op jit(solution)/shard_map/ppermute | solution.py:369

commit v21 on v20

--- a/solution.py
+++ b/solution.py
@@ -9,7 +9,6 @@
 from jax.sharding import PartitionSpec as P
 
 NO_KEY = -1e30
-ROW_CHUNK = 128
 LARGEST = 64.0
 ROUND = (8,)
 
@@ -134,8 +133,12 @@
             copy.wait()
 
 
-def chunks_of(kv_dev, rows_all):
-    return [(h, first) for first in range(0, rows_all, ROW_CHUNK) for h in range(kv_dev)]
+def row_chunk(blocks):
+    return 512 if blocks % 2 else 256
+
+
+def chunks_of(kv_dev, rows_all, chunk):
+    return [(h, first) for first in range(0, rows_all, chunk) for h in range(kv_dev)]
 
 
 def in_turns(stages, jobs):
@@ -178,6 +181,7 @@
 
     def run(others, final):
         keys = (others + 1) * tokens
+        chunk = row_chunk(others + 1)
         output = Output(out_ref, out_hbm, sems, kv_dev, group)
 
         def keys_of(h):
@@ -192,12 +196,12 @@
             return with_ones(jnp.concatenate([v_own_ref[h], rest], axis=0))
 
         k_ready, v_ready = Once(keys_of), Once(values_of)
-        past = lax.broadcasted_iota(jnp.int32, (ROW_CHUNK, tokens), 0)
-        past -= group * lax.broadcasted_iota(jnp.int32, (ROW_CHUNK, tokens), 1)
+        past = lax.broadcasted_iota(jnp.int32, (chunk, tokens), 0)
+        past -= group * lax.broadcasted_iota(jnp.int32, (chunk, tokens), 1)
 
         def score(job, _):
             h, first = job
-            return scores_of(q_ref[h, pl.ds(first, ROW_CHUNK), :], k_ready[h])
+            return scores_of(q_ref[h, pl.ds(first, chunk), :], k_ready[h])
 
         def weigh(job, s):
             first = job[1]
@@ -214,11 +218,11 @@
             if final:
                 output.put(h, first, both)
             else:
-                rows = pl.ds(first, ROW_CHUNK)
-                state[0][h, rows, :] = jnp.broadcast_to(top, (ROW_CHUNK, dim))
+                rows = pl.ds(first, chunk)
+                state[0][h, rows, :] = jnp.broadcast_to(top, (chunk, dim))
                 state[1][h, rows, :] = both
 
-        in_turns([score, weigh, add_up], chunks_of(kv_dev, rows_all))
+        in_turns([score, weigh, add_up], chunks_of(kv_dev, rows_all, chunk))
         output.wait()
 
     unfinished = False if last is None else has(bits, last)
@@ -253,7 +257,7 @@
             pltpu.VMEM((rest, dim), jnp.float32),
             pltpu.VMEM((rest, dim), jnp.float32),
             pltpu.VMEM(out.shape, jnp.bfloat16),
-            pltpu.SemaphoreType.DMA((rows // ROW_CHUNK,)),
+            pltpu.SemaphoreType.DMA((rows // row_chunk(0),)),
         ],
         compiler_params=params(),
         name="attend",
@@ -274,24 +278,25 @@
         v_wide[...] = v_ref[...].astype(jnp.float32)
         k_ready = Once(lambda h: by_head(k_wide, h, kv_dev, tokens))
         v_ready = Once(lambda h: with_ones(by_head(v_wide, h, kv_dev, tokens)))
-        jobs = chunks_of(kv_dev, rows_all)
+        chunk = row_chunk(1)
+        jobs = chunks_of(kv_dev, rows_all, chunk)
         output = Output(out_ref, out_hbm, sems, kv_dev, group)
         shifts = []
 
         def score(job, _):
             h, first = job
-            return scores_of(q_ref[h, pl.ds(first, ROW_CHUNK), :], k_ready[h])
+            return scores_of(q_ref[h, pl.ds(first, chunk), :], k_ready[h])
 
         def weigh(job, s):
             h, first = job
-            shifted = (s - top_ref[h, pl.ds(first, ROW_CHUNK), :]) * factor
-            shifts.append(jnp.max(shifted.reshape(ROW_CHUNK // 8, 8, tokens), axis=0))
+            shifted = (s - top_ref[h, pl.ds(first, chunk), :]) * factor
+            shifts.append(jnp.max(shifted.reshape(chunk // 8, 8, tokens), axis=0))
             return jnp.exp2(shifted).astype(jnp.bfloat16)
 
         def add_up(job, probs):
             h, first = job
             both = jnp.dot(probs, v_ready[h], preferred_element_type=jnp.float32)
-            output.put(h, first, both + both_ref[h, pl.ds(first, ROW_CHUNK), :])
+            output.put(h, first, both + both_ref[h, pl.ds(first, chunk), :])
 
         in_turns([score, weigh, add_up], jobs)
         output.wait()
@@ -300,7 +305,7 @@
         def _rescale():
             again = Output(out_ref, out_hbm, sems, kv_dev, group)
             for h, first in jobs:
-                rows = pl.ds(first, ROW_CHUNK)
+                rows = pl.ds(first, chunk)
                 s = scores_of(q_ref[h, rows, :], k_ready[h])
                 before = top_ref[h, rows, :]
                 top = jnp.maximum(before, jnp.max(s, axis=1, keepdims=True))
@@ -325,7 +330,7 @@
             pltpu.VMEM(k_last.shape, jnp.float32),
             pltpu.VMEM(k_last.shape, jnp.float32),
             pltpu.VMEM(out.shape, jnp.bfloat16),
-            pltpu.SemaphoreType.DMA((queries.shape[1] // ROW_CHUNK,)),
+            pltpu.SemaphoreType.DMA((queries.shape[1] // row_chunk(0),)),
         ],
         compiler_params=params(),
         name="attend_last",

time: 30.2 us -> 29 us (0.960)
  the two profiles are of different devices: /device:TPU:0 before, /device:TPU:20 now
where the time goes in v21:
time: 29 us; the launch traced here: 28.8 us
  starting transfers between devices  14.7 us (51%)
  waiting for transfers between devices  7.1 us (24%)
  Pallas kernels  6.76 us (23%)
    ppermute x12, starting transfers between devices, send(): lax.ppermute(x, 'seq', [(ring[p], ring[(p + turn) % members]) for p in ra...  12.5 us
    ppermute x12, waiting for transfers between devices, send(): lax.ppermute(x, 'seq', [(ring[p], ring[(p + turn) % members]) for p in ra...  7.1 us
    pallas_call x1, Pallas kernels, attend(): pl.pallas_call(functools.partial(attend_kernel, codes=codes, code=code, l...  2.93 us
    ppermute x2, starting transfers between devices, send_last(): return lax.ppermute(x, ('seq', 'head'), pairs)  2.25 us
    pallas_call x1, Pallas kernels, attend_last(): pl.pallas_call(functools.partial(last_kernel, code=code, last=last), out_...  2.24 us
    pallas_call x1, Pallas kernels, prepare(): pl.pallas_call(functools.partial(prepare_kernel, kv_dev=kv_dev), out_shap...  1.58 us
  transfers between devices with their start and end apart: 14, of which 7 were waited for; matrix products, arithmetic and copies ran while one was open for 0% of the time, Pallas kernels for 16%

profile of v21, /device:TPU:20, one launch (start us, length us, event | category | flops | bytes accessed | tf_op | source)
XLA Modules:
  0.0 28.8 jit_solution(4747510063477676514)
XLA Ops:
  0.0 1.6 %collective-permute-start = (bf16[512,128]{1,0:T(8,128)(2,1)}, bf16[512,128]{1,0:T(8,128)(2,1)S(1)}, u32[]{:S(2)}, u32[]{:S(2)}) collective-permute-start(bf16[512,128]{1,0:T(8,128)(2,1)} %bitcast.6), channel_id=1, source_target_pairs={{0,4},{4,8},{8,12},{12,14},{14,10},{10,6},{6,2},{2,0},{1,5},{5,9},... | collective-permute-start | bytes 393224 | tf_op jit(solution)/shard_map/ppermute | solution.py:362
  1.6 0.4 %collective-permute-start.1 = (bf16[512,128]{1,0:T(8,128)(2,1)}, bf16[512,128]{1,0:T(8,128)(2,1)S(1)}, u32[]{:S(2)}, u32[]{:S(2)}) collective-permute-start(bf16[512,128]{1,0:T(8,128)(2,1)} %bitcast.3), channel_id=1, source_target_pairs={{0,2},{4,0},{8,4},{12,8},{14,12},{10,14},{6,10},{2,6},{1,3},{5,1},... | collective-permute-start | bytes 393224 | tf_op jit(solution)/shard_map/ppermute | solution.py:362
  2.0 1.6 %prepare.1 = (s32[4,8]{1,0:T(4,128)S(1)}, bf16[4,1024,128]{2,1,0:T(8,128)(2,1)S(1)}, bf16[4,128,128]{2,1,0:T(8,128)(2,1)S(1)}, bf16[4,128,128]{2,1,0:T(8,128)(2,1)S(1)}) custom-call(s32[4,8]{1,0:T(4,128)} %bitcast.9, bf16[128,32,128]{2,1,0:T(8,128)(2,1)} %q_hbm.1, bf16[512,128]{1,0:T(8,128)(2,1)} %bitcast.7, bf16[512,128]{1,0:T(8,128)(2,1)} %bitcast.4), custom_call_target="tpu_custom_call" | custom-call | tf_op jit(solution)/shard_map/prepare/pallas_call | solution.py:54
  3.6 1.6 %collective-permute-start.2 = (bf16[512,128]{1,0:T(8,128)(2,1)}, bf16[512,128]{1,0:T(8,128)(2,1)S(1)}, u32[]{:S(2)}, u32[]{:S(2)}) collective-permute-start(bf16[512,128]{1,0:T(8,128)(2,1)} %bitcast.5), channel_id=1, source_target_pairs={{0,4},{4,8},{8,12},{12,14},{14,10},{10,6},{6,2},{2,0},{1,5},{5,9},... | collective-permute-start | bytes 393224 | tf_op jit(solution)/shard_map/ppermute | solution.py:362
  5.2 0.4 %collective-permute-start.3 = (bf16[512,128]{1,0:T(8,128)(2,1)}, bf16[512,128]{1,0:T(8,128)(2,1)S(1)}, u32[]{:S(2)}, u32[]{:S(2)}) collective-permute-start(bf16[512,128]{1,0:T(8,128)(2,1)} %bitcast.8), channel_id=1, source_target_pairs={{0,2},{4,0},{8,4},{12,8},{14,12},{10,14},{6,10},{2,6},{1,3},{5,1},... | collective-permute-start | bytes 393224 | tf_op jit(solution)/shard_map/ppermute | solution.py:362
  5.7 0.0 collective-permute-done.refs_0_
  5.7 1.1 %collective-permute-done.1.refs_7_ = bf16[512,128]{1,0:T(8,128)(2,1)S(1)} collective-permute-done((bf16[512,128]{1,0:T(8,128)(2,1)}, bf16[512,128]{1,0:T(8,128)(2,1)S(1)}, u32[]{:S(2)}, u32[]{:S(2)}) %collective-permute-start.1) | collective-permute-done | bytes 131104 | tf_op jit(solution)/shard_map/ppermute | solution.py:362
  6.8 0.4 %collective-permute-start.5 = (bf16[512,128]{1,0:T(8,128)(2,1)S(1)}, bf16[512,128]{1,0:T(8,128)(2,1)S(1)}, u32[]{:S(2)}, u32[]{:S(2)}) collective-permute-start(bf16[512,128]{1,0:T(8,128)(2,1)S(1)} %collective-permute-done.1.refs_7_), channel_id=1, source_target_pairs={{0,2},{4,0},{8,4},{12,8},{14,12},{10,14},{6,10},{2,6},{1,3},{5,1},... | collective-permute-start | bytes 393224 | tf_op jit(solution)/shard_map/ppermute | solution.py:362
  7.2 1.6 %collective-permute-start.4 = (bf16[512,128]{1,0:T(8,128)(2,1)S(1)}, bf16[512,128]{1,0:T(8,128)(2,1)S(1)}, u32[]{:S(2)}, u32[]{:S(2)}) collective-permute-start(bf16[512,128]{1,0:T(8,128)(2,1)S(1)} %collective-permute-done.refs_0_), channel_id=1, source_target_pairs={{0,4},{4,8},{8,12},{12,14},{14,10},{10,6},{6,2},{2,0},{1,5},{5,9},... | collective-permute-start | bytes 393224 | tf_op jit(solution)/shard_map/ppermute | solution.py:362
  8.8 0.7 %collective-permute-done.2.refs_6_ = bf16[512,128]{1,0:T(8,128)(2,1)S(1)} collective-permute-done((bf16[512,128]{1,0:T(8,128)(2,1)}, bf16[512,128]{1,0:T(8,128)(2,1)S(1)}, u32[]{:S(2)}, u32[]{:S(2)}) %collective-permute-start.2) | collective-permute-done | bytes 131104 | tf_op jit(solution)/shard_map/ppermute | solution.py:362
  9.5 1.8 %collective-permute-done.3.refs_1_ = bf16[512,128]{1,0:T(8,128)(2,1)S(1)} collective-permute-done((bf16[512,128]{1,0:T(8,128)(2,1)}, bf16[512,128]{1,0:T(8,128)(2,1)S(1)}, u32[]{:S(2)}, u32[]{:S(2)}) %collective-permute-start.3) | collective-permute-done | bytes 131104 | tf_op jit(solution)/shard_map/ppermute | solution.py:362
  11.3 1.5 %collective-permute-start.6 = (bf16[512,128]{1,0:T(8,128)(2,1)S(1)}, bf16[512,128]{1,0:T(8,128)(2,1)S(1)}, u32[]{:S(2)}, u32[]{:S(2)}) collective-permute-start(bf16[512,128]{1,0:T(8,128)(2,1)S(1)} %collective-permute-done.2.refs_6_), channel_id=1, source_target_pairs={{0,4},{4,8},{8,12},{12,14},{14,10},{10,6},{6,2},{2,0},{1,5},{5,9},... | collective-permute-start | bytes 393224 | tf_op jit(solution)/shard_map/ppermute | solution.py:362
  12.8 0.5 %collective-permute-start.7 = (bf16[512,128]{1,0:T(8,128)(2,1)S(1)}, bf16[512,128]{1,0:T(8,128)(2,1)S(1)}, u32[]{:S(2)}, u32[]{:S(2)}) collective-permute-start(bf16[512,128]{1,0:T(8,128)(2,1)S(1)} %collective-permute-done.3.refs_1_), channel_id=1, source_target_pairs={{0,2},{4,0},{8,4},{12,8},{14,12},{10,14},{6,10},{2,6},{1,3},{5,1},... | collective-permute-start | bytes 393224 | tf_op jit(solution)/shard_map/ppermute | solution.py:362
  13.3 0.0 collective-permute-done.5.refs_9_
  13.3 0.0 collective-permute-done.4.refs_2_
  13.3 0.5 %collective-permute-start.9 = (bf16[512,128]{1,0:T(8,128)(2,1)S(1)}, bf16[512,128]{1,0:T(8,128)(2,1)S(1)}, u32[]{:S(2)}, u32[]{:S(2)}) collective-permute-start(bf16[512,128]{1,0:T(8,128)(2,1)S(1)} %collective-permute-done.5.refs_9_), channel_id=1, source_target_pairs={{0,2},{4,0},{8,4},{12,8},{14,12},{10,14},{6,10},{2,6},{1,3},{5,1},... | collective-permute-start | bytes 393224 | tf_op jit(solution)/shard_map/ppermute | solution.py:362
  13.7 1.9 %collective-permute-start.8 = (bf16[512,128]{1,0:T(8,128)(2,1)S(1)}, bf16[512,128]{1,0:T(8,128)(2,1)S(1)}, u32[]{:S(2)}, u32[]{:S(2)}) collective-permute-start(bf16[512,128]{1,0:T(8,128)(2,1)S(1)} %collective-permute-done.4.refs_2_), channel_id=1, source_target_pairs={{0,4},{4,8},{8,12},{12,14},{14,10},{10,6},{6,2},{2,0},{1,5},{5,9},... | collective-permute-start | bytes 393224 | tf_op jit(solution)/shard_map/ppermute | solution.py:362
  15.6 0.8 %collective-permute-done.6.refs_8_ = bf16[512,128]{1,0:T(8,128)(2,1)S(1)} collective-permute-done((bf16[512,128]{1,0:T(8,128)(2,1)S(1)}, bf16[512,128]{1,0:T(8,128)(2,1)S(1)}, u32[]{:S(2)}, u32[]{:S(2)}) %collective-permute-start.6) | collective-permute-done | bytes 131104 | tf_op jit(solution)/shard_map/ppermute | solution.py:362
  16.4 1.4 %collective-permute-done.7.refs_3_ = bf16[512,128]{1,0:T(8,128)(2,1)S(1)} collective-permute-done((bf16[512,128]{1,0:T(8,128)(2,1)S(1)}, bf16[512,128]{1,0:T(8,128)(2,1)S(1)}, u32[]{:S(2)}, u32[]{:S(2)}) %collective-permute-start.7) | collective-permute-done | bytes 131104 | tf_op jit(solution)/shard_map/ppermute | solution.py:362
  17.7 0.7 %collective-permute-start.10 = (bf16[512,128]{1,0:T(8,128)(2,1)S(1)}, bf16[512,128]{1,0:T(8,128)(2,1)S(1)}, u32[]{:S(2)}, u32[]{:S(2)}) collective-permute-start(bf16[512,128]{1,0:T(8,128)(2,1)S(1)} %collective-permute-done.6.refs_8_), channel_id=1, source_target_pairs={{0,4},{4,8},{8,12},{12,14},{14,10},{10,6},{6,2},{2,0},{1,5},{5,9},... | collective-permute-start | bytes 393224 | tf_op jit(solution)/shard_map/ppermute | solution.py:362
  18.4 1.4 %collective-permute-start.11 = (bf16[512,128]{1,0:T(8,128)(2,1)S(1)}, bf16[512,128]{1,0:T(8,128)(2,1)S(1)}, u32[]{:S(2)}, u32[]{:S(2)}) collective-permute-start(bf16[512,128]{1,0:T(8,128)(2,1)S(1)} %collective-permute-done.7.refs_3_), channel_id=1, source_target_pairs={{0,2},{4,0},{8,4},{12,8},{14,12},{10,14},{6,10},{2,6},{1,3},{5,1},... | collective-permute-start | bytes 393224 | tf_op jit(solution)/shard_map/ppermute | solution.py:362
  19.8 0.5 %collective-permute-done.9.refs_11_ = bf16[512,128]{1,0:T(8,128)(2,1)S(1)} collective-permute-done((bf16[512,128]{1,0:T(8,128)(2,1)S(1)}, bf16[512,128]{1,0:T(8,128)(2,1)S(1)}, u32[]{:S(2)}, u32[]{:S(2)}) %collective-permute-start.9) | collective-permute-done | bytes 131104 | tf_op jit(solution)/shard_map/ppermute | solution.py:362
  20.3 0.0 collective-permute-done.8.refs_4_
  20.3 0.9 %collective-permute-start.13 = (bf16[512,128]{1,0:T(8,128)(2,1)S(1)}, bf16[512,128]{1,0:T(8,128)(2,1)S(1)}, u32[]{:S(2)}, u32[]{:S(2)}) collective-permute-start(bf16[512,128]{1,0:T(8,128)(2,1)S(1)} %fusion.1), channel_id=1, source_target_pairs={{0,1},{1,0},{4,6},{5,7},{8,10},{9,11},{12,4},{13,5},{14,12},{15,13... | collective-permute-start | bytes 393224 | tf_op jit(solution)/shard_map/ppermute | solution.py:374
  21.2 1.3 %collective-permute-start.12 = (bf16[512,128]{1,0:T(8,128)(2,1)S(1)}, bf16[512,128]{1,0:T(8,128)(2,1)S(1)}, u32[]{:S(2)}, u32[]{:S(2)}) collective-permute-start(bf16[512,128]{1,0:T(8,128)(2,1)S(1)} %collective-permute-done.8.refs_4_), channel_id=1, source_target_pairs={{0,1},{1,0},{4,8},{5,9},{8,12},{9,13},{12,14},{13,15},{14,10},{15,... | collective-permute-start | bytes 393224 | tf_op jit(solution)/shard_map/ppermute | solution.py:374
  22.6 0.9 %collective-permute-done.10.refs_10_ = bf16[512,128]{1,0:T(8,128)(2,1)S(1)} collective-permute-done((bf16[512,128]{1,0:T(8,128)(2,1)S(1)}, bf16[512,128]{1,0:T(8,128)(2,1)S(1)}, u32[]{:S(2)}, u32[]{:S(2)}) %collective-permute-start.10) | collective-permute-done | bytes 131104 | tf_op jit(solution)/shard_map/ppermute | solution.py:362
  23.5 0.0 collective-permute-done.11.refs_5_
  23.5 2.9 %attend.1 = (bf16[128,32,128]{2,1,0:T(8,128)(2,1)}, f32[4,1024,128]{2,1,0:T(8,128)S(1)}, f32[4,1024,256]{2,1,0:T(8,128)S(1)}) custom-call(s32[4,8]{1,0:T(4,128)S(1)} %get-tuple-element.34.lists_ref, bf16[4,1024,128]{2,1,0:T(8,128)(2,1)S(1)} %get-tuple-element.35.q_ref, bf16[4,128,128]{2,1,0:T(8,128)(2,1)S(1)} %get-tuple-element.36.k_own_ref, ...), custom_call_target="tpu_custom_call" | custom-call | tf_op jit(solution)/shard_map/attend/pallas_call | solution.py:251
  26.4 0.0 collective-permute-done.13.v_ref
  26.4 0.0 collective-permute-done.12.k_ref
  26.4 2.2 %attend_last.1 = bf16[128,32,128]{2,1,0:T(8,128)(2,1)} custom-call(s32[4,8]{1,0:T(4,128)S(1)} %get-tuple-element.34.lists_ref, bf16[4,1024,128]{2,1,0:T(8,128)(2,1)S(1)} %get-tuple-element.35.q_ref, f32[4,1024,128]{2,1,0:T(8,128)S(1)} %get-tuple-element.52.top_ref, f32[4,1024,256]{2,1,0:T(8,128)S(1)} %get-tuple-element.53.both_ref, ...), custom_call_target="tpu_custom_call", output_to_operand_aliasing={{}: (6, {})} | custom-call | tf_op jit(solution)/shard_map/attend_last/pallas_call | solution.py:323
  (1 shorter events, 0.0 us)
Async XLA Ops:
  0.0 5.7 %collective-permute-start = (bf16[512,128]{1,0:T(8,128)(2,1)}, bf16[512,128]{1,0:T(8,128)(2,1)S(1)}, u32[]{:S(2)}, u32[]{:S(2)}) collective-permute-start(bf16[512,128]{1,0:T(8,128)(2,1)} %bitcast.6), channel_id=1, source_target_pairs={{0,4},{4,8},{8,12},{12,14},{14,10},{10,6},{6,2},{2,0},{1,5},{5,9},... | collective-permute-start | bytes 393224 | tf_op jit(solution)/shard_map/ppermute | solution.py:362
  1.6 5.2 %collective-permute-start.1 = (bf16[512,128]{1,0:T(8,128)(2,1)}, bf16[512,128]{1,0:T(8,128)(2,1)S(1)}, u32[]{:S(2)}, u32[]{:S(2)}) collective-permute-start(bf16[512,128]{1,0:T(8,128)(2,1)} %bitcast.3), channel_id=1, source_target_pairs={{0,2},{4,0},{8,4},{12,8},{14,12},{10,14},{6,10},{2,6},{1,3},{5,1},... | collective-permute-start | bytes 393224 | tf_op jit(solution)/shard_map/ppermute | solution.py:362
  3.6 5.9 %collective-permute-start.2 = (bf16[512,128]{1,0:T(8,128)(2,1)}, bf16[512,128]{1,0:T(8,128)(2,1)S(1)}, u32[]{:S(2)}, u32[]{:S(2)}) collective-permute-start(bf16[512,128]{1,0:T(8,128)(2,1)} %bitcast.5), channel_id=1, source_target_pairs={{0,4},{4,8},{8,12},{12,14},{14,10},{10,6},{6,2},{2,0},{1,5},{5,9},... | collective-permute-start | bytes 393224 | tf_op jit(solution)/shard_map/ppermute | solution.py:362
  5.2 6.0 %collective-permute-start.3 = (bf16[512,128]{1,0:T(8,128)(2,1)}, bf16[512,128]{1,0:T(8,128)(2,1)S(1)}, u32[]{:S(2)}, u32[]{:S(2)}) collective-permute-start(bf16[512,128]{1,0:T(8,128)(2,1)} %bitcast.8), channel_id=1, source_target_pairs={{0,2},{4,0},{8,4},{12,8},{14,12},{10,14},{6,10},{2,6},{1,3},{5,1},... | collective-permute-start | bytes 393224 | tf_op jit(solution)/shard_map/ppermute | solution.py:362
  6.8 6.5 %collective-permute-start.5 = (bf16[512,128]{1,0:T(8,128)(2,1)S(1)}, bf16[512,128]{1,0:T(8,128)(2,1)S(1)}, u32[]{:S(2)}, u32[]{:S(2)}) collective-permute-start(bf16[512,128]{1,0:T(8,128)(2,1)S(1)} %collective-permute-done.1.refs_7_), channel_id=1, source_target_pairs={{0,2},{4,0},{8,4},{12,8},{14,12},{10,14},{6,10},{2,6},{1,3},{5,1},... | collective-permute-start | bytes 393224 | tf_op jit(solution)/shard_map/ppermute | solution.py:362
  7.2 6.1 %collective-permute-start.4 = (bf16[512,128]{1,0:T(8,128)(2,1)S(1)}, bf16[512,128]{1,0:T(8,128)(2,1)S(1)}, u32[]{:S(2)}, u32[]{:S(2)}) collective-permute-start(bf16[512,128]{1,0:T(8,128)(2,1)S(1)} %collective-permute-done.refs_0_), channel_id=1, source_target_pairs={{0,4},{4,8},{8,12},{12,14},{14,10},{10,6},{6,2},{2,0},{1,5},{5,9},... | collective-permute-start | bytes 393224 | tf_op jit(solution)/shard_map/ppermute | solution.py:362
  11.3 5.1 %collective-permute-start.6 = (bf16[512,128]{1,0:T(8,128)(2,1)S(1)}, bf16[512,128]{1,0:T(8,128)(2,1)S(1)}, u32[]{:S(2)}, u32[]{:S(2)}) collective-permute-start(bf16[512,128]{1,0:T(8,128)(2,1)S(1)} %collective-permute-done.2.refs_6_), channel_id=1, source_target_pairs={{0,4},{4,8},{8,12},{12,14},{14,10},{10,6},{6,2},{2,0},{1,5},{5,9},... | collective-permute-start | bytes 393224 | tf_op jit(solution)/shard_map/ppermute | solution.py:362
  12.8 5.0 %collective-permute-start.7 = (bf16[512,128]{1,0:T(8,128)(2,1)S(1)}, bf16[512,128]{1,0:T(8,128)(2,1)S(1)}, u32[]{:S(2)}, u32[]{:S(2)}) collective-permute-start(bf16[512,128]{1,0:T(8,128)(2,1)S(1)} %collective-permute-done.3.refs_1_), channel_id=1, source_target_pairs={{0,2},{4,0},{8,4},{12,8},{14,12},{10,14},{6,10},{2,6},{1,3},{5,1},... | collective-permute-start | bytes 393224 | tf_op jit(solution)/shard_map/ppermute | solution.py:362
  13.3 7.0 %collective-permute-start.9 = (bf16[512,128]{1,0:T(8,128)(2,1)S(1)}, bf16[512,128]{1,0:T(8,128)(2,1)S(1)}, u32[]{:S(2)}, u32[]{:S(2)}) collective-permute-start(bf16[512,128]{1,0:T(8,128)(2,1)S(1)} %collective-permute-done.5.refs_9_), channel_id=1, source_target_pairs={{0,2},{4,0},{8,4},{12,8},{14,12},{10,14},{6,10},{2,6},{1,3},{5,1},... | collective-permute-start | bytes 393224 | tf_op jit(solution)/shard_map/ppermute | solution.py:362
  13.7 6.5 %collective-permute-start.8 = (bf16[512,128]{1,0:T(8,128)(2,1)S(1)}, bf16[512,128]{1,0:T(8,128)(2,1)S(1)}, u32[]{:S(2)}, u32[]{:S(2)}) collective-permute-start(bf16[512,128]{1,0:T(8,128)(2,1)S(1)} %collective-permute-done.4.refs_2_), channel_id=1, source_target_pairs={{0,4},{4,8},{8,12},{12,14},{14,10},{10,6},{6,2},{2,0},{1,5},{5,9},... | collective-permute-start | bytes 393224 | tf_op jit(solution)/shard_map/ppermute | solution.py:362
  17.7 5.7 %collective-permute-start.10 = (bf16[512,128]{1,0:T(8,128)(2,1)S(1)}, bf16[512,128]{1,0:T(8,128)(2,1)S(1)}, u32[]{:S(2)}, u32[]{:S(2)}) collective-permute-start(bf16[512,128]{1,0:T(8,128)(2,1)S(1)} %collective-permute-done.6.refs_8_), channel_id=1, source_target_pairs={{0,4},{4,8},{8,12},{12,14},{14,10},{10,6},{6,2},{2,0},{1,5},{5,9},... | collective-permute-start | bytes 393224 | tf_op jit(solution)/shard_map/ppermute | solution.py:362
  18.4 5.1 %collective-permute-start.11 = (bf16[512,128]{1,0:T(8,128)(2,1)S(1)}, bf16[512,128]{1,0:T(8,128)(2,1)S(1)}, u32[]{:S(2)}, u32[]{:S(2)}) collective-permute-start(bf16[512,128]{1,0:T(8,128)(2,1)S(1)} %collective-permute-done.7.refs_3_), channel_id=1, source_target_pairs={{0,2},{4,0},{8,4},{12,8},{14,12},{10,14},{6,10},{2,6},{1,3},{5,1},... | collective-permute-start | bytes 393224 | tf_op jit(solution)/shard_map/ppermute | solution.py:362
  20.3 6.1 %collective-permute-start.13 = (bf16[512,128]{1,0:T(8,128)(2,1)S(1)}, bf16[512,128]{1,0:T(8,128)(2,1)S(1)}, u32[]{:S(2)}, u32[]{:S(2)}) collective-permute-start(bf16[512,128]{1,0:T(8,128)(2,1)S(1)} %fusion.1), channel_id=1, source_target_pairs={{0,1},{1,0},{4,6},{5,7},{8,10},{9,11},{12,4},{13,5},{14,12},{15,13... | collective-permute-start | bytes 393224 | tf_op jit(solution)/shard_map/ppermute | solution.py:374
  21.2 5.2 %collective-permute-start.12 = (bf16[512,128]{1,0:T(8,128)(2,1)S(1)}, bf16[512,128]{1,0:T(8,128)(2,1)S(1)}, u32[]{:S(2)}, u32[]{:S(2)}) collective-permute-start(bf16[512,128]{1,0:T(8,128)(2,1)S(1)} %collective-permute-done.8.refs_4_), channel_id=1, source_target_pairs={{0,1},{1,0},{4,8},{5,9},{8,12},{9,13},{12,14},{13,15},{14,10},{15,... | collective-permute-start | bytes 393224 | tf_op jit(solution)/shard_map/ppermute | solution.py:374

commit v22 on v19

--- a/solution.py
+++ b/solution.py
@@ -362,7 +362,6 @@
             k_two[1], v_two[0], ready = lax.optimization_barrier((k_two[1], v_two[0], ready))
         behind = send(v_two[0], 1), send(k_two[1], -1)
         ahead = lax.optimization_barrier(ahead)
-        behind = lax.optimization_barrier(behind)
         k_two, v_two = [ahead[0], behind[1]], [behind[0], ahead[1]]
         k_all += k_two
         v_all += v_two

time: 28.9 us -> 29.2 us (1.010)
  the two profiles are of different devices: /device:TPU:0 before, /device:TPU:20 now
where the time goes in v22:
time: 29.2 us; the launch traced here: 29 us
  starting transfers between devices  13.8 us (47%)
  waiting for transfers between devices  8.3 us (28%)
  Pallas kernels  6.69 us (23%)
    ppermute x12, starting transfers between devices, send(): lax.ppermute(x, 'seq', [(ring[p], ring[(p + turn) % members]) for p in ra...  12.2 us
    ppermute x12, waiting for transfers between devices, send(): lax.ppermute(x, 'seq', [(ring[p], ring[(p + turn) % members]) for p in ra...  7.15 us
    pallas_call x1, Pallas kernels, attend(): pl.pallas_call(functools.partial(attend_kernel, codes=codes, code=code, l...  2.93 us
    pallas_call x1, Pallas kernels, attend_last(): pl.pallas_call(functools.partial(last_kernel, code=code, last=last), out_...  2.17 us
    ppermute x2, starting transfers between devices, send_last(): return lax.ppermute(x, ('seq', 'head'), pairs)  1.6 us
    pallas_call x1, Pallas kernels, prepare(): pl.pallas_call(functools.partial(prepare_kernel, kv_dev=kv_dev), out_shap...  1.58 us
    ppermute x2, waiting for transfers between devices, send_last(): return lax.ppermute(x, ('seq', 'head'), pairs)  1.16 us
  transfers between devices with their start and end apart: 14, of which 8 were waited for; matrix products, arithmetic and copies ran while one was open for 0% of the time, Pallas kernels for 16%

profile of v22, /device:TPU:20, one launch (start us, length us, event | category | flops | bytes accessed | tf_op | source)
XLA Modules:
  0.0 29.0 jit_solution(10479565784272181647)
XLA Ops:
  0.0 1.6 %collective-permute-start = (bf16[512,128]{1,0:T(8,128)(2,1)}, bf16[512,128]{1,0:T(8,128)(2,1)S(1)}, u32[]{:S(2)}, u32[]{:S(2)}) collective-permute-start(bf16[512,128]{1,0:T(8,128)(2,1)} %bitcast.6), channel_id=1, source_target_pairs={{0,4},{4,8},{8,12},{12,14},{14,10},{10,6},{6,2},{2,0},{1,5},{5,9},... | collective-permute-start | bytes 393224 | tf_op jit(solution)/shard_map/ppermute | solution.py:343
  1.6 0.4 %collective-permute-start.1 = (bf16[512,128]{1,0:T(8,128)(2,1)}, bf16[512,128]{1,0:T(8,128)(2,1)S(1)}, u32[]{:S(2)}, u32[]{:S(2)}) collective-permute-start(bf16[512,128]{1,0:T(8,128)(2,1)} %bitcast.3), channel_id=1, source_target_pairs={{0,2},{4,0},{8,4},{12,8},{14,12},{10,14},{6,10},{2,6},{1,3},{5,1},... | collective-permute-start | bytes 393224 | tf_op jit(solution)/shard_map/ppermute | solution.py:343
  2.0 1.6 %prepare.1 = (s32[4,8]{1,0:T(4,128)S(1)}, bf16[4,1024,128]{2,1,0:T(8,128)(2,1)S(1)}, bf16[4,128,128]{2,1,0:T(8,128)(2,1)S(1)}, bf16[4,128,128]{2,1,0:T(8,128)(2,1)S(1)}) custom-call(s32[4,8]{1,0:T(4,128)} %bitcast.9, bf16[128,32,128]{2,1,0:T(8,128)(2,1)} %q_hbm.1, bf16[512,128]{1,0:T(8,128)(2,1)} %bitcast.7, bf16[512,128]{1,0:T(8,128)(2,1)} %bitcast.4), custom_call_target="tpu_custom_call" | custom-call | tf_op jit(solution)/shard_map/prepare/pallas_call | solution.py:55
  3.6 1.6 %collective-permute-start.9 = (bf16[512,128]{1,0:T(8,128)(2,1)}, bf16[512,128]{1,0:T(8,128)(2,1)S(1)}, u32[]{:S(2)}, u32[]{:S(2)}) collective-permute-start(bf16[512,128]{1,0:T(8,128)(2,1)} %bitcast.5), channel_id=1, source_target_pairs={{0,4},{4,8},{8,12},{12,14},{14,10},{10,6},{6,2},{2,0},{1,5},{5,9},... | collective-permute-start | bytes 393224 | tf_op jit(solution)/shard_map/ppermute | solution.py:343
  5.2 0.4 %collective-permute-start.2 = (bf16[512,128]{1,0:T(8,128)(2,1)}, bf16[512,128]{1,0:T(8,128)(2,1)S(1)}, u32[]{:S(2)}, u32[]{:S(2)}) collective-permute-start(bf16[512,128]{1,0:T(8,128)(2,1)} %bitcast.8), channel_id=1, source_target_pairs={{0,2},{4,0},{8,4},{12,8},{14,12},{10,14},{6,10},{2,6},{1,3},{5,1},... | collective-permute-start | bytes 393224 | tf_op jit(solution)/shard_map/ppermute | solution.py:343
  5.7 0.0 collective-permute-done.refs_0_
  5.7 1.1 %collective-permute-done.1.refs_7_ = bf16[512,128]{1,0:T(8,128)(2,1)S(1)} collective-permute-done((bf16[512,128]{1,0:T(8,128)(2,1)}, bf16[512,128]{1,0:T(8,128)(2,1)S(1)}, u32[]{:S(2)}, u32[]{:S(2)}) %collective-permute-start.1) | collective-permute-done | bytes 131104 | tf_op jit(solution)/shard_map/ppermute | solution.py:343
  6.8 0.4 %collective-permute-start.4 = (bf16[512,128]{1,0:T(8,128)(2,1)S(1)}, bf16[512,128]{1,0:T(8,128)(2,1)S(1)}, u32[]{:S(2)}, u32[]{:S(2)}) collective-permute-start(bf16[512,128]{1,0:T(8,128)(2,1)S(1)} %collective-permute-done.1.refs_7_), channel_id=1, source_target_pairs={{0,2},{4,0},{8,4},{12,8},{14,12},{10,14},{6,10},{2,6},{1,3},{5,1},... | collective-permute-start | bytes 393224 | tf_op jit(solution)/shard_map/ppermute | solution.py:343
  7.2 1.6 %collective-permute-start.3 = (bf16[512,128]{1,0:T(8,128)(2,1)S(1)}, bf16[512,128]{1,0:T(8,128)(2,1)S(1)}, u32[]{:S(2)}, u32[]{:S(2)}) collective-permute-start(bf16[512,128]{1,0:T(8,128)(2,1)S(1)} %collective-permute-done.refs_0_), channel_id=1, source_target_pairs={{0,4},{4,8},{8,12},{12,14},{14,10},{10,6},{6,2},{2,0},{1,5},{5,9},... | collective-permute-start | bytes 393224 | tf_op jit(solution)/shard_map/ppermute | solution.py:343
  8.8 0.7 %collective-permute-done.9.refs_6_ = bf16[512,128]{1,0:T(8,128)(2,1)S(1)} collective-permute-done((bf16[512,128]{1,0:T(8,128)(2,1)}, bf16[512,128]{1,0:T(8,128)(2,1)S(1)}, u32[]{:S(2)}, u32[]{:S(2)}) %collective-permute-start.9) | collective-permute-done | bytes 131104 | tf_op jit(solution)/shard_map/ppermute | solution.py:343
  9.5 1.6 %collective-permute-start.10 = (bf16[512,128]{1,0:T(8,128)(2,1)S(1)}, bf16[512,128]{1,0:T(8,128)(2,1)S(1)}, u32[]{:S(2)}, u32[]{:S(2)}) collective-permute-start(bf16[512,128]{1,0:T(8,128)(2,1)S(1)} %collective-permute-done.9.refs_6_), channel_id=1, source_target_pairs={{0,4},{4,8},{8,12},{12,14},{14,10},{10,6},{6,2},{2,0},{1,5},{5,9},... | collective-permute-start | bytes 393224 | tf_op jit(solution)/shard_map/ppermute | solution.py:343
  11.1 0.2 collective-permute-done.2.refs_1_
  11.3 0.4 %collective-permute-start.5 = (bf16[512,128]{1,0:T(8,128)(2,1)S(1)}, bf16[512,128]{1,0:T(8,128)(2,1)S(1)}, u32[]{:S(2)}, u32[]{:S(2)}) collective-permute-start(bf16[512,128]{1,0:T(8,128)(2,1)S(1)} %collective-permute-done.2.refs_1_), channel_id=1, source_target_pairs={{0,2},{4,0},{8,4},{12,8},{14,12},{10,14},{6,10},{2,6},{1,3},{5,1},... | collective-permute-start | bytes 393224 | tf_op jit(solution)/shard_map/ppermute | solution.py:343
  11.7 2.4 %collective-permute-done.4.refs_9_ = bf16[512,128]{1,0:T(8,128)(2,1)S(1)} collective-permute-done((bf16[512,128]{1,0:T(8,128)(2,1)S(1)}, bf16[512,128]{1,0:T(8,128)(2,1)S(1)}, u32[]{:S(2)}, u32[]{:S(2)}) %collective-permute-start.4) | collective-permute-done | bytes 131104 | tf_op jit(solution)/shard_map/ppermute | solution.py:343
  14.1 0.0 collective-permute-done.3.refs_2_
  14.1 0.5 %collective-permute-start.7 = (bf16[512,128]{1,0:T(8,128)(2,1)S(1)}, bf16[512,128]{1,0:T(8,128)(2,1)S(1)}, u32[]{:S(2)}, u32[]{:S(2)}) collective-permute-start(bf16[512,128]{1,0:T(8,128)(2,1)S(1)} %collective-permute-done.4.refs_9_), channel_id=1, source_target_pairs={{0,2},{4,0},{8,4},{12,8},{14,12},{10,14},{6,10},{2,6},{1,3},{5,1},... | collective-permute-start | bytes 393224 | tf_op jit(solution)/shard_map/ppermute | solution.py:343
  14.6 1.6 %collective-permute-start.6 = (bf16[512,128]{1,0:T(8,128)(2,1)S(1)}, bf16[512,128]{1,0:T(8,128)(2,1)S(1)}, u32[]{:S(2)}, u32[]{:S(2)}) collective-permute-start(bf16[512,128]{1,0:T(8,128)(2,1)S(1)} %collective-permute-done.3.refs_2_), channel_id=1, source_target_pairs={{0,4},{4,8},{8,12},{12,14},{14,10},{10,6},{6,2},{2,0},{1,5},{5,9},... | collective-permute-start | bytes 393224 | tf_op jit(solution)/shard_map/ppermute | solution.py:343
  16.1 0.0 collective-permute-done.10.refs_8_
  16.1 1.5 %collective-permute-start.11 = (bf16[512,128]{1,0:T(8,128)(2,1)S(1)}, bf16[512,128]{1,0:T(8,128)(2,1)S(1)}, u32[]{:S(2)}, u32[]{:S(2)}) collective-permute-start(bf16[512,128]{1,0:T(8,128)(2,1)S(1)} %collective-permute-done.10.refs_8_), channel_id=1, source_target_pairs={{0,4},{4,8},{8,12},{12,14},{14,10},{10,6},{6,2},{2,0},{1,5},{5,9},... | collective-permute-start | bytes 393224 | tf_op jit(solution)/shard_map/ppermute | solution.py:343
  17.6 0.0 collective-permute-done.5.refs_3_
  17.6 0.5 %collective-permute-start.8 = (bf16[512,128]{1,0:T(8,128)(2,1)S(1)}, bf16[512,128]{1,0:T(8,128)(2,1)S(1)}, u32[]{:S(2)}, u32[]{:S(2)}) collective-permute-start(bf16[512,128]{1,0:T(8,128)(2,1)S(1)} %collective-permute-done.5.refs_3_), channel_id=1, source_target_pairs={{0,2},{4,0},{8,4},{12,8},{14,12},{10,14},{6,10},{2,6},{1,3},{5,1},... | collective-permute-start | bytes 393224 | tf_op jit(solution)/shard_map/ppermute | solution.py:343
  18.2 2.3 %collective-permute-done.7.refs_11_ = bf16[512,128]{1,0:T(8,128)(2,1)S(1)} collective-permute-done((bf16[512,128]{1,0:T(8,128)(2,1)S(1)}, bf16[512,128]{1,0:T(8,128)(2,1)S(1)}, u32[]{:S(2)}, u32[]{:S(2)}) %collective-permute-start.7) | collective-permute-done | bytes 131104 | tf_op jit(solution)/shard_map/ppermute | solution.py:343
  20.5 0.0 collective-permute-done.6.refs_4_
  20.5 1.2 %collective-permute-start.13 = (bf16[512,128]{1,0:T(8,128)(2,1)S(1)}, bf16[512,128]{1,0:T(8,128)(2,1)S(1)}, u32[]{:S(2)}, u32[]{:S(2)}) collective-permute-start(bf16[512,128]{1,0:T(8,128)(2,1)S(1)} %fusion.1), channel_id=1, source_target_pairs={{0,1},{1,0},{4,6},{5,7},{8,10},{9,11},{12,4},{13,5},{14,12},{15,13... | collective-permute-start | bytes 393224 | tf_op jit(solution)/shard_map/ppermute | solution.py:355
  21.7 0.4 %collective-permute-start.12 = (bf16[512,128]{1,0:T(8,128)(2,1)S(1)}, bf16[512,128]{1,0:T(8,128)(2,1)S(1)}, u32[]{:S(2)}, u32[]{:S(2)}) collective-permute-start(bf16[512,128]{1,0:T(8,128)(2,1)S(1)} %collective-permute-done.6.refs_4_), channel_id=1, source_target_pairs={{0,1},{1,0},{4,8},{5,9},{8,12},{9,13},{12,14},{13,15},{14,10},{15,... | collective-permute-start | bytes 393224 | tf_op jit(solution)/shard_map/ppermute | solution.py:355
  22.1 0.2 collective-permute-done.11.refs_10_
  22.3 0.3 collective-permute-done.8.refs_5_
  22.6 2.9 %attend.1 = (bf16[128,32,128]{2,1,0:T(8,128)(2,1)}, f32[4,1024,128]{2,1,0:T(8,128)S(1)}, f32[4,1024,256]{2,1,0:T(8,128)S(1)}) custom-call(s32[4,8]{1,0:T(4,128)S(1)} %get-tuple-element.28.lists_ref, bf16[4,1024,128]{2,1,0:T(8,128)(2,1)S(1)} %get-tuple-element.29.q_ref, bf16[4,128,128]{2,1,0:T(8,128)(2,1)S(1)} %get-tuple-element.30.k_own_ref, ...), custom_call_target="tpu_custom_call" | custom-call | tf_op jit(solution)/shard_map/attend/pallas_call | solution.py:233
  25.5 0.0 collective-permute-done.13.v_ref
  25.6 1.2 %collective-permute-done.12.k_ref = bf16[512,128]{1,0:T(8,128)(2,1)S(1)} collective-permute-done((bf16[512,128]{1,0:T(8,128)(2,1)S(1)}, bf16[512,128]{1,0:T(8,128)(2,1)S(1)}, u32[]{:S(2)}, u32[]{:S(2)}) %collective-permute-start.12) | collective-permute-done | bytes 131104 | tf_op jit(solution)/shard_map/ppermute | solution.py:355
  26.7 2.2 %attend_last.1 = bf16[128,32,128]{2,1,0:T(8,128)(2,1)} custom-call(s32[4,8]{1,0:T(4,128)S(1)} %get-tuple-element.28.lists_ref, bf16[4,1024,128]{2,1,0:T(8,128)(2,1)S(1)} %get-tuple-element.29.q_ref, f32[4,1024,128]{2,1,0:T(8,128)S(1)} %get-tuple-element.40.top_ref, f32[4,1024,256]{2,1,0:T(8,128)S(1)} %get-tuple-element.41.both_ref, ...), custom_call_target="tpu_custom_call", output_to_operand_aliasing={{}: (6, {})} | custom-call | tf_op jit(solution)/shard_map/attend_last/pallas_call | solution.py:304
  (1 shorter events, 0.0 us)
Async XLA Ops:
  0.0 5.7 %collective-permute-start = (bf16[512,128]{1,0:T(8,128)(2,1)}, bf16[512,128]{1,0:T(8,128)(2,1)S(1)}, u32[]{:S(2)}, u32[]{:S(2)}) collective-permute-start(bf16[512,128]{1,0:T(8,128)(2,1)} %bitcast.6), channel_id=1, source_target_pairs={{0,4},{4,8},{8,12},{12,14},{14,10},{10,6},{6,2},{2,0},{1,5},{5,9},... | collective-permute-start | bytes 393224 | tf_op jit(solution)/shard_map/ppermute | solution.py:343
  1.6 5.2 %collective-permute-start.1 = (bf16[512,128]{1,0:T(8,128)(2,1)}, bf16[512,128]{1,0:T(8,128)(2,1)S(1)}, u32[]{:S(2)}, u32[]{:S(2)}) collective-permute-start(bf16[512,128]{1,0:T(8,128)(2,1)} %bitcast.3), channel_id=1, source_target_pairs={{0,2},{4,0},{8,4},{12,8},{14,12},{10,14},{6,10},{2,6},{1,3},{5,1},... | collective-permute-start | bytes 393224 | tf_op jit(solution)/shard_map/ppermute | solution.py:343
  3.6 5.9 %collective-permute-start.9 = (bf16[512,128]{1,0:T(8,128)(2,1)}, bf16[512,128]{1,0:T(8,128)(2,1)S(1)}, u32[]{:S(2)}, u32[]{:S(2)}) collective-permute-start(bf16[512,128]{1,0:T(8,128)(2,1)} %bitcast.5), channel_id=1, source_target_pairs={{0,4},{4,8},{8,12},{12,14},{14,10},{10,6},{6,2},{2,0},{1,5},{5,9},... | collective-permute-start | bytes 393224 | tf_op jit(solution)/shard_map/ppermute | solution.py:343
  5.2 6.0 %collective-permute-start.2 = (bf16[512,128]{1,0:T(8,128)(2,1)}, bf16[512,128]{1,0:T(8,128)(2,1)S(1)}, u32[]{:S(2)}, u32[]{:S(2)}) collective-permute-start(bf16[512,128]{1,0:T(8,128)(2,1)} %bitcast.8), channel_id=1, source_target_pairs={{0,2},{4,0},{8,4},{12,8},{14,12},{10,14},{6,10},{2,6},{1,3},{5,1},... | collective-permute-start | bytes 393224 | tf_op jit(solution)/shard_map/ppermute | solution.py:343
  6.8 7.3 %collective-permute-start.4 = (bf16[512,128]{1,0:T(8,128)(2,1)S(1)}, bf16[512,128]{1,0:T(8,128)(2,1)S(1)}, u32[]{:S(2)}, u32[]{:S(2)}) collective-permute-start(bf16[512,128]{1,0:T(8,128)(2,1)S(1)} %collective-permute-done.1.refs_7_), channel_id=1, source_target_pairs={{0,2},{4,0},{8,4},{12,8},{14,12},{10,14},{6,10},{2,6},{1,3},{5,1},... | collective-permute-start | bytes 393224 | tf_op jit(solution)/shard_map/ppermute | solution.py:343
  7.2 6.9 %collective-permute-start.3 = (bf16[512,128]{1,0:T(8,128)(2,1)S(1)}, bf16[512,128]{1,0:T(8,128)(2,1)S(1)}, u32[]{:S(2)}, u32[]{:S(2)}) collective-permute-start(bf16[512,128]{1,0:T(8,128)(2,1)S(1)} %collective-permute-done.refs_0_), channel_id=1, source_target_pairs={{0,4},{4,8},{8,12},{12,14},{14,10},{10,6},{6,2},{2,0},{1,5},{5,9},... | collective-permute-start | bytes 393224 | tf_op jit(solution)/shard_map/ppermute | solution.py:343
  9.5 6.6 %collective-permute-start.10 = (bf16[512,128]{1,0:T(8,128)(2,1)S(1)}, bf16[512,128]{1,0:T(8,128)(2,1)S(1)}, u32[]{:S(2)}, u32[]{:S(2)}) collective-permute-start(bf16[512,128]{1,0:T(8,128)(2,1)S(1)} %collective-permute-done.9.refs_6_), channel_id=1, source_target_pairs={{0,4},{4,8},{8,12},{12,14},{14,10},{10,6},{6,2},{2,0},{1,5},{5,9},... | collective-permute-start | bytes 393224 | tf_op jit(solution)/shard_map/ppermute | solution.py:343
  11.3 6.3 %collective-permute-start.5 = (bf16[512,128]{1,0:T(8,128)(2,1)S(1)}, bf16[512,128]{1,0:T(8,128)(2,1)S(1)}, u32[]{:S(2)}, u32[]{:S(2)}) collective-permute-start(bf16[512,128]{1,0:T(8,128)(2,1)S(1)} %collective-permute-done.2.refs_1_), channel_id=1, source_target_pairs={{0,2},{4,0},{8,4},{12,8},{14,12},{10,14},{6,10},{2,6},{1,3},{5,1},... | collective-permute-start | bytes 393224 | tf_op jit(solution)/shard_map/ppermute | solution.py:343
  14.1 6.4 %collective-permute-start.7 = (bf16[512,128]{1,0:T(8,128)(2,1)S(1)}, bf16[512,128]{1,0:T(8,128)(2,1)S(1)}, u32[]{:S(2)}, u32[]{:S(2)}) collective-permute-start(bf16[512,128]{1,0:T(8,128)(2,1)S(1)} %collective-permute-done.4.refs_9_), channel_id=1, source_target_pairs={{0,2},{4,0},{8,4},{12,8},{14,12},{10,14},{6,10},{2,6},{1,3},{5,1},... | collective-permute-start | bytes 393224 | tf_op jit(solution)/shard_map/ppermute | solution.py:343
  14.6 5.9 %collective-permute-start.6 = (bf16[512,128]{1,0:T(8,128)(2,1)S(1)}, bf16[512,128]{1,0:T(8,128)(2,1)S(1)}, u32[]{:S(2)}, u32[]{:S(2)}) collective-permute-start(bf16[512,128]{1,0:T(8,128)(2,1)S(1)} %collective-permute-done.3.refs_2_), channel_id=1, source_target_pairs={{0,4},{4,8},{8,12},{12,14},{14,10},{10,6},{6,2},{2,0},{1,5},{5,9},... | collective-permute-start | bytes 393224 | tf_op jit(solution)/shard_map/ppermute | solution.py:343
  16.1 6.2 %collective-permute-start.11 = (bf16[512,128]{1,0:T(8,128)(2,1)S(1)}, bf16[512,128]{1,0:T(8,128)(2,1)S(1)}, u32[]{:S(2)}, u32[]{:S(2)}) collective-permute-start(bf16[512,128]{1,0:T(8,128)(2,1)S(1)} %collective-permute-done.10.refs_8_), channel_id=1, source_target_pairs={{0,4},{4,8},{8,12},{12,14},{14,10},{10,6},{6,2},{2,0},{1,5},{5,9},... | collective-permute-start | bytes 393224 | tf_op jit(solution)/shard_map/ppermute | solution.py:343
  17.6 5.0 %collective-permute-start.8 = (bf16[512,128]{1,0:T(8,128)(2,1)S(1)}, bf16[512,128]{1,0:T(8,128)(2,1)S(1)}, u32[]{:S(2)}, u32[]{:S(2)}) collective-permute-start(bf16[512,128]{1,0:T(8,128)(2,1)S(1)} %collective-permute-done.5.refs_3_), channel_id=1, source_target_pairs={{0,2},{4,0},{8,4},{12,8},{14,12},{10,14},{6,10},{2,6},{1,3},{5,1},... | collective-permute-start | bytes 393224 | tf_op jit(solution)/shard_map/ppermute | solution.py:343
  20.5 5.0 %collective-permute-start.13 = (bf16[512,128]{1,0:T(8,128)(2,1)S(1)}, bf16[512,128]{1,0:T(8,128)(2,1)S(1)}, u32[]{:S(2)}, u32[]{:S(2)}) collective-permute-start(bf16[512,128]{1,0:T(8,128)(2,1)S(1)} %fusion.1), channel_id=1, source_target_pairs={{0,1},{1,0},{4,6},{5,7},{8,10},{9,11},{12,4},{13,5},{14,12},{15,13... | collective-permute-start | bytes 393224 | tf_op jit(solution)/shard_map/ppermute | solution.py:355
  21.7 5.0 %collective-permute-start.12 = (bf16[512,128]{1,0:T(8,128)(2,1)S(1)}, bf16[512,128]{1,0:T(8,128)(2,1)S(1)}, u32[]{:S(2)}, u32[]{:S(2)}) collective-permute-start(bf16[512,128]{1,0:T(8,128)(2,1)S(1)} %collective-permute-done.6.refs_4_), channel_id=1, source_target_pairs={{0,1},{1,0},{4,8},{5,9},{8,12},{9,13},{12,14},{13,15},{14,10},{15,... | collective-permute-start | bytes 393224 | tf_op jit(solution)/shard_map/ppermute | solution.py:355

commit v23 on v21

--- a/solution.py
+++ b/solution.py
@@ -181,7 +181,7 @@
 
     def run(others, final):
         keys = (others + 1) * tokens
-        chunk = row_chunk(others + 1)
+        chunk = row_chunk(others + 1 if final else 0)
         output = Output(out_ref, out_hbm, sems, kv_dev, group)
 
         def keys_of(h):
@@ -278,7 +278,7 @@
         v_wide[...] = v_ref[...].astype(jnp.float32)
         k_ready = Once(lambda h: by_head(k_wide, h, kv_dev, tokens))
         v_ready = Once(lambda h: with_ones(by_head(v_wide, h, kv_dev, tokens)))
-        chunk = row_chunk(1)
+        chunk = row_chunk(0)
         jobs = chunks_of(kv_dev, rows_all, chunk)
         output = Output(out_ref, out_hbm, sems, kv_dev, group)
         shifts = []
@@ -349,7 +349,7 @@
     return code
 
 
-LAST_KEYS = {1: 2, 2: 3, 3: 4, 4: 5, 5: 6, 6: 1}, {}
+LAST_KEYS = {1: 2, 2: 3, 3: 4, 4: 5, 5: 1}, {}
 LAST_VALUES = {1: 6, 2: 5, 3: 1, 4: 3, 5: 2, 6: 4}, {2: 0, 4: 4, 5: 1, 6: 3}
 
 

time: 29 us -> 28.9 us (level)
  the two profiles are of different devices: /device:TPU:20 before, /device:TPU:0 now
where the time goes in v23:
time: 28.9 us; the launch traced here: 28.4 us
  starting transfers between devices  13.8 us (48%)
  waiting for transfers between devices  10.4 us (36%)
  Pallas kernels  3.95 us (14%)
    ppermute x12, starting transfers between devices, send(): lax.ppermute(x, 'seq', [(ring[p], ring[(p + turn) % members]) for p in ra...  13.2 us
    ppermute x12, waiting for transfers between devices, send(): lax.ppermute(x, 'seq', [(ring[p], ring[(p + turn) % members]) for p in ra...  10.4 us
    pallas_call x1, Pallas kernels, attend(): pl.pallas_call(functools.partial(attend_kernel, codes=codes, code=code, l...  2.19 us
    pallas_call x1, Pallas kernels, prepare(): pl.pallas_call(functools.partial(prepare_kernel, kv_dev=kv_dev), out_shap...  1.58 us
  transfers between devices with their start and end apart: 14, of which 8 were waited for; matrix products, arithmetic and copies ran while one was open for 0% of the time, Pallas kernels for 13%

profile of v23, /device:TPU:0, one launch (start us, length us, event | category | flops | bytes accessed | tf_op | source)
XLA Modules:
  0.0 28.4 jit_solution(8940600631806019340)
XLA Ops:
  0.0 3.0 %collective-permute-start = (bf16[512,128]{1,0:T(8,128)(2,1)}, bf16[512,128]{1,0:T(8,128)(2,1)S(1)}, u32[]{:S(2)}, u32[]{:S(2)}) collective-permute-start(bf16[512,128]{1,0:T(8,128)(2,1)} %bitcast.6), channel_id=1, source_target_pairs={{0,4},{4,8},{8,12},{12,14},{14,10},{10,6},{6,2},{2,0},{1,5},{5,9},... | collective-permute-start | bytes 393224 | tf_op jit(solution)/shard_map/ppermute | solution.py:362
  3.0 0.0 collective-permute-start.1
  3.0 1.6 %prepare.1 = (s32[4,8]{1,0:T(4,128)S(1)}, bf16[4,1024,128]{2,1,0:T(8,128)(2,1)S(1)}, bf16[4,128,128]{2,1,0:T(8,128)(2,1)S(1)}, bf16[4,128,128]{2,1,0:T(8,128)(2,1)S(1)}) custom-call(s32[4,8]{1,0:T(4,128)} %bitcast.9, bf16[128,32,128]{2,1,0:T(8,128)(2,1)} %q_hbm.1, bf16[512,128]{1,0:T(8,128)(2,1)} %bitcast.7, bf16[512,128]{1,0:T(8,128)(2,1)} %bitcast.4), custom_call_target="tpu_custom_call" | custom-call | tf_op jit(solution)/shard_map/prepare/pallas_call | solution.py:54
  4.6 2.1 %collective-permute-start.2 = (bf16[512,128]{1,0:T(8,128)(2,1)}, bf16[512,128]{1,0:T(8,128)(2,1)S(1)}, u32[]{:S(2)}, u32[]{:S(2)}) collective-permute-start(bf16[512,128]{1,0:T(8,128)(2,1)} %bitcast.5), channel_id=1, source_target_pairs={{0,4},{4,8},{8,12},{12,14},{14,10},{10,6},{6,2},{2,0},{1,5},{5,9},... | collective-permute-start | bytes 393224 | tf_op jit(solution)/shard_map/ppermute | solution.py:362
  6.7 0.0 collective-permute-start.3
  6.7 0.0 collective-permute-done.refs_0_
  6.7 1.5 %collective-permute-done.1.refs_7_ = bf16[512,128]{1,0:T(8,128)(2,1)S(1)} collective-permute-done((bf16[512,128]{1,0:T(8,128)(2,1)}, bf16[512,128]{1,0:T(8,128)(2,1)S(1)}, u32[]{:S(2)}, u32[]{:S(2)}) %collective-permute-start.1) | collective-permute-done | bytes 131104 | tf_op jit(solution)/shard_map/ppermute | solution.py:362
  8.2 0.4 %collective-permute-start.5 = (bf16[512,128]{1,0:T(8,128)(2,1)S(1)}, bf16[512,128]{1,0:T(8,128)(2,1)S(1)}, u32[]{:S(2)}, u32[]{:S(2)}) collective-permute-start(bf16[512,128]{1,0:T(8,128)(2,1)S(1)} %collective-permute-done.1.refs_7_), channel_id=1, source_target_pairs={{0,2},{4,0},{8,4},{12,8},{14,12},{10,14},{6,10},{2,6},{1,3},{5,1},... | collective-permute-start | bytes 393224 | tf_op jit(solution)/shard_map/ppermute | solution.py:362
  8.6 1.6 %collective-permute-start.4 = (bf16[512,128]{1,0:T(8,128)(2,1)S(1)}, bf16[512,128]{1,0:T(8,128)(2,1)S(1)}, u32[]{:S(2)}, u32[]{:S(2)}) collective-permute-start(bf16[512,128]{1,0:T(8,128)(2,1)S(1)} %collective-permute-done.refs_0_), channel_id=1, source_target_pairs={{0,4},{4,8},{8,12},{12,14},{14,10},{10,6},{6,2},{2,0},{1,5},{5,9},... | collective-permute-start | bytes 393224 | tf_op jit(solution)/shard_map/ppermute | solution.py:362
  10.2 0.1 collective-permute-done.2.refs_6_
  10.3 2.4 %collective-permute-done.3.refs_1_ = bf16[512,128]{1,0:T(8,128)(2,1)S(1)} collective-permute-done((bf16[512,128]{1,0:T(8,128)(2,1)}, bf16[512,128]{1,0:T(8,128)(2,1)S(1)}, u32[]{:S(2)}, u32[]{:S(2)}) %collective-permute-start.3) | collective-permute-done | bytes 131104 | tf_op jit(solution)/shard_map/ppermute | solution.py:362
  12.7 1.6 %collective-permute-start.6 = (bf16[512,128]{1,0:T(8,128)(2,1)S(1)}, bf16[512,128]{1,0:T(8,128)(2,1)S(1)}, u32[]{:S(2)}, u32[]{:S(2)}) collective-permute-start(bf16[512,128]{1,0:T(8,128)(2,1)S(1)} %collective-permute-done.2.refs_6_), channel_id=1, source_target_pairs={{0,4},{4,8},{8,12},{12,14},{14,10},{10,6},{6,2},{2,0},{1,5},{5,9},... | collective-permute-start | bytes 393224 | tf_op jit(solution)/shard_map/ppermute | solution.py:362
  14.3 0.4 %collective-permute-start.7 = (bf16[512,128]{1,0:T(8,128)(2,1)S(1)}, bf16[512,128]{1,0:T(8,128)(2,1)S(1)}, u32[]{:S(2)}, u32[]{:S(2)}) collective-permute-start(bf16[512,128]{1,0:T(8,128)(2,1)S(1)} %collective-permute-done.3.refs_1_), channel_id=1, source_target_pairs={{0,2},{4,0},{8,4},{12,8},{14,12},{10,14},{6,10},{2,6},{1,3},{5,1},... | collective-permute-start | bytes 393224 | tf_op jit(solution)/shard_map/ppermute | solution.py:362
  14.7 0.0 collective-permute-done.5.refs_9_
  14.7 0.0 collective-permute-done.4.refs_2_
  14.7 1.3 %collective-permute-start.9 = (bf16[512,128]{1,0:T(8,128)(2,1)S(1)}, bf16[512,128]{1,0:T(8,128)(2,1)S(1)}, u32[]{:S(2)}, u32[]{:S(2)}) collective-permute-start(bf16[512,128]{1,0:T(8,128)(2,1)S(1)} %collective-permute-done.5.refs_9_), channel_id=1, source_target_pairs={{0,2},{4,0},{8,4},{12,8},{14,12},{10,14},{6,10},{2,6},{1,3},{5,1},... | collective-permute-start | bytes 393224 | tf_op jit(solution)/shard_map/ppermute | solution.py:362
  16.0 0.8 %collective-permute-start.8 = (bf16[512,128]{1,0:T(8,128)(2,1)S(1)}, bf16[512,128]{1,0:T(8,128)(2,1)S(1)}, u32[]{:S(2)}, u32[]{:S(2)}) collective-permute-start(bf16[512,128]{1,0:T(8,128)(2,1)S(1)} %collective-permute-done.4.refs_2_), channel_id=1, source_target_pairs={{0,4},{4,8},{8,12},{12,14},{14,10},{10,6},{6,2},{2,0},{1,5},{5,9},... | collective-permute-start | bytes 393224 | tf_op jit(solution)/shard_map/ppermute | solution.py:362
  16.8 2.1 %collective-permute-done.6.refs_8_ = bf16[512,128]{1,0:T(8,128)(2,1)S(1)} collective-permute-done((bf16[512,128]{1,0:T(8,128)(2,1)S(1)}, bf16[512,128]{1,0:T(8,128)(2,1)S(1)}, u32[]{:S(2)}, u32[]{:S(2)}) %collective-permute-start.6) | collective-permute-done | bytes 131104 | tf_op jit(solution)/shard_map/ppermute | solution.py:362
  18.9 0.4 %collective-permute-done.7.refs_3_ = bf16[512,128]{1,0:T(8,128)(2,1)S(1)} collective-permute-done((bf16[512,128]{1,0:T(8,128)(2,1)S(1)}, bf16[512,128]{1,0:T(8,128)(2,1)S(1)}, u32[]{:S(2)}, u32[]{:S(2)}) %collective-permute-start.7) | collective-permute-done | bytes 131104 | tf_op jit(solution)/shard_map/ppermute | solution.py:362
  19.3 1.6 %collective-permute-start.10 = (bf16[512,128]{1,0:T(8,128)(2,1)S(1)}, bf16[512,128]{1,0:T(8,128)(2,1)S(1)}, u32[]{:S(2)}, u32[]{:S(2)}) collective-permute-start(bf16[512,128]{1,0:T(8,128)(2,1)S(1)} %collective-permute-done.6.refs_8_), channel_id=1, source_target_pairs={{0,4},{4,8},{8,12},{12,14},{14,10},{10,6},{6,2},{2,0},{1,5},{5,9},... | collective-permute-start | bytes 393224 | tf_op jit(solution)/shard_map/ppermute | solution.py:362
  20.8 0.4 %collective-permute-start.11 = (bf16[512,128]{1,0:T(8,128)(2,1)S(1)}, bf16[512,128]{1,0:T(8,128)(2,1)S(1)}, u32[]{:S(2)}, u32[]{:S(2)}) collective-permute-start(bf16[512,128]{1,0:T(8,128)(2,1)S(1)} %collective-permute-done.7.refs_3_), channel_id=1, source_target_pairs={{0,2},{4,0},{8,4},{12,8},{14,12},{10,14},{6,10},{2,6},{1,3},{5,1},... | collective-permute-start | bytes 393224 | tf_op jit(solution)/shard_map/ppermute | solution.py:362
  21.3 0.8 %collective-permute-done.9.refs_11_ = bf16[512,128]{1,0:T(8,128)(2,1)S(1)} collective-permute-done((bf16[512,128]{1,0:T(8,128)(2,1)S(1)}, bf16[512,128]{1,0:T(8,128)(2,1)S(1)}, u32[]{:S(2)}, u32[]{:S(2)}) %collective-permute-start.9) | collective-permute-done | bytes 131104 | tf_op jit(solution)/shard_map/ppermute | solution.py:362
  22.0 0.0 collective-permute-done.8.refs_4_
  22.1 0.1 collective-permute-start.13
  22.1 0.5 %collective-permute-start.12 = (bf16[512,128]{1,0:T(8,128)(2,1)S(1)}, bf16[512,128]{1,0:T(8,128)(2,1)S(1)}, u32[]{:S(2)}, u32[]{:S(2)}) collective-permute-start(bf16[512,128]{1,0:T(8,128)(2,1)S(1)} %collective-permute-done.8.refs_4_), channel_id=1, source_target_pairs={{0,1},{1,0},{4,8},{5,9},{8,12},{9,13},{12,14},{13,15},{14,10},{15,... | collective-permute-start | bytes 393224 | tf_op jit(solution)/shard_map/ppermute | solution.py:374
  22.6 1.6 %collective-permute-done.10.refs_10_ = bf16[512,128]{1,0:T(8,128)(2,1)S(1)} collective-permute-done((bf16[512,128]{1,0:T(8,128)(2,1)S(1)}, bf16[512,128]{1,0:T(8,128)(2,1)S(1)}, u32[]{:S(2)}, u32[]{:S(2)}) %collective-permute-start.10) | collective-permute-done | bytes 131104 | tf_op jit(solution)/shard_map/ppermute | solution.py:362
  24.2 1.6 %collective-permute-done.11.refs_5_ = bf16[512,128]{1,0:T(8,128)(2,1)S(1)} collective-permute-done((bf16[512,128]{1,0:T(8,128)(2,1)S(1)}, bf16[512,128]{1,0:T(8,128)(2,1)S(1)}, u32[]{:S(2)}, u32[]{:S(2)}) %collective-permute-start.11) | collective-permute-done | bytes 131104 | tf_op jit(solution)/shard_map/ppermute | solution.py:362
  25.8 2.2 %attend.1 = (bf16[128,32,128]{2,1,0:T(8,128)(2,1)}, f32[4,1024,128]{2,1,0:T(8,128)S(1)}, f32[4,1024,256]{2,1,0:T(8,128)S(1)}) custom-call(s32[4,8]{1,0:T(4,128)S(1)} %get-tuple-element.34.lists_ref, bf16[4,1024,128]{2,1,0:T(8,128)(2,1)S(1)} %get-tuple-element.35.q_ref, bf16[4,128,128]{2,1,0:T(8,128)(2,1)S(1)} %get-tuple-element.36.k_own_ref, ...), custom_call_target="tpu_custom_call" | custom-call | tf_op jit(solution)/shard_map/attend/pallas_call | solution.py:251
  28.0 0.0 collective-permute-done.13.v_ref
  28.0 0.0 collective-permute-done.12.k_ref
  28.0 0.2 attend_last.1
  (1 shorter events, 0.0 us)
Async XLA Ops:
  0.0 6.7 %collective-permute-start = (bf16[512,128]{1,0:T(8,128)(2,1)}, bf16[512,128]{1,0:T(8,128)(2,1)S(1)}, u32[]{:S(2)}, u32[]{:S(2)}) collective-permute-start(bf16[512,128]{1,0:T(8,128)(2,1)} %bitcast.6), channel_id=1, source_target_pairs={{0,4},{4,8},{8,12},{12,14},{14,10},{10,6},{6,2},{2,0},{1,5},{5,9},... | collective-permute-start | bytes 393224 | tf_op jit(solution)/shard_map/ppermute | solution.py:362
  3.0 5.2 %collective-permute-start.1 = (bf16[512,128]{1,0:T(8,128)(2,1)}, bf16[512,128]{1,0:T(8,128)(2,1)S(1)}, u32[]{:S(2)}, u32[]{:S(2)}) collective-permute-start(bf16[512,128]{1,0:T(8,128)(2,1)} %bitcast.3), channel_id=1, source_target_pairs={{0,2},{4,0},{8,4},{12,8},{14,12},{10,14},{6,10},{2,6},{1,3},{5,1},... | collective-permute-start | bytes 393224 | tf_op jit(solution)/shard_map/ppermute | solution.py:362
  4.6 5.7 %collective-permute-start.2 = (bf16[512,128]{1,0:T(8,128)(2,1)}, bf16[512,128]{1,0:T(8,128)(2,1)S(1)}, u32[]{:S(2)}, u32[]{:S(2)}) collective-permute-start(bf16[512,128]{1,0:T(8,128)(2,1)} %bitcast.5), channel_id=1, source_target_pairs={{0,4},{4,8},{8,12},{12,14},{14,10},{10,6},{6,2},{2,0},{1,5},{5,9},... | collective-permute-start | bytes 393224 | tf_op jit(solution)/shard_map/ppermute | solution.py:362
  6.7 6.0 %collective-permute-start.3 = (bf16[512,128]{1,0:T(8,128)(2,1)}, bf16[512,128]{1,0:T(8,128)(2,1)S(1)}, u32[]{:S(2)}, u32[]{:S(2)}) collective-permute-start(bf16[512,128]{1,0:T(8,128)(2,1)} %bitcast.8), channel_id=1, source_target_pairs={{0,2},{4,0},{8,4},{12,8},{14,12},{10,14},{6,10},{2,6},{1,3},{5,1},... | collective-permute-start | bytes 393224 | tf_op jit(solution)/shard_map/ppermute | solution.py:362
  8.2 6.5 %collective-permute-start.5 = (bf16[512,128]{1,0:T(8,128)(2,1)S(1)}, bf16[512,128]{1,0:T(8,128)(2,1)S(1)}, u32[]{:S(2)}, u32[]{:S(2)}) collective-permute-start(bf16[512,128]{1,0:T(8,128)(2,1)S(1)} %collective-permute-done.1.refs_7_), channel_id=1, source_target_pairs={{0,2},{4,0},{8,4},{12,8},{14,12},{10,14},{6,10},{2,6},{1,3},{5,1},... | collective-permute-start | bytes 393224 | tf_op jit(solution)/shard_map/ppermute | solution.py:362
  8.6 6.1 %collective-permute-start.4 = (bf16[512,128]{1,0:T(8,128)(2,1)S(1)}, bf16[512,128]{1,0:T(8,128)(2,1)S(1)}, u32[]{:S(2)}, u32[]{:S(2)}) collective-permute-start(bf16[512,128]{1,0:T(8,128)(2,1)S(1)} %collective-permute-done.refs_0_), channel_id=1, source_target_pairs={{0,4},{4,8},{8,12},{12,14},{14,10},{10,6},{6,2},{2,0},{1,5},{5,9},... | collective-permute-start | bytes 393224 | tf_op jit(solution)/shard_map/ppermute | solution.py:362
  12.7 6.2 %collective-permute-start.6 = (bf16[512,128]{1,0:T(8,128)(2,1)S(1)}, bf16[512,128]{1,0:T(8,128)(2,1)S(1)}, u32[]{:S(2)}, u32[]{:S(2)}) collective-permute-start(bf16[512,128]{1,0:T(8,128)(2,1)S(1)} %collective-permute-done.2.refs_6_), channel_id=1, source_target_pairs={{0,4},{4,8},{8,12},{12,14},{14,10},{10,6},{6,2},{2,0},{1,5},{5,9},... | collective-permute-start | bytes 393224 | tf_op jit(solution)/shard_map/ppermute | solution.py:362
  14.3 5.0 %collective-permute-start.7 = (bf16[512,128]{1,0:T(8,128)(2,1)S(1)}, bf16[512,128]{1,0:T(8,128)(2,1)S(1)}, u32[]{:S(2)}, u32[]{:S(2)}) collective-permute-start(bf16[512,128]{1,0:T(8,128)(2,1)S(1)} %collective-permute-done.3.refs_1_), channel_id=1, source_target_pairs={{0,2},{4,0},{8,4},{12,8},{14,12},{10,14},{6,10},{2,6},{1,3},{5,1},... | collective-permute-start | bytes 393224 | tf_op jit(solution)/shard_map/ppermute | solution.py:362
  14.7 7.3 %collective-permute-start.9 = (bf16[512,128]{1,0:T(8,128)(2,1)S(1)}, bf16[512,128]{1,0:T(8,128)(2,1)S(1)}, u32[]{:S(2)}, u32[]{:S(2)}) collective-permute-start(bf16[512,128]{1,0:T(8,128)(2,1)S(1)} %collective-permute-done.5.refs_9_), channel_id=1, source_target_pairs={{0,2},{4,0},{8,4},{12,8},{14,12},{10,14},{6,10},{2,6},{1,3},{5,1},... | collective-permute-start | bytes 393224 | tf_op jit(solution)/shard_map/ppermute | solution.py:362
  16.0 6.0 %collective-permute-start.8 = (bf16[512,128]{1,0:T(8,128)(2,1)S(1)}, bf16[512,128]{1,0:T(8,128)(2,1)S(1)}, u32[]{:S(2)}, u32[]{:S(2)}) collective-permute-start(bf16[512,128]{1,0:T(8,128)(2,1)S(1)} %collective-permute-done.4.refs_2_), channel_id=1, source_target_pairs={{0,4},{4,8},{8,12},{12,14},{14,10},{10,6},{6,2},{2,0},{1,5},{5,9},... | collective-permute-start | bytes 393224 | tf_op jit(solution)/shard_map/ppermute | solution.py:362
  19.3 5.0 %collective-permute-start.10 = (bf16[512,128]{1,0:T(8,128)(2,1)S(1)}, bf16[512,128]{1,0:T(8,128)(2,1)S(1)}, u32[]{:S(2)}, u32[]{:S(2)}) collective-permute-start(bf16[512,128]{1,0:T(8,128)(2,1)S(1)} %collective-permute-done.6.refs_8_), channel_id=1, source_target_pairs={{0,4},{4,8},{8,12},{12,14},{14,10},{10,6},{6,2},{2,0},{1,5},{5,9},... | collective-permute-start | bytes 393224 | tf_op jit(solution)/shard_map/ppermute | solution.py:362
  20.8 5.0 %collective-permute-start.11 = (bf16[512,128]{1,0:T(8,128)(2,1)S(1)}, bf16[512,128]{1,0:T(8,128)(2,1)S(1)}, u32[]{:S(2)}, u32[]{:S(2)}) collective-permute-start(bf16[512,128]{1,0:T(8,128)(2,1)S(1)} %collective-permute-done.7.refs_3_), channel_id=1, source_target_pairs={{0,2},{4,0},{8,4},{12,8},{14,12},{10,14},{6,10},{2,6},{1,3},{5,1},... | collective-permute-start | bytes 393224 | tf_op jit(solution)/shard_map/ppermute | solution.py:362
  22.1 5.9 %collective-permute-start.13 = (bf16[512,128]{1,0:T(8,128)(2,1)S(1)}, bf16[512,128]{1,0:T(8,128)(2,1)S(1)}, u32[]{:S(2)}, u32[]{:S(2)}) collective-permute-start(bf16[512,128]{1,0:T(8,128)(2,1)S(1)} %fusion.1), channel_id=1, source_target_pairs={{0,1},{1,0},{4,6},{5,7},{8,10},{9,11},{12,4},{13,5},{14,12},{15,13... | collective-permute-start | bytes 393224 | tf_op jit(solution)/shard_map/ppermute | solution.py:374
  22.1 5.9 %collective-permute-start.12 = (bf16[512,128]{1,0:T(8,128)(2,1)S(1)}, bf16[512,128]{1,0:T(8,128)(2,1)S(1)}, u32[]{:S(2)}, u32[]{:S(2)}) collective-permute-start(bf16[512,128]{1,0:T(8,128)(2,1)S(1)} %collective-permute-done.8.refs_4_), channel_id=1, source_target_pairs={{0,1},{1,0},{4,8},{5,9},{8,12},{9,13},{12,14},{13,15},{14,10},{15,... | collective-permute-start | bytes 393224 | tf_op jit(solution)/shard_map/ppermute | solution.py:374

commit v24 on v23

--- a/solution.py
+++ b/solution.py
@@ -381,7 +381,8 @@
             k_two[1], v_two[0], ready = lax.optimization_barrier((k_two[1], v_two[0], ready))
         behind = send(v_two[0], 1), send(k_two[1], -1)
         ahead = lax.optimization_barrier(ahead)
-        behind = lax.optimization_barrier(behind)
+        if distance < half - 2:
+            behind = lax.optimization_barrier(behind)
         k_two, v_two = [ahead[0], behind[1]], [behind[0], ahead[1]]
         k_all += k_two
         v_all += v_two

time: 28.9 us -> 28.8 us (level)
  the two profiles are of different devices: /device:TPU:0 before, /device:TPU:16 now
where the time goes in v24:
time: 28.8 us; the launch traced here: 28.7 us
  starting transfers between devices  14.4 us (50%)
  waiting for transfers between devices  7.35 us (26%)
  Pallas kernels  6.69 us (23%)
    ppermute x12, starting transfers between devices, send(): lax.ppermute(x, 'seq', [(ring[p], ring[(p + turn) % members]) for p in ra...  12.5 us
    ppermute x12, waiting for transfers between devices, send(): lax.ppermute(x, 'seq', [(ring[p], ring[(p + turn) % members]) for p in ra...  7.35 us
    pallas_call x1, Pallas kernels, attend(): pl.pallas_call(functools.partial(attend_kernel, codes=codes, code=code, l...  2.92 us
    pallas_call x1, Pallas kernels, attend_last(): pl.pallas_call(functools.partial(last_kernel, code=code, last=last), out_...  2.18 us
    ppermute x2, starting transfers between devices, send_last(): return lax.ppermute(x, ('seq', 'head'), pairs)  1.9 us
    pallas_call x1, Pallas kernels, prepare(): pl.pallas_call(functools.partial(prepare_kernel, kv_dev=kv_dev), out_shap...  1.58 us
  transfers between devices with their start and end apart: 14, of which 7 were waited for; matrix products, arithmetic and copies ran while one was open for 0% of the time, Pallas kernels for 16%

profile of v24, /device:TPU:16, one launch (start us, length us, event | category | flops | bytes accessed | tf_op | source)
XLA Modules:
  0.0 28.7 jit_solution(1249411300712438618)
XLA Ops:
  0.0 1.6 %collective-permute-start = (bf16[512,128]{1,0:T(8,128)(2,1)}, bf16[512,128]{1,0:T(8,128)(2,1)S(1)}, u32[]{:S(2)}, u32[]{:S(2)}) collective-permute-start(bf16[512,128]{1,0:T(8,128)(2,1)} %bitcast.6), channel_id=1, source_target_pairs={{0,4},{4,8},{8,12},{12,14},{14,10},{10,6},{6,2},{2,0},{1,5},{5,9},... | collective-permute-start | bytes 393224 | tf_op jit(solution)/shard_map/ppermute | solution.py:362
  1.6 0.4 %collective-permute-start.1 = (bf16[512,128]{1,0:T(8,128)(2,1)}, bf16[512,128]{1,0:T(8,128)(2,1)S(1)}, u32[]{:S(2)}, u32[]{:S(2)}) collective-permute-start(bf16[512,128]{1,0:T(8,128)(2,1)} %bitcast.3), channel_id=1, source_target_pairs={{0,2},{4,0},{8,4},{12,8},{14,12},{10,14},{6,10},{2,6},{1,3},{5,1},... | collective-permute-start | bytes 393224 | tf_op jit(solution)/shard_map/ppermute | solution.py:362
  2.0 1.6 %prepare.1 = (s32[4,8]{1,0:T(4,128)S(1)}, bf16[4,1024,128]{2,1,0:T(8,128)(2,1)S(1)}, bf16[4,128,128]{2,1,0:T(8,128)(2,1)S(1)}, bf16[4,128,128]{2,1,0:T(8,128)(2,1)S(1)}) custom-call(s32[4,8]{1,0:T(4,128)} %bitcast.9, bf16[128,32,128]{2,1,0:T(8,128)(2,1)} %q_hbm.1, bf16[512,128]{1,0:T(8,128)(2,1)} %bitcast.7, bf16[512,128]{1,0:T(8,128)(2,1)} %bitcast.4), custom_call_target="tpu_custom_call" | custom-call | tf_op jit(solution)/shard_map/prepare/pallas_call | solution.py:54
  3.6 1.6 %collective-permute-start.2 = (bf16[512,128]{1,0:T(8,128)(2,1)}, bf16[512,128]{1,0:T(8,128)(2,1)S(1)}, u32[]{:S(2)}, u32[]{:S(2)}) collective-permute-start(bf16[512,128]{1,0:T(8,128)(2,1)} %bitcast.5), channel_id=1, source_target_pairs={{0,4},{4,8},{8,12},{12,14},{14,10},{10,6},{6,2},{2,0},{1,5},{5,9},... | collective-permute-start | bytes 393224 | tf_op jit(solution)/shard_map/ppermute | solution.py:362
  5.2 0.4 %collective-permute-start.3 = (bf16[512,128]{1,0:T(8,128)(2,1)}, bf16[512,128]{1,0:T(8,128)(2,1)S(1)}, u32[]{:S(2)}, u32[]{:S(2)}) collective-permute-start(bf16[512,128]{1,0:T(8,128)(2,1)} %bitcast.8), channel_id=1, source_target_pairs={{0,2},{4,0},{8,4},{12,8},{14,12},{10,14},{6,10},{2,6},{1,3},{5,1},... | collective-permute-start | bytes 393224 | tf_op jit(solution)/shard_map/ppermute | solution.py:362
  5.7 0.0 collective-permute-done.refs_0_
  5.7 1.1 %collective-permute-done.1.refs_7_ = bf16[512,128]{1,0:T(8,128)(2,1)S(1)} collective-permute-done((bf16[512,128]{1,0:T(8,128)(2,1)}, bf16[512,128]{1,0:T(8,128)(2,1)S(1)}, u32[]{:S(2)}, u32[]{:S(2)}) %collective-permute-start.1) | collective-permute-done | bytes 131104 | tf_op jit(solution)/shard_map/ppermute | solution.py:362
  6.8 0.4 %collective-permute-start.5 = (bf16[512,128]{1,0:T(8,128)(2,1)S(1)}, bf16[512,128]{1,0:T(8,128)(2,1)S(1)}, u32[]{:S(2)}, u32[]{:S(2)}) collective-permute-start(bf16[512,128]{1,0:T(8,128)(2,1)S(1)} %collective-permute-done.1.refs_7_), channel_id=1, source_target_pairs={{0,2},{4,0},{8,4},{12,8},{14,12},{10,14},{6,10},{2,6},{1,3},{5,1},... | collective-permute-start | bytes 393224 | tf_op jit(solution)/shard_map/ppermute | solution.py:362
  7.2 1.6 %collective-permute-start.4 = (bf16[512,128]{1,0:T(8,128)(2,1)S(1)}, bf16[512,128]{1,0:T(8,128)(2,1)S(1)}, u32[]{:S(2)}, u32[]{:S(2)}) collective-permute-start(bf16[512,128]{1,0:T(8,128)(2,1)S(1)} %collective-permute-done.refs_0_), channel_id=1, source_target_pairs={{0,4},{4,8},{8,12},{12,14},{14,10},{10,6},{6,2},{2,0},{1,5},{5,9},... | collective-permute-start | bytes 393224 | tf_op jit(solution)/shard_map/ppermute | solution.py:362
  8.8 0.7 %collective-permute-done.2.refs_6_ = bf16[512,128]{1,0:T(8,128)(2,1)S(1)} collective-permute-done((bf16[512,128]{1,0:T(8,128)(2,1)}, bf16[512,128]{1,0:T(8,128)(2,1)S(1)}, u32[]{:S(2)}, u32[]{:S(2)}) %collective-permute-start.2) | collective-permute-done | bytes 131104 | tf_op jit(solution)/shard_map/ppermute | solution.py:362
  9.5 1.8 %collective-permute-done.3.refs_1_ = bf16[512,128]{1,0:T(8,128)(2,1)S(1)} collective-permute-done((bf16[512,128]{1,0:T(8,128)(2,1)}, bf16[512,128]{1,0:T(8,128)(2,1)S(1)}, u32[]{:S(2)}, u32[]{:S(2)}) %collective-permute-start.3) | collective-permute-done | bytes 131104 | tf_op jit(solution)/shard_map/ppermute | solution.py:362
  11.3 1.5 %collective-permute-start.10 = (bf16[512,128]{1,0:T(8,128)(2,1)S(1)}, bf16[512,128]{1,0:T(8,128)(2,1)S(1)}, u32[]{:S(2)}, u32[]{:S(2)}) collective-permute-start(bf16[512,128]{1,0:T(8,128)(2,1)S(1)} %collective-permute-done.2.refs_6_), channel_id=1, source_target_pairs={{0,4},{4,8},{8,12},{12,14},{14,10},{10,6},{6,2},{2,0},{1,5},{5,9},... | collective-permute-start | bytes 393224 | tf_op jit(solution)/shard_map/ppermute | solution.py:362
  12.8 0.5 %collective-permute-start.6 = (bf16[512,128]{1,0:T(8,128)(2,1)S(1)}, bf16[512,128]{1,0:T(8,128)(2,1)S(1)}, u32[]{:S(2)}, u32[]{:S(2)}) collective-permute-start(bf16[512,128]{1,0:T(8,128)(2,1)S(1)} %collective-permute-done.3.refs_1_), channel_id=1, source_target_pairs={{0,2},{4,0},{8,4},{12,8},{14,12},{10,14},{6,10},{2,6},{1,3},{5,1},... | collective-permute-start | bytes 393224 | tf_op jit(solution)/shard_map/ppermute | solution.py:362
  13.3 0.0 collective-permute-done.5.refs_9_
  13.3 0.0 collective-permute-done.4.refs_2_
  13.3 0.5 %collective-permute-start.8 = (bf16[512,128]{1,0:T(8,128)(2,1)S(1)}, bf16[512,128]{1,0:T(8,128)(2,1)S(1)}, u32[]{:S(2)}, u32[]{:S(2)}) collective-permute-start(bf16[512,128]{1,0:T(8,128)(2,1)S(1)} %collective-permute-done.5.refs_9_), channel_id=1, source_target_pairs={{0,2},{4,0},{8,4},{12,8},{14,12},{10,14},{6,10},{2,6},{1,3},{5,1},... | collective-permute-start | bytes 393224 | tf_op jit(solution)/shard_map/ppermute | solution.py:362
  13.7 1.9 %collective-permute-start.7 = (bf16[512,128]{1,0:T(8,128)(2,1)S(1)}, bf16[512,128]{1,0:T(8,128)(2,1)S(1)}, u32[]{:S(2)}, u32[]{:S(2)}) collective-permute-start(bf16[512,128]{1,0:T(8,128)(2,1)S(1)} %collective-permute-done.4.refs_2_), channel_id=1, source_target_pairs={{0,4},{4,8},{8,12},{12,14},{14,10},{10,6},{6,2},{2,0},{1,5},{5,9},... | collective-permute-start | bytes 393224 | tf_op jit(solution)/shard_map/ppermute | solution.py:362
  15.6 1.2 %collective-permute-done.10.refs_8_ = bf16[512,128]{1,0:T(8,128)(2,1)S(1)} collective-permute-done((bf16[512,128]{1,0:T(8,128)(2,1)S(1)}, bf16[512,128]{1,0:T(8,128)(2,1)S(1)}, u32[]{:S(2)}, u32[]{:S(2)}) %collective-permute-start.10) | collective-permute-done | bytes 131104 | tf_op jit(solution)/shard_map/ppermute | solution.py:362
  16.8 1.2 %collective-permute-start.11 = (bf16[512,128]{1,0:T(8,128)(2,1)S(1)}, bf16[512,128]{1,0:T(8,128)(2,1)S(1)}, u32[]{:S(2)}, u32[]{:S(2)}) collective-permute-start(bf16[512,128]{1,0:T(8,128)(2,1)S(1)} %collective-permute-done.10.refs_8_), channel_id=1, source_target_pairs={{0,4},{4,8},{8,12},{12,14},{14,10},{10,6},{6,2},{2,0},{1,5},{5,9},... | collective-permute-start | bytes 393224 | tf_op jit(solution)/shard_map/ppermute | solution.py:362
  18.0 0.0 collective-permute-done.6.refs_3_
  18.0 0.8 %collective-permute-start.9 = (bf16[512,128]{1,0:T(8,128)(2,1)S(1)}, bf16[512,128]{1,0:T(8,128)(2,1)S(1)}, u32[]{:S(2)}, u32[]{:S(2)}) collective-permute-start(bf16[512,128]{1,0:T(8,128)(2,1)S(1)} %collective-permute-done.6.refs_3_), channel_id=1, source_target_pairs={{0,2},{4,0},{8,4},{12,8},{14,12},{10,14},{6,10},{2,6},{1,3},{5,1},... | collective-permute-start | bytes 393224 | tf_op jit(solution)/shard_map/ppermute | solution.py:362
  18.8 1.9 %collective-permute-done.8.refs_11_ = bf16[512,128]{1,0:T(8,128)(2,1)S(1)} collective-permute-done((bf16[512,128]{1,0:T(8,128)(2,1)S(1)}, bf16[512,128]{1,0:T(8,128)(2,1)S(1)}, u32[]{:S(2)}, u32[]{:S(2)}) %collective-permute-start.8) | collective-permute-done | bytes 131104 | tf_op jit(solution)/shard_map/ppermute | solution.py:362
  20.7 0.0 collective-permute-done.7.refs_4_
  20.7 0.5 %collective-permute-start.13 = (bf16[512,128]{1,0:T(8,128)(2,1)S(1)}, bf16[512,128]{1,0:T(8,128)(2,1)S(1)}, u32[]{:S(2)}, u32[]{:S(2)}) collective-permute-start(bf16[512,128]{1,0:T(8,128)(2,1)S(1)} %fusion.1), channel_id=1, source_target_pairs={{0,1},{1,0},{4,6},{5,7},{8,10},{9,11},{12,4},{13,5},{14,12},{15,13... | collective-permute-start | bytes 393224 | tf_op jit(solution)/shard_map/ppermute | solution.py:374
  21.2 1.4 %collective-permute-start.12 = (bf16[512,128]{1,0:T(8,128)(2,1)S(1)}, bf16[512,128]{1,0:T(8,128)(2,1)S(1)}, u32[]{:S(2)}, u32[]{:S(2)}) collective-permute-start(bf16[512,128]{1,0:T(8,128)(2,1)S(1)} %collective-permute-done.7.refs_4_), channel_id=1, source_target_pairs={{0,1},{1,0},{4,8},{5,9},{8,12},{9,13},{12,14},{13,15},{14,10},{15,... | collective-permute-start | bytes 393224 | tf_op jit(solution)/shard_map/ppermute | solution.py:374
  22.6 0.2 collective-permute-done.11.refs_10_
  22.8 0.6 %collective-permute-done.9.refs_5_ = bf16[512,128]{1,0:T(8,128)(2,1)S(1)} collective-permute-done((bf16[512,128]{1,0:T(8,128)(2,1)S(1)}, bf16[512,128]{1,0:T(8,128)(2,1)S(1)}, u32[]{:S(2)}, u32[]{:S(2)}) %collective-permute-start.9) | collective-permute-done | bytes 131104 | tf_op jit(solution)/shard_map/ppermute | solution.py:362
  23.4 2.9 %attend.1 = (bf16[128,32,128]{2,1,0:T(8,128)(2,1)}, f32[4,1024,128]{2,1,0:T(8,128)S(1)}, f32[4,1024,256]{2,1,0:T(8,128)S(1)}) custom-call(s32[4,8]{1,0:T(4,128)S(1)} %get-tuple-element.30.lists_ref, bf16[4,1024,128]{2,1,0:T(8,128)(2,1)S(1)} %get-tuple-element.31.q_ref, bf16[4,128,128]{2,1,0:T(8,128)(2,1)S(1)} %get-tuple-element.32.k_own_ref, ...), custom_call_target="tpu_custom_call" | custom-call | tf_op jit(solution)/shard_map/attend/pallas_call | solution.py:251
  26.3 0.0 collective-permute-done.13.v_ref
  26.3 0.0 collective-permute-done.12.k_ref
  26.3 2.2 %attend_last.1 = bf16[128,32,128]{2,1,0:T(8,128)(2,1)} custom-call(s32[4,8]{1,0:T(4,128)S(1)} %get-tuple-element.30.lists_ref, bf16[4,1024,128]{2,1,0:T(8,128)(2,1)S(1)} %get-tuple-element.31.q_ref, f32[4,1024,128]{2,1,0:T(8,128)S(1)} %get-tuple-element.44.top_ref, f32[4,1024,256]{2,1,0:T(8,128)S(1)} %get-tuple-element.45.both_ref, ...), custom_call_target="tpu_custom_call", output_to_operand_aliasing={{}: (6, {})} | custom-call | tf_op jit(solution)/shard_map/attend_last/pallas_call | solution.py:323
  (1 shorter events, 0.0 us)
Async XLA Ops:
  0.0 5.7 %collective-permute-start = (bf16[512,128]{1,0:T(8,128)(2,1)}, bf16[512,128]{1,0:T(8,128)(2,1)S(1)}, u32[]{:S(2)}, u32[]{:S(2)}) collective-permute-start(bf16[512,128]{1,0:T(8,128)(2,1)} %bitcast.6), channel_id=1, source_target_pairs={{0,4},{4,8},{8,12},{12,14},{14,10},{10,6},{6,2},{2,0},{1,5},{5,9},... | collective-permute-start | bytes 393224 | tf_op jit(solution)/shard_map/ppermute | solution.py:362
  1.6 5.2 %collective-permute-start.1 = (bf16[512,128]{1,0:T(8,128)(2,1)}, bf16[512,128]{1,0:T(8,128)(2,1)S(1)}, u32[]{:S(2)}, u32[]{:S(2)}) collective-permute-start(bf16[512,128]{1,0:T(8,128)(2,1)} %bitcast.3), channel_id=1, source_target_pairs={{0,2},{4,0},{8,4},{12,8},{14,12},{10,14},{6,10},{2,6},{1,3},{5,1},... | collective-permute-start | bytes 393224 | tf_op jit(solution)/shard_map/ppermute | solution.py:362
  3.6 5.9 %collective-permute-start.2 = (bf16[512,128]{1,0:T(8,128)(2,1)}, bf16[512,128]{1,0:T(8,128)(2,1)S(1)}, u32[]{:S(2)}, u32[]{:S(2)}) collective-permute-start(bf16[512,128]{1,0:T(8,128)(2,1)} %bitcast.5), channel_id=1, source_target_pairs={{0,4},{4,8},{8,12},{12,14},{14,10},{10,6},{6,2},{2,0},{1,5},{5,9},... | collective-permute-start | bytes 393224 | tf_op jit(solution)/shard_map/ppermute | solution.py:362
  5.2 6.0 %collective-permute-start.3 = (bf16[512,128]{1,0:T(8,128)(2,1)}, bf16[512,128]{1,0:T(8,128)(2,1)S(1)}, u32[]{:S(2)}, u32[]{:S(2)}) collective-permute-start(bf16[512,128]{1,0:T(8,128)(2,1)} %bitcast.8), channel_id=1, source_target_pairs={{0,2},{4,0},{8,4},{12,8},{14,12},{10,14},{6,10},{2,6},{1,3},{5,1},... | collective-permute-start | bytes 393224 | tf_op jit(solution)/shard_map/ppermute | solution.py:362
  6.8 6.5 %collective-permute-start.5 = (bf16[512,128]{1,0:T(8,128)(2,1)S(1)}, bf16[512,128]{1,0:T(8,128)(2,1)S(1)}, u32[]{:S(2)}, u32[]{:S(2)}) collective-permute-start(bf16[512,128]{1,0:T(8,128)(2,1)S(1)} %collective-permute-done.1.refs_7_), channel_id=1, source_target_pairs={{0,2},{4,0},{8,4},{12,8},{14,12},{10,14},{6,10},{2,6},{1,3},{5,1},... | collective-permute-start | bytes 393224 | tf_op jit(solution)/shard_map/ppermute | solution.py:362
  7.2 6.1 %collective-permute-start.4 = (bf16[512,128]{1,0:T(8,128)(2,1)S(1)}, bf16[512,128]{1,0:T(8,128)(2,1)S(1)}, u32[]{:S(2)}, u32[]{:S(2)}) collective-permute-start(bf16[512,128]{1,0:T(8,128)(2,1)S(1)} %collective-permute-done.refs_0_), channel_id=1, source_target_pairs={{0,4},{4,8},{8,12},{12,14},{14,10},{10,6},{6,2},{2,0},{1,5},{5,9},... | collective-permute-start | bytes 393224 | tf_op jit(solution)/shard_map/ppermute | solution.py:362
  11.3 5.5 %collective-permute-start.10 = (bf16[512,128]{1,0:T(8,128)(2,1)S(1)}, bf16[512,128]{1,0:T(8,128)(2,1)S(1)}, u32[]{:S(2)}, u32[]{:S(2)}) collective-permute-start(bf16[512,128]{1,0:T(8,128)(2,1)S(1)} %collective-permute-done.2.refs_6_), channel_id=1, source_target_pairs={{0,4},{4,8},{8,12},{12,14},{14,10},{10,6},{6,2},{2,0},{1,5},{5,9},... | collective-permute-start | bytes 393224 | tf_op jit(solution)/shard_map/ppermute | solution.py:362
  12.8 5.2 %collective-permute-start.6 = (bf16[512,128]{1,0:T(8,128)(2,1)S(1)}, bf16[512,128]{1,0:T(8,128)(2,1)S(1)}, u32[]{:S(2)}, u32[]{:S(2)}) collective-permute-start(bf16[512,128]{1,0:T(8,128)(2,1)S(1)} %collective-permute-done.3.refs_1_), channel_id=1, source_target_pairs={{0,2},{4,0},{8,4},{12,8},{14,12},{10,14},{6,10},{2,6},{1,3},{5,1},... | collective-permute-start | bytes 393224 | tf_op jit(solution)/shard_map/ppermute | solution.py:362
  13.3 7.4 %collective-permute-start.8 = (bf16[512,128]{1,0:T(8,128)(2,1)S(1)}, bf16[512,128]{1,0:T(8,128)(2,1)S(1)}, u32[]{:S(2)}, u32[]{:S(2)}) collective-permute-start(bf16[512,128]{1,0:T(8,128)(2,1)S(1)} %collective-permute-done.5.refs_9_), channel_id=1, source_target_pairs={{0,2},{4,0},{8,4},{12,8},{14,12},{10,14},{6,10},{2,6},{1,3},{5,1},... | collective-permute-start | bytes 393224 | tf_op jit(solution)/shard_map/ppermute | solution.py:362
  13.7 6.9 %collective-permute-start.7 = (bf16[512,128]{1,0:T(8,128)(2,1)S(1)}, bf16[512,128]{1,0:T(8,128)(2,1)S(1)}, u32[]{:S(2)}, u32[]{:S(2)}) collective-permute-start(bf16[512,128]{1,0:T(8,128)(2,1)S(1)} %collective-permute-done.4.refs_2_), channel_id=1, source_target_pairs={{0,4},{4,8},{8,12},{12,14},{14,10},{10,6},{6,2},{2,0},{1,5},{5,9},... | collective-permute-start | bytes 393224 | tf_op jit(solution)/shard_map/ppermute | solution.py:362
  16.8 6.0 %collective-permute-start.11 = (bf16[512,128]{1,0:T(8,128)(2,1)S(1)}, bf16[512,128]{1,0:T(8,128)(2,1)S(1)}, u32[]{:S(2)}, u32[]{:S(2)}) collective-permute-start(bf16[512,128]{1,0:T(8,128)(2,1)S(1)} %collective-permute-done.10.refs_8_), channel_id=1, source_target_pairs={{0,4},{4,8},{8,12},{12,14},{14,10},{10,6},{6,2},{2,0},{1,5},{5,9},... | collective-permute-start | bytes 393224 | tf_op jit(solution)/shard_map/ppermute | solution.py:362
  18.0 5.4 %collective-permute-start.9 = (bf16[512,128]{1,0:T(8,128)(2,1)S(1)}, bf16[512,128]{1,0:T(8,128)(2,1)S(1)}, u32[]{:S(2)}, u32[]{:S(2)}) collective-permute-start(bf16[512,128]{1,0:T(8,128)(2,1)S(1)} %collective-permute-done.6.refs_3_), channel_id=1, source_target_pairs={{0,2},{4,0},{8,4},{12,8},{14,12},{10,14},{6,10},{2,6},{1,3},{5,1},... | collective-permute-start | bytes 393224 | tf_op jit(solution)/shard_map/ppermute | solution.py:362
  20.7 5.6 %collective-permute-start.13 = (bf16[512,128]{1,0:T(8,128)(2,1)S(1)}, bf16[512,128]{1,0:T(8,128)(2,1)S(1)}, u32[]{:S(2)}, u32[]{:S(2)}) collective-permute-start(bf16[512,128]{1,0:T(8,128)(2,1)S(1)} %fusion.1), channel_id=1, source_target_pairs={{0,1},{1,0},{4,6},{5,7},{8,10},{9,11},{12,4},{13,5},{14,12},{15,13... | collective-permute-start | bytes 393224 | tf_op jit(solution)/shard_map/ppermute | solution.py:374
  21.2 5.1 %collective-permute-start.12 = (bf16[512,128]{1,0:T(8,128)(2,1)S(1)}, bf16[512,128]{1,0:T(8,128)(2,1)S(1)}, u32[]{:S(2)}, u32[]{:S(2)}) collective-permute-start(bf16[512,128]{1,0:T(8,128)(2,1)S(1)} %collective-permute-done.7.refs_4_), channel_id=1, source_target_pairs={{0,1},{1,0},{4,8},{5,9},{8,12},{9,13},{12,14},{13,15},{14,10},{15,... | collective-permute-start | bytes 393224 | tf_op jit(solution)/shard_map/ppermute | solution.py:374
